TPU v7x, 32 devices: a whole 2x2x4 slice. The times are simulated.
32 devices in a mesh: ctx: 8 (over y, x, core), head: 4 (over z).
Axes of the slice: x: 2, y: 2, z: 4, core: 2. Of those that a mesh axis runs over, the one named last changes fastest.
Arguments:
- q_lin: float32 [2048, 4096], P('ctx', 'head'), may hold values from -6 to 6
- k_lin: float32 [2048, 4096], P('ctx', 'head'), may hold values from -0.9722718 to 0.9722718
- v_lin: float32 [2048, 4096], P('ctx', 'head'), may hold values from -201 to 201
- log_decay: float32 [32, 2048], P('head', 'ctx'), may hold values from -1 to 0
- lin_gain: float32 [4096], P('head'), may hold values from 0.1 to 1.9
- q_soft: float32 [2048, 6144], P('ctx', 'head'), may hold values from -36 to 36
- k_soft: float32 [2048, 1024], P('ctx', 'head'), may hold values from -4 to 4
- v_soft: float32 [2048, 1024], P('ctx', 'head'), may hold values from -6 to 6
Outputs:
- lin_out: float32 [2048, 4096], P('ctx', 'head')
- soft_out: float32 [2048, 6144], P('ctx', 'head')
All inputs are finite; a program needn't handle non-finite values.
Results may differ from a plain program's by a relative error of at most 0.0003.
Values sent between devices are 32-bit elements; how exact they have to be, the bound alone decides.
No kernel may reach another device: no remote copies, remote signals or barrier semaphores. Data moves between devices by JAX's collectives and lax.ppermute only.
A program may use at most 128 MiB of HBM per device.

v0:
```python
import math

import jax
import jax.numpy as jnp
from jax import lax
from jax.sharding import PartitionSpec as P

HD = 128
LH = 32


HIGHEST = lax.Precision.HIGHEST
NEGATIVE = -1e30
EPSILON = 1e-05


def entering(value, axis, combine, identity):
    count, mine = (lax.axis_size(axis), lax.axis_index(axis))
    everything = jax.tree.map(lambda part: lax.all_gather(part, axis), value)
    start = jax.tree.map(
        lambda part, zero: jnp.broadcast_to(jnp.asarray(zero, part.dtype), part.shape),
        value,
        identity,
    )

    def turn(k, before):
        reached = k < mine
        new = combine(before, jax.tree.map(lambda part: part[k], everything))
        return jax.tree.map(lambda a, b: jnp.where(reached, a, b), new, before)

    return lax.fori_loop(0, count, turn, start)


def block_terms(queries, key_rows, value_rows, log_rates):
    length = queries.shape[0]
    cumulative = jnp.cumsum(log_rates, axis=1)
    positions = jnp.arange(length)
    causal = (positions[:, None] >= positions[None, :])[None]
    decay_gaps = cumulative[:, :, None] - cumulative[:, None, :]
    weights = jnp.where(causal, jnp.exp(jnp.where(causal, decay_gaps, 0.0)), 0.0)
    scores = jnp.einsum("thd,shd->hts", queries, key_rows, precision=HIGHEST)
    inside = jnp.einsum("hts,shd->thd", scores * weights, value_rows, precision=HIGHEST)
    block_total = cumulative[:, -1]
    trailing = jnp.exp(block_total[:, None] - cumulative)
    scaled_keys = key_rows * jnp.transpose(trailing)[:, :, None]
    local_state = jnp.einsum("shd,she->hde", scaled_keys, value_rows, precision=HIGHEST)
    leading = jnp.transpose(jnp.exp(cumulative))[:, :, None]
    return (inside, leading, block_total, local_state)


def attend(partial_value, query_rows, query_pos, key_slab, value_slab, key_pos, score_scale):
    old_max, old_total, weighted = partial_value
    scores = jnp.einsum("tkgd,skd->kgts", query_rows, key_slab, precision=HIGHEST) * score_scale
    visible = (key_pos[None, :] <= query_pos[:, None])[None, None]
    scores = jnp.where(visible, scores, NEGATIVE)
    new_max = jnp.maximum(old_max, jnp.max(scores, axis=3))
    weights = jnp.where(visible, jnp.exp(scores - new_max[..., None]), 0.0)
    shrink = jnp.exp(old_max - new_max)
    new_total = old_total * shrink + jnp.sum(weights, axis=3)
    weighted = weighted * shrink[..., None] + jnp.einsum(
        "kgts,skd->kgtd", weights, value_slab, precision=HIGHEST
    )
    return (new_max, new_total, weighted)


def soft_layer(query_sets, k_soft, v_soft, score_scale):
    kv_heads = k_soft.shape[1] // HD
    initial = []
    for query_rows, query_pos in query_sets:
        shape = (query_rows.shape[1], query_rows.shape[2], query_rows.shape[0])
        initial.append(
            (
                jnp.full(shape, NEGATIVE, jnp.float32),
                jnp.zeros(shape, jnp.float32),
                jnp.zeros(shape + (HD,), jnp.float32),
            )
        )
    initial = tuple(initial)
    key_rows = lax.all_gather(k_soft, "ctx", axis=0, tiled=True)
    value_rows = lax.all_gather(v_soft, "ctx", axis=0, tiled=True)
    shard_rows = key_rows.shape[0]
    key_block = math.gcd(shard_rows, 512)
    key_rows = key_rows.reshape(shard_rows // key_block, key_block, kv_heads, HD)
    value_rows = value_rows.reshape(shard_rows // key_block, key_block, kv_heads, HD)

    def visit(block_index, partials):
        key_slab = lax.dynamic_index_in_dim(key_rows, block_index, 0, keepdims=False)
        value_slab = lax.dynamic_index_in_dim(value_rows, block_index, 0, keepdims=False)
        first_key = block_index * key_block
        key_pos = first_key + jnp.arange(key_block)
        updated = []
        for (query_rows, query_pos), partial_value in zip(query_sets, partials):

            def engage(current, query_rows=query_rows, query_pos=query_pos):
                return attend(
                    current, query_rows, query_pos, key_slab, value_slab, key_pos, score_scale
                )

            def remain(current):
                return current

            updated.append(lax.cond(first_key <= jnp.max(query_pos), engage, remain, partial_value))
        return tuple(updated)

    finals = lax.fori_loop(0, shard_rows // key_block, visit, initial)
    results = []
    for final in finals:
        maxima, totals, weighted = final
        merged = weighted / totals[..., None]
        row_count = merged.shape[2]
        results.append(jnp.transpose(merged, (2, 0, 1, 3)).reshape(row_count, -1))
    return results


def body(q_lin, k_lin, v_lin, log_decay, lin_gain, q_soft, k_soft, v_soft):
    row_count = q_lin.shape[0]
    head_count = log_decay.shape[0]
    position = lax.axis_index("ctx")
    queries = q_lin.reshape(row_count, head_count, HD)
    key_rows = k_lin.reshape(row_count, head_count, HD)
    value_rows = v_lin.reshape(row_count, head_count, HD)
    inside, leading, block_total, local_state = block_terms(
        queries, key_rows, value_rows, log_decay
    )

    def chain_step(earlier, later):
        return (earlier[0] + later[0], jnp.exp(later[0])[:, None, None] * earlier[1] + later[1])

    identity = (jnp.zeros_like(block_total), jnp.zeros_like(local_state))
    prefix_pair = entering((block_total, local_state), "ctx", chain_step, identity)
    prior_state = prefix_pair[1]
    linear = inside + leading * jnp.einsum("thd,hde->the", queries, prior_state, precision=HIGHEST)
    linear = linear.reshape(row_count, head_count * HD)
    energy = lax.psum(jnp.sum(linear * linear, axis=1, keepdims=True), "head")
    lin_out = linear * lax.rsqrt(energy / (LH * HD) + EPSILON) * lin_gain
    score_scale = 1.0 / math.sqrt(HD)
    kv_heads = k_soft.shape[1] // HD
    group_size = q_soft.shape[1] // (kv_heads * HD)
    soft_queries = q_soft.reshape(row_count, kv_heads, group_size, HD)
    query_pos = position * row_count + jnp.arange(row_count)
    soft_out = soft_layer([(soft_queries, query_pos)], k_soft, v_soft, score_scale)[0]
    return (lin_out, soft_out)


def solution(mesh):
    return jax.shard_map(
        body,
        mesh=mesh,
        in_specs=(
            P("ctx", "head"),
            P("ctx", "head"),
            P("ctx", "head"),
            P("head", "ctx"),
            P("head"),
            P("ctx", "head"),
            P("ctx", "head"),
            P("ctx", "head"),
        ),
        out_specs=(P("ctx", "head"), P("ctx", "head")),
        check_vma=False,
    )
```

profile of v0, /device:TPU:6, one launch (start us, length us, event | category | flops | bytes accessed | tf_op | source)
XLA Modules:
  0.0 208.5 jit_solution(15325372133794225744)
XLA Ops:
  7.2 0.7 all-gather.6.cloned.1.call-update
  8.0 0.7 all-gather.8.cloned.1.call-update
  8.7 1.3 reduce-window.6
  10.0 0.2 slice_reduce_fusion
  10.2 1.6 copy.69
  11.8 0.2 slice_reduce_fusion.1
  12.1 2.0 fusion.35
  14.2 0.6 dynamic-slice
  15.4 0.2 dynamic-update-slice
  15.7 10.2 %all-reduce = f32[64]{0:T(128)S(1)} all-reduce(f32[64]{0:T(128)S(1)} %dynamic-update-slice), channel_id=2, replica_groups=mesh['ctx'=8,'head'=4] {'ctx'}, use_global_device_ids=true, to_apply=%add | all-reduce | flops 64 | bytes 512
  26.0 0.7 add_reduce_fusion
  26.7 3.0 %copy.59 = f32[256,1536]{0,1:T(8,128)} copy(f32[256,1536]{1,0:T(8,128)} %param.19) | data formatting | bytes 3145728 | tf_op args[5]
  29.7 1.9 copy.61
  31.7 4.4 %fusion.38 = f32[8,256,256]{2,1,0:T(8,128)} fusion(f32[256,8,128]{0,2,1:T(8,128)} %bitcast.91, f32[256,1024]{1,0:T(8,128)S(1)} %copy-done), kind=kOutput, calls=%fused_computation.44 | convolution fusion | flops 805306368 | bytes 4194304 | tf_op jit(solution)/shard_map/thd,shd->hts/dot_general | solution.py:41
  36.0 2.1 %all-gather.6.cloned.1.call-done = f32[2048,256]{1,0:T(8,128)} async-done(((f32[256,256]{1,0:T(8,128)}), f32[2048,256]{1,0:T(8,128)}) %all-gather.6.cloned.1.call-update) | async-done | bytes 2097168 | tf_op jit(solution)/shard_map/all_gather | solution.py:79
  38.2 3.2 %reshape.121 = f32[4,512,2,128]{3,2,1,0:T(2,128)} reshape(f32[2048,256]{1,0:T(8,128)} %all-gather.6.cloned.1.call-done) | data formatting | bytes 4194304 | tf_op jit(solution)/shard_map/reshape | solution.py:83
  41.4 3.1 %copy.60 = f32[4,512,2,128]{3,1,2,0:T(8,128)} copy(f32[4,512,2,128]{3,2,1,0:T(2,128)} %reshape.121) | data formatting | bytes 4194304
  44.5 23.5 %all-gather.8.cloned.1.call-done = f32[2048,256]{1,0:T(8,128)} async-done(((f32[256,256]{1,0:T(8,128)}), f32[2048,256]{1,0:T(8,128)}) %all-gather.8.cloned.1.call-update) | async-done | bytes 2097168 | tf_op jit(solution)/shard_map/all_gather | solution.py:80
  68.0 3.2 %reshape.123 = f32[4,512,2,128]{3,2,1,0:T(2,128)} reshape(f32[2048,256]{1,0:T(8,128)} %all-gather.8.cloned.1.call-done) | data formatting | bytes 4194304 | tf_op jit(solution)/shard_map/reshape | solution.py:84
  71.2 3.1 %copy.62 = f32[4,512,2,128]{3,1,2,0:T(8,128)} copy(f32[4,512,2,128]{3,2,1,0:T(2,128)} %reshape.123) | data formatting | bytes 4194304
  74.4 1.3 broadcast_in_dim.87
  75.7 90.8 %while.33 = (s32[]{:T(128)}, f32[2,6,256]{2,1,0:T(8,128)S(1)}, f32[2,6,256]{2,1,0:T(8,128)S(1)}, f32[2,6,256,128]{3,2,1,0:T(8,128)}, s32[]{:T(128)}, /*index=5*/...) while((s32[]{:T(128)}, f32[2,6,256]{2,1,0:T(8,128)S(1)}, ...), condition=%wide.region_12.13_spmd.clone, body=%wide.region_7.0_spmd.clone.sunk | while | flops 4851637248 | bytes 37959000 | solution.py:105
  76.3 22.1 %conditional.3 = ((f32[2,6,256]{2,1,0:T(8,128)S(1)}, f32[2,6,256]{2,1,0:T(8,128)S(1)}, f32[2,6,256,128]{3,2,1,0:T(8,128)})) conditional(s32[]{:T(128)} %convert_element_type.10, (f32[2,6,256]{2,1,0:T(8,128)S(1)}, f32[2,6,256]{2,1,0:T(8,128)S(1)}, f32[2,6,256,128]{3,2,1,0:T(8,128)}) %tuple.98, (s32[]{:T(128)}, s32[512]{0:T(512)S(1)}, s32[]{:T(128)}, ...), branch_computations={%region_8.8_spmd, %region_9.11_spmd} | conditional | flops 4851637248 | bytes 37955680 | solution.py:102
  76.3 0.1 broadcast_compare_fusion
  76.5 6.9 %fusion.2 = (f32[2,6,256]{2,1,0:T(8,128)S(1)}, f32[2,512,256,6]{2,1,3,0:T(8,128)S(1)}) fusion(pred[256,512]{0,1:T(8,128)(4,1)S(1)} %broadcast_compare_fusion, f32[256,2,6,128]{3,0,2,1:T(8,128)S(1)} %get-tuple-element.399, f32[4,512,2,128]{3,1,2,0:T(8,128)} %get-tuple-element.397, s32[]{:T(128)} %get-tuple-element.398), kind=kOutput, calls=%fused_computation.3 | convolution fusion | flops 2420634624 | bytes 8532480 | tf_op jit(solution)/shard_map/while/body/eval_jaxpr/cond/branch_1_fun/tkgd,skd->kgts/dot_general | solution.py:53
  83.5 1.5 fusion.4
  85.0 12.2 %multiply_add_fusion = f32[2,6,256,128]{3,2,1,0:T(8,128)S(1)} fusion(f32[2,6,256,128]{3,2,1,0:T(8,128)S(1)} %copy-done.3, f32[2,512,256,6]{2,1,3,0:T(8,128)S(1)} %get-tuple-element.535, f32[2,6,256]{2,1,0:T(8,128)S(1)} %max.6, pred[256,512]{0,1:T(8,128)(4,1)S(1)} %broadcast_compare_fusion, f32[2,6,256]{2,1,0:T(8,128)S(1)} %get-tuple-element.531, ...), kind=kOutput, calls=%fused_computation.11 | convolution fusion | flops 2422996992 | bytes 10117632 | tf_op jit(solution)/shard_map/while/body/eval_jaxpr/cond/branch_1_fun/kgts,skd->kgtd/dot_general | solution.py:60
  97.2 1.1 copy-done.4
  99.0 22.1 %conditional.3 = ((f32[2,6,256]{2,1,0:T(8,128)S(1)}, f32[2,6,256]{2,1,0:T(8,128)S(1)}, f32[2,6,256,128]{3,2,1,0:T(8,128)})) conditional(s32[]{:T(128)} %convert_element_type.10, (f32[2,6,256]{2,1,0:T(8,128)S(1)}, f32[2,6,256]{2,1,0:T(8,128)S(1)}, f32[2,6,256,128]{3,2,1,0:T(8,128)}) %tuple.98, (s32[]{:T(128)}, s32[512]{0:T(512)S(1)}, s32[]{:T(128)}, ...), branch_computations={%region_8.8_spmd, %region_9.11_spmd} | conditional | flops 4851637248 | bytes 37955680 | solution.py:102
  99.0 0.1 broadcast_compare_fusion
  99.2 6.9 %fusion.2 = (f32[2,6,256]{2,1,0:T(8,128)S(1)}, f32[2,512,256,6]{2,1,3,0:T(8,128)S(1)}) fusion(pred[256,512]{0,1:T(8,128)(4,1)S(1)} %broadcast_compare_fusion, f32[256,2,6,128]{3,0,2,1:T(8,128)S(1)} %get-tuple-element.399, f32[4,512,2,128]{3,1,2,0:T(8,128)} %get-tuple-element.397, s32[]{:T(128)} %get-tuple-element.398), kind=kOutput, calls=%fused_computation.3 | convolution fusion | flops 2420634624 | bytes 8532480 | tf_op jit(solution)/shard_map/while/body/eval_jaxpr/cond/branch_1_fun/tkgd,skd->kgts/dot_general | solution.py:53
  106.1 1.5 fusion.4
  107.7 12.2 %multiply_add_fusion = f32[2,6,256,128]{3,2,1,0:T(8,128)S(1)} fusion(f32[2,6,256,128]{3,2,1,0:T(8,128)S(1)} %copy-done.3, f32[2,512,256,6]{2,1,3,0:T(8,128)S(1)} %get-tuple-element.535, f32[2,6,256]{2,1,0:T(8,128)S(1)} %max.6, pred[256,512]{0,1:T(8,128)(4,1)S(1)} %broadcast_compare_fusion, f32[2,6,256]{2,1,0:T(8,128)S(1)} %get-tuple-element.531, ...), kind=kOutput, calls=%fused_computation.11 | convolution fusion | flops 2422996992 | bytes 10117632 | tf_op jit(solution)/shard_map/while/body/eval_jaxpr/cond/branch_1_fun/kgts,skd->kgtd/dot_general | solution.py:60
  119.9 1.1 copy-done.4
  121.7 22.1 %conditional.3 = ((f32[2,6,256]{2,1,0:T(8,128)S(1)}, f32[2,6,256]{2,1,0:T(8,128)S(1)}, f32[2,6,256,128]{3,2,1,0:T(8,128)})) conditional(s32[]{:T(128)} %convert_element_type.10, (f32[2,6,256]{2,1,0:T(8,128)S(1)}, f32[2,6,256]{2,1,0:T(8,128)S(1)}, f32[2,6,256,128]{3,2,1,0:T(8,128)}) %tuple.98, (s32[]{:T(128)}, s32[512]{0:T(512)S(1)}, s32[]{:T(128)}, ...), branch_computations={%region_8.8_spmd, %region_9.11_spmd} | conditional | flops 4851637248 | bytes 37955680 | solution.py:102
  121.7 0.1 broadcast_compare_fusion
  121.9 6.9 %fusion.2 = (f32[2,6,256]{2,1,0:T(8,128)S(1)}, f32[2,512,256,6]{2,1,3,0:T(8,128)S(1)}) fusion(pred[256,512]{0,1:T(8,128)(4,1)S(1)} %broadcast_compare_fusion, f32[256,2,6,128]{3,0,2,1:T(8,128)S(1)} %get-tuple-element.399, f32[4,512,2,128]{3,1,2,0:T(8,128)} %get-tuple-element.397, s32[]{:T(128)} %get-tuple-element.398), kind=kOutput, calls=%fused_computation.3 | convolution fusion | flops 2420634624 | bytes 8532480 | tf_op jit(solution)/shard_map/while/body/eval_jaxpr/cond/branch_1_fun/tkgd,skd->kgts/dot_general | solution.py:53
  128.8 1.5 fusion.4
  130.4 12.2 %multiply_add_fusion = f32[2,6,256,128]{3,2,1,0:T(8,128)S(1)} fusion(f32[2,6,256,128]{3,2,1,0:T(8,128)S(1)} %copy-done.3, f32[2,512,256,6]{2,1,3,0:T(8,128)S(1)} %get-tuple-element.535, f32[2,6,256]{2,1,0:T(8,128)S(1)} %max.6, pred[256,512]{0,1:T(8,128)(4,1)S(1)} %broadcast_compare_fusion, f32[2,6,256]{2,1,0:T(8,128)S(1)} %get-tuple-element.531, ...), kind=kOutput, calls=%fused_computation.11 | convolution fusion | flops 2422996992 | bytes 10117632 | tf_op jit(solution)/shard_map/while/body/eval_jaxpr/cond/branch_1_fun/kgts,skd->kgtd/dot_general | solution.py:60
  142.6 1.1 copy-done.4
  144.4 22.1 %conditional.3 = ((f32[2,6,256]{2,1,0:T(8,128)S(1)}, f32[2,6,256]{2,1,0:T(8,128)S(1)}, f32[2,6,256,128]{3,2,1,0:T(8,128)})) conditional(s32[]{:T(128)} %convert_element_type.10, (f32[2,6,256]{2,1,0:T(8,128)S(1)}, f32[2,6,256]{2,1,0:T(8,128)S(1)}, f32[2,6,256,128]{3,2,1,0:T(8,128)}) %tuple.98, (s32[]{:T(128)}, s32[512]{0:T(512)S(1)}, s32[]{:T(128)}, ...), branch_computations={%region_8.8_spmd, %region_9.11_spmd} | conditional | flops 4851637248 | bytes 37955680 | solution.py:102
  144.4 0.1 broadcast_compare_fusion
  144.6 6.9 %fusion.2 = (f32[2,6,256]{2,1,0:T(8,128)S(1)}, f32[2,512,256,6]{2,1,3,0:T(8,128)S(1)}) fusion(pred[256,512]{0,1:T(8,128)(4,1)S(1)} %broadcast_compare_fusion, f32[256,2,6,128]{3,0,2,1:T(8,128)S(1)} %get-tuple-element.399, f32[4,512,2,128]{3,1,2,0:T(8,128)} %get-tuple-element.397, s32[]{:T(128)} %get-tuple-element.398), kind=kOutput, calls=%fused_computation.3 | convolution fusion | flops 2420634624 | bytes 8532480 | tf_op jit(solution)/shard_map/while/body/eval_jaxpr/cond/branch_1_fun/tkgd,skd->kgts/dot_general | solution.py:53
  151.5 1.5 fusion.4
  153.1 12.2 %multiply_add_fusion = f32[2,6,256,128]{3,2,1,0:T(8,128)S(1)} fusion(f32[2,6,256,128]{3,2,1,0:T(8,128)S(1)} %copy-done.3, f32[2,512,256,6]{2,1,3,0:T(8,128)S(1)} %get-tuple-element.535, f32[2,6,256]{2,1,0:T(8,128)S(1)} %max.6, pred[256,512]{0,1:T(8,128)(4,1)S(1)} %broadcast_compare_fusion, f32[2,6,256]{2,1,0:T(8,128)S(1)} %get-tuple-element.531, ...), kind=kOutput, calls=%fused_computation.11 | convolution fusion | flops 2422996992 | bytes 10117632 | tf_op jit(solution)/shard_map/while/body/eval_jaxpr/cond/branch_1_fun/kgts,skd->kgtd/dot_general | solution.py:60
  165.3 1.1 copy-done.4
  166.4 1.9 copy.63
  168.3 1.3 broadcast_divide_fusion
  169.6 3.0 %copy.64 = f32[256,1536]{1,0:T(8,128)} copy(f32[256,1536]{0,1:T(8,128)} %bitcast.92) | data formatting | bytes 3145728
  172.7 9.8 %while.34 = (s32[]{:T(128)}, f32[8,128,128]{2,1,0:T(8,128)S(1)}, s32[]{:T(128)}, f32[8,8]{1,0:T(8,128)S(1)}, f32[8,8,128,128]{3,2,1,0:T(8,128)}, /*index=5*/s32[]{:T(128)}, s32[]{:T(128)}) while((s32[]{:T(128)}, f32[8,128,128]{2,1,0:T(8,128)S(1)}, s32[]{:T(128)}, f32[8,8]{1,0:T(8,128)S(1)}, f32[8,8,128,128]{3,2,1,0:T(8,128)}, ...), condition=%wide.region_3.4_spmd.clone, body=%wide.region_2.3_spmd.clone.sunk | while | flops 524292 | bytes 1573065 | solution.py:31
  172.7 1.3 fusion.59
  174.0 1.2 fusion.59
  175.2 1.2 fusion.59
  176.4 1.2 fusion.59
  177.6 1.2 fusion.59
  178.8 1.2 fusion.59
  180.0 1.2 fusion.59
  181.2 1.2 fusion.59
  182.4 1.1 fusion.33
  183.5 0.5 copy-done.2
  184.0 3.6 %multiply_reduce_fusion = (f32[256]{0:T(256)S(1)}, f32[256,8,128]{0,2,1:T(8,128)}) fusion(f32[256,8,128]{0,2,1:T(8,128)S(1)} %fusion.33, f32[8,256,256]{2,1,0:T(8,128)S(1)} %copy-done.2, f32[8,256]{1,0:T(8,128)S(1)} %get-tuple-element.533, pred[256,256]{1,0:T(8,128)(4,1)S(1)} %iota_compare_fusion, f32[256,1024]{1,0:T(8,128)S(1)} %copy-done.6), kind=kOutput, calls=%fused_computation.47 | convolution fusion | flops 808189696 | bytes 5317632 | tf_op jit(solution)/shard_map/hts,shd->thd/dot_general | solution.py:42
  187.6 1.6 copy.58
  189.2 11.7 %psum.7 = f32[256,1]{0,1:T(1,128)S(1)} all-reduce(f32[256,1]{0,1:T(1,128)S(1)} %bitcast.97), channel_id=1, replica_groups=mesh['ctx'=8,'head'=4] {'head'}, use_global_device_ids=true, to_apply=%region_5.6 | all-reduce | flops 256 | bytes 2048 | tf_op jit(solution)/shard_map/psum | solution.py:134
  200.9 1.1 multiply_multiply_fusion
  (77 shorter events, 0.8 us)
Async XLA Ops:
  7.2 24.5 %copy-start = (f32[256,1024]{1,0:T(8,128)S(1)}, f32[256,1024]{1,0:T(8,128)}, u32[]{:S(2)}) copy-start(f32[256,1024]{1,0:T(8,128)} %param.14) | copy-start | bytes 3145732
  7.2 4.9 %copy-start.5 = (f32[256,1024]{1,0:T(8,128)S(1)}, f32[256,1024]{1,0:T(8,128)}, u32[]{:S(2)}) copy-start(f32[256,1024]{1,0:T(8,128)} %param.16) | copy-start | bytes 3145732
  7.2 31.0 %all-gather.6.cloned.1.call-start = ((), (), s32[]{:S(2)}) async-start(), calls=%async_computation | async-start | bytes 2359296 | tf_op jit(solution)/shard_map/all_gather | solution.py:79
  7.9 60.1 %all-gather.8.cloned.1.call-start = ((), (), s32[]{:S(2)}) async-start(), calls=%async_computation.1 | async-start | bytes 2359296 | tf_op jit(solution)/shard_map/all_gather | solution.py:80
  8.7 164.0 %all-gather.10.cloned.1.call-start = ((), (), s32[]{:S(2)}) async-start(), calls=%async_computation.2 | async-start | bytes 4718592 | tf_op jit(solution)/shard_map/all_gather | solution.py:19
  11.7 2.4 %copy-start.1 = (f32[256,1024]{0,1:T(8,128)}, f32[256,1024]{0,1:T(8,128)S(1)}, u32[]{:S(2)}) copy-start(f32[256,1024]{0,1:T(8,128)S(1)} %copy.69) | copy-start | bytes 3145732
  11.7 2.4 %copy-start.8 = (u32[32]{0:T(128)S(1)}, u32[32]{0:T(128)}, u32[]{:S(2)}) copy-start(u32[32]{0:T(128)} %constant.131) | copy-start | bytes 388
  83.4 1.5 copy-start.3
  97.2 1.1 copy-start.4
  106.1 1.5 copy-start.3
  119.9 1.1 copy-start.4
  128.8 1.5 copy-start.3
  142.6 1.1 copy-start.4
  151.5 1.5 copy-start.3
  165.3 1.1 copy-start.4
  172.7 10.9 %copy-start.6 = (f32[256,1024]{1,0:T(8,128)S(1)}, f32[256,1024]{1,0:T(8,128)}, u32[]{:S(2)}) copy-start(f32[256,1024]{1,0:T(8,128)} %param.16) | copy-start | bytes 3145732
  182.4 1.6 copy-start.2
  187.6 13.3 %copy-start.7 = (f32[1024]{0:T(1024)S(1)}, f32[1024]{0:T(1024)}, u32[]{:S(2)}) copy-start(f32[1024]{0:T(1024)} %param.18) | copy-start | bytes 12292
Sparse Core Ops, SparseCore 0:
  9.9 28.2 all-gather.5
  40.1 27.8 all-gather.7
  69.9 36.7 all-gather.9
where the time goes:
time: 210 us; the launch traced here: 209 us
  matrix products  87.6 us (42%)
  local copies, waits for them, and re-layouts  33.3 us (16%)
  waiting for transfers between devices  27 us (13%)
  blocking collectives  21.9 us (10%)
  other arithmetic  20.8 us (10%)
  between operations  14.6 us (7%)
  loops' own time  3.18 us (2%)
    dot_general x4, matrix products, attend(): jnp.einsum('kgts,skd->kgtd', weights, value_slab, precision=HIGHEST)  48.9 us
    dot_general x4, matrix products, attend(): jnp.einsum('tkgd,skd->kgts', query_rows, key_slab, precision=HIGHEST)  27.7 us
    all_gather x1, waiting for transfers between devices, soft_layer(): value_rows = lax.all_gather(v_soft, 'ctx', axis=0, tiled=True)  23.5 us
    unnamed x22, local copies, waits for them, and re-layouts  15.5 us
    psum x1, blocking collectives, body(): energy = lax.psum(jnp.sum(linear * linear, axis=1, keepdims=True), 'head')  11.7 us
    unnamed x1, blocking collectives  10.2 us
    select_n x8, other arithmetic, turn(): return jax.tree.map(lambda a, b: jnp.where(reached, a, b), new, before)  9.47 us
    reduce_sum x4, other arithmetic, attend(): new_total = old_total * shrink + jnp.sum(weights, axis=3)  6.01 us
  transfers between devices with their start and end apart: 3, of which 2 were waited for; matrix products, arithmetic and copies ran while one was open for 57% of the time, Pallas kernels for 0%

commit v1 on v0

v1 whole, which is shorter than its diff:
```python
import functools
import math

import jax
import jax.numpy as jnp
from jax import lax
from jax.experimental import pallas as pl
from jax.experimental.pallas import tpu as pltpu
from jax.sharding import PartitionSpec as P

HD = 128
NEGATIVE = -1e30
EPSILON = 1e-05
F32 = jnp.float32
BF16 = jnp.bfloat16
NT = (((1,), (1,)), ((), ()))
VMEM_LIMIT = 32 * 1024 * 1024


def split(x):
    high = x.astype(BF16)
    low = (x - high.astype(F32)).astype(BF16)
    return high, low


def dot(a, b):
    return jnp.dot(a, b, preferred_element_type=F32)


def three_term(a, b):
    a_high, a_low = split(a)
    b_high, b_low = split(b)
    wide = dot(a_high, jnp.concatenate([b_high, b_low], axis=1))
    n = b.shape[1]
    return wide[:, :n] + wide[:, n:] + dot(a_low, b_high)


def three_term_nt(a, b):
    a_high, a_low = split(a)
    b_high, b_low = split(b)
    left = jnp.concatenate([a_high, a_low, a_high], axis=1)
    right = jnp.concatenate([b_high, b_high, b_low], axis=1)
    return lax.dot_general(left, right, NT, preferred_element_type=F32)


def column(array, lane):
    lanes = lax.broadcasted_iota(jnp.int32, array.shape, 1)
    return jnp.sum(jnp.where(lanes == lane, array, 0.0), axis=1, keepdims=True)


def cost(flops, size, exps=0):
    return pl.CostEstimate(flops=int(flops), bytes_accessed=int(size), transcendentals=int(exps))


def smem():
    return pl.BlockSpec(memory_space=pltpu.SMEM)


def call(kernel, grid, in_specs, out_specs, out_shape, estimate, scratch=()):
    return pl.pallas_call(
        kernel,
        grid=grid,
        in_specs=in_specs,
        out_specs=out_specs,
        out_shape=out_shape,
        scratch_shapes=list(scratch),
        cost_estimate=estimate,
        compiler_params=pltpu.CompilerParams(
            dimension_semantics=("arbitrary",) * len(grid), vmem_limit_bytes=VMEM_LIMIT
        ),
    )


def state_kernel(half, rate_ref, k_ref, v_ref, state_ref, col_ref, row_ref):
    step = pl.program_id(0)
    rows = k_ref.shape[0]

    @pl.when(step == 0)
    def _():
        upto = lax.broadcasted_iota(jnp.int32, (rows, rows), 0)
        upto = (upto >= lax.broadcasted_iota(jnp.int32, (rows, rows), 1)).astype(F32)
        rates = rate_ref[...]
        heads = rates.shape[0]
        row_ref[...] = lax.dot_general(
            rates, upto, NT, precision=lax.Precision.HIGHEST, preferred_element_type=F32
        )
        padded = jnp.concatenate([rates, jnp.zeros((HD - heads, rows), F32)], axis=0)
        col_ref[...] = lax.dot_general(
            upto, padded, NT, precision=lax.Precision.HIGHEST, preferred_element_type=F32
        )

    state_ref[0, half * HD :, :] = jnp.zeros((8, HD), F32)
    for i in range(half):
        cumulative = column(col_ref[...], step * half + i)
        total = cumulative[rows - 1 : rows, :]
        scaled = k_ref[:, i * HD : (i + 1) * HD] * jnp.exp(total - cumulative)
        state_ref[0, i * HD : (i + 1) * HD, :] = three_term(
            scaled.T, v_ref[:, i * HD : (i + 1) * HD]
        )
        state_ref[0, half * HD + i : half * HD + i + 1, :] = jnp.broadcast_to(total, (1, HD))


def local_states(k_lin, v_lin, rates):
    rows, width = k_lin.shape
    heads = rates.shape[0]
    half = heads // 2
    block = pl.BlockSpec((rows, half * HD), lambda j: (0, j))
    packed = half * HD + 8
    return call(
        functools.partial(state_kernel, half),
        (2,),
        [pl.BlockSpec((heads, rows), lambda j: (0, 0)), block, block],
        [
            pl.BlockSpec((1, packed, HD), lambda j: (j, 0, 0)),
            pl.BlockSpec((rows, HD), lambda j: (0, 0)),
            pl.BlockSpec((heads, rows), lambda j: (0, 0)),
        ],
        [
            jax.ShapeDtypeStruct((2, packed, HD), F32),
            jax.ShapeDtypeStruct((rows, HD), F32),
            jax.ShapeDtypeStruct((heads, rows), F32),
        ],
        cost(6 * rows * width * HD, 10 * rows * width, rows * heads),
    )(rates, k_lin, v_lin)


def inside_kernel(half, q_ref, k_ref, v_ref, col_ref, row_ref, out_ref):
    step = pl.program_id(0)
    rows = q_ref.shape[0]
    causal = lax.broadcasted_iota(jnp.int32, (rows, rows), 0) >= lax.broadcasted_iota(
        jnp.int32, (rows, rows), 1
    )
    for i in range(half):
        at = slice(i * HD, (i + 1) * HD)
        scores = three_term_nt(q_ref[:, at], k_ref[:, at])
        gaps = column(col_ref[...], step * half + i) - row_ref[pl.ds(step * half + i, 1), :]
        weights = jnp.where(causal, jnp.exp(jnp.where(causal, gaps, 0.0)), 0.0)
        out_ref[:, at] = three_term(scores * weights, v_ref[:, at])


def inside_blocks(q_lin, k_lin, v_lin, col, row):
    rows, width = q_lin.shape
    heads = row.shape[0]
    half = heads // 2
    block = pl.BlockSpec((rows, half * HD), lambda j: (0, j))
    return call(
        functools.partial(inside_kernel, half),
        (2,),
        [
            block,
            block,
            block,
            pl.BlockSpec((rows, HD), lambda j: (0, 0)),
            pl.BlockSpec((heads, rows), lambda j: (0, 0)),
        ],
        block,
        jax.ShapeDtypeStruct((rows, width), F32),
        cost(12 * rows * rows * width, 16 * rows * width, rows * rows * heads),
    )(q_lin, k_lin, v_lin, col, row)


def joined(half, first, second):
    decay = jnp.exp(second[half * HD :, :])
    parts = [
        first[i * HD : (i + 1) * HD] * decay[i : i + 1] + second[i * HD : (i + 1) * HD]
        for i in range(half)
    ]
    parts.append(first[half * HD :] + second[half * HD :])
    return jnp.concatenate(parts, axis=0)


def chip_kernel(half, core_ref, mine_ref, theirs_ref, out_ref):
    mine, theirs = mine_ref[0], theirs_ref[0]
    late = core_ref[0] == 1
    out_ref[...] = joined(half, jnp.where(late, theirs, mine), jnp.where(late, mine, theirs))


def chip_total(core, states, other):
    _, packed, _ = states.shape
    half = (packed - 8) // HD
    spec = pl.BlockSpec((1, packed, HD), lambda j, core: (core[0], 0, 0))
    return pl.pallas_call(
        functools.partial(chip_kernel, half),
        grid_spec=pltpu.PrefetchScalarGridSpec(
            num_scalar_prefetch=1,
            grid=(1,),
            in_specs=[spec, spec],
            out_specs=pl.BlockSpec((packed, HD), lambda j, core: (0, 0)),
        ),
        out_shape=jax.ShapeDtypeStruct((packed, HD), F32),
        cost_estimate=cost(packed * HD * 2, packed * HD * 12),
        compiler_params=pltpu.CompilerParams(vmem_limit_bytes=VMEM_LIMIT),
    )(core, states, other)


def turn_kernel(half, first, last, late_ref, total_ref, theirs_ref, *refs):
    late = late_ref[0] == 1
    refs = list(refs)
    before_ref = None if first else refs.pop(0)
    prefix_ref = refs.pop(0)
    total, theirs = total_ref[...], theirs_ref[...]
    if first:
        prefix_ref[...] = jnp.where(late, theirs, 0.0)
    else:
        before = before_ref[...]
        prefix_ref[...] = jnp.where(late, joined(half, theirs, before), before)
    if not last:
        refs.pop(0)[...] = joined(
            half, jnp.where(late, theirs, total), jnp.where(late, total, theirs)
        )


def turn(late, total, theirs, before, last):
    packed = total.shape[0]
    half = (packed - 8) // HD
    whole = pl.BlockSpec((packed, HD), lambda j: (0, 0))
    operands = [total, theirs] + ([] if before is None else [before])
    count = 1 if last else 2
    out = call(
        functools.partial(turn_kernel, half, before is None, last),
        (1,),
        [smem()] + [whole] * len(operands),
        [whole] * count,
        [jax.ShapeDtypeStruct((packed, HD), F32)] * count,
        cost(packed * HD * 4, packed * HD * 16),
    )(late, *operands)
    return out[0], (None if last else out[1])


def linear_kernel(
    half, core_ref, q_ref, inside_ref, col_ref, mine_ref, theirs_ref, earlier_ref,
    out_ref, energy_ref, squares,
):
    step = pl.program_id(0)
    rows = q_ref.shape[0]
    core = core_ref[0]
    own = core == step
    summed = jnp.zeros((rows, HD), F32)
    decay = jnp.exp(earlier_ref[0, half * HD :, :])
    for i in range(half):
        at = slice(i * HD, (i + 1) * HD)
        prior = jnp.where(own, mine_ref[at, :], theirs_ref[at, :])
        prior = jnp.where(core == 1, prior * decay[i : i + 1] + earlier_ref[0, at, :], prior)
        leading = jnp.exp(column(col_ref[...], step * half + i))
        linear = inside_ref[:, at] + leading * three_term(q_ref[:, at], prior)
        out_ref[:, at] = linear
        summed = summed + linear * linear

    @pl.when(step == 0)
    def _():
        squares[...] = summed

    @pl.when(step == 1)
    def _():
        energy_ref[...] = lax.dot_general(
            jnp.ones((8, HD), F32),
            squares[...] + summed,
            NT,
            precision=lax.Precision.HIGHEST,
            preferred_element_type=F32,
        )


def linear_blocks(core, q_lin, inside, col, mine, theirs, earlier):
    rows, width = q_lin.shape
    packed = mine.shape[0]
    half = (packed - 8) // HD
    block = pl.BlockSpec((rows, half * HD), lambda j: (0, j))
    whole = pl.BlockSpec((packed, HD), lambda j: (0, 0))
    return call(
        functools.partial(linear_kernel, half),
        (2,),
        [
            smem(),
            block,
            block,
            pl.BlockSpec((rows, HD), lambda j: (0, 0)),
            whole,
            whole,
            pl.BlockSpec((1, packed, HD), lambda j: (j, 0, 0)),
        ],
        [block, pl.BlockSpec((8, rows), lambda j: (0, 0))],
        [jax.ShapeDtypeStruct((rows, width), F32), jax.ShapeDtypeStruct((8, rows), F32)],
        cost(6 * rows * width * HD, 14 * rows * width),
        [pltpu.VMEM((rows, HD), F32)],
    )(core, q_lin, inside, col, mine, theirs, earlier)


def norm_kernel(columns, *refs):
    linear_ref, gain_ref, out_ref = refs[-3:]
    energy = refs[0][...]
    for ref in refs[1:-3]:
        energy = energy + ref[...]
    factor = lax.rsqrt(energy / columns + EPSILON).T[:, 0:1]
    out_ref[...] = linear_ref[...] * factor * gain_ref[...]


def normalized(energies, linear, gain, columns):
    rows, width = linear.shape
    block = pl.BlockSpec((rows, width // 2), lambda j: (0, j))
    return call(
        functools.partial(norm_kernel, columns),
        (2,),
        [pl.BlockSpec((8, rows), lambda j: (0, 0))] * len(energies)
        + [block, pl.BlockSpec((1, width // 2), lambda j: (0, j))],
        block,
        jax.ShapeDtypeStruct((rows, width), F32),
        cost(rows * width * 2, rows * width * 8),
    )(*energies, linear, gain)


def soft_kernel(group, own, last, factor, flag_ref, q_ref, k0_ref, v0_ref, k1_ref, v1_ref, *refs):
    refs = list(refs)
    acc_ref, stat_ref = (None, None) if own else (refs.pop(0), refs.pop(0))
    out_ref = refs.pop(0)
    new_ref = None if last else refs.pop(0)
    rows = q_ref.shape[0]

    def visit(key_refs, value_refs):
        keys = jnp.concatenate([ref[...] for ref in key_refs], axis=0)
        values = jnp.concatenate([ref[...] for ref in value_refs], axis=0)
        k_high, k_low = split(keys)
        k_terms = jnp.concatenate([k_high, k_high, k_low], axis=1)
        v_high, v_low = split(values)
        v_terms = jnp.concatenate([v_high, v_low], axis=1)
        count = keys.shape[0]
        lanes = lax.broadcasted_iota(jnp.int32, (rows, HD), 1)
        stats = jnp.zeros((rows, HD), F32)
        if own:
            key_at = lax.broadcasted_iota(jnp.int32, (rows, count), 1)
            visible = key_at <= lax.broadcasted_iota(jnp.int32, (rows, count), 0) + (count - rows)
        else:
            old_stats = stat_ref[0]
        for g in range(group):
            at = slice(g * HD, (g + 1) * HD)
            q_high, q_low = split(q_ref[:, at] * factor)
            q_terms = jnp.concatenate([q_high, q_low, q_high], axis=1)
            scores = lax.dot_general(q_terms, k_terms, NT, preferred_element_type=F32)
            if own:
                scores = jnp.where(visible, scores, NEGATIVE)
            peak = jnp.max(scores, axis=1, keepdims=True)
            if not own:
                old_peak = old_stats[:, g : g + 1]
                peak = jnp.maximum(peak, old_peak)
            weights = jnp.exp2(scores - peak)
            total = jnp.sum(weights, axis=1, keepdims=True)
            w_high, w_low = split(weights)
            wide = dot(w_high, v_terms)
            summed = wide[:, :HD] + wide[:, HD:] + dot(w_low, v_high)
            if not own:
                shrink = jnp.exp2(old_peak - peak)
                total = total + old_stats[:, 64 + g : 65 + g] * shrink
                summed = summed + acc_ref[:, at] * shrink
            if last:
                summed = summed / total
            else:
                stats = jnp.where(lanes == g, peak, stats)
                stats = jnp.where(lanes == 64 + g, total, stats)
            out_ref[:, at] = summed
        if not last:
            new_ref[0] = stats

    if own:

        @pl.when(flag_ref[0] == 0)
        def _():
            visit([k0_ref], [v0_ref])

    else:

        @pl.when(flag_ref[0] == 0)
        def _():
            if last:
                for g in range(group):
                    at = slice(g * HD, (g + 1) * HD)
                    out_ref[:, at] = acc_ref[:, at] / stat_ref[0, :, 64 + g : 65 + g]
            else:
                out_ref[...] = acc_ref[...]
                new_ref[...] = stat_ref[...]

    @pl.when(flag_ref[0] == 1)
    def _():
        visit([k1_ref, k0_ref], [v1_ref, v0_ref])


def soft_stage(flag, q_soft, first, second, carried, last):
    rows, width = q_soft.shape
    kv_heads = first[0].shape[1] // HD
    group = width // (kv_heads * HD)
    own = carried is None
    factor = math.log2(math.e) / math.sqrt(HD)
    wide = pl.BlockSpec((rows, group * HD), lambda j: (0, j))
    narrow = pl.BlockSpec((first[0].shape[0], HD), lambda j: (0, j))
    stat = pl.BlockSpec((1, rows, HD), lambda j: (j, 0, 0))
    out_specs, out_shape = [wide], [jax.ShapeDtypeStruct((rows, width), F32)]
    if not last:
        out_specs.append(stat)
        out_shape.append(jax.ShapeDtypeStruct((kv_heads, rows, HD), F32))
    out = call(
        functools.partial(soft_kernel, group, own, last, factor),
        (kv_heads,),
        [smem(), wide] + [narrow] * 4 + ([] if own else [wide, stat]),
        out_specs,
        out_shape,
        cost(24 * rows * width * 2 * rows, rows * width * 12, 2 * rows * rows * width // HD),
    )(flag, q_soft, *first, *second, *(() if own else carried))
    return out[0] if last else out


def body(q_lin, k_lin, v_lin, log_decay, lin_gain, q_soft, k_soft, v_soft):
    devices = lax.axis_size("ctx")
    chips = devices // 2
    heads = lax.axis_size("head")
    me = lax.axis_index("ctx")
    core, chip = me % 2, me // 2
    as_flag = lambda value: jnp.reshape(value, (1,)).astype(jnp.int32)
    core_flag = as_flag(core)

    def send(array, pairs):
        return lax.ppermute(array, "ctx", pairs)

    swap = [(2 * c + e, 2 * c + 1 - e) for c in range(chips) for e in range(2)]

    def near(distance):
        return [
            (2 * (c ^ distance) + e, 2 * c + e)
            for c in range(chips)
            if c ^ distance < c
            for e in range(2)
        ]

    def far(distance):
        return [
            (2 * c + e, 2 * c + 1 - e)
            for c in range(chips)
            if c ^ distance < c
            for e in range(2)
        ]

    arrived = {}
    for distance in range(1, chips):
        here = [send(array, near(distance)) for array in (k_soft, v_soft)]
        arrived[distance] = (here, [send(array, far(distance)) for array in here])
    beside = [send(array, [(2 * c, 2 * c + 1) for c in range(chips)]) for array in (k_soft, v_soft)]

    states, col, row = local_states(k_lin, v_lin, log_decay)
    other = send(states, swap)
    total = chip_total(core_flag, states, other)
    prefix = None
    distance = 1
    while distance < chips:
        last = 2 * distance >= chips
        pairs = [
            (2 * (c ^ distance) + e, 2 * c + e)
            for c in range(chips)
            if not last or c ^ distance < c
            for e in range(2)
        ]
        theirs = send(total, pairs)
        late = as_flag((chip // distance) % 2)
        prefix, total = turn(late, total, theirs, prefix, last)
        distance *= 2
    prefix_other = send(prefix, swap)

    carried = soft_stage(core_flag, q_soft, (k_soft, v_soft), beside, None, False)
    inside = inside_blocks(q_lin, k_lin, v_lin, col, row)

    def energies_of(energy):
        count = heads
        parts = [energy]
        for shift in range(1, count):
            parts.append(
                lax.ppermute(energy, "head", [(i, (i + shift) % count) for i in range(count)])
            )
        return parts

    soft_out = None
    for distance in range(1, chips):
        last = distance == chips - 1
        if last:
            linear, energy = linear_blocks(
                core_flag, q_lin, inside, col, prefix, prefix_other, other
            )
            energies = energies_of(energy)
        flag = as_flag((chip ^ distance) < chip)
        out = soft_stage(flag, q_soft, *arrived[distance], carried, last)
        if last:
            soft_out = out
        else:
            carried = out
    columns = q_lin.shape[1] * heads
    lin_out = normalized(energies, linear, lin_gain.reshape(1, -1), columns)
    return (lin_out, soft_out)


def solution(mesh):
    return jax.shard_map(
        body,
        mesh=mesh,
        in_specs=(
            P("ctx", "head"),
            P("ctx", "head"),
            P("ctx", "head"),
            P("head", "ctx"),
            P("head"),
            P("ctx", "head"),
            P("ctx", "head"),
            P("ctx", "head"),
        ),
        out_specs=(P("ctx", "head"), P("ctx", "head")),
        check_vma=False,
    )
```

time: 210 us -> 93.7 us (0.45)
  the two profiles are of different devices: /device:TPU:6 before, /device:TPU:4 now
where the time goes in v1:
time: 93.7 us; the launch traced here: 93 us
  Pallas kernels  34.1 us (36%)
  starting transfers between devices  34 us (36%)
  waiting for transfers between devices  20.7 us (22%)
  local copies, waits for them, and re-layouts  3.17 us (3%)
  between operations  1.02 us (1%)
    ppermute x18, starting transfers between devices, send(): return lax.ppermute(array, 'ctx', pairs)  28.5 us
    pallas_call x4, Pallas kernels, soft_stage(): call(functools.partial(soft_kernel, group, own, last, factor), (kv_heads,...  23.2 us
    ppermute x18, waiting for transfers between devices, send(): return lax.ppermute(array, 'ctx', pairs)  20.7 us
    ppermute x3, starting transfers between devices, energies_of(): lax.ppermute(energy, 'head', [(i, (i + shift) % count) for i in range(cou...  5.55 us
    unnamed x20, local copies, waits for them, and re-layouts  3.17 us
    pallas_call x1, Pallas kernels, local_states(): call(functools.partial(state_kernel, half), (2,), [pl.BlockSpec((heads, r...  2.64 us
    pallas_call x1, Pallas kernels, inside_blocks(): call(functools.partial(inside_kernel, half), (2,), [block, block, block,...  2.52 us
    pallas_call x1, Pallas kernels, linear_blocks(): call(functools.partial(linear_kernel, half), (2,), [smem(), block, block,...  2.15 us
  transfers between devices with their start and end apart: 21, of which 4 were waited for; matrix products, arithmetic and copies ran while one was open for 0% of the time, Pallas kernels for 32%

profile of v1, /device:TPU:4, one launch (start us, length us, event | category | flops | bytes accessed | tf_op | source)
XLA Modules:
  0.0 93.0 jit_solution(4400357302066505587)
XLA Ops:
  0.6 0.0 copy-start
  0.6 1.2 %copy-done = f32[256,1024]{1,0:T(8,128)S(1)} copy-done((f32[256,1024]{1,0:T(8,128)S(1)}, f32[256,1024]{1,0:T(8,128)}, u32[]{:S(2)}) %copy-start) | copy-done | bytes 1048600
  1.9 1.2 %copy-done.2 = f32[256,1024]{1,0:T(8,128)S(1)} copy-done((f32[256,1024]{1,0:T(8,128)S(1)}, f32[256,1024]{1,0:T(8,128)}, u32[]{:S(2)}) %copy-start.2) | copy-done | bytes 1048600
  3.1 0.7 copy-done.5
  3.8 2.6 %shard_map.95 = (f32[2,520,128]{2,1,0:T(8,128)}, f32[256,128]{1,0:T(8,128)S(1)}, f32[8,256]{1,0:T(8,128)S(1)}) custom-call(f32[8,256]{1,0:T(8,128)S(1)} %copy-done.5, f32[256,1024]{1,0:T(8,128)S(1)} %copy-done, f32[256,1024]{1,0:T(8,128)S(1)} %copy-done.2), custom_call_target="tpu_custom_call" | custom-call | flops 201326592 | bytes 2621440 | tf_op jit(solution)/shard_map/pallas_call | solution.py:109
  6.4 0.0 collective-permute-start
  6.4 3.1 %collective-permute-start.19 = (f32[256,256]{1,0:T(8,128)}, f32[256,256]{1,0:T(8,128)}, u32[]{:S(2)}, u32[]{:S(2)}) collective-permute-start(f32[256,256]{1,0:T(8,128)} %k0_ref.1), channel_id=1, source_target_pairs={{0,4},{8,12},{16,20},{24,28},{1,5},{9,13},{17,21},{25,29},{2,6},{1... | collective-permute-start | bytes 786440 | tf_op jit(solution)/shard_map/ppermute | solution.py:420
  9.5 0.0 collective-permute-done.theirs_ref.earlier_ref
  9.5 1.1 %shard_map.97.total_ref = f32[520,128]{1,0:T(8,128)S(1)} custom-call(s32[1]{0:T(128)} %bitcast.core_ref.flag_ref, f32[2,520,128]{2,1,0:T(8,128)} %get-tuple-element.17.mine_ref, f32[2,520,128]{2,1,0:T(8,128)} %collective-permute-done.theirs_ref.earlier_ref), custom_call_target="tpu_custom_call" | custom-call | flops 133120 | bytes 798720 | tf_op jit(solution)/shard_map/pallas_call | solution.py:182
  10.6 1.5 %collective-permute-start.1 = (f32[520,128]{1,0:T(8,128)S(1)}, f32[520,128]{1,0:T(8,128)}, u32[]{:S(2)}, u32[]{:S(2)}) collective-permute-start(f32[520,128]{1,0:T(8,128)S(1)} %shard_map.97.total_ref), channel_id=1, source_target_pairs={{8,0},{12,4},{0,8},{4,12},{24,16},{28,20},{16,24},{20,28},{9,1},{1... | collective-permute-start | bytes 798728 | tf_op jit(solution)/shard_map/ppermute | solution.py:420
  12.2 2.0 %collective-permute-start.20 = (f32[256,256]{1,0:T(8,128)}, f32[256,256]{1,0:T(8,128)}, u32[]{:S(2)}, u32[]{:S(2)}) collective-permute-start(f32[256,256]{1,0:T(8,128)} %v0_ref.1), channel_id=1, source_target_pairs={{0,4},{8,12},{16,20},{24,28},{1,5},{9,13},{17,21},{25,29},{2,6},{1... | collective-permute-start | bytes 786440 | tf_op jit(solution)/shard_map/ppermute | solution.py:420
  14.2 3.1 %collective-permute-start.15 = (f32[256,256]{1,0:T(8,128)}, f32[256,256]{1,0:T(8,128)}, u32[]{:S(2)}, u32[]{:S(2)}) collective-permute-start(f32[256,256]{1,0:T(8,128)} %k0_ref.1), channel_id=1, source_target_pairs={{0,8},{4,12},{16,24},{20,28},{1,9},{5,13},{17,25},{21,29},{2,10},{... | collective-permute-start | bytes 786440 | tf_op jit(solution)/shard_map/ppermute | solution.py:420
  17.3 2.0 %collective-permute-start.16 = (f32[256,256]{1,0:T(8,128)}, f32[256,256]{1,0:T(8,128)}, u32[]{:S(2)}, u32[]{:S(2)}) collective-permute-start(f32[256,256]{1,0:T(8,128)} %v0_ref.1), channel_id=1, source_target_pairs={{0,8},{4,12},{16,24},{20,28},{1,9},{5,13},{17,25},{21,29},{2,10},{... | collective-permute-start | bytes 786440 | tf_op jit(solution)/shard_map/ppermute | solution.py:420
  19.3 0.0 collective-permute-done.19.k1_ref
  19.3 1.3 %collective-permute-start.11 = (f32[256,256]{1,0:T(8,128)}, f32[256,256]{1,0:T(8,128)}, u32[]{:S(2)}, u32[]{:S(2)}) collective-permute-start(f32[256,256]{1,0:T(8,128)} %k0_ref.1), channel_id=1, source_target_pairs={{0,16},{4,20},{8,24},{12,28},{1,17},{5,21},{9,25},{13,29},{2,18},{... | collective-permute-start | bytes 786440 | tf_op jit(solution)/shard_map/ppermute | solution.py:420
  20.7 0.0 copy-done.1
  20.7 0.0 copy-done.3
  20.7 0.0 copy-done.4
  20.7 0.0 copy-start.8
  20.7 0.0 copy-start.9
  20.7 0.0 copy-start.7
  20.7 2.5 %shard_map.96.inside_ref = f32[256,1024]{1,0:T(8,128)S(1)} custom-call(f32[256,1024]{1,0:T(8,128)S(1)} %copy-done.4, f32[256,1024]{1,0:T(8,128)S(1)} %copy-done.1, f32[256,1024]{1,0:T(8,128)S(1)} %copy-done.3, f32[256,128]{1,0:T(8,128)S(1)} %get-tuple-element.15.col_ref, f32[8,256]{1,0:T(8,128)S(1)} %get-tuple-element.16.row_ref), custom_call_target="tpu_custom_call" | custom-call | flops 805306368 | bytes 4194304 | tf_op jit(solution)/shard_map/pallas_call | solution.py:146
  23.3 0.0 collective-permute-done.20.v1_ref
  23.3 0.0 copy-done.8
  23.3 1.3 %collective-permute-start.12 = (f32[256,256]{1,0:T(8,128)S(1)}, f32[256,256]{1,0:T(8,128)S(1)}, u32[]{:S(2)}, u32[]{:S(2)}) collective-permute-start(f32[256,256]{1,0:T(8,128)S(1)} %copy-done.8), channel_id=1, source_target_pairs={{0,16},{4,20},{8,24},{12,28},{1,17},{5,21},{9,25},{13,29},{2,18},{... | collective-permute-start | bytes 786440 | tf_op jit(solution)/shard_map/ppermute | solution.py:420
  24.6 0.2 collective-permute-done.15.k0_ref
  24.7 1.3 %collective-permute-start.8 = (f32[256,256]{1,0:T(8,128)S(1)}, f32[256,256]{1,0:T(8,128)S(1)}, u32[]{:S(2)}, u32[]{:S(2)}) collective-permute-start(f32[256,256]{1,0:T(8,128)S(1)} %copy-done.8), channel_id=1, source_target_pairs={{8,16},{12,20},{0,24},{4,28},{9,17},{13,21},{1,25},{5,29},{10,18},... | collective-permute-start | bytes 786440 | tf_op jit(solution)/shard_map/ppermute | solution.py:420
  26.0 2.6 %collective-permute-done.16.v0_ref = f32[256,256]{1,0:T(8,128)} collective-permute-done((f32[256,256]{1,0:T(8,128)}, f32[256,256]{1,0:T(8,128)}, u32[]{:S(2)}, u32[]{:S(2)}) %collective-permute-start.16) | collective-permute-done | bytes 262176 | tf_op jit(solution)/shard_map/ppermute | solution.py:420
  28.6 0.0 copy-done.9
  28.6 1.3 %collective-permute-start.7 = (f32[256,256]{1,0:T(8,128)S(1)}, f32[256,256]{1,0:T(8,128)S(1)}, u32[]{:S(2)}, u32[]{:S(2)}) collective-permute-start(f32[256,256]{1,0:T(8,128)S(1)} %copy-done.9), channel_id=1, source_target_pairs={{8,16},{12,20},{0,24},{4,28},{9,17},{13,21},{1,25},{5,29},{10,18},... | collective-permute-start | bytes 786440 | tf_op jit(solution)/shard_map/ppermute | solution.py:420
  29.9 10.5 %collective-permute-done.11.k0_ref = f32[256,256]{1,0:T(8,128)} collective-permute-done((f32[256,256]{1,0:T(8,128)}, f32[256,256]{1,0:T(8,128)}, u32[]{:S(2)}, u32[]{:S(2)}) %collective-permute-start.11) | collective-permute-done | bytes 262176 | tf_op jit(solution)/shard_map/ppermute | solution.py:420
  40.4 0.7 collective-permute-start.17
  41.1 0.0 collective-permute-done.1.theirs_ref
  41.1 0.7 collective-permute-start.18
  41.8 4.3 %shard_map.102 = (f32[256,1536]{1,0:T(8,128)S(1)}, f32[2,256,128]{2,1,0:T(8,128)S(1)}) custom-call(s32[1]{0:T(128)} %bitcast.core_ref.flag_ref, f32[256,1536]{1,0:T(8,128)S(1)} %copy-done.7, f32[256,256]{1,0:T(8,128)S(1)} %copy-done.9, f32[256,256]{1,0:T(8,128)S(1)} %copy-done.8, f32[256,256]{1,0:T(8,128)} %collective-permute-done.19.k1_ref, ...), custom_call_target="tpu_custom_call" | custom-call | flops 4831838208 | bytes 4718592 | tf_op jit(solution)/shard_map/pallas_call | solution.py:399
  46.1 1.0 %shard_map.98 = (f32[520,128]{1,0:T(8,128)S(1)}, f32[520,128]{1,0:T(8,128)S(1)}) custom-call(s32[1]{0:T(128)} %bitcast.2.late_ref, f32[520,128]{1,0:T(8,128)S(1)} %shard_map.97.total_ref, f32[520,128]{1,0:T(8,128)} %collective-permute-done.1.theirs_ref), custom_call_target="tpu_custom_call" | custom-call | flops 266240 | bytes 1064960 | tf_op jit(solution)/shard_map/pallas_call | solution.py:219
  47.2 0.0 collective-permute-done.12.v0_ref
  47.2 1.9 %collective-permute-start.13 = (f32[256,256]{1,0:T(8,128)}, f32[256,256]{1,0:T(8,128)S(1)}, u32[]{:S(2)}, u32[]{:S(2)}) collective-permute-start(f32[256,256]{1,0:T(8,128)} %collective-permute-done.11.k0_ref), channel_id=1, source_target_pairs={{16,20},{20,16},{24,28},{28,24},{17,21},{21,17},{25,29},{29,25},{1... | collective-permute-start | bytes 786440 | tf_op jit(solution)/shard_map/ppermute | solution.py:420
  49.1 0.0 collective-permute-done.8.v0_ref
  49.1 2.4 %collective-permute-start.14 = (f32[256,256]{1,0:T(8,128)S(1)}, f32[256,256]{1,0:T(8,128)S(1)}, u32[]{:S(2)}, u32[]{:S(2)}) collective-permute-start(f32[256,256]{1,0:T(8,128)S(1)} %collective-permute-done.12.v0_ref), channel_id=1, source_target_pairs={{16,20},{20,16},{24,28},{28,24},{17,21},{21,17},{25,29},{29,25},{1... | collective-permute-start | bytes 786440 | tf_op jit(solution)/shard_map/ppermute | solution.py:420
  51.5 0.0 collective-permute-done.7.k0_ref
  51.5 1.9 %collective-permute-start.10 = (f32[256,256]{1,0:T(8,128)S(1)}, f32[256,256]{1,0:T(8,128)S(1)}, u32[]{:S(2)}, u32[]{:S(2)}) collective-permute-start(f32[256,256]{1,0:T(8,128)S(1)} %collective-permute-done.8.v0_ref), channel_id=1, source_target_pairs={{16,20},{20,16},{24,28},{28,24},{17,21},{21,17},{25,29},{29,25},{1... | collective-permute-start | bytes 786440 | tf_op jit(solution)/shard_map/ppermute | solution.py:420
  53.5 0.0 collective-permute-done.17.k1_ref
  53.5 2.4 %collective-permute-start.9 = (f32[256,256]{1,0:T(8,128)S(1)}, f32[256,256]{1,0:T(8,128)S(1)}, u32[]{:S(2)}, u32[]{:S(2)}) collective-permute-start(f32[256,256]{1,0:T(8,128)S(1)} %collective-permute-done.7.k0_ref), channel_id=1, source_target_pairs={{16,20},{20,16},{24,28},{28,24},{17,21},{21,17},{25,29},{29,25},{1... | collective-permute-start | bytes 786440 | tf_op jit(solution)/shard_map/ppermute | solution.py:420
  55.9 0.0 collective-permute-done.18.v1_ref
  55.9 1.5 %collective-permute-start.2 = (f32[520,128]{1,0:T(8,128)S(1)}, f32[520,128]{1,0:T(8,128)S(1)}, u32[]{:S(2)}, u32[]{:S(2)}) collective-permute-start(f32[520,128]{1,0:T(8,128)S(1)} %get-tuple-element.18.total_ref), channel_id=1, source_target_pairs={{0,16},{4,20},{8,24},{12,28},{1,17},{5,21},{9,25},{13,29},{2,18},{... | collective-permute-start | bytes 798728 | tf_op jit(solution)/shard_map/ppermute | solution.py:420
  57.4 1.4 %shard_map.103 = (f32[256,1536]{1,0:T(8,128)S(1)}, f32[2,256,128]{2,1,0:T(8,128)S(1)}) custom-call(s32[1]{0:T(128)} %bitcast.6.flag_ref, f32[256,1536]{1,0:T(8,128)S(1)} %copy-done.7, f32[256,256]{1,0:T(8,128)} %collective-permute-done.15.k0_ref, f32[256,256]{1,0:T(8,128)} %collective-permute-done.16.v0_ref, f32[256,256]{1,0:T(8,128)S(1)} %collective-permute-done.17.k1_ref, ...), custom_call_target="tpu_custom_call" | custom-call | flops 4831838208 | bytes 4718592 | tf_op jit(solution)/shard_map/pallas_call | solution.py:399
  58.8 7.3 %collective-permute-done.2.theirs_ref = f32[520,128]{1,0:T(8,128)S(1)} collective-permute-done((f32[520,128]{1,0:T(8,128)S(1)}, f32[520,128]{1,0:T(8,128)S(1)}, u32[]{:S(2)}, u32[]{:S(2)}) %collective-permute-start.2) | collective-permute-done | bytes 266272 | tf_op jit(solution)/shard_map/ppermute | solution.py:420
  66.2 0.1 collective-permute-start.3
  66.2 0.0 collective-permute-done.13.k1_ref
  66.2 0.0 collective-permute-done.14.v1_ref
  66.3 8.7 %shard_map.104 = (f32[256,1536]{1,0:T(8,128)S(1)}, f32[2,256,128]{2,1,0:T(8,128)S(1)}) custom-call(s32[1]{0:T(128)} %bitcast.5.flag_ref, f32[256,1536]{1,0:T(8,128)S(1)} %copy-done.7, f32[256,256]{1,0:T(8,128)} %collective-permute-done.11.k0_ref, f32[256,256]{1,0:T(8,128)S(1)} %collective-permute-done.12.v0_ref, ...), custom_call_target="tpu_custom_call" | custom-call | flops 4831838208 | bytes 4718592 | tf_op jit(solution)/shard_map/pallas_call | solution.py:399
  75.0 0.0 collective-permute-done.3.theirs_ref
  75.0 2.1 %shard_map.100 = (f32[256,1024]{1,0:T(8,128)S(1)}, f32[8,256]{1,0:T(8,128)S(1)}) custom-call(s32[1]{0:T(128)} %bitcast.core_ref.flag_ref, f32[256,1024]{1,0:T(8,128)S(1)} %copy-done.4, f32[256,1024]{1,0:T(8,128)S(1)} %shard_map.96.inside_ref, f32[256,128]{1,0:T(8,128)S(1)} %get-tuple-element.15.col_ref, f32[520,128]{1,0:T(8,128)S(1)} %shard_map.99.mine_ref, ...), custom_call_target="tpu_custom_call" | custom-call | flops 201326592 | bytes 3670016 | tf_op jit(solution)/shard_map/pallas_call | solution.py:270
  77.2 1.6 %collective-permute-start.4 = (f32[8,256]{1,0:T(8,128)S(1)}, f32[8,256]{1,0:T(8,128)S(1)}, u32[]{:S(2)}, u32[]{:S(2)}) collective-permute-start(f32[8,256]{1,0:T(8,128)S(1)} %get-tuple-element.20.refs_0_), channel_id=1, source_target_pairs={{0,1},{1,2},{2,3},{3,0},{4,5},{5,6},{6,7},{7,4},{8,9},{9,10},{10,1... | collective-permute-start | bytes 24584 | tf_op jit(solution)/shard_map/ppermute | solution.py:473
  78.8 2.6 %collective-permute-start.5 = (f32[8,256]{1,0:T(8,128)S(1)}, f32[8,256]{1,0:T(8,128)S(1)}, u32[]{:S(2)}, u32[]{:S(2)}) collective-permute-start(f32[8,256]{1,0:T(8,128)S(1)} %get-tuple-element.20.refs_0_), channel_id=1, source_target_pairs={{0,2},{1,3},{2,0},{3,1},{4,6},{5,7},{6,4},{7,5},{8,10},{9,11},{10,... | collective-permute-start | bytes 24584 | tf_op jit(solution)/shard_map/ppermute | solution.py:473
  81.4 1.3 %collective-permute-start.6 = (f32[8,256]{1,0:T(8,128)S(1)}, f32[8,256]{1,0:T(8,128)S(1)}, u32[]{:S(2)}, u32[]{:S(2)}) collective-permute-start(f32[8,256]{1,0:T(8,128)S(1)} %get-tuple-element.20.refs_0_), channel_id=1, source_target_pairs={{0,3},{1,0},{2,1},{3,2},{4,7},{5,4},{6,5},{7,6},{8,11},{9,8},{10,9... | collective-permute-start | bytes 24584 | tf_op jit(solution)/shard_map/ppermute | solution.py:473
  82.7 0.0 collective-permute-done.10.v1_ref
  82.7 0.0 collective-permute-done.9.k1_ref
  82.7 8.8 %shard_map.105 = f32[256,1536]{1,0:T(8,128)} custom-call(s32[1]{0:T(128)} %bitcast.4.flag_ref, f32[256,1536]{1,0:T(8,128)S(1)} %copy-done.7, f32[256,256]{1,0:T(8,128)S(1)} %collective-permute-done.7.k0_ref, f32[256,256]{1,0:T(8,128)S(1)} %collective-permute-done.8.v0_ref, f32[256,256]{1,0:T(8,128)S(1)} %collective-permute-done.9.k1_ref, ...), custom_call_target="tpu_custom_call" | custom-call | flops 4831838208 | bytes 4718592 | tf_op jit(solution)/shard_map/pallas_call | solution.py:399
  91.6 0.0 collective-permute-done.4.refs_1_
  91.6 0.0 collective-permute-done.5.refs_2_
  91.6 0.0 collective-permute-done.6.refs_3_
  91.6 1.4 %shard_map.101 = f32[256,1024]{1,0:T(8,128)} custom-call(f32[8,256]{1,0:T(8,128)S(1)} %get-tuple-element.20.refs_0_, f32[8,256]{1,0:T(8,128)S(1)} %collective-permute-done.4.refs_1_, f32[8,256]{1,0:T(8,128)S(1)} %collective-permute-done.5.refs_2_, f32[8,256]{1,0:T(8,128)S(1)} %collective-permute-done.6.refs_3_, f32[256,1024]{1,0:T(8,128)S(1)} %get-tuple-element.21.refs_4_, ...), custom_call_target="tpu_custom_call" | custom-call | flops 524288 | bytes 2097152 | tf_op jit(solution)/shard_map/pallas_call | solution.py:301
  (9 shorter events, 0.1 us)
Async XLA Ops:
  0.6 1.2 %copy-start = (f32[256,1024]{1,0:T(8,128)S(1)}, f32[256,1024]{1,0:T(8,128)}, u32[]{:S(2)}) copy-start(f32[256,1024]{1,0:T(8,128)} %k_ref.3) | copy-start | bytes 3145732
  1.9 1.2 %copy-start.2 = (f32[256,1024]{1,0:T(8,128)S(1)}, f32[256,1024]{1,0:T(8,128)}, u32[]{:S(2)}) copy-start(f32[256,1024]{1,0:T(8,128)} %v_ref.3) | copy-start | bytes 3145732
  3.1 0.7 copy-start.5
  3.8 16.9 %copy-start.1 = (f32[256,1024]{1,0:T(8,128)S(1)}, f32[256,1024]{1,0:T(8,128)}, u32[]{:S(2)}) copy-start(f32[256,1024]{1,0:T(8,128)} %k_ref.3) | copy-start | bytes 3145732
  3.8 16.9 %copy-start.3 = (f32[256,1024]{1,0:T(8,128)S(1)}, f32[256,1024]{1,0:T(8,128)}, u32[]{:S(2)}) copy-start(f32[256,1024]{1,0:T(8,128)} %v_ref.3) | copy-start | bytes 3145732
  3.8 16.9 %copy-start.4 = (f32[256,1024]{1,0:T(8,128)S(1)}, f32[256,1024]{1,0:T(8,128)}, u32[]{:S(2)}) copy-start(f32[256,1024]{1,0:T(8,128)} %q_ref.7) | copy-start | bytes 3145732
  6.4 3.1 %collective-permute-start = (f32[2,520,128]{2,1,0:T(8,128)}, f32[2,520,128]{2,1,0:T(8,128)}, u32[]{:S(2)}, u32[]{:S(2)}) collective-permute-start(f32[2,520,128]{2,1,0:T(8,128)} %get-tuple-element.17.mine_ref), channel_id=1, source_target_pairs={{0,4},{4,0},{8,12},{12,8},{16,20},{20,16},{24,28},{28,24},{1,5},{5... | collective-permute-start | bytes 1597448 | tf_op jit(solution)/shard_map/ppermute | solution.py:420
  6.4 12.9 %collective-permute-start.19 = (f32[256,256]{1,0:T(8,128)}, f32[256,256]{1,0:T(8,128)}, u32[]{:S(2)}, u32[]{:S(2)}) collective-permute-start(f32[256,256]{1,0:T(8,128)} %k0_ref.1), channel_id=1, source_target_pairs={{0,4},{8,12},{16,20},{24,28},{1,5},{9,13},{17,21},{25,29},{2,6},{1... | collective-permute-start | bytes 786440 | tf_op jit(solution)/shard_map/ppermute | solution.py:420
  10.6 30.5 %collective-permute-start.1 = (f32[520,128]{1,0:T(8,128)S(1)}, f32[520,128]{1,0:T(8,128)}, u32[]{:S(2)}, u32[]{:S(2)}) collective-permute-start(f32[520,128]{1,0:T(8,128)S(1)} %shard_map.97.total_ref), channel_id=1, source_target_pairs={{8,0},{12,4},{0,8},{4,12},{24,16},{28,20},{16,24},{20,28},{9,1},{1... | collective-permute-start | bytes 798728 | tf_op jit(solution)/shard_map/ppermute | solution.py:420
  12.2 11.1 %collective-permute-start.20 = (f32[256,256]{1,0:T(8,128)}, f32[256,256]{1,0:T(8,128)}, u32[]{:S(2)}, u32[]{:S(2)}) collective-permute-start(f32[256,256]{1,0:T(8,128)} %v0_ref.1), channel_id=1, source_target_pairs={{0,4},{8,12},{16,20},{24,28},{1,5},{9,13},{17,21},{25,29},{2,6},{1... | collective-permute-start | bytes 786440 | tf_op jit(solution)/shard_map/ppermute | solution.py:420
  14.2 10.6 %collective-permute-start.15 = (f32[256,256]{1,0:T(8,128)}, f32[256,256]{1,0:T(8,128)}, u32[]{:S(2)}, u32[]{:S(2)}) collective-permute-start(f32[256,256]{1,0:T(8,128)} %k0_ref.1), channel_id=1, source_target_pairs={{0,8},{4,12},{16,24},{20,28},{1,9},{5,13},{17,25},{21,29},{2,10},{... | collective-permute-start | bytes 786440 | tf_op jit(solution)/shard_map/ppermute | solution.py:420
  17.3 11.3 %collective-permute-start.16 = (f32[256,256]{1,0:T(8,128)}, f32[256,256]{1,0:T(8,128)}, u32[]{:S(2)}, u32[]{:S(2)}) collective-permute-start(f32[256,256]{1,0:T(8,128)} %v0_ref.1), channel_id=1, source_target_pairs={{0,8},{4,12},{16,24},{20,28},{1,9},{5,13},{17,25},{21,29},{2,10},{... | collective-permute-start | bytes 786440 | tf_op jit(solution)/shard_map/ppermute | solution.py:420
  19.3 21.1 %collective-permute-start.11 = (f32[256,256]{1,0:T(8,128)}, f32[256,256]{1,0:T(8,128)}, u32[]{:S(2)}, u32[]{:S(2)}) collective-permute-start(f32[256,256]{1,0:T(8,128)} %k0_ref.1), channel_id=1, source_target_pairs={{0,16},{4,20},{8,24},{12,28},{1,17},{5,21},{9,25},{13,29},{2,18},{... | collective-permute-start | bytes 786440 | tf_op jit(solution)/shard_map/ppermute | solution.py:420
  20.7 2.6 %copy-start.8 = (f32[256,256]{1,0:T(8,128)S(1)}, f32[256,256]{1,0:T(8,128)}, u32[]{:S(2)}) copy-start(f32[256,256]{1,0:T(8,128)} %v0_ref.1) | copy-start | bytes 786436
  20.7 7.9 %copy-start.9 = (f32[256,256]{1,0:T(8,128)S(1)}, f32[256,256]{1,0:T(8,128)}, u32[]{:S(2)}) copy-start(f32[256,256]{1,0:T(8,128)} %k0_ref.1) | copy-start | bytes 786436
  20.7 21.1 %copy-start.7 = (f32[256,1536]{1,0:T(8,128)S(1)}, f32[256,1536]{1,0:T(8,128)}, u32[]{:S(2)}) copy-start(f32[256,1536]{1,0:T(8,128)} %q_ref.11) | copy-start | bytes 4718596
  23.3 23.9 %collective-permute-start.12 = (f32[256,256]{1,0:T(8,128)S(1)}, f32[256,256]{1,0:T(8,128)S(1)}, u32[]{:S(2)}, u32[]{:S(2)}) collective-permute-start(f32[256,256]{1,0:T(8,128)S(1)} %copy-done.8), channel_id=1, source_target_pairs={{0,16},{4,20},{8,24},{12,28},{1,17},{5,21},{9,25},{13,29},{2,18},{... | collective-permute-start | bytes 786440 | tf_op jit(solution)/shard_map/ppermute | solution.py:420
  24.7 24.4 %collective-permute-start.8 = (f32[256,256]{1,0:T(8,128)S(1)}, f32[256,256]{1,0:T(8,128)S(1)}, u32[]{:S(2)}, u32[]{:S(2)}) collective-permute-start(f32[256,256]{1,0:T(8,128)S(1)} %copy-done.8), channel_id=1, source_target_pairs={{8,16},{12,20},{0,24},{4,28},{9,17},{13,21},{1,25},{5,29},{10,18},... | collective-permute-start | bytes 786440 | tf_op jit(solution)/shard_map/ppermute | solution.py:420
  28.6 22.9 %collective-permute-start.7 = (f32[256,256]{1,0:T(8,128)S(1)}, f32[256,256]{1,0:T(8,128)S(1)}, u32[]{:S(2)}, u32[]{:S(2)}) collective-permute-start(f32[256,256]{1,0:T(8,128)S(1)} %copy-done.9), channel_id=1, source_target_pairs={{8,16},{12,20},{0,24},{4,28},{9,17},{13,21},{1,25},{5,29},{10,18},... | collective-permute-start | bytes 786440 | tf_op jit(solution)/shard_map/ppermute | solution.py:420
  40.4 13.0 %collective-permute-start.17 = (f32[256,256]{1,0:T(8,128)}, f32[256,256]{1,0:T(8,128)S(1)}, u32[]{:S(2)}, u32[]{:S(2)}) collective-permute-start(f32[256,256]{1,0:T(8,128)} %collective-permute-done.15.k0_ref), channel_id=1, source_target_pairs={{8,12},{12,8},{24,28},{28,24},{9,13},{13,9},{25,29},{29,25},{10,14... | collective-permute-start | bytes 786440 | tf_op jit(solution)/shard_map/ppermute | solution.py:420
  41.1 14.8 %collective-permute-start.18 = (f32[256,256]{1,0:T(8,128)}, f32[256,256]{1,0:T(8,128)S(1)}, u32[]{:S(2)}, u32[]{:S(2)}) collective-permute-start(f32[256,256]{1,0:T(8,128)} %collective-permute-done.16.v0_ref), channel_id=1, source_target_pairs={{8,12},{12,8},{24,28},{28,24},{9,13},{13,9},{25,29},{29,25},{10,14... | collective-permute-start | bytes 786440 | tf_op jit(solution)/shard_map/ppermute | solution.py:420
  47.2 19.1 %collective-permute-start.13 = (f32[256,256]{1,0:T(8,128)}, f32[256,256]{1,0:T(8,128)S(1)}, u32[]{:S(2)}, u32[]{:S(2)}) collective-permute-start(f32[256,256]{1,0:T(8,128)} %collective-permute-done.11.k0_ref), channel_id=1, source_target_pairs={{16,20},{20,16},{24,28},{28,24},{17,21},{21,17},{25,29},{29,25},{1... | collective-permute-start | bytes 786440 | tf_op jit(solution)/shard_map/ppermute | solution.py:420
  49.1 17.1 %collective-permute-start.14 = (f32[256,256]{1,0:T(8,128)S(1)}, f32[256,256]{1,0:T(8,128)S(1)}, u32[]{:S(2)}, u32[]{:S(2)}) collective-permute-start(f32[256,256]{1,0:T(8,128)S(1)} %collective-permute-done.12.v0_ref), channel_id=1, source_target_pairs={{16,20},{20,16},{24,28},{28,24},{17,21},{21,17},{25,29},{29,25},{1... | collective-permute-start | bytes 786440 | tf_op jit(solution)/shard_map/ppermute | solution.py:420
  51.5 31.2 %collective-permute-start.10 = (f32[256,256]{1,0:T(8,128)S(1)}, f32[256,256]{1,0:T(8,128)S(1)}, u32[]{:S(2)}, u32[]{:S(2)}) collective-permute-start(f32[256,256]{1,0:T(8,128)S(1)} %collective-permute-done.8.v0_ref), channel_id=1, source_target_pairs={{16,20},{20,16},{24,28},{28,24},{17,21},{21,17},{25,29},{29,25},{1... | collective-permute-start | bytes 786440 | tf_op jit(solution)/shard_map/ppermute | solution.py:420
  53.5 29.2 %collective-permute-start.9 = (f32[256,256]{1,0:T(8,128)S(1)}, f32[256,256]{1,0:T(8,128)S(1)}, u32[]{:S(2)}, u32[]{:S(2)}) collective-permute-start(f32[256,256]{1,0:T(8,128)S(1)} %collective-permute-done.7.k0_ref), channel_id=1, source_target_pairs={{16,20},{20,16},{24,28},{28,24},{17,21},{21,17},{25,29},{29,25},{1... | collective-permute-start | bytes 786440 | tf_op jit(solution)/shard_map/ppermute | solution.py:420
  55.9 10.2 %collective-permute-start.2 = (f32[520,128]{1,0:T(8,128)S(1)}, f32[520,128]{1,0:T(8,128)S(1)}, u32[]{:S(2)}, u32[]{:S(2)}) collective-permute-start(f32[520,128]{1,0:T(8,128)S(1)} %get-tuple-element.18.total_ref), channel_id=1, source_target_pairs={{0,16},{4,20},{8,24},{12,28},{1,17},{5,21},{9,25},{13,29},{2,18},{... | collective-permute-start | bytes 798728 | tf_op jit(solution)/shard_map/ppermute | solution.py:420
  66.2 8.8 %collective-permute-start.3 = (f32[520,128]{1,0:T(8,128)S(1)}, f32[520,128]{1,0:T(8,128)S(1)}, u32[]{:S(2)}, u32[]{:S(2)}) collective-permute-start(f32[520,128]{1,0:T(8,128)S(1)} %shard_map.99.mine_ref), channel_id=1, source_target_pairs={{0,4},{4,0},{8,12},{12,8},{16,20},{20,16},{24,28},{28,24},{1,5},{5... | collective-permute-start | bytes 798728 | tf_op jit(solution)/shard_map/ppermute | solution.py:420
  77.2 14.4 %collective-permute-start.4 = (f32[8,256]{1,0:T(8,128)S(1)}, f32[8,256]{1,0:T(8,128)S(1)}, u32[]{:S(2)}, u32[]{:S(2)}) collective-permute-start(f32[8,256]{1,0:T(8,128)S(1)} %get-tuple-element.20.refs_0_), channel_id=1, source_target_pairs={{0,1},{1,2},{2,3},{3,0},{4,5},{5,6},{6,7},{7,4},{8,9},{9,10},{10,1... | collective-permute-start | bytes 24584 | tf_op jit(solution)/shard_map/ppermute | solution.py:473
  78.8 12.8 %collective-permute-start.5 = (f32[8,256]{1,0:T(8,128)S(1)}, f32[8,256]{1,0:T(8,128)S(1)}, u32[]{:S(2)}, u32[]{:S(2)}) collective-permute-start(f32[8,256]{1,0:T(8,128)S(1)} %get-tuple-element.20.refs_0_), channel_id=1, source_target_pairs={{0,2},{1,3},{2,0},{3,1},{4,6},{5,7},{6,4},{7,5},{8,10},{9,11},{10,... | collective-permute-start | bytes 24584 | tf_op jit(solution)/shard_map/ppermute | solution.py:473
  81.4 10.2 %collective-permute-start.6 = (f32[8,256]{1,0:T(8,128)S(1)}, f32[8,256]{1,0:T(8,128)S(1)}, u32[]{:S(2)}, u32[]{:S(2)}) collective-permute-start(f32[8,256]{1,0:T(8,128)S(1)} %get-tuple-element.20.refs_0_), channel_id=1, source_target_pairs={{0,3},{1,0},{2,1},{3,2},{4,7},{5,4},{6,5},{7,6},{8,11},{9,8},{10,9... | collective-permute-start | bytes 24584 | tf_op jit(solution)/shard_map/ppermute | solution.py:473
  82.7 8.9 %copy-start.6 = (f32[1024]{0:T(1024)S(1)}, f32[1024]{0:T(1024)}, u32[]{:S(2)}) copy-start(f32[1024]{0:T(1024)} %param.12) | copy-start | bytes 12292

commit v2 on v0

v2 whole, which is shorter than its diff:
```python
import functools
import math

import jax
import jax.numpy as jnp
from jax import lax
from jax.experimental import pallas as pl
from jax.experimental.pallas import tpu as pltpu
from jax.sharding import PartitionSpec as P

HD = 128
NEGATIVE = -1e30
EPSILON = 1e-05
F32 = jnp.float32
BF16 = jnp.bfloat16
NT = (((1,), (1,)), ((), ()))
VMEM_LIMIT = 32 * 1024 * 1024
VMEM = pl.BlockSpec(memory_space=pltpu.VMEM)
SMEM = pl.BlockSpec(memory_space=pltpu.SMEM)


def split(x):
    high = x.astype(BF16)
    low = (x - high.astype(F32)).astype(BF16)
    return high, low


def dot(a, b):
    return jnp.dot(a, b, preferred_element_type=F32)


def three_term(a, b):
    a_high, a_low = split(a)
    b_high, b_low = split(b)
    wide = dot(a_high, jnp.concatenate([b_high, b_low], axis=1))
    n = b.shape[1]
    return wide[:, :n] + wide[:, n:] + dot(a_low, b_high)


def three_term_nt(a, b):
    a_high, a_low = split(a)
    b_high, b_low = split(b)
    left = jnp.concatenate([a_high, a_low, a_high], axis=1)
    right = jnp.concatenate([b_high, b_high, b_low], axis=1)
    return lax.dot_general(left, right, NT, preferred_element_type=F32)


def call(kernel, in_specs, out_specs, out_shape, flops, size, exps=0, scratch=(), grid=(), alias=None):
    return pl.pallas_call(
        kernel,
        grid=grid,
        in_specs=in_specs,
        out_specs=out_specs,
        out_shape=out_shape,
        scratch_shapes=list(scratch),
        input_output_aliases=alias or {},
        cost_estimate=pl.CostEstimate(
            flops=int(flops), bytes_accessed=int(size), transcendentals=int(exps)
        ),
        compiler_params=pltpu.CompilerParams(vmem_limit_bytes=VMEM_LIMIT),
    )


def state_kernel(rate_ref, k_ref, v_ref, packed_ref, sums_ref):
    tokens = k_ref.shape[0]
    heads = rate_ref.shape[0]
    part = packed_ref.shape[1] - 8
    upto = lax.broadcasted_iota(jnp.int32, (tokens, tokens), 0)
    upto = (upto <= lax.broadcasted_iota(jnp.int32, (tokens, tokens), 1)).astype(F32)
    sums = jnp.dot(
        rate_ref[...], upto, precision=lax.Precision.HIGHEST, preferred_element_type=F32
    )
    sums_ref[...] = sums
    totals = sums[:, tokens - 1 : tokens]
    trailing = jnp.exp(totals - sums)
    for h in range(heads):
        at = slice(h * HD, (h + 1) * HD)
        state = three_term(k_ref[:, at].T * trailing[h : h + 1], v_ref[:, at])
        total = jnp.broadcast_to(totals[h : h + 1], (8, HD))
        for j in range(HD // part):
            packed_ref[h * (HD // part) + j, :part] = state[j * part : (j + 1) * part]
            packed_ref[h * (HD // part) + j, part:] = total


def local_states(rates, k_lin, v_lin, count):
    tokens, width = k_lin.shape
    heads = rates.shape[0]
    part = width // count
    assert part <= HD and part % 8 == 0
    return call(
        state_kernel,
        [VMEM] * 3,
        [VMEM] * 2,
        [
            jax.ShapeDtypeStruct((count, part + 8, HD), F32),
            jax.ShapeDtypeStruct((heads, tokens), F32),
        ],
        6 * tokens * width * HD,
        10 * tokens * width,
        tokens * heads,
    )(rates, k_lin, v_lin)


def chain_kernel(states_ref, prior_ref):
    count, part, _ = prior_ref.shape
    prior = jnp.zeros((part, HD), F32)
    for c in range(count):
        prior_ref[c] = prior
        if c < count - 1:
            prior = prior * jnp.exp(states_ref[c, part : part + 1, :]) + states_ref[c, :part, :]


def chained(states):
    count, packed, _ = states.shape
    return call(
        chain_kernel,
        [VMEM],
        VMEM,
        jax.ShapeDtypeStruct((count, packed - 8, HD), F32),
        states.size * 2,
        states.size * 8,
    )(states)


def inside_kernel(q_ref, k_ref, v_ref, sums_ref, out_ref):
    tokens = q_ref.shape[0]
    heads = sums_ref.shape[0]
    causal = lax.broadcasted_iota(jnp.int32, (tokens, tokens), 0) >= lax.broadcasted_iota(
        jnp.int32, (tokens, tokens), 1
    )
    columns = sums_ref[...].T
    for h in range(heads):
        at = slice(h * HD, (h + 1) * HD)
        scores = three_term_nt(q_ref[:, at], k_ref[:, at])
        gaps = columns[:, h : h + 1] - sums_ref[h : h + 1, :]
        weights = jnp.where(causal, jnp.exp(jnp.where(causal, gaps, 0.0)), 0.0)
        out_ref[:, at] = three_term(scores * weights, v_ref[:, at])


def inside_blocks(q_lin, k_lin, v_lin, sums):
    tokens, width = q_lin.shape
    return call(
        inside_kernel,
        [VMEM] * 4,
        VMEM,
        jax.ShapeDtypeStruct((tokens, width), F32),
        12 * tokens * tokens * width,
        16 * tokens * width,
        tokens * tokens * sums.shape[0],
    )(q_lin, k_lin, v_lin, sums)


def linear_kernel(q_ref, inside_ref, sums_ref, prior_ref, out_ref, energy_ref):
    tokens = q_ref.shape[0]
    heads = sums_ref.shape[0]
    leading = jnp.exp(sums_ref[...]).T
    squares = jnp.zeros((tokens, HD), F32)
    for h in range(heads):
        at = slice(h * HD, (h + 1) * HD)
        carried = three_term(q_ref[:, at], prior_ref[at, :])
        linear = inside_ref[:, at] + leading[:, h : h + 1] * carried
        out_ref[:, at] = linear
        squares = squares + linear * linear
    energy = lax.dot_general(
        jnp.ones((8, HD), F32),
        squares,
        NT,
        precision=lax.Precision.HIGHEST,
        preferred_element_type=F32,
    )
    for i in range(energy_ref.shape[0]):
        energy_ref[i] = energy


def linear_blocks(q_lin, inside, sums, prior, copies):
    tokens, width = q_lin.shape
    return call(
        linear_kernel,
        [VMEM] * 4,
        [VMEM] * 2,
        [
            jax.ShapeDtypeStruct((tokens, width), F32),
            jax.ShapeDtypeStruct((copies, 8, tokens), F32),
        ],
        6 * tokens * width * HD,
        14 * tokens * width,
    )(q_lin, inside, sums, prior)


def pair_kernel(core_ref, k_ref, v_ref, k_other_ref, v_other_ref, out_ref):
    core = core_ref[0]
    tokens = k_ref.shape[0]
    at = pl.ds(pl.multiple_of(core * HD, HD), HD)
    first = core == 0
    for side, (mine_ref, other_ref) in enumerate([(k_ref, k_other_ref), (v_ref, v_other_ref)]):
        mine, other = mine_ref[:, at], other_ref[:, at]
        to = slice(side * HD, (side + 1) * HD)
        out_ref[:tokens, to] = jnp.where(first, mine, other)
        out_ref[tokens:, to] = jnp.where(first, other, mine)


def pair_block(core, k_soft, v_soft, k_other, v_other):
    tokens = k_soft.shape[0]
    return call(
        pair_kernel,
        [SMEM] + [VMEM] * 4,
        VMEM,
        jax.ShapeDtypeStruct((2 * tokens, 2 * HD), F32),
        tokens * HD * 4,
        tokens * HD * 48,
    )(core, k_soft, v_soft, k_other, v_other)


def run_tiles(count, load, soften, gather):
    load(0, 0)
    load(1, 1)
    soften(0, 0)

    def turn(j, carry):
        for i, slot in ((2 * j + 1, 1), (2 * j + 2, 0)):
            load(i + 1, 1 - slot)
            gather(i - 1, 1 - slot)
            soften(i, slot)
        return carry

    lax.fori_loop(0, count // 2 - 1, turn, 0)
    gather(count - 2, 0)
    soften(count - 1, 1)
    gather(count - 1, 1)


def key_terms(kv_ref):
    k_high, k_low = split(kv_ref[:, :HD])
    v_high, v_low = split(kv_ref[:, HD:].T)
    return (
        jnp.concatenate([k_high, k_high, k_low], axis=1),
        jnp.concatenate([v_high, v_low], axis=0),
    )


def own_kernel(factor, core_ref, q_ref, q_other_ref, kv_ref, q_out, acc_out, stat_out, *scratch):
    keys_ref, values_ref = scratch[:2]
    scores, highs, lows, peaks = scratch[2:4], scratch[4:6], scratch[6:8], scratch[8:10]
    core = core_ref[0]
    tokens = q_ref.shape[0]
    group = q_out.shape[0] // 2
    keys_ref[...], values_ref[...] = key_terms(kv_ref)
    first = core == 0
    for g in range(group):
        at = pl.ds(pl.multiple_of(core * (group * HD) + g * HD, HD), HD)
        mine, other = q_ref[:, at], q_other_ref[:, at]
        for t, rows in enumerate(
            (jnp.where(first, mine, other), jnp.where(first, other, mine))
        ):
            high, low = split(rows.T * factor)
            q_out[2 * g + t, :HD] = high
            q_out[2 * g + t, HD:] = low

    def load(i, slot):
        count = tokens * (slot + 1)
        high_low = q_out[i]
        terms = jnp.concatenate([high_low, high_low[:HD]], axis=0)
        s = dot(keys_ref[:count], terms)
        key_at = lax.broadcasted_iota(jnp.int32, (tokens, tokens), 0)
        seen = key_at <= lax.broadcasted_iota(jnp.int32, (tokens, tokens), 1)
        edge = jnp.where(seen, s[count - tokens :], NEGATIVE)
        peak = jnp.max(edge, axis=0, keepdims=True)
        scores[slot][count - tokens : count] = edge
        if slot:
            scores[slot][:tokens] = s[:tokens]
            peak = jnp.maximum(peak, jnp.max(s[:tokens], axis=0, keepdims=True))
        peaks[slot][...] = jnp.broadcast_to(peak, (8, tokens))

    def soften(i, slot):
        peak = peaks[slot][0:1]
        total = jnp.zeros((1, tokens), F32)
        for c in range(slot + 1):
            at = slice(c * tokens, (c + 1) * tokens)
            w = jnp.exp2(scores[slot][at] - peak)
            total = total + jnp.sum(w, axis=0, keepdims=True)
            highs[slot][at], lows[slot][at] = split(w)
        stat_out[i, 0:1] = peak
        stat_out[i, 1:2] = total

    def gather(i, slot):
        count = tokens * (slot + 1)
        wide = dot(values_ref[:, :count], highs[slot][:count])
        acc_out[i] = wide[:HD] + wide[HD:] + dot(values_ref[:HD, :count], lows[slot][:count])

    run_tiles(2 * group, load, soften, gather)


def stage_scratch(tokens):
    return [
        pltpu.VMEM((2 * tokens, 3 * HD), BF16),
        pltpu.VMEM((2 * HD, 2 * tokens), BF16),
        *[pltpu.VMEM((2 * tokens, tokens), F32)] * 2,
        *[pltpu.VMEM((2 * tokens, tokens), BF16)] * 4,
        *[pltpu.VMEM((8, tokens), F32)] * 2,
    ]


def own_stage(core, q_soft, q_other, kv):
    tokens, width = q_soft.shape
    tiles = width // HD
    return call(
        functools.partial(own_kernel, math.log2(math.e) / math.sqrt(HD)),
        [SMEM] + [VMEM] * 3,
        [VMEM] * 3,
        [
            jax.ShapeDtypeStruct((tiles, 2 * HD, tokens), BF16),
            jax.ShapeDtypeStruct((tiles, HD, tokens), F32),
            jax.ShapeDtypeStruct((tiles, 8, tokens), F32),
        ],
        16 * tokens * width * 2 * tokens,
        tokens * width * 12,
        2 * tokens * tokens * tiles,
        stage_scratch(tokens),
    )(core, q_soft, q_other, kv)


def later_kernel(last, flag_ref, kv_ref, q_ref, acc_ref, stat_ref, *refs):
    if last:
        out_ref, *scratch = refs
    else:
        acc_out, stat_out, *scratch = refs
    keys_ref, values_ref = scratch[:2]
    scores, highs, lows, peaks = scratch[2:4], scratch[4:6], scratch[6:8], scratch[8:10]
    tiles, _, tokens = q_ref.shape
    group = tiles // 2

    def place(i):
        return 2 * i + flag_ref[1] if last else i

    def finish(i, acc, total):
        out_ref[:, pl.ds(pl.multiple_of(i * HD, HD), HD)] = (acc / total).T

    def load(i, slot):
        high_low = q_ref[place(i)]
        terms = jnp.concatenate([high_low, high_low[:HD]], axis=0)
        s = dot(keys_ref[...], terms)
        scores[slot][...] = s
        peaks[slot][0:1] = jnp.max(s, axis=0, keepdims=True)

    def soften(i, slot):
        old_peak = stat_ref[place(i), 0:1]
        peak = jnp.maximum(peaks[slot][0:1], old_peak)
        shrink = jnp.exp2(old_peak - peak)
        total = stat_ref[place(i), 1:2] * shrink
        for c in range(2):
            at = slice(c * tokens, (c + 1) * tokens)
            w = jnp.exp2(scores[slot][at] - peak)
            total = total + jnp.sum(w, axis=0, keepdims=True)
            highs[slot][at], lows[slot][at] = split(w)
        peaks[slot][1:2] = shrink
        peaks[slot][2:3] = total
        if not last:
            stat_out[place(i), 0:1] = peak
            stat_out[place(i), 1:2] = total

    def gather(i, slot):
        wide = dot(values_ref[...], highs[slot][...])
        new = wide[:HD] + wide[HD:] + dot(values_ref[:HD], lows[slot][...])
        acc = acc_ref[place(i)] * peaks[slot][1:2] + new
        if last:
            finish(i, acc, peaks[slot][2:3])
        else:
            acc_out[place(i)] = acc

    @pl.when(flag_ref[0] == 1)
    def _():
        keys_ref[...], values_ref[...] = key_terms(kv_ref)
        run_tiles(group if last else tiles, load, soften, gather)

    if last:

        @pl.when(flag_ref[0] == 0)
        def _():
            def only(i, carry):
                finish(i, acc_ref[place(i)], stat_ref[place(i), 1:2])
                return carry

            lax.fori_loop(0, group, only, 0)


def later_stage(flags, kv, q_terms, acc, stats, last):
    tiles, _, tokens = q_terms.shape
    if last:
        width = tiles // 2 * HD
        out_shape, out_specs, alias = jax.ShapeDtypeStruct((tokens, width), F32), VMEM, None
    else:
        out_shape = [jax.ShapeDtypeStruct(a.shape, F32) for a in (acc, stats)]
        out_specs, alias = [VMEM] * 2, {3: 0, 4: 1}
    share = 1 if last else 2
    return call(
        functools.partial(later_kernel, last),
        [SMEM] + [VMEM] * 4,
        out_specs,
        out_shape,
        share * 6 * tiles * HD * tokens * 2 * tokens,
        share * acc.size * 5,
        share * tokens * tokens * tiles,
        stage_scratch(tokens),
        alias=alias,
    )(flags, kv, q_terms, acc, stats)


def final_kernel(columns, core_ref, energy_ref, gain_ref, linear_ref, mine_ref, other_ref, lin_ref, soft_ref):
    energy = energy_ref[0]
    for i in range(1, energy_ref.shape[0]):
        energy = energy + energy_ref[i]
    factor = lax.rsqrt(energy / columns + EPSILON).T[:, 0:1]
    lin_ref[...] = linear_ref[...] * factor * gain_ref[...]
    soft_ref[...] = jnp.where(core_ref[0] == pl.program_id(0), mine_ref[...], other_ref[...])


def final(core, energies, gain, linear, mine, other, columns):
    tokens, width = linear.shape
    soft_half = mine.shape[1]
    half = pl.BlockSpec((tokens, width // 2), lambda j: (0, j))
    whole = pl.BlockSpec((tokens, soft_half), lambda j: (0, 0))
    return call(
        functools.partial(final_kernel, columns),
        [
            SMEM,
            pl.BlockSpec(energies.shape, lambda j: (0, 0, 0)),
            pl.BlockSpec((1, width // 2), lambda j: (0, j)),
            half,
            whole,
            whole,
        ],
        [half, pl.BlockSpec((tokens, soft_half), lambda j: (0, j))],
        [
            jax.ShapeDtypeStruct((tokens, width), F32),
            jax.ShapeDtypeStruct((tokens, 2 * soft_half), F32),
        ],
        tokens * width * 2,
        tokens * (width + 2 * soft_half) * 8,
        grid=(2,),
    )(core, energies, gain, linear, mine, other)


def body(q_lin, k_lin, v_lin, log_decay, lin_gain, q_soft, k_soft, v_soft):
    devices = lax.axis_size("ctx")
    chips = devices // 2
    heads = lax.axis_size("head")
    me = lax.axis_index("ctx")
    core, chip = me % 2, me // 2
    assert k_soft.shape[1] == 2 * HD

    def as_flags(*values):
        return jnp.stack([jnp.asarray(value).astype(jnp.int32) for value in values])

    core_flag = as_flags(core)
    swap_pairs = [(2 * c + e, 2 * c + 1 - e) for c in range(chips) for e in range(2)]

    def swap(array):
        return lax.ppermute(array, "ctx", swap_pairs)

    k_other, v_other, q_other = swap(k_soft), swap(v_soft), swap(q_soft)
    kv = pair_block(core_flag, k_soft, v_soft, k_other, v_other)
    arrived = [
        lax.ppermute(
            kv,
            "ctx",
            [
                (2 * (c ^ distance) + e, 2 * c + e)
                for c in range(chips)
                if c ^ distance < c
                for e in range(2)
            ],
        )
        for distance in range(1, chips)
    ]

    states, sums = local_states(log_decay, k_lin, v_lin, devices)
    states = lax.all_to_all(states, "ctx", 0, 0, tiled=True)
    prior = lax.all_to_all(chained(states), "ctx", 0, 0, tiled=True)
    prior = prior.reshape(-1, HD)
    inside = inside_blocks(q_lin, k_lin, v_lin, sums)

    q_terms, acc, stats = own_stage(core_flag, q_soft, q_other, kv)
    for distance in range(1, chips - 1):
        flags = as_flags((chip ^ distance) < chip, 0)
        acc, stats = later_stage(flags, arrived[distance - 1], q_terms, acc, stats, False)

    linear, energy = linear_blocks(q_lin, inside, sums, prior, heads)
    energies = lax.all_to_all(energy, "head", 0, 0, tiled=True)

    visible = (chip ^ (chips - 1)) < chip
    theirs = later_stage(as_flags(visible, 1 - core), arrived[-1], q_terms, acc, stats, True)
    other = swap(theirs)
    mine = later_stage(as_flags(visible, core), arrived[-1], q_terms, acc, stats, True)
    columns = q_lin.shape[1] * heads
    return final(core_flag, energies, lin_gain.reshape(1, -1), linear, mine, other, columns)


def solution(mesh):
    return jax.shard_map(
        body,
        mesh=mesh,
        in_specs=(
            P("ctx", "head"),
            P("ctx", "head"),
            P("ctx", "head"),
            P("head", "ctx"),
            P("head"),
            P("ctx", "head"),
            P("ctx", "head"),
            P("ctx", "head"),
        ),
        out_specs=(P("ctx", "head"), P("ctx", "head")),
        check_vma=False,
    )
```

time: 210 us -> 91.1 us (0.43)
  the two profiles are of different devices: /device:TPU:6 before, /device:TPU:0 now
where the time goes in v2:
time: 91.1 us; the launch traced here: 90.1 us
  starting transfers between devices  31 us (34%)
  local copies, waits for them, and re-layouts  20.2 us (22%)
  waiting for transfers between devices  19.4 us (21%)
  Pallas kernels  18.4 us (20%)
    unnamed x44, local copies, waits for them, and re-layouts  20.2 us
    ppermute x3, waiting for transfers between devices, body(): lax.ppermute(kv, 'ctx', [(2 * (c ^ distance) + e, 2 * c + e) for c in ran...  13.3 us
    all_to_all x1, starting transfers between devices, body(): prior = lax.all_to_all(chained(states), 'ctx', 0, 0, tiled=True)  11.3 us
    ppermute x3, starting transfers between devices, body(): lax.ppermute(kv, 'ctx', [(2 * (c ^ distance) + e, 2 * c + e) for c in ran...  8.69 us
    all_to_all x1, starting transfers between devices, body(): energies = lax.all_to_all(energy, 'head', 0, 0, tiled=True)  5.08 us
    all_to_all x1, starting transfers between devices, body(): states = lax.all_to_all(states, 'ctx', 0, 0, tiled=True)  4.85 us
    pallas_call x4, Pallas kernels, later_stage(): call(functools.partial(later_kernel, last), [SMEM] + [VMEM] * 4, out_spec...  4.41 us
    pallas_call x1, Pallas kernels, own_stage(): call(functools.partial(own_kernel, math.log2(math.e) / math.sqrt(HD)), [S...  3.87 us
  transfers between devices with their start and end apart: 10, of which 4 were waited for; matrix products, arithmetic and copies ran while one was open for 0% of the time, Pallas kernels for 17%

profile of v2, /device:TPU:0, one launch (start us, length us, event | category | flops | bytes accessed | tf_op | source)
XLA Modules:
  0.0 90.1 jit_solution(4007445845720740575)
XLA Ops:
  0.6 0.5 collective-permute-start.3
  1.1 0.1 collective-permute-start
  1.2 0.4 collective-permute-start.1
  1.7 0.0 copy-start
  1.7 1.2 %copy-done = f32[256,1024]{1,0:T(8,128)S(1)} copy-done((f32[256,1024]{1,0:T(8,128)S(1)}, f32[256,1024]{1,0:T(8,128)}, u32[]{:S(2)}) %copy-start) | copy-done | bytes 1048600
  2.9 0.0 copy-start.2
  2.9 1.2 %copy-done.2 = f32[256,1024]{1,0:T(8,128)S(1)} copy-done((f32[256,1024]{1,0:T(8,128)S(1)}, f32[256,1024]{1,0:T(8,128)}, u32[]{:S(2)}) %copy-start.2) | copy-done | bytes 1048600
  4.1 0.0 copy-start.17
  4.1 0.7 copy-done.17
  4.8 1.7 %shard_map.95 = (f32[8,136,128]{2,1,0:T(8,128)}, f32[8,256]{1,0:T(8,128)S(1)}) custom-call(f32[8,256]{1,0:T(8,128)S(1)} %copy-done.17, f32[256,1024]{1,0:T(8,128)S(1)} %copy-done, f32[256,1024]{1,0:T(8,128)S(1)} %copy-done.2), custom_call_target="tpu_custom_call" | custom-call | flops 201326592 | bytes 2621440 | tf_op jit(solution)/shard_map/pallas_call | solution.py:90
  6.5 4.8 %all-to-all-start = ((f32[8,136,128]{2,1,0:T(8,128)}), f32[8,136,128]{2,1,0:T(8,128)}, u32[]{:S(2)}, u32[]{:S(2)}) async-start(f32[8,136,128]{2,1,0:T(8,128)} %get-tuple-element.14), calls=%async_computation | async-start | bytes 1114112 | tf_op jit(solution)/shard_map/all_to_all | solution.py:477
  11.4 0.1 fusion.1.flag_ref
  11.5 0.0 collective-permute-done.k_other_ref
  11.5 0.0 collective-permute-done.1.v_other_ref
  11.5 0.0 copy-done.15
  11.5 0.0 copy-done.16
  11.5 4.0 %collective-permute-start.5 = (f32[512,256]{1,0:T(8,128)S(1)}, f32[512,256]{1,0:T(8,128)S(1)}, u32[]{:S(2)}, u32[]{:S(2)}) collective-permute-start(f32[512,256]{1,0:T(8,128)S(1)} %shard_map.99.kv_ref), channel_id=1, source_target_pairs={{0,8},{4,12},{16,24},{20,28},{1,9},{5,13},{17,25},{21,29},{2,10},{... | collective-permute-start | bytes 1572872 | tf_op jit(solution)/shard_map/ppermute | solution.py:463
  15.5 0.1 fusion.flag_ref
  15.6 0.1 pad_add_fusion.3.flag_ref
  15.7 3.4 %collective-permute-start.4 = (f32[512,256]{1,0:T(8,128)S(1)}, f32[512,256]{1,0:T(8,128)S(1)}, u32[]{:S(2)}, u32[]{:S(2)}) collective-permute-start(f32[512,256]{1,0:T(8,128)S(1)} %shard_map.99.kv_ref), channel_id=1, source_target_pairs={{0,16},{4,20},{8,24},{12,28},{1,17},{5,21},{9,25},{13,29},{2,18},{... | collective-permute-start | bytes 1572872 | tf_op jit(solution)/shard_map/ppermute | solution.py:463
  19.1 1.3 %collective-permute-start.2 = (f32[512,256]{1,0:T(8,128)S(1)}, f32[512,256]{1,0:T(8,128)S(1)}, u32[]{:S(2)}, u32[]{:S(2)}) collective-permute-start(f32[512,256]{1,0:T(8,128)S(1)} %shard_map.99.kv_ref), channel_id=1, source_target_pairs={{8,16},{12,20},{0,24},{4,28},{9,17},{13,21},{1,25},{5,29},{10,18},... | collective-permute-start | bytes 1572872 | tf_op jit(solution)/shard_map/ppermute | solution.py:463
  20.4 0.0 collective-permute-done.3.q_other_ref
  20.4 0.0 copy-start.20
  20.4 1.1 %copy-done.20 = f32[256,1536]{1,0:T(8,128)} copy-done((f32[256,1536]{1,0:T(8,128)}, f32[256,1536]{1,0:T(8,128)S(1)}, u32[]{:S(2)}) %copy-start.20) | copy-done | bytes 1572888
  21.6 1.4 %copy-done.19 = f32[256,1536]{1,0:T(8,128)S(1)} copy-done((f32[256,1536]{1,0:T(8,128)S(1)}, f32[256,1536]{1,0:T(8,128)}, u32[]{:S(2)}) %copy-start.19) | copy-done | bytes 1572888
  23.0 1.4 %copy-done.21 = f32[256,1536]{1,0:T(8,128)S(1)} copy-done((f32[256,1536]{1,0:T(8,128)S(1)}, f32[256,1536]{1,0:T(8,128)}, u32[]{:S(2)}) %copy-start.21) | copy-done | bytes 1572888
  24.4 3.9 %shard_map.100 = (bf16[12,256,256]{2,1,0:T(8,128)(2,1)S(1)}, f32[12,128,256]{2,1,0:T(8,128)S(1)}, f32[12,8,256]{2,1,0:T(8,128)S(1)}) custom-call(s32[1]{0:T(128)} %bitcast.core_ref, f32[256,1536]{1,0:T(8,128)S(1)} %copy-done.19, f32[256,1536]{1,0:T(8,128)S(1)} %copy-done.21, f32[512,256]{1,0:T(8,128)S(1)} %shard_map.99.kv_ref), custom_call_target="tpu_custom_call" | custom-call | flops 3221225472 | bytes 4718592 | tf_op jit(solution)/shard_map/pallas_call | solution.py:306
  28.2 1.7 %collective-permute-done.5.kv_ref = f32[512,256]{1,0:T(8,128)S(1)} collective-permute-done((f32[512,256]{1,0:T(8,128)S(1)}, f32[512,256]{1,0:T(8,128)S(1)}, u32[]{:S(2)}, u32[]{:S(2)}) %collective-permute-start.5) | collective-permute-done | bytes 524320 | tf_op jit(solution)/shard_map/ppermute | solution.py:463
  29.9 0.5 shard_map.101
  30.5 11.6 %collective-permute-done.4.kv_ref = f32[512,256]{1,0:T(8,128)S(1)} collective-permute-done((f32[512,256]{1,0:T(8,128)S(1)}, f32[512,256]{1,0:T(8,128)S(1)}, u32[]{:S(2)}, u32[]{:S(2)}) %collective-permute-start.4) | collective-permute-done | bytes 524320 | tf_op jit(solution)/shard_map/ppermute | solution.py:463
  42.1 0.5 shard_map.102
  42.7 0.0 collective-permute-done.2.kv_ref
  42.7 0.0 copy-start.10
  42.7 2.1 %shard_map.104 = f32[256,768]{1,0:T(8,128)} custom-call(s32[2]{0:T(128)S(1)} %pad_add_fusion.3.flag_ref, f32[512,256]{1,0:T(8,128)S(1)} %collective-permute-done.2.kv_ref, bf16[12,256,256]{2,1,0:T(8,128)(2,1)S(1)} %get-tuple-element.17.q_ref, f32[12,128,256]{2,1,0:T(8,128)S(1)} %get-tuple-element.22.acc_ref, f32[12,8,256]{2,1,0:T(8,128)S(1)} %get-tuple-element.23.stat_ref), custom_call_target="tpu_custom_call" | custom-call | flops 1207959552 | bytes 1966080 | tf_op jit(solution)/shard_map/pallas_call | solution.py:395
  44.8 0.0 copy-done.10
  44.8 0.0 collective-permute-start.6
  44.8 0.0 all-to-all-done.states_ref
  44.8 1.1 %shard_map.97 = f32[8,128,128]{2,1,0:T(8,128)S(1)} custom-call(f32[8,136,128]{2,1,0:T(8,128)} %all-to-all-done.states_ref), custom_call_target="tpu_custom_call" | custom-call | flops 278528 | bytes 1114112 | tf_op jit(solution)/shard_map/pallas_call | solution.py:115
  45.9 0.0 copy-start.12
  45.9 0.8 copy-done.12
  46.7 11.3 %all-to-all-start.1 = ((f32[8,128,128]{2,1,0:T(8,128)}), f32[8,128,128]{2,1,0:T(8,128)}, u32[]{:S(2)}, u32[]{:S(2)}) async-start(f32[8,128,128]{2,1,0:T(8,128)} %copy-done.12), calls=%async_computation.1 | async-start | bytes 1048576 | tf_op jit(solution)/shard_map/all_to_all | solution.py:478
  58.0 1.2 %copy-done.1 = f32[256,1024]{1,0:T(8,128)S(1)} copy-done((f32[256,1024]{1,0:T(8,128)S(1)}, f32[256,1024]{1,0:T(8,128)}, u32[]{:S(2)}) %copy-start.1) | copy-done | bytes 1048600
  59.3 1.2 %copy-done.3 = f32[256,1024]{1,0:T(8,128)S(1)} copy-done((f32[256,1024]{1,0:T(8,128)S(1)}, f32[256,1024]{1,0:T(8,128)}, u32[]{:S(2)}) %copy-start.3) | copy-done | bytes 1048600
  60.5 1.2 %copy-done.4 = f32[256,1024]{1,0:T(8,128)S(1)} copy-done((f32[256,1024]{1,0:T(8,128)S(1)}, f32[256,1024]{1,0:T(8,128)}, u32[]{:S(2)}) %copy-start.4) | copy-done | bytes 1048600
  61.7 1.7 %shard_map.96.inside_ref = f32[256,1024]{1,0:T(8,128)S(1)} custom-call(f32[256,1024]{1,0:T(8,128)S(1)} %copy-done.4, f32[256,1024]{1,0:T(8,128)S(1)} %copy-done.1, f32[256,1024]{1,0:T(8,128)S(1)} %copy-done.3, f32[8,256]{1,0:T(8,128)S(1)} %get-tuple-element.13.sums_ref), custom_call_target="tpu_custom_call" | custom-call | flops 805306368 | bytes 4194304 | tf_op jit(solution)/shard_map/pallas_call | solution.py:142
  63.4 0.0 copy-start.6
  63.4 1.0 %copy-done.6 = f32[256,1024]{1,0:T(8,128)} copy-done((f32[256,1024]{1,0:T(8,128)}, f32[256,1024]{1,0:T(8,128)S(1)}, u32[]{:S(2)}) %copy-start.6) | copy-done | bytes 1048600
  64.4 0.1 pad_add_fusion.2.flag_ref
  64.4 3.5 %all-to-all-done.1 = f32[8,128,128]{2,1,0:T(8,128)} async-done(((f32[8,128,128]{2,1,0:T(8,128)}), f32[8,128,128]{2,1,0:T(8,128)}, u32[]{:S(2)}, u32[]{:S(2)}) %all-to-all-start.1) | async-done | bytes 524320 | tf_op jit(solution)/shard_map/all_to_all | solution.py:478
  68.0 1.2 %copy-done.5 = f32[256,1024]{1,0:T(8,128)S(1)} copy-done((f32[256,1024]{1,0:T(8,128)S(1)}, f32[256,1024]{1,0:T(8,128)}, u32[]{:S(2)}) %copy-start.5) | copy-done | bytes 1048600
  69.2 1.2 %copy-done.7 = f32[256,1024]{1,0:T(8,128)S(1)} copy-done((f32[256,1024]{1,0:T(8,128)S(1)}, f32[256,1024]{1,0:T(8,128)}, u32[]{:S(2)}) %copy-start.7) | copy-done | bytes 1048600
  70.4 2.6 %shard_map.98 = (f32[256,1024]{1,0:T(8,128)S(1)}, f32[4,8,256]{2,1,0:T(8,128)}) custom-call(f32[256,1024]{1,0:T(8,128)S(1)} %copy-done.5, f32[256,1024]{1,0:T(8,128)S(1)} %copy-done.7, f32[8,256]{1,0:T(8,128)S(1)} %get-tuple-element.13.sums_ref, f32[1024,128]{1,0:T(8,128)} %bitcast.1.prior_ref), custom_call_target="tpu_custom_call" | custom-call | flops 201326592 | bytes 3670016 | tf_op jit(solution)/shard_map/pallas_call | solution.py:177
  73.0 1.0 %copy-done.13 = f32[256,1024]{1,0:T(8,128)} copy-done((f32[256,1024]{1,0:T(8,128)}, f32[256,1024]{1,0:T(8,128)S(1)}, u32[]{:S(2)}) %copy-start.13) | copy-done | bytes 1048600
  74.0 5.1 %all-to-all-start.2 = ((f32[4,8,256]{2,1,0:T(8,128)}), f32[4,8,256]{2,1,0:T(8,128)S(1)}, u32[]{:S(2)}, u32[]{:S(2)}) async-start(f32[4,8,256]{2,1,0:T(8,128)} %get-tuple-element.15), calls=%async_computation.2 | async-start | bytes 65536 | tf_op jit(solution)/shard_map/all_to_all | solution.py:488
  79.1 1.0 %copy-done.11 = f32[512,256]{1,0:T(8,128)S(1)} copy-done((f32[512,256]{1,0:T(8,128)S(1)}, f32[512,256]{1,0:T(8,128)}, u32[]{:S(2)}) %copy-start.11) | copy-done | bytes 524312
  80.1 1.2 %shard_map.103.mine_ref = f32[256,768]{1,0:T(8,128)S(1)} custom-call(s32[2]{0:T(128)S(1)} %pad_add_fusion.2.flag_ref, f32[512,256]{1,0:T(8,128)S(1)} %copy-done.11, bf16[12,256,256]{2,1,0:T(8,128)(2,1)S(1)} %get-tuple-element.17.q_ref, f32[12,128,256]{2,1,0:T(8,128)S(1)} %get-tuple-element.22.acc_ref, f32[12,8,256]{2,1,0:T(8,128)S(1)} %get-tuple-element.23.stat_ref), custom_call_target="tpu_custom_call" | custom-call | flops 1207959552 | bytes 1966080 | tf_op jit(solution)/shard_map/pallas_call | solution.py:395
  81.3 0.0 copy-start.8
  81.3 0.9 copy-done.8
  82.2 2.5 %all-to-all-done.2.energy_ref = f32[4,8,256]{2,1,0:T(8,128)S(1)} async-done(((f32[4,8,256]{2,1,0:T(8,128)}), f32[4,8,256]{2,1,0:T(8,128)S(1)}, u32[]{:S(2)}, u32[]{:S(2)}) %all-to-all-start.2) | async-done | bytes 32800 | tf_op jit(solution)/shard_map/all_to_all | solution.py:488
  84.7 0.0 collective-permute-done.6.other_ref
  84.7 0.0 copy-done.18
  84.7 1.1 %copy-done.9 = f32[256,768]{1,0:T(8,128)S(1)} copy-done((f32[256,768]{1,0:T(8,128)S(1)}, f32[256,768]{1,0:T(8,128)}, u32[]{:S(2)}) %copy-start.9) | copy-done | bytes 786456
  85.9 1.2 %copy-done.14 = f32[256,1024]{1,0:T(8,128)S(1)} copy-done((f32[256,1024]{1,0:T(8,128)S(1)}, f32[256,1024]{1,0:T(8,128)}, u32[]{:S(2)}) %copy-start.14) | copy-done | bytes 1048600
  87.1 3.0 %shard_map.105 = (f32[256,1024]{1,0:T(8,128)}, f32[256,1536]{1,0:T(8,128)}) custom-call(s32[1]{0:T(128)} %bitcast.core_ref, f32[4,8,256]{2,1,0:T(8,128)S(1)} %all-to-all-done.2.energy_ref, f32[1,1024]{1,0:T(1,128)S(1)} %bitcast.7, f32[256,1024]{1,0:T(8,128)S(1)} %copy-done.14, f32[256,768]{1,0:T(8,128)S(1)} %copy-done.9, ...), custom_call_target="tpu_custom_call" | custom-call | flops 524288 | bytes 5242880 | tf_op jit(solution)/shard_map/pallas_call | solution.py:422
  (15 shorter events, 0.1 us)
Async XLA Ops:
  0.6 19.8 %collective-permute-start.3 = (f32[256,1536]{1,0:T(8,128)}, f32[256,1536]{1,0:T(8,128)S(1)}, u32[]{:S(2)}, u32[]{:S(2)}) collective-permute-start(f32[256,1536]{1,0:T(8,128)} %q_ref.5), channel_id=1, source_target_pairs={{0,4},{4,0},{8,12},{12,8},{16,20},{20,16},{24,28},{28,24},{1,5},{5... | collective-permute-start | bytes 4718600 | tf_op jit(solution)/shard_map/ppermute | solution.py:458
  1.1 10.3 %collective-permute-start = (f32[256,256]{1,0:T(8,128)}, f32[256,256]{1,0:T(8,128)S(1)}, u32[]{:S(2)}, u32[]{:S(2)}) collective-permute-start(f32[256,256]{1,0:T(8,128)} %k_ref.5), channel_id=1, source_target_pairs={{0,4},{4,0},{8,12},{12,8},{16,20},{20,16},{24,28},{28,24},{1,5},{5... | collective-permute-start | bytes 786440 | tf_op jit(solution)/shard_map/ppermute | solution.py:458
  1.2 10.2 %collective-permute-start.1 = (f32[256,256]{1,0:T(8,128)}, f32[256,256]{1,0:T(8,128)S(1)}, u32[]{:S(2)}, u32[]{:S(2)}) collective-permute-start(f32[256,256]{1,0:T(8,128)} %v_ref.5), channel_id=1, source_target_pairs={{0,4},{4,0},{8,12},{12,8},{16,20},{20,16},{24,28},{28,24},{1,5},{5... | collective-permute-start | bytes 786440 | tf_op jit(solution)/shard_map/ppermute | solution.py:458
  1.7 1.2 %copy-start = (f32[256,1024]{1,0:T(8,128)S(1)}, f32[256,1024]{1,0:T(8,128)}, u32[]{:S(2)}) copy-start(f32[256,1024]{1,0:T(8,128)} %k_ref.4) | copy-start | bytes 3145732
  2.9 1.2 %copy-start.2 = (f32[256,1024]{1,0:T(8,128)S(1)}, f32[256,1024]{1,0:T(8,128)}, u32[]{:S(2)}) copy-start(f32[256,1024]{1,0:T(8,128)} %v_ref.4) | copy-start | bytes 3145732
  4.1 0.7 copy-start.17
  4.8 6.7 %copy-start.15 = (f32[256,256]{1,0:T(8,128)S(1)}, f32[256,256]{1,0:T(8,128)}, u32[]{:S(2)}) copy-start(f32[256,256]{1,0:T(8,128)} %k_ref.5) | copy-start | bytes 786436
  4.8 6.7 %copy-start.16 = (f32[256,256]{1,0:T(8,128)S(1)}, f32[256,256]{1,0:T(8,128)}, u32[]{:S(2)}) copy-start(f32[256,256]{1,0:T(8,128)} %v_ref.5) | copy-start | bytes 786436
  6.5 38.3 %all-to-all-start = ((f32[8,136,128]{2,1,0:T(8,128)}), f32[8,136,128]{2,1,0:T(8,128)}, u32[]{:S(2)}, u32[]{:S(2)}) async-start(f32[8,136,128]{2,1,0:T(8,128)} %get-tuple-element.14), calls=%async_computation | async-start | bytes 1114112 | tf_op jit(solution)/shard_map/all_to_all | solution.py:477
  11.5 18.4 %collective-permute-start.5 = (f32[512,256]{1,0:T(8,128)S(1)}, f32[512,256]{1,0:T(8,128)S(1)}, u32[]{:S(2)}, u32[]{:S(2)}) collective-permute-start(f32[512,256]{1,0:T(8,128)S(1)} %shard_map.99.kv_ref), channel_id=1, source_target_pairs={{0,8},{4,12},{16,24},{20,28},{1,9},{5,13},{17,25},{21,29},{2,10},{... | collective-permute-start | bytes 1572872 | tf_op jit(solution)/shard_map/ppermute | solution.py:463
  15.7 26.5 %collective-permute-start.4 = (f32[512,256]{1,0:T(8,128)S(1)}, f32[512,256]{1,0:T(8,128)S(1)}, u32[]{:S(2)}, u32[]{:S(2)}) collective-permute-start(f32[512,256]{1,0:T(8,128)S(1)} %shard_map.99.kv_ref), channel_id=1, source_target_pairs={{0,16},{4,20},{8,24},{12,28},{1,17},{5,21},{9,25},{13,29},{2,18},{... | collective-permute-start | bytes 1572872 | tf_op jit(solution)/shard_map/ppermute | solution.py:463
  19.1 23.6 %collective-permute-start.2 = (f32[512,256]{1,0:T(8,128)S(1)}, f32[512,256]{1,0:T(8,128)S(1)}, u32[]{:S(2)}, u32[]{:S(2)}) collective-permute-start(f32[512,256]{1,0:T(8,128)S(1)} %shard_map.99.kv_ref), channel_id=1, source_target_pairs={{8,16},{12,20},{0,24},{4,28},{9,17},{13,21},{1,25},{5,29},{10,18},... | collective-permute-start | bytes 1572872 | tf_op jit(solution)/shard_map/ppermute | solution.py:463
  20.4 1.1 %copy-start.20 = (f32[256,1536]{1,0:T(8,128)}, f32[256,1536]{1,0:T(8,128)S(1)}, u32[]{:S(2)}) copy-start(f32[256,1536]{1,0:T(8,128)S(1)} %collective-permute-done.3.q_other_ref) | copy-start | bytes 4718596
  21.6 1.4 %copy-start.19 = (f32[256,1536]{1,0:T(8,128)S(1)}, f32[256,1536]{1,0:T(8,128)}, u32[]{:S(2)}) copy-start(f32[256,1536]{1,0:T(8,128)} %q_ref.5) | copy-start | bytes 4718596
  23.0 1.4 %copy-start.21 = (f32[256,1536]{1,0:T(8,128)S(1)}, f32[256,1536]{1,0:T(8,128)}, u32[]{:S(2)}) copy-start(f32[256,1536]{1,0:T(8,128)} %copy-done.20) | copy-start | bytes 4718596
  42.7 2.1 %copy-start.10 = (f32[512,256]{1,0:T(8,128)}, f32[512,256]{1,0:T(8,128)S(1)}, u32[]{:S(2)}) copy-start(f32[512,256]{1,0:T(8,128)S(1)} %collective-permute-done.2.kv_ref) | copy-start | bytes 1572868
  44.8 39.9 %collective-permute-start.6 = (f32[256,768]{1,0:T(8,128)}, f32[256,768]{1,0:T(8,128)}, u32[]{:S(2)}, u32[]{:S(2)}) collective-permute-start(f32[256,768]{1,0:T(8,128)} %shard_map.104), channel_id=1, source_target_pairs={{0,4},{4,0},{8,12},{12,8},{16,20},{20,16},{24,28},{28,24},{1,5},{5... | collective-permute-start | bytes 2359304 | tf_op jit(solution)/shard_map/ppermute | solution.py:458
  45.9 0.8 copy-start.12
  46.7 21.2 %all-to-all-start.1 = ((f32[8,128,128]{2,1,0:T(8,128)}), f32[8,128,128]{2,1,0:T(8,128)}, u32[]{:S(2)}, u32[]{:S(2)}) async-start(f32[8,128,128]{2,1,0:T(8,128)} %copy-done.12), calls=%async_computation.1 | async-start | bytes 1048576 | tf_op jit(solution)/shard_map/all_to_all | solution.py:478
  58.0 1.2 %copy-start.1 = (f32[256,1024]{1,0:T(8,128)S(1)}, f32[256,1024]{1,0:T(8,128)}, u32[]{:S(2)}) copy-start(f32[256,1024]{1,0:T(8,128)} %k_ref.4) | copy-start | bytes 3145732
  59.3 1.2 %copy-start.3 = (f32[256,1024]{1,0:T(8,128)S(1)}, f32[256,1024]{1,0:T(8,128)}, u32[]{:S(2)}) copy-start(f32[256,1024]{1,0:T(8,128)} %v_ref.4) | copy-start | bytes 3145732
  60.5 1.2 %copy-start.4 = (f32[256,1024]{1,0:T(8,128)S(1)}, f32[256,1024]{1,0:T(8,128)}, u32[]{:S(2)}) copy-start(f32[256,1024]{1,0:T(8,128)} %q_ref.4) | copy-start | bytes 3145732
  63.4 1.0 %copy-start.6 = (f32[256,1024]{1,0:T(8,128)}, f32[256,1024]{1,0:T(8,128)S(1)}, u32[]{:S(2)}) copy-start(f32[256,1024]{1,0:T(8,128)S(1)} %shard_map.96.inside_ref) | copy-start | bytes 3145732
  68.0 1.2 %copy-start.5 = (f32[256,1024]{1,0:T(8,128)S(1)}, f32[256,1024]{1,0:T(8,128)}, u32[]{:S(2)}) copy-start(f32[256,1024]{1,0:T(8,128)} %q_ref.4) | copy-start | bytes 3145732
  69.2 1.2 %copy-start.7 = (f32[256,1024]{1,0:T(8,128)S(1)}, f32[256,1024]{1,0:T(8,128)}, u32[]{:S(2)}) copy-start(f32[256,1024]{1,0:T(8,128)} %copy-done.6) | copy-start | bytes 3145732
  73.0 1.0 %copy-start.13 = (f32[256,1024]{1,0:T(8,128)}, f32[256,1024]{1,0:T(8,128)S(1)}, u32[]{:S(2)}) copy-start(f32[256,1024]{1,0:T(8,128)S(1)} %get-tuple-element.16.linear_ref) | copy-start | bytes 3145732
  74.0 10.7 %all-to-all-start.2 = ((f32[4,8,256]{2,1,0:T(8,128)}), f32[4,8,256]{2,1,0:T(8,128)S(1)}, u32[]{:S(2)}, u32[]{:S(2)}) async-start(f32[4,8,256]{2,1,0:T(8,128)} %get-tuple-element.15), calls=%async_computation.2 | async-start | bytes 65536 | tf_op jit(solution)/shard_map/all_to_all | solution.py:488
  79.1 1.0 %copy-start.11 = (f32[512,256]{1,0:T(8,128)S(1)}, f32[512,256]{1,0:T(8,128)}, u32[]{:S(2)}) copy-start(f32[512,256]{1,0:T(8,128)} %copy-done.10) | copy-start | bytes 1572868
  80.1 4.6 %copy-start.18 = (f32[1024]{0:T(1024)S(1)}, f32[1024]{0:T(1024)}, u32[]{:S(2)}) copy-start(f32[1024]{0:T(1024)} %param.12) | copy-start | bytes 12292
  81.3 0.9 copy-start.8
  84.7 1.1 %copy-start.9 = (f32[256,768]{1,0:T(8,128)S(1)}, f32[256,768]{1,0:T(8,128)}, u32[]{:S(2)}) copy-start(f32[256,768]{1,0:T(8,128)} %copy-done.8) | copy-start | bytes 2359300
  85.9 1.2 %copy-start.14 = (f32[256,1024]{1,0:T(8,128)S(1)}, f32[256,1024]{1,0:T(8,128)}, u32[]{:S(2)}) copy-start(f32[256,1024]{1,0:T(8,128)} %copy-done.13) | copy-start | bytes 3145732

commit v3 on v0

v3 whole, which is shorter than its diff:
```python
import functools
import math

import jax
import jax.numpy as jnp
from jax import lax
from jax.experimental import pallas as pl
from jax.experimental.pallas import tpu as pltpu
from jax.sharding import PartitionSpec as P

HD = 128
NEGATIVE = -1e30
EPSILON = 1e-05
F32 = jnp.float32
BF16 = jnp.bfloat16
NT = (((1,), (1,)), ((), ()))
VMEM_LIMIT = 32 * 1024 * 1024
VMEM = pl.BlockSpec(memory_space=pltpu.VMEM)
SMEM = pl.BlockSpec(memory_space=pltpu.SMEM)
ANY = pl.BlockSpec(memory_space=pl.ANY)
HBM = pl.BlockSpec(memory_space=pltpu.HBM)


def split(x):
    high = x.astype(BF16)
    low = (x - high.astype(F32)).astype(BF16)
    return high, low


def dot(a, b):
    return jnp.dot(a, b, preferred_element_type=F32)


def three_term(a, b):
    a_high, a_low = split(a)
    b_high, b_low = split(b)
    wide = dot(a_high, jnp.concatenate([b_high, b_low], axis=1))
    n = b.shape[1]
    return wide[:, :n] + wide[:, n:] + dot(a_low, b_high)


def call(kernel, in_specs, out_specs, out_shape, flops, size, exps=0, scratch=(), alias=None, after=()):
    count = len(in_specs)

    def ordered(*refs):
        kernel(*refs[:count], *refs[count + len(after) :])

    made = pl.pallas_call(
        ordered,
        in_specs=in_specs + [ANY] * len(after),
        out_specs=out_specs,
        out_shape=out_shape,
        scratch_shapes=list(scratch),
        input_output_aliases=alias or {},
        cost_estimate=pl.CostEstimate(flops=1, bytes_accessed=1, transcendentals=0),
        compiler_params=pltpu.CompilerParams(vmem_limit_bytes=VMEM_LIMIT),
    )
    return lambda *operands: made(*operands, *after)


def column_copy(source, at, target, sem):
    copy = pltpu.make_async_copy(source.at[:, at], target, sem)
    copy.start()
    return copy


def head_copies(source, target, sems):
    return [
        column_copy(source, pl.ds(h * HD, HD), target.at[h], sems.at[h])
        for h in range(target.shape[0])
    ]


def state_kernel(rate_hbm, k_hbm, v_hbm, packed_ref, sums_ref, rate_ref, k_ref, v_ref, sem, k_sem, v_sem):
    tokens = k_hbm.shape[0]
    heads = rate_hbm.shape[0]
    half = heads // 2
    rate_copy = pltpu.make_async_copy(rate_hbm, rate_ref, sem)
    rate_copy.start()
    copies = list(zip(head_copies(k_hbm, k_ref, k_sem), head_copies(v_hbm, v_ref, v_sem)))
    upto = lax.broadcasted_iota(jnp.int32, (tokens, tokens), 0)
    upto = (upto <= lax.broadcasted_iota(jnp.int32, (tokens, tokens), 1)).astype(F32)
    rate_copy.wait()
    sums = jnp.dot(
        rate_ref[...], upto, precision=lax.Precision.HIGHEST, preferred_element_type=F32
    )
    sums_ref[...] = sums
    totals = sums[:, tokens - 1 : tokens]
    trailing = jnp.exp(totals - sums)
    for side in range(2):
        packed_ref[side, half * HD :] = jnp.zeros((8, HD), F32)
    for h in range(heads):
        side, i = h // half, h % half
        for copy in copies[h]:
            copy.wait()
        packed_ref[side, i * HD : (i + 1) * HD] = three_term(
            k_ref[h].T * trailing[h : h + 1], v_ref[h]
        )
        packed_ref[side, half * HD + i : half * HD + i + 1] = jnp.broadcast_to(
            totals[h : h + 1], (1, HD)
        )


def local_states(rates, k_lin, v_lin, after):
    tokens, width = k_lin.shape
    heads = rates.shape[0]
    return call(
        state_kernel,
        [HBM] * 3,
        [VMEM] * 2,
        [
            jax.ShapeDtypeStruct((2, heads // 2 * HD + 8, HD), F32),
            jax.ShapeDtypeStruct((heads, tokens), F32),
        ],
        6 * tokens * width * HD,
        10 * tokens * width,
        tokens * heads,
        [
            pltpu.VMEM((heads, tokens), F32),
            pltpu.VMEM((heads, tokens, HD), F32),
            pltpu.VMEM((heads, tokens, HD), F32),
            pltpu.SemaphoreType.DMA,
            pltpu.SemaphoreType.DMA((heads,)),
            pltpu.SemaphoreType.DMA((heads,)),
        ],
        after=after,
    )(rates, k_lin, v_lin)


def join(half, first, second, out_ref):
    decay = jnp.exp(second[half * HD :, :])
    for i in range(half):
        at = slice(i * HD, (i + 1) * HD)
        out_ref[at] = first[at] * decay[i : i + 1] + second[at]
    out_ref[half * HD :] = first[half * HD :] + second[half * HD :]


def chip_kernel(half, flags_ref, states_ref, others_ref, out_ref):
    core = flags_ref[0]

    @pl.when(core == 0)
    def _():
        join(half, states_ref[0], others_ref[0], out_ref)

    @pl.when(core == 1)
    def _():
        join(half, others_ref[1], states_ref[1], out_ref)


def chip_total(flags, states, others, after):
    _, packed, _ = states.shape
    return call(
        functools.partial(chip_kernel, (packed - 8) // HD),
        [SMEM, VMEM, VMEM],
        VMEM,
        jax.ShapeDtypeStruct((packed, HD), F32),
        packed * HD * 2,
        packed * HD * 12,
        after=after,
    )(flags, states, others)


def turn_kernel(half, bit, first, last, flags_ref, total_ref, theirs_ref, *refs):
    refs = list(refs)
    before_ref = None if first else refs.pop(0)
    prefix_ref = refs.pop(0)
    total_out = None if last else refs.pop(0)
    late = lax.rem(lax.div(flags_ref[1], 1 << bit), 2)

    @pl.when(late == 0)
    def _():
        prefix_ref[...] = jnp.zeros_like(prefix_ref) if first else before_ref[...]
        if not last:
            join(half, total_ref[...], theirs_ref[...], total_out)

    @pl.when(late == 1)
    def _():
        if first:
            prefix_ref[...] = theirs_ref[...]
        else:
            join(half, theirs_ref[...], before_ref[...], prefix_ref)
        if not last:
            join(half, theirs_ref[...], total_ref[...], total_out)


def turn(flags, bit, total, theirs, before, last, after):
    packed = total.shape[0]
    operands = [total, theirs] + ([] if before is None else [before])
    count = 1 if last else 2
    out = call(
        functools.partial(turn_kernel, (packed - 8) // HD, bit, before is None, last),
        [SMEM] + [VMEM] * len(operands),
        [VMEM] * count,
        [jax.ShapeDtypeStruct((packed, HD), F32)] * count,
        packed * HD * 4,
        packed * HD * 16,
        after=after,
    )(flags, *operands)
    return out[0], (None if last else out[1])


def inside_kernel(q_hbm, k_hbm, v_hbm, sums_ref, out_ref, terms_ref, q_ref, k_ref, v_ref, q_sem, k_sem, v_sem):
    tokens = q_hbm.shape[0]
    heads = sums_ref.shape[0]
    copies = list(
        zip(
            head_copies(q_hbm, q_ref, q_sem),
            head_copies(k_hbm, k_ref, k_sem),
            head_copies(v_hbm, v_ref, v_sem),
        )
    )
    causal = lax.broadcasted_iota(jnp.int32, (tokens, tokens), 0) >= lax.broadcasted_iota(
        jnp.int32, (tokens, tokens), 1
    )
    columns = sums_ref[...].T
    for h in range(heads):
        for copy in copies[h]:
            copy.wait()
        q_high, q_low = split(q_ref[h])
        k_high, k_low = split(k_ref[h])
        terms_ref[h, :, :HD] = q_high
        terms_ref[h, :, HD:] = q_low
        scores = lax.dot_general(
            jnp.concatenate([q_high, q_low, q_high], axis=1),
            jnp.concatenate([k_high, k_high, k_low], axis=1),
            NT,
            preferred_element_type=F32,
        )
        gaps = columns[:, h : h + 1] - sums_ref[h : h + 1, :]
        weights = jnp.where(causal, jnp.exp(jnp.where(causal, gaps, 0.0)), 0.0)
        out_ref[h] = three_term(scores * weights, v_ref[h])


def inside_blocks(q_lin, k_lin, v_lin, sums):
    tokens, width = q_lin.shape
    heads = sums.shape[0]
    return call(
        inside_kernel,
        [HBM] * 3 + [VMEM],
        [VMEM] * 2,
        [
            jax.ShapeDtypeStruct((heads, tokens, HD), F32),
            jax.ShapeDtypeStruct((heads, tokens, 2 * HD), BF16),
        ],
        12 * tokens * tokens * width,
        16 * tokens * width,
        tokens * tokens * heads,
        [pltpu.VMEM((heads, tokens, HD), F32)] * 3 + [pltpu.SemaphoreType.DMA((heads,))] * 3,
    )(q_lin, k_lin, v_lin, sums)


def linear_kernel(flags_ref, terms_ref, inside_ref, sums_ref, mine_ref, theirs_ref, other_ref, out_ref, energy_ref):
    heads, tokens, _ = out_ref.shape
    half = heads // 2
    core = flags_ref[0]
    leading = jnp.exp(sums_ref[...]).T
    squares = jnp.zeros((tokens, HD), F32)
    for side in range(2):
        decay = jnp.exp(other_ref[side, half * HD :])
        for i in range(half):
            h = side * half + i
            at = slice(i * HD, (i + 1) * HD)
            prior = jnp.where(core == side, mine_ref[at], theirs_ref[at])
            prior = jnp.where(core == 1, prior * decay[i : i + 1] + other_ref[side, at], prior)
            high, low = split(prior)
            wide = dot(terms_ref[h, :, :HD], jnp.concatenate([high, low], axis=1))
            carried = wide[:, :HD] + wide[:, HD:] + dot(terms_ref[h, :, HD:], high)
            linear = inside_ref[h] + leading[:, h : h + 1] * carried
            out_ref[h] = linear
            squares = squares + linear * linear
    energy_ref[...] = lax.dot_general(
        jnp.ones((8, HD), F32),
        squares,
        NT,
        precision=lax.Precision.HIGHEST,
        preferred_element_type=F32,
    )


def linear_blocks(flags, terms, inside, sums, mine, theirs, other, after):
    heads, tokens, _ = inside.shape
    width = heads * HD
    return call(
        linear_kernel,
        [SMEM] + [VMEM] * 6,
        [VMEM] * 2,
        [
            jax.ShapeDtypeStruct(inside.shape, F32),
            jax.ShapeDtypeStruct((8, tokens), F32),
        ],
        6 * tokens * width * HD,
        14 * tokens * width,
        after=after,
    )(flags, terms, inside, sums, mine, theirs, other)


def norm_kernel(columns, energy_ref, other_ref, gain_ref, linear_ref, out_hbm, out_ref, sems):
    heads = linear_ref.shape[0]
    factor = lax.rsqrt((energy_ref[...] + other_ref[...]) / columns + EPSILON).T[:, 0:1]
    copies = []
    for h in range(heads):
        at = slice(h * HD, (h + 1) * HD)
        out_ref[h] = linear_ref[h] * factor * gain_ref[:, at]
        copy = pltpu.make_async_copy(out_ref.at[h], out_hbm.at[:, pl.ds(h * HD, HD)], sems.at[h])
        copy.start()
        copies.append(copy)
    for copy in copies:
        copy.wait()


def normalized(energy, other, gain, linear, columns, after):
    heads, tokens, _ = linear.shape
    return call(
        functools.partial(norm_kernel, columns),
        [VMEM] * 4,
        ANY,
        jax.ShapeDtypeStruct((tokens, heads * HD), F32),
        linear.size * 2,
        linear.size * 8,
        0,
        [pltpu.VMEM(linear.shape, F32), pltpu.SemaphoreType.DMA((heads,))],
        after=after,
    )(energy, other, gain, linear)


def pair_kernel(flags_ref, k_ref, v_ref, k_other_ref, v_other_ref, out_ref):
    core = flags_ref[0]
    tokens = k_ref.shape[0]
    at = pl.ds(pl.multiple_of(core * HD, HD), HD)
    for side, (mine_ref, other_ref) in enumerate([(k_ref, k_other_ref), (v_ref, v_other_ref)]):
        to = slice(side * HD, (side + 1) * HD)
        out_ref[pl.ds(core * tokens, tokens), to] = mine_ref[:, at]
        out_ref[pl.ds((1 - core) * tokens, tokens), to] = other_ref[:, at]


def pair_block(flags, k_soft, v_soft, k_other, v_other):
    tokens = k_soft.shape[0]
    return call(
        pair_kernel,
        [SMEM] + [VMEM] * 4,
        VMEM,
        jax.ShapeDtypeStruct((2 * tokens, 2 * HD), F32),
        tokens * HD * 4,
        tokens * HD * 48,
    )(flags, k_soft, v_soft, k_other, v_other)


def run_heads(count, load, soften, gather):
    load(0, 0)
    load(1, 1)
    soften(0, 0)

    def turn(j, carry):
        for i, slot in ((2 * j + 1, 1), (2 * j + 2, 0)):
            load(i + 1, 1 - slot)
            gather(i - 1, 1 - slot)
            soften(i, slot)
        return carry

    lax.fori_loop(0, count // 2 - 1, turn, 0)
    gather(count - 2, 0)
    soften(count - 1, 1)
    gather(count - 1, 1)


def fill_terms(kv_ref, keys_ref, values_ref):
    k_high, k_low = split(kv_ref[:, :HD].T)
    keys_ref[:HD] = k_high
    keys_ref[HD : 2 * HD] = k_high
    keys_ref[2 * HD :] = k_low
    v_high, v_low = split(kv_ref[:, HD:])
    values_ref[:, :HD] = v_high
    values_ref[:, HD:] = v_low


def lane_max(array):
    peak = array[:, :HD]
    for c in range(1, array.shape[1] // HD):
        peak = jnp.maximum(peak, array[:, c * HD : (c + 1) * HD])
    return peak


def score_terms(pair):
    return jnp.concatenate([pair, pair[:, :HD]], axis=1)


def weigh(scores_ref, rows, count, peak, total, high_ref, low_ref):
    for c in range(count // HD):
        at = slice(c * HD, (c + 1) * HD)
        w = jnp.exp2(scores_ref[rows, at] - peak)
        total = total + w
        high_ref[rows, at], low_ref[rows, at] = split(w)
    return total


def summed(high, low, values):
    wide = dot(high, values)
    return wide[:, :HD] + wide[:, HD:] + dot(low, values[:, :HD])


def own_kernel(factor, flags_ref, q_hbm, q_other_hbm, kv_ref, q_out, acc_out, peak_out, total_out, *scratch):
    keys_ref, values_ref = scratch[:2]
    scores, highs, lows, peaks = scratch[2:4], scratch[4:6], scratch[6:8], scratch[8:10]
    q_ref, sems = scratch[12:]
    core = flags_ref[0]
    tokens = q_hbm.shape[0]
    group = q_out.shape[0]
    copies = []
    for g in range(group):
        at = pl.ds(pl.multiple_of((core * group + g) * HD, HD), HD)
        mine = q_ref.at[g, pl.ds(pl.multiple_of(core * tokens, tokens), tokens)]
        other = q_ref.at[g, pl.ds(pl.multiple_of((1 - core) * tokens, tokens), tokens)]
        copies.append(
            (
                column_copy(q_hbm, at, mine, sems.at[g, 0]),
                column_copy(q_other_hbm, at, other, sems.at[g, 1]),
            )
        )
    fill_terms(kv_ref, keys_ref, values_ref)
    for g in range(group):
        for copy in copies[g]:
            copy.wait()
        high, low = split(q_ref[g] * factor)
        q_out[g, :, :HD] = high
        q_out[g, :, HD:] = low

    seen = lax.broadcasted_iota(jnp.int32, (tokens, tokens), 1)
    seen = seen <= lax.broadcasted_iota(jnp.int32, (tokens, tokens), 0)
    early, late = slice(0, tokens), slice(tokens, 2 * tokens)

    def load(g, slot):
        terms = score_terms(q_out[g])
        left = dot(terms, keys_ref[:, early])
        right = dot(terms[late], keys_ref[:, late])
        edge = jnp.where(seen, left[early], NEGATIVE)
        far = jnp.where(seen, right, NEGATIVE)
        scores[slot][early, early] = edge
        scores[slot][late, early] = left[late]
        scores[slot][late, late] = far
        peaks[slot][early] = lane_max(edge)
        peaks[slot][late] = jnp.maximum(lane_max(left[late]), lane_max(far))

    def soften(g, slot):
        peak = jnp.max(peaks[slot][...], axis=1, keepdims=True)
        peak = jnp.broadcast_to(peak, (2 * tokens, HD))
        peak_out[g] = peak
        zero = jnp.zeros((tokens, HD), F32)
        total_out[g, early] = weigh(
            scores[slot], early, tokens, peak[early], zero, highs[slot], lows[slot]
        )
        total_out[g, late] = weigh(
            scores[slot], late, 2 * tokens, peak[late], zero, highs[slot], lows[slot]
        )

    def gather(g, slot):
        acc_out[g, early] = summed(
            highs[slot][early, early], lows[slot][early, early], values_ref[early]
        )
        acc_out[g, late] = summed(highs[slot][late], lows[slot][late], values_ref[...])

    run_heads(group, load, soften, gather)


def stage_scratch(rows, keys):
    return [
        *[pltpu.VMEM((rows, keys), F32)] * 2,
        *[pltpu.VMEM((rows, keys), BF16)] * 4,
        *[pltpu.VMEM((rows, HD), F32)] * 4,
    ]


def own_stage(flags, q_soft, q_other, kv, after):
    tokens, width = q_soft.shape
    group = width // (2 * HD)
    stat = jax.ShapeDtypeStruct((group, 2 * tokens, HD), F32)
    return call(
        functools.partial(own_kernel, math.log2(math.e) / math.sqrt(HD)),
        [SMEM, HBM, ANY, VMEM],
        [VMEM] * 4,
        [jax.ShapeDtypeStruct((group, 2 * tokens, 2 * HD), BF16), stat, stat, stat],
        16 * tokens * width * 2 * tokens,
        tokens * width * 12,
        4 * tokens * tokens * group,
        [
            pltpu.VMEM((3 * HD, 2 * tokens), BF16),
            pltpu.VMEM((2 * tokens, 2 * HD), BF16),
            *stage_scratch(2 * tokens, 2 * tokens),
            pltpu.VMEM((group, 2 * tokens, HD), F32),
            pltpu.SemaphoreType.DMA((group, 2)),
        ],
        after=after,
    )(flags, q_soft, q_other, kv)


def later_kernel(distance, flags_ref, kv_ref, q_ref, acc_ref, peak_ref, total_ref, acc_out, peak_out, total_out, *scratch):
    keys_ref, values_ref = scratch[:2]
    scores, highs, lows, peaks = scratch[2:4], scratch[4:6], scratch[6:8], scratch[8:10]
    shrinks = scratch[10:12]
    group, rows, _ = q_ref.shape
    everything = slice(0, rows)
    chip = flags_ref[1]

    def load(g, slot):
        s = dot(score_terms(q_ref[g]), keys_ref[...])
        scores[slot][...] = s
        peaks[slot][...] = lane_max(s)

    def soften(g, slot):
        old = peak_ref[g]
        peak = jnp.maximum(jnp.max(peaks[slot][...], axis=1, keepdims=True), old)
        shrink = jnp.exp2(old - peak)
        peak_out[g] = peak
        total_out[g] = weigh(
            scores[slot], everything, keys_ref.shape[1], peak, total_ref[g] * shrink,
            highs[slot], lows[slot],
        )
        shrinks[slot][...] = shrink

    def gather(g, slot):
        acc_out[g] = acc_ref[g] * shrinks[slot][...] + summed(
            highs[slot][...], lows[slot][...], values_ref[...]
        )

    @pl.when(lax.bitwise_xor(chip, distance) < chip)
    def _():
        fill_terms(kv_ref, keys_ref, values_ref)
        run_heads(group, load, soften, gather)


def later_stage(flags, distance, kv, q_terms, acc, peak, total, after):
    group, rows, _ = q_terms.shape
    keys = kv.shape[0]
    return call(
        functools.partial(later_kernel, distance),
        [SMEM] + [VMEM] * 5,
        [VMEM] * 3,
        [jax.ShapeDtypeStruct(acc.shape, F32)] * 3,
        12 * group * HD * rows * keys,
        acc.size * 8,
        rows * keys * group,
        [
            pltpu.VMEM((3 * HD, keys), BF16),
            pltpu.VMEM((keys, 2 * HD), BF16),
            *stage_scratch(rows, keys),
        ],
        alias={3: 0, 4: 1, 5: 2},
        after=after,
    )(flags, kv, q_terms, acc, peak, total)


def last_kernel(distance, whose, flags_ref, kv_ref, q_ref, acc_ref, peak_ref, total_ref, out, *scratch):
    keys_ref, values_ref = scratch[:2]
    scores, highs, lows, peaks = scratch[2:4], scratch[4:6], scratch[6:8], scratch[8:10]
    shrinks, totals, scratch = scratch[10:12], scratch[12:14], scratch[14:]
    group, rows, _ = q_ref.shape
    tokens = rows // 2
    everything = slice(0, tokens)
    core, chip = flags_ref[0], flags_ref[1]
    side = core if whose == "own" else 1 - core
    at = pl.ds(pl.multiple_of(side * tokens, tokens), tokens)

    def copy_out(g):
        out_ref, sems = scratch
        to = pl.ds(pl.multiple_of((core * group + g) * HD, HD), HD)
        return pltpu.make_async_copy(out_ref.at[g], out.at[:, to], sems.at[g])

    def finish(g, acc, total):
        result = acc / jnp.sum(total, axis=1, keepdims=True)
        if whose == "own":
            scratch[0][g] = result
            copy_out(g).start()
        else:
            out[g] = result

    def load(g, slot):
        s = dot(score_terms(q_ref[g, at]), keys_ref[...])
        scores[slot][...] = s
        peaks[slot][...] = lane_max(s)

    def soften(g, slot):
        old = peak_ref[g, at]
        peak = jnp.maximum(jnp.max(peaks[slot][...], axis=1, keepdims=True), old)
        shrink = jnp.exp2(old - peak)
        totals[slot][...] = weigh(
            scores[slot], everything, keys_ref.shape[1], peak, total_ref[g, at] * shrink,
            highs[slot], lows[slot],
        )
        shrinks[slot][...] = shrink

    def gather(g, slot):
        acc = acc_ref[g, at] * shrinks[slot][...] + summed(
            highs[slot][...], lows[slot][...], values_ref[...]
        )
        finish(g, acc, totals[slot][...])

    visible = lax.bitwise_xor(chip, distance) < chip

    @pl.when(visible)
    def _():
        fill_terms(kv_ref, keys_ref, values_ref)
        run_heads(group, load, soften, gather)

    @pl.when(jnp.logical_not(visible))
    def _():
        for g in range(group):
            finish(g, acc_ref[g, at], total_ref[g, at])

    if whose == "own":
        for g in range(group):
            copy_out(g).wait()


def last_stage(flags, distance, whose, kv, q_terms, acc, peak, total, after):
    group, rows, _ = q_terms.shape
    keys, tokens = kv.shape[0], rows // 2
    scratch = [
        pltpu.VMEM((3 * HD, keys), BF16),
        pltpu.VMEM((keys, 2 * HD), BF16),
        *stage_scratch(tokens, keys),
        *[pltpu.VMEM((tokens, HD), F32)] * 2,
    ]
    if whose == "own":
        out_shape, out_spec = jax.ShapeDtypeStruct((tokens, 2 * group * HD), F32), ANY
        scratch += [pltpu.VMEM((group, tokens, HD), F32), pltpu.SemaphoreType.DMA((group,))]
    else:
        out_shape, out_spec = jax.ShapeDtypeStruct((group, tokens, HD), F32), VMEM
    return call(
        functools.partial(last_kernel, distance, whose),
        [SMEM] + [VMEM] * 5,
        out_spec,
        out_shape,
        6 * group * HD * rows * keys,
        acc.size * 4,
        rows * keys * group // 2,
        scratch,
        after=after,
    )(flags, kv, q_terms, acc, peak, total)


def place_kernel(flags_ref, other_ref, soft_hbm, out_hbm, sems):
    group = other_ref.shape[0]
    copies = []
    for g in range(group):
        to = pl.ds(pl.multiple_of(((1 - flags_ref[0]) * group + g) * HD, HD), HD)
        copy = pltpu.make_async_copy(other_ref.at[g], out_hbm.at[:, to], sems.at[g])
        copy.start()
        copies.append(copy)
    for copy in copies:
        copy.wait()


def placed(flags, other, soft):
    return call(
        place_kernel,
        [SMEM, VMEM, ANY],
        ANY,
        jax.ShapeDtypeStruct(soft.shape, F32),
        0,
        other.size * 8,
        0,
        [pltpu.SemaphoreType.DMA((other.shape[0],))],
        alias={2: 0},
    )(flags, other, soft)


def plus_kernel(a_ref, b_ref, out_ref):
    out_ref[...] = a_ref[...] + b_ref[...]


def plus(a, b, after):
    return call(
        plus_kernel, [VMEM] * 2, VMEM, jax.ShapeDtypeStruct(a.shape, F32), a.size, a.size * 12, after=after
    )(a, b)


def relay_kernel(flags_ref, beside_ref, across_ref, out_ref):
    @pl.when(flags_ref[0] == 0)
    def _():
        out_ref[...] = beside_ref[...]

    @pl.when(flags_ref[0] == 1)
    def _():
        out_ref[...] = across_ref[...]


def relayed(flags, beside, across, after):
    return call(
        relay_kernel,
        [SMEM, VMEM, VMEM],
        VMEM,
        jax.ShapeDtypeStruct(beside.shape, F32),
        beside.size,
        beside.size * 8,
        after=after,
    )(flags, beside, across)


def body(q_lin, k_lin, v_lin, log_decay, lin_gain, q_soft, k_soft, v_soft):
    chips = lax.axis_size("ctx") // 2
    heads = lax.axis_size("head")
    me = lax.axis_index("ctx")
    flags = jnp.stack([me & 1, me >> 1]).astype(jnp.int32)
    assert k_soft.shape[1] == 2 * HD
    swap_pairs = [(2 * c + e, 2 * c + 1 - e) for c in range(chips) for e in range(2)]

    def swap(array):
        return lax.ppermute(array, "ctx", swap_pairs)

    def across(array, distance, wanted=lambda c, e: True):
        pairs = [
            (2 * (c ^ distance) + e, 2 * c + e)
            for c in range(chips)
            for e in range(2)
            if wanted(c, e)
        ]
        return lax.ppermute(array, "ctx", pairs)

    square = chips == 4
    k_other, v_other, q_other = swap(k_soft), swap(v_soft), swap(q_soft)
    kv = pair_block(flags, k_soft, v_soft, k_other, v_other)
    arrived = {}
    for distance in range(1, chips - 1 if square else chips):
        arrived[distance] = across(
            kv,
            distance,
            lambda c, e, d=distance: c ^ d < c or (square and d == 1 and c == 0 and e == 0),
        )

    states, sums = local_states(log_decay, k_lin, v_lin, [kv])
    others = swap(states)
    inside, terms = inside_blocks(q_lin, k_lin, v_lin, sums)
    total, prefix = chip_total(flags, states, others, [inside]), None

    q_terms, *carried = own_stage(flags, q_soft, q_other, kv, [total])
    if square:
        relay = relayed(flags, arrived[1], arrived[2], [carried[0]])
        pairs = [(2, 6), (0, 4), (5, 7), (7, 5)]
        arrived[3] = lax.ppermute(relay, "ctx", pairs)
        token = relay
    else:
        token = carried[0]

    bits = chips.bit_length() - 1
    for bit in range(bits):
        last = bit == bits - 1
        theirs = across(total, 1 << bit, lambda c, e: not last or c ^ (1 << bit) < c)
        prefix, total = turn(flags, bit, total, theirs, prefix, last, [token])
        distance = bit + 1
        carried = later_stage(flags, distance, arrived[distance], q_terms, *carried, [prefix])
        token = carried[0]
    prefix_other = swap(prefix)
    for distance in range(bits + 1, chips - 1):
        carried = later_stage(flags, distance, arrived[distance], q_terms, *carried, [])

    linear, energy = linear_blocks(
        flags, terms, inside, sums, prefix, prefix_other, others, [carried[0]]
    )

    def exchanged(array, step):
        return lax.ppermute(array, "head", [(i, i ^ step) for i in range(heads)])

    operands = (arrived[chips - 1], q_terms, *carried)
    theirs = last_stage(flags, chips - 1, "other", *operands, [energy])
    step, other = 1, exchanged(energy, 1)
    while 2 * step < heads:
        step *= 2
        energy = plus(energy, other, [theirs])
        other = exchanged(energy, step)
    soft_out = last_stage(flags, chips - 1, "own", *operands, [energy])
    columns = q_lin.shape[1] * heads
    lin_out = normalized(energy, other, lin_gain.reshape(1, -1), linear, columns, [])
    soft_out = placed(flags, swap(theirs), soft_out)
    return (lin_out, soft_out)


def solution(mesh):
    return jax.shard_map(
        body,
        mesh=mesh,
        in_specs=(
            P("ctx", "head"),
            P("ctx", "head"),
            P("ctx", "head"),
            P("head", "ctx"),
            P("head"),
            P("ctx", "head"),
            P("ctx", "head"),
            P("ctx", "head"),
        ),
        out_specs=(P("ctx", "head"), P("ctx", "head")),
        check_vma=False,
    )
```

time: 210 us -> 71.5 us (0.34)
  matrix products: 87.6 us -> 0 us
  Pallas kernels: 0 us -> 40.1 us
  local copies, waits for them, and re-layouts: 33.3 us -> 3.24 us
  blocking collectives: 21.9 us -> 0 us
  other arithmetic: 20.8 us -> 0.07 us
  waiting for transfers between devices: 27 us -> 13.2 us
  between operations: 14.6 us -> 1.01 us
  starting transfers between devices: 0.11 us -> 13.5 us
  loops' own time: 3.18 us -> 0 us
    dot_general x12 -> x0, matrix products: 87.6 us -> none  [the longest x4 48.9 us: attend(): jnp.einsum('kgts,skd->kgtd', weights, value_slab, precision=HIGHEST)]
    pallas_call x0 -> x16, Pallas kernels: none -> 40.1 us  [call(): return lambda *operands: made(*operands, *after)]
    all_gather x3 -> x0, waiting for transfers between devices: 25.6 us -> none  [the longest x1 23.5 us: soft_layer(): value_rows = lax.all_gather(v_soft, 'ctx', axis=0, tiled=True)]
    ppermute x0 -> x13, starting transfers between devices: none -> 13.5 us  [the longest x4 6.61 us: across(): return lax.ppermute(array, 'ctx', pairs)]
    ppermute x0 -> x13, waiting for transfers between devices: none -> 13.2 us  [the longest x4 7.44 us: across(): return lax.ppermute(array, 'ctx', pairs)]
    unnamed x22 -> x16, local copies, waits for them, and re-layouts: 15.5 us -> 3.24 us
    psum x1 -> x0, blocking collectives: 11.7 us -> none  [body(): energy = lax.psum(jnp.sum(linear * linear, axis=1, keepdims=True), 'head')]
    unnamed x1 -> x0, blocking collectives: 10.2 us -> none
  transfers between devices with their start and end apart: 3 -> 13, of which waited for: 2 -> 7; matrix products, arithmetic and copies ran while one was open for 57% -> 0% of each run, Pallas kernels for 0% -> 48%
where the time goes in v3:
time: 71.5 us; the launch traced here: 71.2 us
  Pallas kernels  40.1 us (56%)
  starting transfers between devices  13.5 us (19%)
  waiting for transfers between devices  13.2 us (18%)
  local copies, waits for them, and re-layouts  3.24 us (5%)
  between operations  1.01 us (1%)
    pallas_call x16, Pallas kernels, call(): return lambda *operands: made(*operands, *after)  40.1 us
    ppermute x4, waiting for transfers between devices, across(): return lax.ppermute(array, 'ctx', pairs)  7.44 us
    ppermute x4, starting transfers between devices, across(): return lax.ppermute(array, 'ctx', pairs)  6.61 us
    ppermute x2, starting transfers between devices, exchanged(): return lax.ppermute(array, 'head', [(i, i ^ step) for i in range(heads)])  4.15 us
    ppermute x6, waiting for transfers between devices, swap(): return lax.ppermute(array, 'ctx', swap_pairs)  3.71 us
    unnamed x16, local copies, waits for them, and re-layouts  3.24 us
    ppermute x2, waiting for transfers between devices, exchanged(): return lax.ppermute(array, 'head', [(i, i ^ step) for i in range(heads)])  2.08 us
    ppermute x6, starting transfers between devices, swap(): return lax.ppermute(array, 'ctx', swap_pairs)  1.48 us
  transfers between devices with their start and end apart: 13, of which 7 were waited for; matrix products, arithmetic and copies ran while one was open for 0% of the time, Pallas kernels for 48%

profile of v3, /device:TPU:6, one launch (start us, length us, event | category | flops | bytes accessed | tf_op | source)
XLA Modules:
  0.0 71.2 jit_solution(8154349337687307461)
XLA Ops:
  0.6 0.0 copy-start
  0.6 0.1 collective-permute-start.6
  0.7 0.5 collective-permute-start
  1.2 0.1 collective-permute-start.1
  1.3 0.1 pad_add_fusion.refs_0_
  1.4 3.3 %collective-permute-done.refs_3_ = f32[256,256]{1,0:T(8,128)S(1)} collective-permute-done((f32[256,256]{1,0:T(8,128)}, f32[256,256]{1,0:T(8,128)S(1)}, u32[]{:S(2)}, u32[]{:S(2)}) %collective-permute-start) | collective-permute-done | bytes 262176 | tf_op jit(solution)/shard_map/ppermute | solution.py:707
  4.7 0.4 collective-permute-done.1.refs_4_
  5.1 0.0 copy-start.4
  5.1 0.9 %copy-done.4 = f32[256,256]{1,0:T(8,128)S(1)} copy-done((f32[256,256]{1,0:T(8,128)S(1)}, f32[256,256]{1,0:T(8,128)}, u32[]{:S(2)}) %copy-start.4) | copy-done | bytes 262168
  6.0 0.0 copy-start.5
  6.0 0.9 %copy-done.5 = f32[256,256]{1,0:T(8,128)S(1)} copy-done((f32[256,256]{1,0:T(8,128)S(1)}, f32[256,256]{1,0:T(8,128)}, u32[]{:S(2)}) %copy-start.5) | copy-done | bytes 262168
  7.0 0.0 copy-start.6
  7.0 0.6 shard_map.95.refs_3_
  7.6 0.0 copy-done
  7.6 0.1 copy-done.6
  7.7 0.0 copy-start.1
  7.7 1.2 %copy-done.1 = f32[256,1024]{1,0:T(8,128)S(1)} copy-done((f32[256,1024]{1,0:T(8,128)S(1)}, f32[256,1024]{1,0:T(8,128)}, u32[]{:S(2)}) %copy-start.1) | copy-done | bytes 1048600
  8.9 0.0 copy-start.3
  8.9 2.8 %shard_map.96 = (f32[2,520,128]{2,1,0:T(8,128)S(1)}, f32[8,256]{1,0:T(8,128)S(1)}) custom-call(f32[8,256]{1,0:T(8,128)S(1)} %copy-done.6, f32[256,1024]{1,0:T(8,128)S(1)} %copy-done, f32[256,1024]{1,0:T(8,128)S(1)} %copy-done.1, f32[512,256]{1,0:T(8,128)S(1)} %shard_map.95.refs_3_), custom_call_target="tpu_custom_call" | custom-call | flops 1 | bytes 1 | tf_op jit(solution)/shard_map/pallas_call | solution.py:58
  11.7 0.2 collective-permute-start.2
  11.9 1.3 %collective-permute-start.5 = (f32[512,256]{1,0:T(8,128)S(1)}, f32[512,256]{1,0:T(8,128)S(1)}, u32[]{:S(2)}, u32[]{:S(2)}) collective-permute-start(f32[512,256]{1,0:T(8,128)S(1)} %shard_map.95.refs_3_), channel_id=1, source_target_pairs={{0,16},{4,20},{8,24},{12,28},{1,17},{5,21},{9,25},{13,29},{2,18},{... | collective-permute-start | bytes 1572872 | tf_op jit(solution)/shard_map/ppermute | solution.py:716
  13.2 1.3 %collective-permute-start.4 = (f32[512,256]{1,0:T(8,128)S(1)}, f32[512,256]{1,0:T(8,128)S(1)}, u32[]{:S(2)}, u32[]{:S(2)}) collective-permute-start(f32[512,256]{1,0:T(8,128)S(1)} %shard_map.95.refs_3_), channel_id=1, source_target_pairs={{8,0},{0,8},{4,12},{16,24},{20,28},{9,1},{1,9},{5,13},{17,25},{21,... | collective-permute-start | bytes 1572872 | tf_op jit(solution)/shard_map/ppermute | solution.py:716
  14.5 0.0 copy-done.3
  14.5 4.9 %shard_map.97 = (f32[8,256,128]{2,1,0:T(8,128)S(1)}, bf16[8,256,256]{2,1,0:T(8,128)(2,1)S(1)}) custom-call(f32[256,1024]{1,0:T(8,128)S(1)} %copy-done.3, f32[256,1024]{1,0:T(8,128)S(1)} %copy-done, f32[256,1024]{1,0:T(8,128)S(1)} %copy-done.1, f32[8,256]{1,0:T(8,128)S(1)} %get-tuple-element.20.refs_3_), custom_call_target="tpu_custom_call" | custom-call | flops 1 | bytes 1 | tf_op jit(solution)/shard_map/pallas_call | solution.py:58
  19.4 0.0 copy-start.2
  19.4 0.0 collective-permute-done.2.refs_2_.refs_6_
  19.4 0.6 shard_map.98.refs_4_.refs_1_
  20.0 2.7 %collective-permute-start.3 = (f32[520,128]{1,0:T(8,128)S(1)}, f32[520,128]{1,0:T(8,128)S(1)}, u32[]{:S(2)}, u32[]{:S(2)}) collective-permute-start(f32[520,128]{1,0:T(8,128)S(1)} %shard_map.98.refs_4_.refs_1_), channel_id=1, source_target_pairs={{8,0},{12,4},{0,8},{4,12},{24,16},{28,20},{16,24},{20,28},{9,1},{1... | collective-permute-start | bytes 798728 | tf_op jit(solution)/shard_map/ppermute | solution.py:716
  22.8 0.0 collective-permute-done.6.refs_2_
  22.8 0.0 copy-done.2
  22.8 5.0 %shard_map.99 = (bf16[6,512,256]{2,1,0:T(8,128)(2,1)S(1)}, f32[6,512,128]{2,1,0:T(8,128)S(1)}, f32[6,512,128]{2,1,0:T(8,128)S(1)}, f32[6,512,128]{2,1,0:T(8,128)S(1)}) custom-call(s32[2]{0:T(128)S(1)} %pad_add_fusion.refs_0_, f32[256,1536]{1,0:T(8,128)S(1)} %copy-done.2, f32[256,1536]{1,0:T(8,128)S(1)} %collective-permute-done.6.refs_2_, ...), custom_call_target="tpu_custom_call" | custom-call | flops 1 | bytes 1 | tf_op jit(solution)/shard_map/pallas_call | solution.py:58
  27.8 0.3 collective-permute-done.5.refs_2_.refs_1_
  28.0 1.8 %collective-permute-done.4.refs_1_ = f32[512,256]{1,0:T(8,128)S(1)} collective-permute-done((f32[512,256]{1,0:T(8,128)S(1)}, f32[512,256]{1,0:T(8,128)S(1)}, u32[]{:S(2)}, u32[]{:S(2)}) %collective-permute-start.4) | collective-permute-done | bytes 524320 | tf_op jit(solution)/shard_map/ppermute | solution.py:716
  29.9 0.6 shard_map.100.refs_3_
  30.5 4.6 %collective-permute-done.3.refs_2_ = f32[520,128]{1,0:T(8,128)S(1)} collective-permute-done((f32[520,128]{1,0:T(8,128)S(1)}, f32[520,128]{1,0:T(8,128)S(1)}, u32[]{:S(2)}, u32[]{:S(2)}) %collective-permute-start.3) | collective-permute-done | bytes 266272 | tf_op jit(solution)/shard_map/ppermute | solution.py:716
  35.0 0.6 shard_map.101
  35.6 1.3 %collective-permute-start.7 = (f32[520,128]{1,0:T(8,128)S(1)}, f32[520,128]{1,0:T(8,128)S(1)}, u32[]{:S(2)}, u32[]{:S(2)}) collective-permute-start(f32[520,128]{1,0:T(8,128)S(1)} %get-tuple-element.25.refs_1_), channel_id=1, source_target_pairs={{0,16},{4,20},{8,24},{12,28},{1,17},{5,21},{9,25},{13,29},{2,18},{... | collective-permute-start | bytes 798728 | tf_op jit(solution)/shard_map/ppermute | solution.py:716
  36.9 1.3 %collective-permute-start.10 = (f32[512,256]{1,0:T(8,128)S(1)}, f32[512,256]{1,0:T(8,128)S(1)}, u32[]{:S(2)}, u32[]{:S(2)}) collective-permute-start(f32[512,256]{1,0:T(8,128)S(1)} %shard_map.100.refs_3_), channel_id=1, source_target_pairs={{8,24},{0,16},{20,28},{28,20},{9,25},{1,17},{21,29},{29,21},{10,26... | collective-permute-start | bytes 1572872 | tf_op jit(solution)/shard_map/ppermute | solution.py:738
  38.2 6.4 %shard_map.102 = (f32[6,512,128]{2,1,0:T(8,128)S(1)}, f32[6,512,128]{2,1,0:T(8,128)S(1)}, f32[6,512,128]{2,1,0:T(8,128)S(1)}) custom-call(s32[2]{0:T(128)S(1)} %pad_add_fusion.refs_0_, f32[512,256]{1,0:T(8,128)S(1)} %collective-permute-done.4.refs_1_, ...), custom_call_target="tpu_custom_call", output_to_operand_aliasing={{0}: (3, {}), {1}: (4, {}), {2}: (5, {})} | custom-call | flops 1 | bytes 1 | tf_op jit(solution)/shard_map/pallas_call | solution.py:58
  44.6 0.8 %collective-permute-done.7.refs_2_ = f32[520,128]{1,0:T(8,128)S(1)} collective-permute-done((f32[520,128]{1,0:T(8,128)S(1)}, f32[520,128]{1,0:T(8,128)S(1)}, u32[]{:S(2)}, u32[]{:S(2)}) %collective-permute-start.7) | collective-permute-done | bytes 266272 | tf_op jit(solution)/shard_map/ppermute | solution.py:716
  45.4 0.6 shard_map.103.refs_6_.refs_4_
  46.0 0.1 collective-permute-start.8
  46.1 6.2 %shard_map.104 = (f32[6,512,128]{2,1,0:T(8,128)S(1)}, f32[6,512,128]{2,1,0:T(8,128)S(1)}, f32[6,512,128]{2,1,0:T(8,128)S(1)}) custom-call(s32[2]{0:T(128)S(1)} %pad_add_fusion.refs_0_, f32[512,256]{1,0:T(8,128)S(1)} %collective-permute-done.5.refs_2_.refs_1_, ...), custom_call_target="tpu_custom_call", output_to_operand_aliasing={{0}: (3, {}), {1}: (4, {}), {2}: (5, {})} | custom-call | flops 1 | bytes 1 | tf_op jit(solution)/shard_map/pallas_call | solution.py:58
  52.3 0.0 collective-permute-done.8.refs_5_
  52.3 1.5 %shard_map.105 = (f32[8,256,128]{2,1,0:T(8,128)S(1)}, f32[8,256]{1,0:T(8,128)S(1)}) custom-call(s32[2]{0:T(128)S(1)} %pad_add_fusion.refs_0_, bf16[8,256,256]{2,1,0:T(8,128)(2,1)S(1)} %get-tuple-element.21.refs_1_, f32[8,256,128]{2,1,0:T(8,128)S(1)} %get-tuple-element.22.refs_3_.refs_2_, f32[8,256]{1,0:T(8,128)S(1)} %get-tuple-element.20.refs_3_, ...), custom_call_target="tpu_custom_call" | custom-call | flops 1 | bytes 1 | tf_op jit(solution)/shard_map/pallas_call | solution.py:58
  53.8 0.0 collective-permute-done.10.refs_1_
  53.8 3.5 %shard_map.106.refs_2_ = f32[6,256,128]{2,1,0:T(8,128)S(1)} custom-call(s32[2]{0:T(128)S(1)} %pad_add_fusion.refs_0_, f32[512,256]{1,0:T(8,128)S(1)} %collective-permute-done.10.refs_1_, bf16[6,512,256]{2,1,0:T(8,128)(2,1)S(1)} %get-tuple-element.27.refs_2_, f32[6,512,128]{2,1,0:T(8,128)S(1)} %get-tuple-element.33.refs_7_.refs_3_, ...), custom_call_target="tpu_custom_call" | custom-call | flops 1 | bytes 1 | tf_op jit(solution)/shard_map/pallas_call | solution.py:58
  57.3 0.6 collective-permute-start.12
  57.8 1.6 %collective-permute-start.9 = (f32[8,256]{1,0:T(8,128)S(1)}, f32[8,256]{1,0:T(8,128)S(1)}, u32[]{:S(2)}, u32[]{:S(2)}) collective-permute-start(f32[8,256]{1,0:T(8,128)S(1)} %get-tuple-element.34.refs_6_.refs_0_), channel_id=1, source_target_pairs={{0,1},{1,0},{2,3},{3,2},{4,5},{5,4},{6,7},{7,6},{8,9},{9,8},{10,11... | collective-permute-start | bytes 24584 | tf_op jit(solution)/shard_map/ppermute | solution.py:760
  59.4 2.1 %collective-permute-done.9.refs_1_ = f32[8,256]{1,0:T(8,128)S(1)} collective-permute-done((f32[8,256]{1,0:T(8,128)S(1)}, f32[8,256]{1,0:T(8,128)S(1)}, u32[]{:S(2)}, u32[]{:S(2)}) %collective-permute-start.9) | collective-permute-done | bytes 8224 | tf_op jit(solution)/shard_map/ppermute | solution.py:760
  61.5 0.0 copy-start.7
  61.5 2.6 %collective-permute-start.11 = (f32[8,256]{1,0:T(8,128)S(1)}, f32[8,256]{1,0:T(8,128)S(1)}, u32[]{:S(2)}, u32[]{:S(2)}) collective-permute-start(f32[8,256]{1,0:T(8,128)S(1)} %shard_map.107.refs_0_.refs_6_), channel_id=1, source_target_pairs={{0,2},{1,3},{2,0},{3,1},{4,6},{5,7},{6,4},{7,5},{8,10},{9,11},{10,... | collective-permute-start | bytes 24584 | tf_op jit(solution)/shard_map/ppermute | solution.py:760
  64.1 4.1 %shard_map.109.refs_2_ = f32[256,1536]{1,0:T(8,128)} custom-call(s32[2]{0:T(128)S(1)} %pad_add_fusion.refs_0_, f32[512,256]{1,0:T(8,128)S(1)} %collective-permute-done.10.refs_1_, bf16[6,512,256]{2,1,0:T(8,128)(2,1)S(1)} %get-tuple-element.27.refs_2_, f32[6,512,128]{2,1,0:T(8,128)S(1)} %get-tuple-element.33.refs_7_.refs_3_, ...), custom_call_target="tpu_custom_call" | custom-call | flops 1 | bytes 1 | tf_op jit(solution)/shard_map/pallas_call | solution.py:58
  68.2 0.0 collective-permute-done.11.refs_1_
  68.2 0.0 copy-done.7
  68.2 1.3 %shard_map.108 = f32[256,1024]{1,0:T(8,128)} custom-call(f32[8,256]{1,0:T(8,128)S(1)} %shard_map.107.refs_0_.refs_6_, f32[8,256]{1,0:T(8,128)S(1)} %collective-permute-done.11.refs_1_, f32[1,1024]{1,0:T(1,128)S(1)} %bitcast.3, f32[8,256,128]{2,1,0:T(8,128)S(1)} %get-tuple-element.37.refs_3_), custom_call_target="tpu_custom_call" | custom-call | flops 1 | bytes 1 | tf_op jit(solution)/shard_map/pallas_call | solution.py:58
  69.5 0.0 collective-permute-done.12.refs_1_
  69.5 1.5 %shard_map.110 = f32[256,1536]{1,0:T(8,128)} custom-call(s32[2]{0:T(128)S(1)} %pad_add_fusion.refs_0_, f32[6,256,128]{2,1,0:T(8,128)S(1)} %collective-permute-done.12.refs_1_, f32[256,1536]{1,0:T(8,128)} %shard_map.109.refs_2_), custom_call_target="tpu_custom_call", output_to_operand_aliasing={{}: (2, {})} | custom-call | flops 1 | bytes 1 | tf_op jit(solution)/shard_map/pallas_call | solution.py:58
  (1 shorter events, 0.0 us)
Async XLA Ops:
  0.6 6.9 %copy-start = (f32[256,1024]{1,0:T(8,128)S(1)}, f32[256,1024]{1,0:T(8,128)}, u32[]{:S(2)}) copy-start(f32[256,1024]{1,0:T(8,128)} %refs_1_.6) | copy-start | bytes 3145732
  0.6 22.1 %collective-permute-start.6 = (f32[256,1536]{1,0:T(8,128)}, f32[256,1536]{1,0:T(8,128)S(1)}, u32[]{:S(2)}, u32[]{:S(2)}) collective-permute-start(f32[256,1536]{1,0:T(8,128)} %refs_1_.7), channel_id=1, source_target_pairs={{0,4},{4,0},{8,12},{12,8},{16,20},{20,16},{24,28},{28,24},{1,5},{5... | collective-permute-start | bytes 4718600 | tf_op jit(solution)/shard_map/ppermute | solution.py:707
  0.7 4.0 %collective-permute-start = (f32[256,256]{1,0:T(8,128)}, f32[256,256]{1,0:T(8,128)S(1)}, u32[]{:S(2)}, u32[]{:S(2)}) collective-permute-start(f32[256,256]{1,0:T(8,128)} %refs_1_.4), channel_id=1, source_target_pairs={{0,4},{4,0},{8,12},{12,8},{16,20},{20,16},{24,28},{28,24},{1,5},{5... | collective-permute-start | bytes 786440 | tf_op jit(solution)/shard_map/ppermute | solution.py:707
  1.2 3.9 %collective-permute-start.1 = (f32[256,256]{1,0:T(8,128)}, f32[256,256]{1,0:T(8,128)S(1)}, u32[]{:S(2)}, u32[]{:S(2)}) collective-permute-start(f32[256,256]{1,0:T(8,128)} %refs_2_.3), channel_id=1, source_target_pairs={{0,4},{4,0},{8,12},{12,8},{16,20},{20,16},{24,28},{28,24},{1,5},{5... | collective-permute-start | bytes 786440 | tf_op jit(solution)/shard_map/ppermute | solution.py:707
  5.1 1.0 %copy-start.4 = (f32[256,256]{1,0:T(8,128)S(1)}, f32[256,256]{1,0:T(8,128)}, u32[]{:S(2)}) copy-start(f32[256,256]{1,0:T(8,128)} %refs_1_.4) | copy-start | bytes 786436
  6.0 0.9 %copy-start.5 = (f32[256,256]{1,0:T(8,128)S(1)}, f32[256,256]{1,0:T(8,128)}, u32[]{:S(2)}) copy-start(f32[256,256]{1,0:T(8,128)} %refs_2_.3) | copy-start | bytes 786436
  7.0 0.7 copy-start.6
  7.7 1.2 %copy-start.1 = (f32[256,1024]{1,0:T(8,128)S(1)}, f32[256,1024]{1,0:T(8,128)}, u32[]{:S(2)}) copy-start(f32[256,1024]{1,0:T(8,128)} %refs_2_.5) | copy-start | bytes 3145732
  8.9 5.6 %copy-start.3 = (f32[256,1024]{1,0:T(8,128)S(1)}, f32[256,1024]{1,0:T(8,128)}, u32[]{:S(2)}) copy-start(f32[256,1024]{1,0:T(8,128)} %refs_0_.3) | copy-start | bytes 3145732
  11.7 7.7 %collective-permute-start.2 = (f32[2,520,128]{2,1,0:T(8,128)S(1)}, f32[2,520,128]{2,1,0:T(8,128)S(1)}, u32[]{:S(2)}, u32[]{:S(2)}) collective-permute-start(f32[2,520,128]{2,1,0:T(8,128)S(1)} %get-tuple-element.23.refs_1_), channel_id=1, source_target_pairs={{0,4},{4,0},{8,12},{12,8},{16,20},{20,16},{24,28},{28,24},{1,5},{5... | collective-permute-start | bytes 1597448 | tf_op jit(solution)/shard_map/ppermute | solution.py:707
  11.9 16.1 %collective-permute-start.5 = (f32[512,256]{1,0:T(8,128)S(1)}, f32[512,256]{1,0:T(8,128)S(1)}, u32[]{:S(2)}, u32[]{:S(2)}) collective-permute-start(f32[512,256]{1,0:T(8,128)S(1)} %shard_map.95.refs_3_), channel_id=1, source_target_pairs={{0,16},{4,20},{8,24},{12,28},{1,17},{5,21},{9,25},{13,29},{2,18},{... | collective-permute-start | bytes 1572872 | tf_op jit(solution)/shard_map/ppermute | solution.py:716
  13.2 16.6 %collective-permute-start.4 = (f32[512,256]{1,0:T(8,128)S(1)}, f32[512,256]{1,0:T(8,128)S(1)}, u32[]{:S(2)}, u32[]{:S(2)}) collective-permute-start(f32[512,256]{1,0:T(8,128)S(1)} %shard_map.95.refs_3_), channel_id=1, source_target_pairs={{8,0},{0,8},{4,12},{16,24},{20,28},{9,1},{1,9},{5,13},{17,25},{21,... | collective-permute-start | bytes 1572872 | tf_op jit(solution)/shard_map/ppermute | solution.py:716
  19.4 3.4 %copy-start.2 = (f32[256,1536]{1,0:T(8,128)S(1)}, f32[256,1536]{1,0:T(8,128)}, u32[]{:S(2)}) copy-start(f32[256,1536]{1,0:T(8,128)} %refs_1_.7) | copy-start | bytes 4718596
  20.0 15.0 %collective-permute-start.3 = (f32[520,128]{1,0:T(8,128)S(1)}, f32[520,128]{1,0:T(8,128)S(1)}, u32[]{:S(2)}, u32[]{:S(2)}) collective-permute-start(f32[520,128]{1,0:T(8,128)S(1)} %shard_map.98.refs_4_.refs_1_), channel_id=1, source_target_pairs={{8,0},{12,4},{0,8},{4,12},{24,16},{28,20},{16,24},{20,28},{9,1},{1... | collective-permute-start | bytes 798728 | tf_op jit(solution)/shard_map/ppermute | solution.py:716
  35.6 9.8 %collective-permute-start.7 = (f32[520,128]{1,0:T(8,128)S(1)}, f32[520,128]{1,0:T(8,128)S(1)}, u32[]{:S(2)}, u32[]{:S(2)}) collective-permute-start(f32[520,128]{1,0:T(8,128)S(1)} %get-tuple-element.25.refs_1_), channel_id=1, source_target_pairs={{0,16},{4,20},{8,24},{12,28},{1,17},{5,21},{9,25},{13,29},{2,18},{... | collective-permute-start | bytes 798728 | tf_op jit(solution)/shard_map/ppermute | solution.py:716
  36.9 16.9 %collective-permute-start.10 = (f32[512,256]{1,0:T(8,128)S(1)}, f32[512,256]{1,0:T(8,128)S(1)}, u32[]{:S(2)}, u32[]{:S(2)}) collective-permute-start(f32[512,256]{1,0:T(8,128)S(1)} %shard_map.100.refs_3_), channel_id=1, source_target_pairs={{8,24},{0,16},{20,28},{28,20},{9,25},{1,17},{21,29},{29,21},{10,26... | collective-permute-start | bytes 1572872 | tf_op jit(solution)/shard_map/ppermute | solution.py:738
  46.0 6.3 %collective-permute-start.8 = (f32[520,128]{1,0:T(8,128)S(1)}, f32[520,128]{1,0:T(8,128)S(1)}, u32[]{:S(2)}, u32[]{:S(2)}) collective-permute-start(f32[520,128]{1,0:T(8,128)S(1)} %shard_map.103.refs_6_.refs_4_), channel_id=1, source_target_pairs={{0,4},{4,0},{8,12},{12,8},{16,20},{20,16},{24,28},{28,24},{1,5},{5... | collective-permute-start | bytes 798728 | tf_op jit(solution)/shard_map/ppermute | solution.py:707
  57.3 12.3 %collective-permute-start.12 = (f32[6,256,128]{2,1,0:T(8,128)S(1)}, f32[6,256,128]{2,1,0:T(8,128)S(1)}, u32[]{:S(2)}, u32[]{:S(2)}) collective-permute-start(f32[6,256,128]{2,1,0:T(8,128)S(1)} %shard_map.106.refs_2_), channel_id=1, source_target_pairs={{0,4},{4,0},{8,12},{12,8},{16,20},{20,16},{24,28},{28,24},{1,5},{5... | collective-permute-start | bytes 2359304 | tf_op jit(solution)/shard_map/ppermute | solution.py:707
  57.8 3.7 %collective-permute-start.9 = (f32[8,256]{1,0:T(8,128)S(1)}, f32[8,256]{1,0:T(8,128)S(1)}, u32[]{:S(2)}, u32[]{:S(2)}) collective-permute-start(f32[8,256]{1,0:T(8,128)S(1)} %get-tuple-element.34.refs_6_.refs_0_), channel_id=1, source_target_pairs={{0,1},{1,0},{2,3},{3,2},{4,5},{5,4},{6,7},{7,6},{8,9},{9,8},{10,11... | collective-permute-start | bytes 24584 | tf_op jit(solution)/shard_map/ppermute | solution.py:760
  61.5 6.7 %copy-start.7 = (f32[1024]{0:T(1024)S(1)}, f32[1024]{0:T(1024)}, u32[]{:S(2)}) copy-start(f32[1024]{0:T(1024)} %param.12) | copy-start | bytes 12292
  61.5 6.7 %collective-permute-start.11 = (f32[8,256]{1,0:T(8,128)S(1)}, f32[8,256]{1,0:T(8,128)S(1)}, u32[]{:S(2)}, u32[]{:S(2)}) collective-permute-start(f32[8,256]{1,0:T(8,128)S(1)} %shard_map.107.refs_0_.refs_6_), channel_id=1, source_target_pairs={{0,2},{1,3},{2,0},{3,1},{4,6},{5,7},{6,4},{7,5},{8,10},{9,11},{10,... | collective-permute-start | bytes 24584 | tf_op jit(solution)/shard_map/ppermute | solution.py:760

commit v4 on v3

v4 whole, which is shorter than its diff:
```python
import functools
import math

import jax
import jax.numpy as jnp
from jax import lax
from jax.experimental import pallas as pl
from jax.experimental.pallas import tpu as pltpu
from jax.sharding import PartitionSpec as P

HD = 128
NEGATIVE = -1e30
EPSILON = 1e-05
F32 = jnp.float32
BF16 = jnp.bfloat16
NT = (((1,), (1,)), ((), ()))
VMEM_LIMIT = 32 * 1024 * 1024
VMEM = pl.BlockSpec(memory_space=pltpu.VMEM)
SMEM = pl.BlockSpec(memory_space=pltpu.SMEM)
ANY = pl.BlockSpec(memory_space=pl.ANY)
HBM = pl.BlockSpec(memory_space=pltpu.HBM)


def split(x):
    high = x.astype(BF16)
    low = (x - high.astype(F32)).astype(BF16)
    return high, low


def dot(a, b):
    return jnp.dot(a, b, preferred_element_type=F32)


def three_term(a, b):
    a_high, a_low = split(a)
    b_high, b_low = split(b)
    wide = dot(a_high, jnp.concatenate([b_high, b_low], axis=1))
    n = b.shape[1]
    return wide[:, :n] + wide[:, n:] + dot(a_low, b_high)


def call(kernel, in_specs, out_specs, out_shape, scratch=(), alias=None, after=()):
    count = len(in_specs)

    def ordered(*refs):
        kernel(*refs[:count], *refs[count + len(after) :])

    made = pl.pallas_call(
        ordered,
        in_specs=in_specs + [ANY] * len(after),
        out_specs=out_specs,
        out_shape=out_shape,
        scratch_shapes=list(scratch),
        input_output_aliases=alias or {},
        cost_estimate=pl.CostEstimate(flops=1, bytes_accessed=1, transcendentals=0),
        compiler_params=pltpu.CompilerParams(vmem_limit_bytes=VMEM_LIMIT),
    )
    return lambda *operands: made(*operands, *after)


def state_kernel(rate_ref, k_ref, v_ref, packed_ref, sums_ref):
    tokens = k_ref.shape[0]
    heads = rate_ref.shape[0]
    half = heads // 2
    upto = lax.broadcasted_iota(jnp.int32, (tokens, tokens), 0)
    upto = (upto <= lax.broadcasted_iota(jnp.int32, (tokens, tokens), 1)).astype(F32)
    sums = jnp.dot(
        rate_ref[...], upto, precision=lax.Precision.HIGHEST, preferred_element_type=F32
    )
    sums_ref[...] = sums
    totals = sums[:, tokens - 1 : tokens]
    trailing = jnp.exp(totals - sums)
    for side in range(2):
        packed_ref[side, half * HD :] = jnp.zeros((8, HD), F32)
    for h in range(heads):
        side, i = h // half, h % half
        at = slice(h * HD, (h + 1) * HD)
        packed_ref[side, i * HD : (i + 1) * HD] = three_term(
            k_ref[:, at].T * trailing[h : h + 1], v_ref[:, at]
        )
        packed_ref[side, half * HD + i : half * HD + i + 1] = jnp.broadcast_to(
            totals[h : h + 1], (1, HD)
        )


def local_states(rates, k_lin, v_lin, after):
    tokens = k_lin.shape[0]
    heads = rates.shape[0]
    return call(
        state_kernel,
        [VMEM] * 3,
        [VMEM] * 2,
        [
            jax.ShapeDtypeStruct((2, heads // 2 * HD + 8, HD), F32),
            jax.ShapeDtypeStruct((heads, tokens), F32),
        ],
        after=after,
    )(rates, k_lin, v_lin)


def join(half, first, second, out_ref):
    decay = jnp.exp(second[half * HD :, :])
    for i in range(half):
        at = slice(i * HD, (i + 1) * HD)
        out_ref[at] = first[at] * decay[i : i + 1] + second[at]
    out_ref[half * HD :] = first[half * HD :] + second[half * HD :]


def chip_kernel(half, me_ref, states_ref, others_ref, out_ref):
    core = me_ref[0] & 1

    @pl.when(core == 0)
    def _():
        join(half, states_ref[0], others_ref[0], out_ref)

    @pl.when(core == 1)
    def _():
        join(half, others_ref[1], states_ref[1], out_ref)


def chip_total(me, states, others, after):
    _, packed, _ = states.shape
    return call(
        functools.partial(chip_kernel, (packed - 8) // HD),
        [SMEM, VMEM, VMEM],
        VMEM,
        jax.ShapeDtypeStruct((packed, HD), F32),
        after=after,
    )(me, states, others)


def turn_kernel(half, bit, first, last, me_ref, total_ref, theirs_ref, *refs):
    refs = list(refs)
    before_ref = None if first else refs.pop(0)
    prefix_ref = refs.pop(0)
    total_out = None if last else refs.pop(0)
    late = (me_ref[0] >> (bit + 1)) & 1

    @pl.when(late == 0)
    def _():
        prefix_ref[...] = jnp.zeros_like(prefix_ref) if first else before_ref[...]
        if not last:
            join(half, total_ref[...], theirs_ref[...], total_out)

    @pl.when(late == 1)
    def _():
        if first:
            prefix_ref[...] = theirs_ref[...]
        else:
            join(half, theirs_ref[...], before_ref[...], prefix_ref)
        if not last:
            join(half, theirs_ref[...], total_ref[...], total_out)


def turn(me, bit, total, theirs, before, last, after):
    packed = total.shape[0]
    operands = [total, theirs] + ([] if before is None else [before])
    count = 1 if last else 2
    out = call(
        functools.partial(turn_kernel, (packed - 8) // HD, bit, before is None, last),
        [SMEM] + [VMEM] * len(operands),
        [VMEM] * count,
        [jax.ShapeDtypeStruct((packed, HD), F32)] * count,
        after=after,
    )(me, *operands)
    return out[0], (None if last else out[1])


def inside_kernel(q_ref, k_ref, v_ref, sums_ref, out_ref, terms_ref):
    tokens = q_ref.shape[0]
    heads = sums_ref.shape[0]
    causal = lax.broadcasted_iota(jnp.int32, (tokens, tokens), 0) >= lax.broadcasted_iota(
        jnp.int32, (tokens, tokens), 1
    )
    columns = sums_ref[...].T
    for h in range(heads):
        at = slice(h * HD, (h + 1) * HD)
        q_high, q_low = split(q_ref[:, at])
        k_high, k_low = split(k_ref[:, at])
        terms_ref[h, :, :HD] = q_high
        terms_ref[h, :, HD:] = q_low
        scores = lax.dot_general(
            jnp.concatenate([q_high, q_low, q_high], axis=1),
            jnp.concatenate([k_high, k_high, k_low], axis=1),
            NT,
            preferred_element_type=F32,
        )
        gaps = columns[:, h : h + 1] - sums_ref[h : h + 1, :]
        weights = jnp.where(causal, jnp.exp(jnp.where(causal, gaps, 0.0)), 0.0)
        out_ref[h] = three_term(scores * weights, v_ref[:, at])


def inside_blocks(q_lin, k_lin, v_lin, sums, after):
    tokens = q_lin.shape[0]
    heads = sums.shape[0]
    return call(
        inside_kernel,
        [VMEM] * 4,
        [VMEM] * 2,
        [
            jax.ShapeDtypeStruct((heads, tokens, HD), F32),
            jax.ShapeDtypeStruct((heads, tokens, 2 * HD), BF16),
        ],
        after=after,
    )(q_lin, k_lin, v_lin, sums)


def linear_kernel(me_ref, terms_ref, inside_ref, sums_ref, mine_ref, theirs_ref, other_ref, out_ref, energy_ref):
    heads, tokens, _ = out_ref.shape
    half = heads // 2
    core = me_ref[0] & 1
    leading = jnp.exp(sums_ref[...]).T
    squares = jnp.zeros((tokens, HD), F32)
    for side in range(2):
        decay = jnp.exp(other_ref[side, half * HD :])
        for i in range(half):
            h = side * half + i
            at = slice(i * HD, (i + 1) * HD)
            prior = jnp.where(core == side, mine_ref[at], theirs_ref[at])
            prior = jnp.where(core == 1, prior * decay[i : i + 1] + other_ref[side, at], prior)
            high, low = split(prior)
            wide = dot(terms_ref[h, :, :HD], jnp.concatenate([high, low], axis=1))
            carried = wide[:, :HD] + wide[:, HD:] + dot(terms_ref[h, :, HD:], high)
            linear = inside_ref[h] + leading[:, h : h + 1] * carried
            out_ref[h] = linear
            squares = squares + linear * linear
    energy_ref[...] = lax.dot_general(
        jnp.ones((8, HD), F32),
        squares,
        NT,
        precision=lax.Precision.HIGHEST,
        preferred_element_type=F32,
    )


def linear_blocks(me, terms, inside, sums, mine, theirs, other, after):
    _, tokens, _ = inside.shape
    return call(
        linear_kernel,
        [SMEM] + [VMEM] * 6,
        [VMEM] * 2,
        [
            jax.ShapeDtypeStruct(inside.shape, F32),
            jax.ShapeDtypeStruct((8, tokens), F32),
        ],
        after=after,
    )(me, terms, inside, sums, mine, theirs, other)


def halves(core, *arrays):
    early = [array[:, :HD] for array in arrays]
    late = [array[:, HD:] for array in arrays]
    mine = jnp.stack([jnp.where(core == 0, a, b) for a, b in zip(early, late)])
    theirs = jnp.stack([jnp.where(core == 0, b, a) for a, b in zip(early, late)])
    return mine, theirs


def pair_kernel(me_ref, mine_ref, other_ref, q_ref, out_ref, send_ref):
    tokens = mine_ref.shape[1]
    group = send_ref.shape[0]
    core = me_ref[0] & 1
    first = core == 0
    for side in range(2):
        mine, other = mine_ref[side], other_ref[side]
        out_ref[side, :tokens] = jnp.where(first, mine, other)
        out_ref[side, tokens:] = jnp.where(first, other, mine)
    for g in range(group):
        at = pl.ds(pl.multiple_of(((1 - core) * group + g) * HD, HD), HD)
        send_ref[g] = q_ref[:, at]


def pair_block(me, mine, other, q_soft, after):
    _, tokens, _ = mine.shape
    group = q_soft.shape[1] // (2 * HD)
    return call(
        pair_kernel,
        [SMEM] + [VMEM] * 3,
        [VMEM] * 2,
        [
            jax.ShapeDtypeStruct((2, 2 * tokens, HD), F32),
            jax.ShapeDtypeStruct((group, tokens, HD), F32),
        ],
        after=after,
    )(me, mine, other, q_soft)


def run_heads(count, load, soften, gather):
    load(0, 0)
    load(1, 1)
    soften(0, 0)

    def turn(j, carry):
        for i, slot in ((2 * j + 1, 1), (2 * j + 2, 0)):
            load(i + 1, 1 - slot)
            gather(i - 1, 1 - slot)
            soften(i, slot)
        return carry

    lax.fori_loop(0, count // 2 - 1, turn, 0)
    gather(count - 2, 0)
    soften(count - 1, 1)
    gather(count - 1, 1)


def fill_terms(kv_ref, keys_ref, values_ref):
    k_high, k_low = split(kv_ref[0].T)
    keys_ref[:HD] = k_high
    keys_ref[HD : 2 * HD] = k_high
    keys_ref[2 * HD :] = k_low
    v_high, v_low = split(kv_ref[1])
    values_ref[:, :HD] = v_high
    values_ref[:, HD:] = v_low


def lane_max(array):
    peak = array[:, :HD]
    for c in range(1, array.shape[1] // HD):
        peak = jnp.maximum(peak, array[:, c * HD : (c + 1) * HD])
    return peak


def score_terms(pair):
    return jnp.concatenate([pair, pair[:, :HD]], axis=1)


def weigh(scores_ref, rows, count, peak, total, high_ref, low_ref):
    for c in range(count // HD):
        at = slice(c * HD, (c + 1) * HD)
        w = jnp.exp2(scores_ref[rows, at] - peak)
        total = total + w
        high_ref[rows, at], low_ref[rows, at] = split(w)
    return total


def summed(high, low, values):
    wide = dot(high, values)
    return wide[:, :HD] + wide[:, HD:] + dot(low, values[:, :HD])


def own_kernel(factor, me_ref, q_ref, q_other_ref, kv_ref, q_out, acc_out, peak_out, total_out, *scratch):
    keys_ref, values_ref = scratch[:2]
    scores, highs, lows, peaks = scratch[2:4], scratch[4:6], scratch[6:8], scratch[8:10]
    group, tokens = q_out.shape[0], q_ref.shape[0]
    core = me_ref[0] & 1
    first = core == 0
    fill_terms(kv_ref, keys_ref, values_ref)
    for g in range(group):
        at = pl.ds(pl.multiple_of((core * group + g) * HD, HD), HD)
        mine, other = q_ref[:, at], q_other_ref[g]
        for t, rows in enumerate(
            (jnp.where(first, mine, other), jnp.where(first, other, mine))
        ):
            high, low = split(rows * factor)
            at = slice(t * tokens, (t + 1) * tokens)
            q_out[g, at, :HD] = high
            q_out[g, at, HD:] = low

    seen = lax.broadcasted_iota(jnp.int32, (tokens, tokens), 1)
    seen = seen <= lax.broadcasted_iota(jnp.int32, (tokens, tokens), 0)
    early, late = slice(0, tokens), slice(tokens, 2 * tokens)

    def load(g, slot):
        terms = score_terms(q_out[g])
        left = dot(terms, keys_ref[:, early])
        right = dot(terms[late], keys_ref[:, late])
        edge = jnp.where(seen, left[early], NEGATIVE)
        far = jnp.where(seen, right, NEGATIVE)
        scores[slot][early, early] = edge
        scores[slot][late, early] = left[late]
        scores[slot][late, late] = far
        peaks[slot][early] = lane_max(edge)
        peaks[slot][late] = jnp.maximum(lane_max(left[late]), lane_max(far))

    def soften(g, slot):
        peak = jnp.max(peaks[slot][...], axis=1, keepdims=True)
        peak = jnp.broadcast_to(peak, (2 * tokens, HD))
        peak_out[g] = peak
        zero = jnp.zeros((tokens, HD), F32)
        total_out[g, early] = weigh(
            scores[slot], early, tokens, peak[early], zero, highs[slot], lows[slot]
        )
        total_out[g, late] = weigh(
            scores[slot], late, 2 * tokens, peak[late], zero, highs[slot], lows[slot]
        )

    def gather(g, slot):
        acc_out[g, early] = summed(
            highs[slot][early, early], lows[slot][early, early], values_ref[early]
        )
        acc_out[g, late] = summed(highs[slot][late], lows[slot][late], values_ref[...])

    run_heads(group, load, soften, gather)


def stage_scratch(rows, keys):
    return [
        *[pltpu.VMEM((rows, keys), F32)] * 2,
        *[pltpu.VMEM((rows, keys), BF16)] * 4,
        *[pltpu.VMEM((rows, HD), F32)] * 4,
    ]


def own_stage(me, q_soft, q_other, kv, after):
    tokens, width = q_soft.shape
    group = width // (2 * HD)
    stat = jax.ShapeDtypeStruct((group, 2 * tokens, HD), F32)
    return call(
        functools.partial(own_kernel, math.log2(math.e) / math.sqrt(HD)),
        [SMEM] + [VMEM] * 3,
        [VMEM] * 4,
        [jax.ShapeDtypeStruct((group, 2 * tokens, 2 * HD), BF16), stat, stat, stat],
        [
            pltpu.VMEM((3 * HD, 2 * tokens), BF16),
            pltpu.VMEM((2 * tokens, 2 * HD), BF16),
            *stage_scratch(2 * tokens, 2 * tokens),
        ],
        after=after,
    )(me, q_soft, q_other, kv)


def later_kernel(distance, form, me_ref, kv_ref, q_ref, acc_ref, peak_ref, total_ref, acc_out, peak_out, total_out, *scratch):
    keys_ref, values_ref = scratch[:2]
    scores, highs, lows, peaks = scratch[2:4], scratch[4:6], scratch[6:8], scratch[8:10]
    shrinks = scratch[10:12]
    group, rows, _ = q_ref.shape
    everything = slice(0, rows)
    chip = me_ref[0] >> 1

    def load(g, slot):
        s = dot(score_terms(q_ref[g]), keys_ref[...])
        scores[slot][...] = s
        peaks[slot][...] = lane_max(s)

    def soften(g, slot):
        old = peak_ref[g]
        peak = jnp.maximum(jnp.max(peaks[slot][...], axis=1, keepdims=True), old)
        shrink = jnp.exp2(old - peak)
        peak_out[g] = peak
        total_out[g] = weigh(
            scores[slot], everything, keys_ref.shape[1], peak, total_ref[g] * shrink,
            highs[slot], lows[slot],
        )
        shrinks[slot][...] = shrink

    def gather(g, slot):
        acc_out[g] = acc_ref[g] * shrinks[slot][...] + summed(
            highs[slot][...], lows[slot][...], values_ref[...]
        )

    tokens = rows // 2

    def score(i):
        at = slice(i % 2 * tokens, (i % 2 + 1) * tokens)
        return dot(score_terms(q_ref[i // 2, at]), keys_ref[...])

    def soft(i, s):
        at = slice(i % 2 * tokens, (i % 2 + 1) * tokens)
        old = peak_ref[i // 2, at]
        peak = jnp.maximum(jnp.max(lane_max(s), axis=1, keepdims=True), old)
        shrink = jnp.exp2(old - peak)
        total = total_ref[i // 2, at] * shrink
        high, low = [], []
        for c in range(s.shape[1] // HD):
            w = jnp.exp2(s[:, c * HD : (c + 1) * HD] - peak)
            total = total + w
            pair = split(w)
            high.append(pair[0])
            low.append(pair[1])
        peak_out[i // 2, at] = peak
        total_out[i // 2, at] = total
        return jnp.concatenate(high, axis=1), jnp.concatenate(low, axis=1), shrink

    def weighted(i, terms):
        at = slice(i % 2 * tokens, (i % 2 + 1) * tokens)
        high, low, shrink = terms
        acc_out[i // 2, at] = acc_ref[i // 2, at] * shrink + summed(high, low, values_ref[...])

    def chunked(i, slot, before, after):
        for c in range(2):
            at = slice(c * tokens, (c + 1) * tokens)
            if after:
                s = dot(score_terms(q_ref[i + 1, at]), keys_ref[...])
                scores[1 - slot][at] = s
                peaks[1 - slot][at] = lane_max(s)
            if before:
                acc_out[i - 1, at] = acc_ref[i - 1, at] * shrinks[1 - slot][at] + summed(
                    highs[1 - slot][at], lows[1 - slot][at], values_ref[...]
                )
            old = peak_ref[i, at]
            peak = jnp.maximum(jnp.max(peaks[slot][at], axis=1, keepdims=True), old)
            shrink = jnp.exp2(old - peak)
            peak_out[i, at] = peak
            total_out[i, at] = weigh(
                scores[slot], at, keys_ref.shape[1], peak, total_ref[i, at] * shrink,
                highs[slot], lows[slot],
            )
            shrinks[slot][at] = shrink

    @pl.when(lax.bitwise_xor(chip, distance) < chip)
    def _():
        fill_terms(kv_ref, keys_ref, values_ref)
        if form == "scratch":
            run_heads(group, load, soften, gather)
        elif form == "values":
            count = 2 * group
            s, before = score(0), None
            for i in range(count):
                following = score(i + 1) if i + 1 < count else None
                if before is not None:
                    weighted(i - 1, before)
                before = soft(i, s)
                s = following
            weighted(count - 1, before)
        else:
            load(0, 0)
            for i in range(group):
                chunked(i, i % 2, i > 0, i + 1 < group)
            gather(group - 1, (group - 1) % 2)


def later_stage(me, distance, kv, q_terms, acc, peak, total, after, form="scratch"):
    group, rows, _ = q_terms.shape
    keys = kv.shape[1]
    return call(
        functools.partial(later_kernel, distance, form),
        [SMEM] + [VMEM] * 5,
        [VMEM] * 3,
        [jax.ShapeDtypeStruct(acc.shape, F32)] * 3,
        [
            pltpu.VMEM((3 * HD, keys), BF16),
            pltpu.VMEM((keys, 2 * HD), BF16),
            *stage_scratch(rows, keys),
        ],
        alias={3: 0, 4: 1, 5: 2},
        after=after,
    )(me, kv, q_terms, acc, peak, total)


def last_kernel(distance, columns, me_ref, kv_ref, q_ref, acc_ref, peak_ref, total_ref, *refs):
    if columns is None:
        out_ref, *scratch = refs
    else:
        theirs_ref, energy_ref, energy_other_ref, gain_ref, linear_ref = refs[:5]
        lin_hbm, soft_hbm, lin_ref, out_ref, sems, *scratch = refs[5:]
    keys_ref, values_ref = scratch[:2]
    scores, highs, lows, peaks = scratch[2:4], scratch[4:6], scratch[6:8], scratch[8:10]
    shrinks, totals = scratch[10:12], scratch[12:14]
    group, rows, _ = q_ref.shape
    tokens = rows // 2
    everything = slice(0, tokens)
    core, chip = me_ref[0] & 1, me_ref[0] >> 1
    side = 1 - core if columns is None else core
    at = pl.ds(pl.multiple_of(side * tokens, tokens), tokens)

    def to_soft(source, whose, g, n):
        to = pl.ds(pl.multiple_of((whose * group + g) * HD, HD), HD)
        return pltpu.make_async_copy(source.at[g], soft_hbm.at[:, to], sems.at[n])

    def to_lin(h):
        return pltpu.make_async_copy(
            lin_ref.at[h], lin_hbm.at[:, pl.ds(h * HD, HD)], sems.at[2 * group + h]
        )

    if columns is not None:
        for g in range(group):
            to_soft(theirs_ref, 1 - core, g, g).start()
        factor = lax.rsqrt((energy_ref[...] + energy_other_ref[...]) / columns + EPSILON)
        factor = factor.T[:, 0:1]
        for h in range(linear_ref.shape[0]):
            lin_ref[h] = linear_ref[h] * factor * gain_ref[:, h * HD : (h + 1) * HD]
            to_lin(h).start()

    def finish(g, acc, total):
        out_ref[g] = acc / jnp.sum(total, axis=1, keepdims=True)
        if columns is not None:
            to_soft(out_ref, core, g, group + g).start()

    def load(g, slot):
        s = dot(score_terms(q_ref[g, at]), keys_ref[...])
        scores[slot][...] = s
        peaks[slot][...] = lane_max(s)

    def soften(g, slot):
        old = peak_ref[g, at]
        peak = jnp.maximum(jnp.max(peaks[slot][...], axis=1, keepdims=True), old)
        shrink = jnp.exp2(old - peak)
        totals[slot][...] = weigh(
            scores[slot], everything, keys_ref.shape[1], peak, total_ref[g, at] * shrink,
            highs[slot], lows[slot],
        )
        shrinks[slot][...] = shrink

    def gather(g, slot):
        acc = acc_ref[g, at] * shrinks[slot][...] + summed(
            highs[slot][...], lows[slot][...], values_ref[...]
        )
        finish(g, acc, totals[slot][...])

    visible = lax.bitwise_xor(chip, distance) < chip

    @pl.when(visible)
    def _():
        fill_terms(kv_ref, keys_ref, values_ref)
        run_heads(group, load, soften, gather)

    @pl.when(jnp.logical_not(visible))
    def _():
        for g in range(group):
            finish(g, acc_ref[g, at], total_ref[g, at])

    if columns is not None:
        for g in range(group):
            to_soft(theirs_ref, 1 - core, g, g).wait()
            to_soft(out_ref, core, g, group + g).wait()
        for h in range(linear_ref.shape[0]):
            to_lin(h).wait()


def last_stage(me, distance, kv, q_terms, acc, peak, total, after, extra=None):
    group, rows, _ = q_terms.shape
    keys, tokens = kv.shape[1], rows // 2
    part = jax.ShapeDtypeStruct((group, tokens, HD), F32)
    scratch = [
        pltpu.VMEM((3 * HD, keys), BF16),
        pltpu.VMEM((keys, 2 * HD), BF16),
        *stage_scratch(tokens, keys),
        *[pltpu.VMEM((tokens, HD), F32)] * 2,
    ]
    operands, columns = [kv, q_terms, acc, peak, total], None
    out_shape, out_spec = part, VMEM
    if extra is not None:
        columns, more = extra
        operands += more
        heads = more[-1].shape[0]
        out_shape = [
            jax.ShapeDtypeStruct((tokens, heads * HD), F32),
            jax.ShapeDtypeStruct((tokens, 2 * group * HD), F32),
        ]
        out_spec = [HBM] * 2
        scratch = [
            pltpu.VMEM((heads, tokens, HD), F32),
            pltpu.VMEM(part.shape, F32),
            pltpu.SemaphoreType.DMA((2 * group + heads,)),
        ] + scratch
    return call(
        functools.partial(last_kernel, distance, columns),
        [SMEM] + [VMEM] * len(operands),
        out_spec,
        out_shape,
        scratch,
        after=after,
    )(me, *operands)


def plus_kernel(a_ref, b_ref, out_ref):
    out_ref[...] = a_ref[...] + b_ref[...]


def plus(a, b, after):
    return call(
        plus_kernel, [VMEM] * 2, VMEM, jax.ShapeDtypeStruct(a.shape, F32), after=after
    )(a, b)


def relay_kernel(me_ref, beside_ref, across_ref, out_ref):
    @pl.when((me_ref[0] & 1) == 0)
    def _():
        out_ref[...] = beside_ref[...]

    @pl.when((me_ref[0] & 1) == 1)
    def _():
        out_ref[...] = across_ref[...]


def relayed(me, beside, across, after):
    return call(
        relay_kernel,
        [SMEM, VMEM, VMEM],
        VMEM,
        jax.ShapeDtypeStruct(beside.shape, F32),
        after=after,
    )(me, beside, across)


def body(q_lin, k_lin, v_lin, log_decay, lin_gain, q_soft, k_soft, v_soft):
    chips = lax.axis_size("ctx") // 2
    heads = lax.axis_size("head")
    me = lax.axis_index("ctx")
    me_flag = me.reshape(1).astype(jnp.int32)
    assert k_soft.shape[1] == 2 * HD
    swap_pairs = [(2 * c + e, 2 * c + 1 - e) for c in range(chips) for e in range(2)]

    def swap(array):
        return lax.ppermute(array, "ctx", swap_pairs)

    def across(array, distance, wanted=lambda c, e: True):
        pairs = [
            (2 * (c ^ distance) + e, 2 * c + e)
            for c in range(chips)
            for e in range(2)
            if wanted(c, e)
        ]
        return lax.ppermute(array, "ctx", pairs)

    square = chips == 4
    kv_mine, kv_send = halves(me & 1, k_soft, v_soft)
    kv_other = swap(kv_send)
    states, sums = local_states(log_decay, k_lin, v_lin, [kv_mine])
    others = swap(states)
    kv, q_send = pair_block(me_flag, kv_mine, kv_other, q_soft, [sums])
    arrived = {}
    for distance in range(1, chips - 1 if square else chips):
        arrived[distance] = across(
            kv,
            distance,
            lambda c, e, d=distance: c ^ d < c or (square and d == 1 and c == 0 and e == 0),
        )
    q_other = swap(q_send)

    total, prefix = chip_total(me_flag, states, others, [q_send]), None
    inside, terms = inside_blocks(q_lin, k_lin, v_lin, sums, [total])
    q_terms, *carried = own_stage(me_flag, q_soft, q_other, kv, [inside])

    def exchanged(array, step):
        return lax.ppermute(array, "head", [(i, i ^ step) for i in range(heads)])

    def stage(distance, carried, after, form):
        return later_stage(
            me_flag, distance, arrived[distance], q_terms, *carried, after, form
        )

    bits = chips.bit_length() - 1
    token = carried[0]
    if square:
        carried = stage(2, carried, [], "values")
        token = carried[0]
    for bit in range(bits):
        last = bit == bits - 1
        theirs = across(total, 1 << bit, lambda c, e: not last or c ^ (1 << bit) < c)
        prefix, total = turn(me_flag, bit, total, theirs, prefix, last, [token])
        if square and bit == 0:
            relay = relayed(me_flag, arrived[1], arrived[2], [prefix])
            arrived[3] = lax.ppermute(relay, "ctx", [(2, 6), (0, 4), (5, 7), (7, 5)])
            carried = stage(1, carried, [relay], "chunks")
            token = carried[0]
        elif not square:
            carried = stage(bit + 1, carried, [prefix], "scratch")
            token = carried[0]
    prefix_other = swap(prefix)
    if not square:
        for distance in range(bits + 1, chips - 1):
            carried = stage(distance, carried, [], "scratch")

    linear, energy = linear_blocks(
        me_flag, terms, inside, sums, prefix, prefix_other, others, [carried[0]]
    )
    operands = (arrived[chips - 1], q_terms, *carried)
    theirs = last_stage(me_flag, chips - 1, *operands, [energy])
    step, other = 1, exchanged(energy, 1)
    while 2 * step < heads:
        step *= 2
        energy = plus(energy, other, [theirs])
        other = exchanged(energy, step)
    columns = q_lin.shape[1] * heads
    more = [swap(theirs), energy, other, lin_gain.reshape(1, -1), linear]
    return tuple(last_stage(me_flag, chips - 1, *operands, [], (columns, more)))


def solution(mesh):
    return jax.shard_map(
        body,
        mesh=mesh,
        in_specs=(
            P("ctx", "head"),
            P("ctx", "head"),
            P("ctx", "head"),
            P("head", "ctx"),
            P("head"),
            P("ctx", "head"),
            P("ctx", "head"),
            P("ctx", "head"),
        ),
        out_specs=(P("ctx", "head"), P("ctx", "head")),
        check_vma=False,
    )
```

time: 71.5 us -> 58.3 us (0.82)
  Pallas kernels: 40.1 us -> 24.3 us
  waiting for transfers between devices: 13.2 us -> 18 us
  local copies, waits for them, and re-layouts: 3.24 us -> 0.36 us
  other arithmetic: 0.07 us -> 1.31 us
    pallas_call x16 -> x14, Pallas kernels: 40.1 us -> 24.3 us  [call(): return lambda *operands: made(*operands, *after)]
    ppermute x1, waiting for transfers between devices: 0.01 us -> 2.99 us  [body(): arrived[3] = lax.ppermute(relay, 'ctx', [(2, 6), (0, 4), (5, 7), (7, 5)])]
    unnamed x16 -> x12, local copies, waits for them, and re-layouts: 3.24 us -> 0.36 us
    ppermute x6 -> x5, waiting for transfers between devices: 3.71 us -> 1.54 us  [swap(): return lax.ppermute(array, 'ctx', swap_pairs)]
    ppermute x4, waiting for transfers between devices: 7.44 us -> 9.47 us  [across(): return lax.ppermute(array, 'ctx', pairs)]
    ppermute x2, waiting for transfers between devices: 2.08 us -> 4.03 us  [exchanged(): return lax.ppermute(array, 'head', [(i, i ^ step) for i in range(heads)])]
    another operation x1 -> x3, other arithmetic: 0.07 us -> 1.31 us  [the longest x2 1.3 us: halves(): jnp.stack([jnp.where(core == 0, b, a) for a, b in zip(early, late)])]
    ppermute x6 -> x5, starting transfers between devices: 1.48 us -> 0.85 us  [swap(): return lax.ppermute(array, 'ctx', swap_pairs)]
  transfers between devices with their start and end apart: 13 -> 12, of which waited for: 7 -> 7; matrix products, arithmetic and copies ran while one was open for 0% -> 0% of each run, Pallas kernels for 48% -> 30%
where the time goes in v4:
time: 58.3 us; the launch traced here: 58 us
  Pallas kernels  24.3 us (42%)
  waiting for transfers between devices  18 us (31%)
  starting transfers between devices  13 us (22%)
  other arithmetic  1.31 us (2%)
  between operations  1.02 us (2%)
    pallas_call x14, Pallas kernels, call(): return lambda *operands: made(*operands, *after)  24.3 us
    ppermute x4, waiting for transfers between devices, across(): return lax.ppermute(array, 'ctx', pairs)  9.47 us
    ppermute x4, starting transfers between devices, across(): return lax.ppermute(array, 'ctx', pairs)  6.6 us
    ppermute x2, starting transfers between devices, exchanged(): return lax.ppermute(array, 'head', [(i, i ^ step) for i in range(heads)])  4.23 us
    ppermute x2, waiting for transfers between devices, exchanged(): return lax.ppermute(array, 'head', [(i, i ^ step) for i in range(heads)])  4.03 us
    ppermute x1, waiting for transfers between devices, body(): arrived[3] = lax.ppermute(relay, 'ctx', [(2, 6), (0, 4), (5, 7), (7, 5)])  2.99 us
    ppermute x5, waiting for transfers between devices, swap(): return lax.ppermute(array, 'ctx', swap_pairs)  1.54 us
    another operation x2, other arithmetic, halves(): jnp.stack([jnp.where(core == 0, b, a) for a, b in zip(early, late)])  1.3 us
  transfers between devices with their start and end apart: 12, of which 7 were waited for; matrix products, arithmetic and copies ran while one was open for 0% of the time, Pallas kernels for 30%

profile of v4, /device:TPU:6, one launch (start us, length us, event | category | flops | bytes accessed | tf_op | source)
XLA Modules:
  0.0 58.0 jit_solution(5166470660437702314)
XLA Ops:
  0.6 0.0 copy-start.2
  0.6 0.0 copy-start.1
  0.7 0.0 copy-start.4
  0.7 1.3 %select_bitcast_fusion = (f32[1,256,128]{2,1,0:T(8,128)S(1)}, f32[1,256,128]{2,1,0:T(8,128)S(1)}, f32[1,256,128]{2,1,0:T(8,128)S(1)}, f32[1,256,128]{2,1,0:T(8,128)S(1)}) fusion(f32[256,256]{1,0:T(8,128)} %param.15, pred[]{:T(512)S(6)} %eq.2, f32[256,256]{1,0:T(8,128)} %param.14), kind=kLoop, calls=%fused_computation.2 | loop fusion | flops 131072 | bytes 1048577 | tf_op jit(solution)/shard_map/stack | solution.py:254
  2.0 0.0 copy-start
  2.0 0.1 collective-permute-start
  2.1 0.0 copy-done.2
  2.1 0.3 copy-done.1
  2.4 0.0 copy-done.4
  2.4 0.9 %shard_map.95 = (f32[2,520,128]{2,1,0:T(8,128)S(1)}, f32[8,256]{1,0:T(8,128)S(1)}) custom-call(f32[8,256]{1,0:T(8,128)S(1)} %copy-done.4, f32[256,1024]{1,0:T(8,128)S(1)} %copy-done.1, f32[256,1024]{1,0:T(8,128)S(1)} %copy-done.2, f32[2,256,128]{2,1,0:T(8,128)S(1)} %pad_maximum_fusion.refs_3_.refs_1_), custom_call_target="tpu_custom_call" | custom-call | flops 1 | bytes 1 | tf_op jit(solution)/shard_map/pallas_call | solution.py:58
  3.3 0.3 collective-permute-start.3
  3.6 0.0 collective-permute-done.refs_2_
  3.6 0.0 copy-done
  3.6 0.1 shard_map.96
  3.7 0.0 copy-start.3
  3.8 0.4 collective-permute-start.5
  4.1 1.3 %collective-permute-start.2 = (f32[2,512,128]{2,1,0:T(8,128)S(1)}, f32[2,512,128]{2,1,0:T(8,128)S(1)}, u32[]{:S(2)}, u32[]{:S(2)}) collective-permute-start(f32[2,512,128]{2,1,0:T(8,128)S(1)} %get-tuple-element.23.refs_3_), channel_id=1, source_target_pairs={{0,16},{4,20},{8,24},{12,28},{1,17},{5,21},{9,25},{13,29},{2,18},{... | collective-permute-start | bytes 1572872 | tf_op jit(solution)/shard_map/ppermute | solution.py:703
  5.4 1.3 %collective-permute-start.1 = (f32[2,512,128]{2,1,0:T(8,128)S(1)}, f32[2,512,128]{2,1,0:T(8,128)S(1)}, u32[]{:S(2)}, u32[]{:S(2)}) collective-permute-start(f32[2,512,128]{2,1,0:T(8,128)S(1)} %get-tuple-element.23.refs_3_), channel_id=1, source_target_pairs={{8,0},{0,8},{4,12},{16,24},{20,28},{9,1},{1,9},{5,13},{17,25},{21,... | collective-permute-start | bytes 1572872 | tf_op jit(solution)/shard_map/ppermute | solution.py:703
  6.7 0.0 collective-permute-done.3.refs_2_.refs_6_
  6.8 2.7 %collective-permute-start.4 = (f32[520,128]{1,0:T(8,128)S(1)}, f32[520,128]{1,0:T(8,128)S(1)}, u32[]{:S(2)}, u32[]{:S(2)}) collective-permute-start(f32[520,128]{1,0:T(8,128)S(1)} %shard_map.97.refs_4_.refs_1_), channel_id=1, source_target_pairs={{8,0},{12,4},{0,8},{4,12},{24,16},{28,20},{16,24},{20,28},{9,1},{1... | collective-permute-start | bytes 798728 | tf_op jit(solution)/shard_map/ppermute | solution.py:703
  9.5 0.0 copy-done.3
  9.5 1.7 %shard_map.98 = (f32[8,256,128]{2,1,0:T(8,128)S(1)}, bf16[8,256,256]{2,1,0:T(8,128)(2,1)S(1)}) custom-call(f32[256,1024]{1,0:T(8,128)S(1)} %copy-done.3, f32[256,1024]{1,0:T(8,128)S(1)} %copy-done.1, f32[256,1024]{1,0:T(8,128)S(1)} %copy-done.2, f32[8,256]{1,0:T(8,128)S(1)} %get-tuple-element.22.refs_4_.refs_3_, f32[520,128]{1,0:T(8,128)S(1)} %shard_map.97.refs_4_.refs_1_), custom_call_target="tpu_custom_call" | custom-call | flops 1 | bytes 1 | tf_op jit(solution)/shard_map/pallas_call | solution.py:58
  11.3 0.0 collective-permute-done.5.refs_2_
  11.3 4.0 %shard_map.99 = (bf16[6,512,256]{2,1,0:T(8,128)(2,1)S(1)}, f32[6,512,128]{2,1,0:T(8,128)S(1)}, f32[6,512,128]{2,1,0:T(8,128)S(1)}, f32[6,512,128]{2,1,0:T(8,128)S(1)}) custom-call(s32[1]{0:T(128)} %bitcast.refs_0_, f32[256,1536]{1,0:T(8,128)S(1)} %copy-done, f32[6,256,128]{2,1,0:T(8,128)S(1)} %collective-permute-done.5.refs_2_, ...), custom_call_target="tpu_custom_call" | custom-call | flops 1 | bytes 1 | tf_op jit(solution)/shard_map/pallas_call | solution.py:58
  15.3 4.9 %collective-permute-done.2.refs_1_.refs_2_ = f32[2,512,128]{2,1,0:T(8,128)S(1)} collective-permute-done((f32[2,512,128]{2,1,0:T(8,128)S(1)}, f32[2,512,128]{2,1,0:T(8,128)S(1)}, u32[]{:S(2)}, u32[]{:S(2)}) %collective-permute-start.2) | collective-permute-done | bytes 524320 | tf_op jit(solution)/shard_map/ppermute | solution.py:703
  20.2 4.6 %shard_map.100 = (f32[6,512,128]{2,1,0:T(8,128)S(1)}, f32[6,512,128]{2,1,0:T(8,128)S(1)}, f32[6,512,128]{2,1,0:T(8,128)S(1)}) custom-call(s32[1]{0:T(128)} %bitcast.refs_0_, f32[2,512,128]{2,1,0:T(8,128)S(1)} %collective-permute-done.2.refs_1_.refs_2_, ...), custom_call_target="tpu_custom_call", output_to_operand_aliasing={{0}: (3, {}), {1}: (4, {}), {2}: (5, {})} | custom-call | flops 1 | bytes 1 | tf_op jit(solution)/shard_map/pallas_call | solution.py:58
  24.8 2.4 %collective-permute-done.4.refs_2_ = f32[520,128]{1,0:T(8,128)S(1)} collective-permute-done((f32[520,128]{1,0:T(8,128)S(1)}, f32[520,128]{1,0:T(8,128)S(1)}, u32[]{:S(2)}, u32[]{:S(2)}) %collective-permute-start.4) | collective-permute-done | bytes 266272 | tf_op jit(solution)/shard_map/ppermute | solution.py:703
  27.2 0.1 shard_map.101
  27.2 1.3 %collective-permute-start.7 = (f32[520,128]{1,0:T(8,128)S(1)}, f32[520,128]{1,0:T(8,128)S(1)}, u32[]{:S(2)}, u32[]{:S(2)}) collective-permute-start(f32[520,128]{1,0:T(8,128)S(1)} %get-tuple-element.39.refs_1_), channel_id=1, source_target_pairs={{0,16},{4,20},{8,24},{12,28},{1,17},{5,21},{9,25},{13,29},{2,18},{... | collective-permute-start | bytes 798728 | tf_op jit(solution)/shard_map/ppermute | solution.py:703
  28.5 0.0 collective-permute-done.1.refs_1_
  28.6 1.3 %collective-permute-start.6 = (f32[2,512,128]{2,1,0:T(8,128)S(1)}, f32[2,512,128]{2,1,0:T(8,128)S(1)}, u32[]{:S(2)}, u32[]{:S(2)}) collective-permute-start(f32[2,512,128]{2,1,0:T(8,128)S(1)} %shard_map.102.refs_6_), channel_id=1, source_target_pairs={{8,24},{0,16},{20,28},{28,20},{9,25},{1,17},{21,29},{29,21},{10,26... | collective-permute-start | bytes 1572872 | tf_op jit(solution)/shard_map/ppermute | solution.py:743
  29.9 4.9 %shard_map.103 = (f32[6,512,128]{2,1,0:T(8,128)S(1)}, f32[6,512,128]{2,1,0:T(8,128)S(1)}, f32[6,512,128]{2,1,0:T(8,128)S(1)}) custom-call(s32[1]{0:T(128)} %bitcast.refs_0_, f32[2,512,128]{2,1,0:T(8,128)S(1)} %collective-permute-done.1.refs_1_, ...), custom_call_target="tpu_custom_call", output_to_operand_aliasing={{0}: (3, {}), {1}: (4, {}), {2}: (5, {})} | custom-call | flops 1 | bytes 1 | tf_op jit(solution)/shard_map/pallas_call | solution.py:58
  34.8 2.2 %collective-permute-done.7.refs_2_ = f32[520,128]{1,0:T(8,128)S(1)} collective-permute-done((f32[520,128]{1,0:T(8,128)S(1)}, f32[520,128]{1,0:T(8,128)S(1)}, u32[]{:S(2)}, u32[]{:S(2)}) %collective-permute-start.7) | collective-permute-done | bytes 266272 | tf_op jit(solution)/shard_map/ppermute | solution.py:703
  37.0 0.1 collective-permute-start.8
  37.1 1.5 %collective-permute-done.8.refs_5_ = f32[520,128]{1,0:T(8,128)S(1)} collective-permute-done((f32[520,128]{1,0:T(8,128)S(1)}, f32[520,128]{1,0:T(8,128)S(1)}, u32[]{:S(2)}, u32[]{:S(2)}) %collective-permute-start.8) | collective-permute-done | bytes 266272 | tf_op jit(solution)/shard_map/ppermute | solution.py:694
  38.6 1.0 %shard_map.105 = (f32[8,256,128]{2,1,0:T(8,128)S(1)}, f32[8,256]{1,0:T(8,128)S(1)}) custom-call(s32[1]{0:T(128)} %bitcast.refs_0_, bf16[8,256,256]{2,1,0:T(8,128)(2,1)S(1)} %get-tuple-element.38.refs_1_, f32[8,256,128]{2,1,0:T(8,128)S(1)} %get-tuple-element.26.refs_4_.refs_2_, f32[8,256]{1,0:T(8,128)S(1)} %get-tuple-element.22.refs_4_.refs_3_, ...), custom_call_target="tpu_custom_call" | custom-call | flops 1 | bytes 1 | tf_op jit(solution)/shard_map/pallas_call | solution.py:58
  39.6 3.0 %collective-permute-done.6.refs_1_ = f32[2,512,128]{2,1,0:T(8,128)S(1)} collective-permute-done((f32[2,512,128]{2,1,0:T(8,128)S(1)}, f32[2,512,128]{2,1,0:T(8,128)S(1)}, u32[]{:S(2)}, u32[]{:S(2)}) %collective-permute-start.6) | collective-permute-done | bytes 524320 | tf_op jit(solution)/shard_map/ppermute | solution.py:743
  42.6 0.0 copy-start.5
  42.6 2.9 %shard_map.106.refs_2_ = f32[6,256,128]{2,1,0:T(8,128)S(1)} custom-call(s32[1]{0:T(128)} %bitcast.refs_0_, f32[2,512,128]{2,1,0:T(8,128)S(1)} %collective-permute-done.6.refs_1_, bf16[6,512,256]{2,1,0:T(8,128)(2,1)S(1)} %get-tuple-element.27.refs_2_, f32[6,512,128]{2,1,0:T(8,128)S(1)} %get-tuple-element.35.refs_4_.refs_7_.refs_3_, ...), custom_call_target="tpu_custom_call" | custom-call | flops 1 | bytes 1 | tf_op jit(solution)/shard_map/pallas_call | solution.py:58
  45.5 0.1 collective-permute-start.9
  45.5 1.6 %collective-permute-start.10 = (f32[8,256]{1,0:T(8,128)S(1)}, f32[8,256]{1,0:T(8,128)S(1)}, u32[]{:S(2)}, u32[]{:S(2)}) collective-permute-start(f32[8,256]{1,0:T(8,128)S(1)} %get-tuple-element.40.refs_6_.refs_0_), channel_id=1, source_target_pairs={{0,1},{1,0},{2,3},{3,2},{4,5},{5,4},{6,7},{7,6},{8,9},{9,8},{10,11... | collective-permute-start | bytes 24584 | tf_op jit(solution)/shard_map/ppermute | solution.py:725
  47.2 2.1 %collective-permute-done.10.refs_1_ = f32[8,256]{1,0:T(8,128)S(1)} collective-permute-done((f32[8,256]{1,0:T(8,128)S(1)}, f32[8,256]{1,0:T(8,128)S(1)}, u32[]{:S(2)}, u32[]{:S(2)}) %collective-permute-start.10) | collective-permute-done | bytes 8224 | tf_op jit(solution)/shard_map/ppermute | solution.py:725
  49.3 2.6 %collective-permute-start.11 = (f32[8,256]{1,0:T(8,128)S(1)}, f32[8,256]{1,0:T(8,128)S(1)}, u32[]{:S(2)}, u32[]{:S(2)}) collective-permute-start(f32[8,256]{1,0:T(8,128)S(1)} %shard_map.107.refs_7_), channel_id=1, source_target_pairs={{0,2},{1,3},{2,0},{3,1},{4,6},{5,7},{6,4},{7,5},{8,10},{9,11},{10,... | collective-permute-start | bytes 24584 | tf_op jit(solution)/shard_map/ppermute | solution.py:725
  51.8 2.0 %collective-permute-done.11.refs_8_ = f32[8,256]{1,0:T(8,128)S(1)} collective-permute-done((f32[8,256]{1,0:T(8,128)S(1)}, f32[8,256]{1,0:T(8,128)S(1)}, u32[]{:S(2)}, u32[]{:S(2)}) %collective-permute-start.11) | collective-permute-done | bytes 8224 | tf_op jit(solution)/shard_map/ppermute | solution.py:725
  53.8 0.0 collective-permute-done.9.refs_6_
  53.8 0.0 copy-done.5
  53.8 4.1 %shard_map.108 = (f32[256,1024]{1,0:T(8,128)}, f32[256,1536]{1,0:T(8,128)}) custom-call(s32[1]{0:T(128)} %bitcast.refs_0_, f32[2,512,128]{2,1,0:T(8,128)S(1)} %collective-permute-done.6.refs_1_, bf16[6,512,256]{2,1,0:T(8,128)(2,1)S(1)} %get-tuple-element.27.refs_2_, f32[6,512,128]{2,1,0:T(8,128)S(1)} %get-tuple-element.35.refs_4_.refs_7_.refs_3_, ...), custom_call_target="tpu_custom_call" | custom-call | flops 1 | bytes 1 | tf_op jit(solution)/shard_map/pallas_call | solution.py:58
  (6 shorter events, 0.2 us)
Async XLA Ops:
  0.6 1.5 %copy-start.2 = (f32[256,1024]{1,0:T(8,128)S(1)}, f32[256,1024]{1,0:T(8,128)}, u32[]{:S(2)}) copy-start(f32[256,1024]{1,0:T(8,128)} %refs_2_.3) | copy-start | bytes 3145732
  0.6 1.8 %copy-start.1 = (f32[256,1024]{1,0:T(8,128)S(1)}, f32[256,1024]{1,0:T(8,128)}, u32[]{:S(2)}) copy-start(f32[256,1024]{1,0:T(8,128)} %refs_1_.4) | copy-start | bytes 3145732
  0.7 1.8 %copy-start.4 = (f32[8,256]{1,0:T(8,128)S(1)}, f32[8,256]{1,0:T(8,128)}, u32[]{:S(2)}) copy-start(f32[8,256]{1,0:T(8,128)} %refs_0_.2) | copy-start | bytes 24580
  2.0 1.6 %copy-start = (f32[256,1536]{1,0:T(8,128)S(1)}, f32[256,1536]{1,0:T(8,128)}, u32[]{:S(2)}) copy-start(f32[256,1536]{1,0:T(8,128)} %refs_1_.5) | copy-start | bytes 4718596
  2.0 1.6 %collective-permute-start = (f32[2,256,128]{2,1,0:T(8,128)S(1)}, f32[2,256,128]{2,1,0:T(8,128)S(1)}, u32[]{:S(2)}, u32[]{:S(2)}) collective-permute-start(f32[2,256,128]{2,1,0:T(8,128)S(1)} %pad_maximum_fusion.1), channel_id=1, source_target_pairs={{0,4},{4,0},{8,12},{12,8},{16,20},{20,16},{24,28},{28,24},{1,5},{5... | collective-permute-start | bytes 786440 | tf_op jit(solution)/shard_map/ppermute | solution.py:694
  3.3 3.4 %collective-permute-start.3 = (f32[2,520,128]{2,1,0:T(8,128)S(1)}, f32[2,520,128]{2,1,0:T(8,128)S(1)}, u32[]{:S(2)}, u32[]{:S(2)}) collective-permute-start(f32[2,520,128]{2,1,0:T(8,128)S(1)} %get-tuple-element.24.refs_1_), channel_id=1, source_target_pairs={{0,4},{4,0},{8,12},{12,8},{16,20},{20,16},{24,28},{28,24},{1,5},{5... | collective-permute-start | bytes 1597448 | tf_op jit(solution)/shard_map/ppermute | solution.py:694
  3.7 5.8 %copy-start.3 = (f32[256,1024]{1,0:T(8,128)S(1)}, f32[256,1024]{1,0:T(8,128)}, u32[]{:S(2)}) copy-start(f32[256,1024]{1,0:T(8,128)} %refs_0_.3) | copy-start | bytes 3145732
  3.8 7.5 %collective-permute-start.5 = (f32[6,256,128]{2,1,0:T(8,128)S(1)}, f32[6,256,128]{2,1,0:T(8,128)S(1)}, u32[]{:S(2)}, u32[]{:S(2)}) collective-permute-start(f32[6,256,128]{2,1,0:T(8,128)S(1)} %get-tuple-element.25.refs_3_), channel_id=1, source_target_pairs={{0,4},{4,0},{8,12},{12,8},{16,20},{20,16},{24,28},{28,24},{1,5},{5... | collective-permute-start | bytes 2359304 | tf_op jit(solution)/shard_map/ppermute | solution.py:694
  4.1 16.0 %collective-permute-start.2 = (f32[2,512,128]{2,1,0:T(8,128)S(1)}, f32[2,512,128]{2,1,0:T(8,128)S(1)}, u32[]{:S(2)}, u32[]{:S(2)}) collective-permute-start(f32[2,512,128]{2,1,0:T(8,128)S(1)} %get-tuple-element.23.refs_3_), channel_id=1, source_target_pairs={{0,16},{4,20},{8,24},{12,28},{1,17},{5,21},{9,25},{13,29},{2,18},{... | collective-permute-start | bytes 1572872 | tf_op jit(solution)/shard_map/ppermute | solution.py:703
  5.4 23.1 %collective-permute-start.1 = (f32[2,512,128]{2,1,0:T(8,128)S(1)}, f32[2,512,128]{2,1,0:T(8,128)S(1)}, u32[]{:S(2)}, u32[]{:S(2)}) collective-permute-start(f32[2,512,128]{2,1,0:T(8,128)S(1)} %get-tuple-element.23.refs_3_), channel_id=1, source_target_pairs={{8,0},{0,8},{4,12},{16,24},{20,28},{9,1},{1,9},{5,13},{17,25},{21,... | collective-permute-start | bytes 1572872 | tf_op jit(solution)/shard_map/ppermute | solution.py:703
  6.8 20.4 %collective-permute-start.4 = (f32[520,128]{1,0:T(8,128)S(1)}, f32[520,128]{1,0:T(8,128)S(1)}, u32[]{:S(2)}, u32[]{:S(2)}) collective-permute-start(f32[520,128]{1,0:T(8,128)S(1)} %shard_map.97.refs_4_.refs_1_), channel_id=1, source_target_pairs={{8,0},{12,4},{0,8},{4,12},{24,16},{28,20},{16,24},{20,28},{9,1},{1... | collective-permute-start | bytes 798728 | tf_op jit(solution)/shard_map/ppermute | solution.py:703
  27.2 9.7 %collective-permute-start.7 = (f32[520,128]{1,0:T(8,128)S(1)}, f32[520,128]{1,0:T(8,128)S(1)}, u32[]{:S(2)}, u32[]{:S(2)}) collective-permute-start(f32[520,128]{1,0:T(8,128)S(1)} %get-tuple-element.39.refs_1_), channel_id=1, source_target_pairs={{0,16},{4,20},{8,24},{12,28},{1,17},{5,21},{9,25},{13,29},{2,18},{... | collective-permute-start | bytes 798728 | tf_op jit(solution)/shard_map/ppermute | solution.py:703
  28.6 14.0 %collective-permute-start.6 = (f32[2,512,128]{2,1,0:T(8,128)S(1)}, f32[2,512,128]{2,1,0:T(8,128)S(1)}, u32[]{:S(2)}, u32[]{:S(2)}) collective-permute-start(f32[2,512,128]{2,1,0:T(8,128)S(1)} %shard_map.102.refs_6_), channel_id=1, source_target_pairs={{8,24},{0,16},{20,28},{28,20},{9,25},{1,17},{21,29},{29,21},{10,26... | collective-permute-start | bytes 1572872 | tf_op jit(solution)/shard_map/ppermute | solution.py:743
  37.0 1.6 %collective-permute-start.8 = (f32[520,128]{1,0:T(8,128)S(1)}, f32[520,128]{1,0:T(8,128)S(1)}, u32[]{:S(2)}, u32[]{:S(2)}) collective-permute-start(f32[520,128]{1,0:T(8,128)S(1)} %shard_map.104.refs_4_), channel_id=1, source_target_pairs={{0,4},{4,0},{8,12},{12,8},{16,20},{20,16},{24,28},{28,24},{1,5},{5... | collective-permute-start | bytes 798728 | tf_op jit(solution)/shard_map/ppermute | solution.py:694
  42.6 11.2 %copy-start.5 = (f32[1024]{0:T(1024)S(1)}, f32[1024]{0:T(1024)}, u32[]{:S(2)}) copy-start(f32[1024]{0:T(1024)} %param.12) | copy-start | bytes 12292
  45.5 8.4 %collective-permute-start.9 = (f32[6,256,128]{2,1,0:T(8,128)S(1)}, f32[6,256,128]{2,1,0:T(8,128)S(1)}, u32[]{:S(2)}, u32[]{:S(2)}) collective-permute-start(f32[6,256,128]{2,1,0:T(8,128)S(1)} %shard_map.106.refs_2_), channel_id=1, source_target_pairs={{0,4},{4,0},{8,12},{12,8},{16,20},{20,16},{24,28},{28,24},{1,5},{5... | collective-permute-start | bytes 2359304 | tf_op jit(solution)/shard_map/ppermute | solution.py:694
  45.5 3.7 %collective-permute-start.10 = (f32[8,256]{1,0:T(8,128)S(1)}, f32[8,256]{1,0:T(8,128)S(1)}, u32[]{:S(2)}, u32[]{:S(2)}) collective-permute-start(f32[8,256]{1,0:T(8,128)S(1)} %get-tuple-element.40.refs_6_.refs_0_), channel_id=1, source_target_pairs={{0,1},{1,0},{2,3},{3,2},{4,5},{5,4},{6,7},{7,6},{8,9},{9,8},{10,11... | collective-permute-start | bytes 24584 | tf_op jit(solution)/shard_map/ppermute | solution.py:725
  49.3 4.5 %collective-permute-start.11 = (f32[8,256]{1,0:T(8,128)S(1)}, f32[8,256]{1,0:T(8,128)S(1)}, u32[]{:S(2)}, u32[]{:S(2)}) collective-permute-start(f32[8,256]{1,0:T(8,128)S(1)} %shard_map.107.refs_7_), channel_id=1, source_target_pairs={{0,2},{1,3},{2,0},{3,1},{4,6},{5,7},{6,4},{7,5},{8,10},{9,11},{10,... | collective-permute-start | bytes 24584 | tf_op jit(solution)/shard_map/ppermute | solution.py:725

commit v5 on v4

v5 whole, which is shorter than its diff:
```python
import functools
import math

import jax
import jax.numpy as jnp
from jax import lax
from jax.experimental import pallas as pl
from jax.experimental.pallas import tpu as pltpu
from jax.sharding import PartitionSpec as P

HD = 128
NEGATIVE = -1e30
EPSILON = 1e-05
ENERGY_ROWS = 64
F32 = jnp.float32
BF16 = jnp.bfloat16
NT = (((1,), (1,)), ((), ()))
VMEM_LIMIT = 32 * 1024 * 1024
VMEM = pl.BlockSpec(memory_space=pltpu.VMEM)
SMEM = pl.BlockSpec(memory_space=pltpu.SMEM)
ANY = pl.BlockSpec(memory_space=pl.ANY)
HBM = pl.BlockSpec(memory_space=pltpu.HBM)


def split(x):
    high = x.astype(BF16)
    low = (x - high.astype(F32)).astype(BF16)
    return high, low


def dot(a, b):
    return jnp.dot(a, b, preferred_element_type=F32)


def three_term(a, b):
    a_high, a_low = split(a)
    b_high, b_low = split(b)
    wide = dot(a_high, jnp.concatenate([b_high, b_low], axis=1))
    n = b.shape[1]
    return wide[:, :n] + wide[:, n:] + dot(a_low, b_high)


def call(kernel, in_specs, out_specs, out_shape, scratch=(), alias=None, after=()):
    count = len(in_specs)

    def ordered(*refs):
        kernel(*refs[:count], *refs[count + len(after) :])

    made = pl.pallas_call(
        ordered,
        in_specs=in_specs + [ANY] * len(after),
        out_specs=out_specs,
        out_shape=out_shape,
        scratch_shapes=list(scratch),
        input_output_aliases=alias or {},
        cost_estimate=pl.CostEstimate(flops=1, bytes_accessed=1, transcendentals=0),
        compiler_params=pltpu.CompilerParams(vmem_limit_bytes=VMEM_LIMIT),
    )
    return lambda *operands: made(*operands, *after)


def state_kernel(rate_ref, k_ref, v_ref, packed_ref, sums_ref):
    tokens = k_ref.shape[0]
    heads = rate_ref.shape[0]
    half = heads // 2
    upto = lax.broadcasted_iota(jnp.int32, (tokens, tokens), 0)
    upto = (upto <= lax.broadcasted_iota(jnp.int32, (tokens, tokens), 1)).astype(F32)
    sums = jnp.dot(
        rate_ref[...], upto, precision=lax.Precision.HIGHEST, preferred_element_type=F32
    )
    sums_ref[...] = sums
    totals = sums[:, tokens - 1 : tokens]
    trailing = jnp.exp(totals - sums)
    for side in range(2):
        packed_ref[side, half * HD :] = jnp.zeros((8, HD), F32)
    for h in range(heads):
        side, i = h // half, h % half
        at = slice(h * HD, (h + 1) * HD)
        packed_ref[side, i * HD : (i + 1) * HD] = three_term(
            k_ref[:, at].T * trailing[h : h + 1], v_ref[:, at]
        )
        packed_ref[side, half * HD + i : half * HD + i + 1] = jnp.broadcast_to(
            totals[h : h + 1], (1, HD)
        )


def local_states(rates, k_lin, v_lin, after):
    tokens = k_lin.shape[0]
    heads = rates.shape[0]
    return call(
        state_kernel,
        [VMEM] * 3,
        [VMEM] * 2,
        [
            jax.ShapeDtypeStruct((2, heads // 2 * HD + 8, HD), F32),
            jax.ShapeDtypeStruct((heads, tokens), F32),
        ],
        after=after,
    )(rates, k_lin, v_lin)


def join(half, first, second, out_ref):
    decay = jnp.exp(second[half * HD :, :])
    for i in range(half):
        at = slice(i * HD, (i + 1) * HD)
        out_ref[at] = first[at] * decay[i : i + 1] + second[at]
    out_ref[half * HD :] = first[half * HD :] + second[half * HD :]


def chip_kernel(half, me_ref, states_ref, others_ref, out_ref):
    core = me_ref[0] & 1

    @pl.when(core == 0)
    def _():
        join(half, states_ref[0], others_ref[0], out_ref)

    @pl.when(core == 1)
    def _():
        join(half, others_ref[1], states_ref[1], out_ref)


def chip_total(me, states, others, after):
    _, packed, _ = states.shape
    return call(
        functools.partial(chip_kernel, (packed - 8) // HD),
        [SMEM, VMEM, VMEM],
        VMEM,
        jax.ShapeDtypeStruct((packed, HD), F32),
        after=after,
    )(me, states, others)


def turn_kernel(half, bit, first, last, me_ref, total_ref, theirs_ref, *refs):
    refs = list(refs)
    before_ref = None if first else refs.pop(0)
    prefix_ref = refs.pop(0)
    total_out = None if last else refs.pop(0)
    late = (me_ref[0] >> (bit + 1)) & 1

    @pl.when(late == 0)
    def _():
        prefix_ref[...] = jnp.zeros_like(prefix_ref) if first else before_ref[...]
        if not last:
            join(half, total_ref[...], theirs_ref[...], total_out)

    @pl.when(late == 1)
    def _():
        if first:
            prefix_ref[...] = theirs_ref[...]
        else:
            join(half, theirs_ref[...], before_ref[...], prefix_ref)
        if not last:
            join(half, theirs_ref[...], total_ref[...], total_out)


def turn(me, bit, total, theirs, before, last, after):
    packed = total.shape[0]
    operands = [total, theirs] + ([] if before is None else [before])
    count = 1 if last else 2
    out = call(
        functools.partial(turn_kernel, (packed - 8) // HD, bit, before is None, last),
        [SMEM] + [VMEM] * len(operands),
        [VMEM] * count,
        [jax.ShapeDtypeStruct((packed, HD), F32)] * count,
        after=after,
    )(me, *operands)
    return out[0], (None if last else out[1])


def inside_kernel(q_ref, k_ref, v_ref, sums_ref, out_ref, terms_ref):
    tokens = q_ref.shape[0]
    heads = sums_ref.shape[0]
    causal = lax.broadcasted_iota(jnp.int32, (tokens, tokens), 0) >= lax.broadcasted_iota(
        jnp.int32, (tokens, tokens), 1
    )
    columns = sums_ref[...].T
    for h in range(heads):
        at = slice(h * HD, (h + 1) * HD)
        q_high, q_low = split(q_ref[:, at])
        k_high, k_low = split(k_ref[:, at])
        terms_ref[h, :, :HD] = q_high
        terms_ref[h, :, HD:] = q_low
        scores = lax.dot_general(
            jnp.concatenate([q_high, q_low, q_high], axis=1),
            jnp.concatenate([k_high, k_high, k_low], axis=1),
            NT,
            preferred_element_type=F32,
        )
        gaps = columns[:, h : h + 1] - sums_ref[h : h + 1, :]
        weights = jnp.where(causal, jnp.exp(jnp.where(causal, gaps, 0.0)), 0.0)
        out_ref[h] = three_term(scores * weights, v_ref[:, at])


def inside_blocks(q_lin, k_lin, v_lin, sums, after):
    tokens = q_lin.shape[0]
    heads = sums.shape[0]
    return call(
        inside_kernel,
        [VMEM] * 4,
        [VMEM] * 2,
        [
            jax.ShapeDtypeStruct((heads, tokens, HD), F32),
            jax.ShapeDtypeStruct((heads, tokens, 2 * HD), BF16),
        ],
        after=after,
    )(q_lin, k_lin, v_lin, sums)


def linear_kernel(me_ref, terms_ref, inside_ref, sums_ref, mine_ref, theirs_ref, other_ref, out_ref, energy_ref):
    heads, tokens, _ = out_ref.shape
    half = heads // 2
    core = me_ref[0] & 1
    leading = jnp.exp(sums_ref[...]).T
    squares = jnp.zeros((tokens, HD), F32)
    for side in range(2):
        decay = jnp.exp(other_ref[side, half * HD :])
        for i in range(half):
            h = side * half + i
            at = slice(i * HD, (i + 1) * HD)
            prior = jnp.where(core == side, mine_ref[at], theirs_ref[at])
            prior = jnp.where(core == 1, prior * decay[i : i + 1] + other_ref[side, at], prior)
            high, low = split(prior)
            wide = dot(terms_ref[h, :, :HD], jnp.concatenate([high, low], axis=1))
            carried = wide[:, :HD] + wide[:, HD:] + dot(terms_ref[h, :, HD:], high)
            linear = inside_ref[h] + leading[:, h : h + 1] * carried
            out_ref[h] = linear
            squares = squares + linear * linear
    energy_ref[...] = lax.dot_general(
        jnp.ones((energy_ref.shape[0], HD), F32),
        squares,
        NT,
        precision=lax.Precision.HIGHEST,
        preferred_element_type=F32,
    )


def linear_blocks(me, terms, inside, sums, mine, theirs, other, after):
    _, tokens, _ = inside.shape
    return call(
        linear_kernel,
        [SMEM] + [VMEM] * 6,
        [VMEM] * 2,
        [
            jax.ShapeDtypeStruct(inside.shape, F32),
            jax.ShapeDtypeStruct((ENERGY_ROWS, tokens), F32),
        ],
        after=after,
    )(me, terms, inside, sums, mine, theirs, other)


def halves(core, *arrays):
    early = [array[:, :HD] for array in arrays]
    late = [array[:, HD:] for array in arrays]
    mine = jnp.stack([jnp.where(core == 0, a, b) for a, b in zip(early, late)])
    theirs = jnp.stack([jnp.where(core == 0, b, a) for a, b in zip(early, late)])
    return mine, theirs


def pair_kernel(me_ref, mine_ref, other_ref, q_ref, out_ref, send_ref):
    tokens = mine_ref.shape[1]
    group = send_ref.shape[0]
    core = me_ref[0] & 1
    first = core == 0
    for side in range(2):
        mine, other = mine_ref[side], other_ref[side]
        out_ref[side, :tokens] = jnp.where(first, mine, other)
        out_ref[side, tokens:] = jnp.where(first, other, mine)
    for g in range(group):
        at = pl.ds(pl.multiple_of(((1 - core) * group + g) * HD, HD), HD)
        send_ref[g] = q_ref[:, at]


def pair_block(me, mine, other, q_soft, after):
    _, tokens, _ = mine.shape
    group = q_soft.shape[1] // (2 * HD)
    return call(
        pair_kernel,
        [SMEM] + [VMEM] * 3,
        [VMEM] * 2,
        [
            jax.ShapeDtypeStruct((2, 2 * tokens, HD), F32),
            jax.ShapeDtypeStruct((group, tokens, HD), F32),
        ],
        after=after,
    )(me, mine, other, q_soft)


def run(count, score, soften, gather):
    scores, before = score(0), None
    for i in range(count):
        following = score(i + 1) if i + 1 < count else None
        if before is not None:
            gather(i - 1, before)
        before = soften(i, scores)
        scores = following
    gather(count - 1, before)


def fill_terms(kv_ref, keys_ref, values_ref):
    k_high, k_low = split(kv_ref[0].T)
    keys_ref[:HD] = k_high
    keys_ref[HD : 2 * HD] = k_high
    keys_ref[2 * HD :] = k_low
    v_high, v_low = split(kv_ref[1])
    values_ref[:, :HD] = v_high
    values_ref[:, HD:] = v_low


def lane_max(array):
    peak = array[:, :HD]
    for c in range(1, array.shape[1] // HD):
        peak = jnp.maximum(peak, array[:, c * HD : (c + 1) * HD])
    return peak


def score_terms(pair):
    return jnp.concatenate([pair, pair[:, :HD]], axis=1)


def weigh(scores, peak, total):
    high, low = [], []
    for c in range(scores.shape[1] // HD):
        w = jnp.exp2(scores[:, c * HD : (c + 1) * HD] - peak)
        total = total + w
        pair = split(w)
        high.append(pair[0])
        low.append(pair[1])
    return jnp.concatenate(high, axis=1), jnp.concatenate(low, axis=1), total


def summed(high, low, values):
    wide = dot(high, values)
    return wide[:, :HD] + wide[:, HD:] + dot(low, values[:, :HD])


def own_kernel(factor, me_ref, q_ref, q_other_ref, kv_ref, q_out, acc_out, peak_out, total_out, keys_ref, values_ref):
    group, tokens = q_out.shape[0], q_ref.shape[0]
    core = me_ref[0] & 1
    first = core == 0
    fill_terms(kv_ref, keys_ref, values_ref)
    seen = lax.broadcasted_iota(jnp.int32, (tokens, tokens), 1)
    seen = seen <= lax.broadcasted_iota(jnp.int32, (tokens, tokens), 0)

    def where(i):
        t = i % 2
        return i // 2, slice(t * tokens, (t + 1) * tokens), slice(0, (t + 1) * tokens)

    def score(i):
        g, rows, keys = where(i)
        at = pl.ds(pl.multiple_of((core * group + g) * HD, HD), HD)
        mine, other = q_ref[:, at], q_other_ref[g]
        queries = jnp.where(first, mine, other) if i % 2 == 0 else jnp.where(first, other, mine)
        pair = jnp.concatenate(split(queries * factor), axis=1)
        q_out[g, rows] = pair
        s = dot(score_terms(pair), keys_ref[:, keys])
        edge = jnp.where(seen, s[:, rows], NEGATIVE)
        return edge if i % 2 == 0 else jnp.concatenate([s[:, :tokens], edge], axis=1)

    def soften(i, s):
        g, rows, _ = where(i)
        peak = jnp.max(lane_max(s), axis=1, keepdims=True)
        peak_out[g, rows] = jnp.broadcast_to(peak, (tokens, HD))
        high, low, total_out[g, rows] = weigh(s, peak, jnp.zeros((tokens, HD), F32))
        return high, low

    def gather(i, terms):
        g, rows, keys = where(i)
        acc_out[g, rows] = summed(*terms, values_ref[keys])

    run(2 * group, score, soften, gather)


def term_scratch(keys):
    return [pltpu.VMEM((3 * HD, keys), BF16), pltpu.VMEM((keys, 2 * HD), BF16)]


def own_stage(me, q_soft, q_other, kv, after):
    tokens, width = q_soft.shape
    group = width // (2 * HD)
    stat = jax.ShapeDtypeStruct((group, 2 * tokens, HD), F32)
    return call(
        functools.partial(own_kernel, math.log2(math.e) / math.sqrt(HD)),
        [SMEM] + [VMEM] * 3,
        [VMEM] * 4,
        [jax.ShapeDtypeStruct((group, 2 * tokens, 2 * HD), BF16), stat, stat, stat],
        term_scratch(2 * tokens),
        after=after,
    )(me, q_soft, q_other, kv)


def later_kernel(distance, parts, me_ref, kv_ref, q_ref, acc_ref, peak_ref, total_ref, acc_out, peak_out, total_out, keys_ref, values_ref):
    group, rows, _ = q_ref.shape
    size = rows // parts
    chip = me_ref[0] >> 1

    def where(i):
        return i // parts, slice(i % parts * size, (i % parts + 1) * size)

    def score(i):
        return dot(score_terms(q_ref[where(i)]), keys_ref[...])

    def soften(i, s):
        at = where(i)
        old = peak_ref[at]
        peak = jnp.maximum(jnp.max(lane_max(s), axis=1, keepdims=True), old)
        shrink = jnp.exp2(old - peak)
        peak_out[at] = peak
        high, low, total_out[at] = weigh(s, peak, total_ref[at] * shrink)
        return high, low, shrink

    def gather(i, terms):
        at = where(i)
        acc_out[at] = acc_ref[at] * terms[2] + summed(*terms[:2], values_ref[...])

    @pl.when(lax.bitwise_xor(chip, distance) < chip)
    def _():
        fill_terms(kv_ref, keys_ref, values_ref)
        run(parts * group, score, soften, gather)


def later_stage(me, distance, kv, q_terms, acc, peak, total, after, parts):
    return call(
        functools.partial(later_kernel, distance, parts),
        [SMEM] + [VMEM] * 5,
        [VMEM] * 3,
        [jax.ShapeDtypeStruct(acc.shape, F32)] * 3,
        term_scratch(kv.shape[1]),
        alias={3: 0, 4: 1, 5: 2},
        after=after,
    )(me, kv, q_terms, acc, peak, total)


def last_kernel(distance, whose, heads, columns, me_ref, kv_ref, q_ref, acc_ref, peak_ref, total_ref, *refs):
    if columns is None:
        out_ref, keys_ref, values_ref = refs
    else:
        theirs_ref, done_ref, energy_ref, energy_other_ref, gain_ref, linear_ref = refs[:6]
        lin_hbm, soft_hbm, lin_ref, out_ref, sems, keys_ref, values_ref = refs[6:]
    group, rows, _ = q_ref.shape
    tokens = rows // 2
    core, chip = me_ref[0] & 1, me_ref[0] >> 1
    side = core if whose == "own" else 1 - core
    at = pl.ds(pl.multiple_of(side * tokens, tokens), tokens)
    copies = []

    def copy_soft(source, whose, g):
        to = pl.ds(pl.multiple_of((whose * group + g) * HD, HD), HD)
        copies.append(pltpu.make_async_copy(source, soft_hbm.at[:, to], sems.at[len(copies)]))
        return copies[-1]

    if columns is not None:
        for g in range(group):
            copy_soft(theirs_ref.at[g], 1 - core, g).start()
        for g in range(done_ref.shape[0]):
            copy_soft(done_ref.at[g], core, g).start()
        factor = lax.rsqrt((energy_ref[:8] + energy_other_ref[:8]) / columns + EPSILON)
        factor = factor.T[:, 0:1]
        for h in range(linear_ref.shape[0]):
            to = slice(h * HD, (h + 1) * HD)
            lin_ref[h] = linear_ref[h] * factor * gain_ref[:, to]
            copies.append(
                pltpu.make_async_copy(lin_ref.at[h], lin_hbm.at[:, to], sems.at[len(copies)])
            )
            copies[-1].start()
        own_copies = [copy_soft(out_ref.at[n], core, g) for n, g in enumerate(heads)]

    def finish(n, acc, total):
        out_ref[n] = acc / jnp.sum(total, axis=1, keepdims=True)
        if columns is not None:
            own_copies[n].start()

    def score(n):
        return dot(score_terms(q_ref[heads[n], at]), keys_ref[...])

    def soften(n, s):
        old = peak_ref[heads[n], at]
        peak = jnp.maximum(jnp.max(lane_max(s), axis=1, keepdims=True), old)
        shrink = jnp.exp2(old - peak)
        return *weigh(s, peak, total_ref[heads[n], at] * shrink), shrink

    def gather(n, terms):
        high, low, total, shrink = terms
        new = summed(high, low, values_ref[...])
        finish(n, acc_ref[heads[n], at] * shrink + new, total)

    visible = lax.bitwise_xor(chip, distance) < chip

    @pl.when(visible)
    def _():
        fill_terms(kv_ref, keys_ref, values_ref)
        run(len(heads), score, soften, gather)

    @pl.when(jnp.logical_not(visible))
    def _():
        for n, g in enumerate(heads):
            finish(n, acc_ref[g, at], total_ref[g, at])

    for copy in copies:
        copy.wait()


def last_stage(me, distance, whose, heads, operands, after, extra=None):
    group, rows, _ = operands[1].shape
    tokens = rows // 2
    part = jax.ShapeDtypeStruct((len(heads), tokens, HD), F32)
    scratch = term_scratch(operands[0].shape[1])
    out_shape, out_spec, columns = part, VMEM, None
    if extra is not None:
        columns, more = extra
        operands = [*operands, *more]
        count = more[-1].shape[0]
        out_shape = [
            jax.ShapeDtypeStruct((tokens, count * HD), F32),
            jax.ShapeDtypeStruct((tokens, 2 * group * HD), F32),
        ]
        out_spec = [HBM] * 2
        scratch = [
            pltpu.VMEM((count, tokens, HD), F32),
            pltpu.VMEM(part.shape, F32),
            pltpu.SemaphoreType.DMA((2 * group + count,)),
        ] + scratch
    return call(
        functools.partial(last_kernel, distance, whose, heads, columns),
        [SMEM] + [VMEM] * len(operands),
        out_spec,
        out_shape,
        scratch,
        after=after,
    )(me, *operands)


def plus_kernel(a_ref, b_ref, out_ref):
    out_ref[...] = a_ref[...] + b_ref[...]


def plus(a, b, after):
    return call(
        plus_kernel, [VMEM] * 2, VMEM, jax.ShapeDtypeStruct(a.shape, F32), after=after
    )(a, b)


def copy_kernel(source_ref, out_ref):
    out_ref[...] = source_ref[...]


def copied(array, after):
    return call(copy_kernel, [VMEM], VMEM, jax.ShapeDtypeStruct(array.shape, F32), after=after)(
        array
    )


def relay_kernel(me_ref, beside_ref, across_ref, out_ref):
    @pl.when((me_ref[0] & 1) == 0)
    def _():
        out_ref[...] = beside_ref[...]

    @pl.when((me_ref[0] & 1) == 1)
    def _():
        out_ref[...] = across_ref[...]


def relayed(me, beside, across, after):
    return call(
        relay_kernel,
        [SMEM, VMEM, VMEM],
        VMEM,
        jax.ShapeDtypeStruct(beside.shape, F32),
        after=after,
    )(me, beside, across)


def body(q_lin, k_lin, v_lin, log_decay, lin_gain, q_soft, k_soft, v_soft):
    chips = lax.axis_size("ctx") // 2
    heads = lax.axis_size("head")
    me = lax.axis_index("ctx")
    me_flag = me.reshape(1).astype(jnp.int32)
    assert k_soft.shape[1] == 2 * HD
    swap_pairs = [(2 * c + e, 2 * c + 1 - e) for c in range(chips) for e in range(2)]

    def swap(array):
        return lax.ppermute(array, "ctx", swap_pairs)

    def across(array, distance, wanted=lambda c, e: True):
        pairs = [
            (2 * (c ^ distance) + e, 2 * c + e)
            for c in range(chips)
            for e in range(2)
            if wanted(c, e)
        ]
        return lax.ppermute(array, "ctx", pairs)

    square = chips == 4
    kv_mine, kv_send = halves(me & 1, k_soft, v_soft)
    kv_other = swap(kv_send)
    states, sums = local_states(log_decay, k_lin, v_lin, [kv_mine])
    others = swap(states)
    kv, q_send = pair_block(me_flag, kv_mine, kv_other, q_soft, [sums])
    q_other = swap(q_send)
    total, prefix = chip_total(me_flag, states, others, [q_send]), None
    inside, terms = inside_blocks(q_lin, k_lin, v_lin, sums, [total])

    def exchanged(array, step):
        return lax.ppermute(array, "head", [(i, i ^ step) for i in range(heads)])

    def sent(distance, array):
        return across(
            array,
            distance,
            lambda c, e: c ^ distance < c or (square and distance == 1 and c == 0 and e == 0),
        )

    def stage(distance, carried, after, parts=2):
        return later_stage(
            me_flag, distance, arrived[distance], q_terms, *carried, after, parts
        )

    bits = chips.bit_length() - 1
    arrived = {}
    if square:
        arrived[2] = sent(2, kv)
        arrived[1] = sent(1, copied(kv, [inside]))
    else:
        for distance in range(1, chips):
            arrived[distance] = sent(distance, kv)
    q_terms, *carried = own_stage(me_flag, q_soft, q_other, kv, [inside])
    token = carried[0]
    for bit in range(bits):
        last = bit == bits - 1
        theirs = across(total, 1 << bit, lambda c, e: not last or c ^ (1 << bit) < c)
        prefix, total = turn(me_flag, bit, total, theirs, prefix, last, [token])
        distance = 2 if square else bit + 1
        if not (square and last):
            carried = stage(distance, carried, [prefix], 1)
            token = carried[0]
    prefix_other = swap(prefix)
    token = prefix
    if square:
        relay = relayed(me_flag, arrived[1], arrived[2], [prefix])
        arrived[3] = lax.ppermute(relay, "ctx", [(2, 6), (0, 4), (5, 7), (7, 5)])
        token = relay
    linear, energy = linear_blocks(
        me_flag, terms, inside, sums, prefix, prefix_other, others, [token]
    )
    energies, step = [], 1
    while step < heads:
        energies.append(step)
        step *= 2
    other = exchanged(energy, energies[0])
    for distance in [1] if square else range(bits + 1, chips - 1):
        carried = stage(distance, carried, [energy])
    for step in energies[1:]:
        energy = plus(energy, other, [carried[0]])
        other = exchanged(energy, step)

    operands = [arrived[chips - 1], q_terms, *carried]
    group = q_terms.shape[0]
    theirs = last_stage(me_flag, chips - 1, "other", range(group), operands, [energy])
    done = last_stage(me_flag, chips - 1, "own", range(group // 2), operands, [theirs])
    columns = q_lin.shape[1] * heads
    more = [swap(theirs), done, energy, other, lin_gain.reshape(1, -1), linear]
    return tuple(
        last_stage(
            me_flag, chips - 1, "own", range(group // 2, group), operands, [], (columns, more)
        )
    )


def solution(mesh):
    return jax.shard_map(
        body,
        mesh=mesh,
        in_specs=(
            P("ctx", "head"),
            P("ctx", "head"),
            P("ctx", "head"),
            P("head", "ctx"),
            P("head"),
            P("ctx", "head"),
            P("ctx", "head"),
            P("ctx", "head"),
        ),
        out_specs=(P("ctx", "head"), P("ctx", "head")),
        check_vma=False,
    )
```

time: 58.3 us -> 51.9 us (0.89)
  the two profiles are of different devices: /device:TPU:6 before, /device:TPU:29 now
where the time goes in v5:
time: 51.9 us; the launch traced here: 51.6 us
  Pallas kernels  17.8 us (34%)
  waiting for transfers between devices  17.8 us (34%)
  starting transfers between devices  13.7 us (26%)
  other arithmetic  1.31 us (3%)
  between operations  1.05 us (2%)
    pallas_call x16, Pallas kernels, call(): return lambda *operands: made(*operands, *after)  17.8 us
    ppermute x2, waiting for transfers between devices, exchanged(): return lax.ppermute(array, 'head', [(i, i ^ step) for i in range(heads)])  8.14 us
    ppermute x4, starting transfers between devices, across(): return lax.ppermute(array, 'ctx', pairs)  6.04 us
    ppermute x4, waiting for transfers between devices, across(): return lax.ppermute(array, 'ctx', pairs)  6.04 us
    ppermute x5, starting transfers between devices, swap(): return lax.ppermute(array, 'ctx', swap_pairs)  4.99 us
    ppermute x5, waiting for transfers between devices, swap(): return lax.ppermute(array, 'ctx', swap_pairs)  2.37 us
    ppermute x1, starting transfers between devices, body(): arrived[3] = lax.ppermute(relay, 'ctx', [(2, 6), (0, 4), (5, 7), (7, 5)])  2.34 us
    another operation x2, other arithmetic, halves(): jnp.stack([jnp.where(core == 0, b, a) for a, b in zip(early, late)])  1.3 us
  transfers between devices with their start and end apart: 12, of which 7 were waited for; matrix products, arithmetic and copies ran while one was open for 0% of the time, Pallas kernels for 25%

profile of v5, /device:TPU:29, one launch (start us, length us, event | category | flops | bytes accessed | tf_op | source)
XLA Modules:
  0.0 51.6 jit_solution(9375299447805430555)
XLA Ops:
  0.6 0.0 copy-start.2
  0.6 0.0 copy-start.1
  0.7 0.0 copy-start.4
  0.7 1.3 %select_bitcast_fusion = (f32[1,256,128]{2,1,0:T(8,128)S(1)}, f32[1,256,128]{2,1,0:T(8,128)S(1)}, f32[1,256,128]{2,1,0:T(8,128)S(1)}, f32[1,256,128]{2,1,0:T(8,128)S(1)}) fusion(f32[256,256]{1,0:T(8,128)} %param.15, pred[]{:T(512)S(6)} %eq.2, f32[256,256]{1,0:T(8,128)} %param.14), kind=kLoop, calls=%fused_computation.2 | loop fusion | flops 131072 | bytes 1048577 | tf_op jit(solution)/shard_map/stack | solution.py:255
  2.0 0.0 copy-start
  2.0 0.7 %collective-permute-start = (f32[2,256,128]{2,1,0:T(8,128)S(1)}, f32[2,256,128]{2,1,0:T(8,128)S(1)}, u32[]{:S(2)}, u32[]{:S(2)}) collective-permute-start(f32[2,256,128]{2,1,0:T(8,128)S(1)} %pad_maximum_fusion.1), channel_id=1, source_target_pairs={{0,4},{4,0},{8,12},{12,8},{16,20},{20,16},{24,28},{28,24},{1,5},{5... | collective-permute-start | bytes 786440 | tf_op jit(solution)/shard_map/ppermute | solution.py:581
  2.7 0.0 copy-done.2
  2.8 0.0 copy-done.1
  2.8 0.0 copy-done.4
  2.8 0.9 %shard_map.95 = (f32[2,520,128]{2,1,0:T(8,128)S(1)}, f32[8,256]{1,0:T(8,128)S(1)}) custom-call(f32[8,256]{1,0:T(8,128)S(1)} %copy-done.4, f32[256,1024]{1,0:T(8,128)S(1)} %copy-done.1, f32[256,1024]{1,0:T(8,128)S(1)} %copy-done.2, f32[2,256,128]{2,1,0:T(8,128)S(1)} %pad_maximum_fusion.refs_3_.refs_1_), custom_call_target="tpu_custom_call" | custom-call | flops 1 | bytes 1 | tf_op jit(solution)/shard_map/pallas_call | solution.py:59
  3.7 0.4 collective-permute-start.1
  4.1 0.0 collective-permute-done.refs_2_
  4.1 0.0 copy-done
  4.1 0.1 shard_map.96
  4.2 0.0 copy-start.3
  4.2 0.3 collective-permute-start.5
  4.5 1.2 %collective-permute-done.1.refs_2_.refs_6_ = f32[2,520,128]{2,1,0:T(8,128)S(1)} collective-permute-done((f32[2,520,128]{2,1,0:T(8,128)S(1)}, f32[2,520,128]{2,1,0:T(8,128)S(1)}, u32[]{:S(2)}, u32[]{:S(2)}) %collective-permute-start.1) | collective-permute-done | bytes 532512 | tf_op jit(solution)/shard_map/ppermute | solution.py:581
  5.7 1.3 %collective-permute-start.4 = (f32[520,128]{1,0:T(8,128)S(1)}, f32[520,128]{1,0:T(8,128)S(1)}, u32[]{:S(2)}, u32[]{:S(2)}) collective-permute-start(f32[520,128]{1,0:T(8,128)S(1)} %shard_map.97.refs_4_.refs_1_), channel_id=1, source_target_pairs={{8,0},{12,4},{0,8},{4,12},{24,16},{28,20},{16,24},{20,28},{9,1},{1... | collective-permute-start | bytes 798728 | tf_op jit(solution)/shard_map/ppermute | solution.py:590
  7.0 1.3 %collective-permute-start.3 = (f32[2,512,128]{2,1,0:T(8,128)S(1)}, f32[2,512,128]{2,1,0:T(8,128)S(1)}, u32[]{:S(2)}, u32[]{:S(2)}) collective-permute-start(f32[2,512,128]{2,1,0:T(8,128)S(1)} %get-tuple-element.23.refs_0_.refs_3_), channel_id=1, source_target_pairs={{0,16},{4,20},{8,24},{12,28},{1,17},{5,21},{9,25},{13,29},{2,18},{... | collective-permute-start | bytes 1572872 | tf_op jit(solution)/shard_map/ppermute | solution.py:590
  8.3 0.0 copy-done.3
  8.3 1.7 %shard_map.98 = (f32[8,256,128]{2,1,0:T(8,128)S(1)}, bf16[8,256,256]{2,1,0:T(8,128)(2,1)S(1)}) custom-call(f32[256,1024]{1,0:T(8,128)S(1)} %copy-done.3, f32[256,1024]{1,0:T(8,128)S(1)} %copy-done.1, f32[256,1024]{1,0:T(8,128)S(1)} %copy-done.2, f32[8,256]{1,0:T(8,128)S(1)} %get-tuple-element.22.refs_4_.refs_3_, f32[520,128]{1,0:T(8,128)S(1)} %shard_map.97.refs_4_.refs_1_), custom_call_target="tpu_custom_call" | custom-call | flops 1 | bytes 1 | tf_op jit(solution)/shard_map/pallas_call | solution.py:59
  10.1 2.2 %collective-permute-start.2 = (f32[2,512,128]{2,1,0:T(8,128)S(1)}, f32[2,512,128]{2,1,0:T(8,128)S(1)}, u32[]{:S(2)}, u32[]{:S(2)}) collective-permute-start(f32[2,512,128]{2,1,0:T(8,128)S(1)} %shard_map.99), channel_id=1, source_target_pairs={{8,0},{0,8},{4,12},{16,24},{20,28},{9,1},{1,9},{5,13},{17,25},{21,... | collective-permute-start | bytes 1572872 | tf_op jit(solution)/shard_map/ppermute | solution.py:590
  12.3 0.0 collective-permute-done.5.refs_2_
  12.3 2.9 %shard_map.100 = (bf16[6,512,256]{2,1,0:T(8,128)(2,1)S(1)}, f32[6,512,128]{2,1,0:T(8,128)S(1)}, f32[6,512,128]{2,1,0:T(8,128)S(1)}, f32[6,512,128]{2,1,0:T(8,128)S(1)}) custom-call(s32[1]{0:T(128)} %bitcast.refs_0_, f32[256,1536]{1,0:T(8,128)S(1)} %copy-done, f32[6,256,128]{2,1,0:T(8,128)S(1)} %collective-permute-done.5.refs_2_, ...), custom_call_target="tpu_custom_call" | custom-call | flops 1 | bytes 1 | tf_op jit(solution)/shard_map/pallas_call | solution.py:59
  15.2 0.0 collective-permute-done.4.refs_2_
  15.2 1.3 %collective-permute-start.6 = (f32[520,128]{1,0:T(8,128)S(1)}, f32[520,128]{1,0:T(8,128)S(1)}, u32[]{:S(2)}, u32[]{:S(2)}) collective-permute-start(f32[520,128]{1,0:T(8,128)S(1)} %get-tuple-element.28.refs_1_), channel_id=1, source_target_pairs={{0,16},{4,20},{8,24},{12,28},{1,17},{5,21},{9,25},{13,29},{2,18},{... | collective-permute-start | bytes 798728 | tf_op jit(solution)/shard_map/ppermute | solution.py:590
  16.5 5.2 %collective-permute-done.3.refs_1_.refs_2_ = f32[2,512,128]{2,1,0:T(8,128)S(1)} collective-permute-done((f32[2,512,128]{2,1,0:T(8,128)S(1)}, f32[2,512,128]{2,1,0:T(8,128)S(1)}, u32[]{:S(2)}, u32[]{:S(2)}) %collective-permute-start.3) | collective-permute-done | bytes 524320 | tf_op jit(solution)/shard_map/ppermute | solution.py:590
  21.7 4.9 %shard_map.102 = (f32[6,512,128]{2,1,0:T(8,128)S(1)}, f32[6,512,128]{2,1,0:T(8,128)S(1)}, f32[6,512,128]{2,1,0:T(8,128)S(1)}) custom-call(s32[1]{0:T(128)} %bitcast.refs_0_, f32[2,512,128]{2,1,0:T(8,128)S(1)} %collective-permute-done.3.refs_1_.refs_2_, ...), custom_call_target="tpu_custom_call", output_to_operand_aliasing={{0}: (3, {}), {1}: (4, {}), {2}: (5, {})} | custom-call | flops 1 | bytes 1 | tf_op jit(solution)/shard_map/pallas_call | solution.py:59
  26.6 0.8 %collective-permute-done.6.refs_2_ = f32[520,128]{1,0:T(8,128)S(1)} collective-permute-done((f32[520,128]{1,0:T(8,128)S(1)}, f32[520,128]{1,0:T(8,128)S(1)}, u32[]{:S(2)}, u32[]{:S(2)}) %collective-permute-start.6) | collective-permute-done | bytes 266272 | tf_op jit(solution)/shard_map/ppermute | solution.py:590
  27.5 0.0 collective-permute-done.2.refs_1_
  27.6 2.3 %collective-permute-start.7 = (f32[2,512,128]{2,1,0:T(8,128)S(1)}, f32[2,512,128]{2,1,0:T(8,128)S(1)}, u32[]{:S(2)}, u32[]{:S(2)}) collective-permute-start(f32[2,512,128]{2,1,0:T(8,128)S(1)} %shard_map.104.refs_7_), channel_id=1, source_target_pairs={{8,24},{0,16},{20,28},{28,20},{9,25},{1,17},{21,29},{29,21},{10,26... | collective-permute-start | bytes 1572872 | tf_op jit(solution)/shard_map/ppermute | solution.py:639
  29.9 0.9 %collective-permute-start.8 = (f32[520,128]{1,0:T(8,128)S(1)}, f32[520,128]{1,0:T(8,128)S(1)}, u32[]{:S(2)}, u32[]{:S(2)}) collective-permute-start(f32[520,128]{1,0:T(8,128)S(1)} %shard_map.103.refs_3_.refs_4_), channel_id=1, source_target_pairs={{0,4},{4,0},{8,12},{12,8},{16,20},{20,16},{24,28},{28,24},{1,5},{5... | collective-permute-start | bytes 798728 | tf_op jit(solution)/shard_map/ppermute | solution.py:581
  30.9 1.2 %collective-permute-done.8.refs_5_ = f32[520,128]{1,0:T(8,128)S(1)} collective-permute-done((f32[520,128]{1,0:T(8,128)S(1)}, f32[520,128]{1,0:T(8,128)S(1)}, u32[]{:S(2)}, u32[]{:S(2)}) %collective-permute-start.8) | collective-permute-done | bytes 266272 | tf_op jit(solution)/shard_map/ppermute | solution.py:581
  32.0 1.0 %shard_map.105 = (f32[8,256,128]{2,1,0:T(8,128)S(1)}, f32[64,256]{1,0:T(8,128)S(1)}) custom-call(s32[1]{0:T(128)} %bitcast.refs_0_, bf16[8,256,256]{2,1,0:T(8,128)(2,1)S(1)} %get-tuple-element.36.refs_1_, f32[8,256,128]{2,1,0:T(8,128)S(1)} %get-tuple-element.26.refs_1_.refs_4_.refs_2_, f32[8,256]{1,0:T(8,128)S(1)} %get-tuple-element.22.refs_4_.refs_3_, ...), custom_call_target="tpu_custom_call" | custom-call | flops 1 | bytes 1 | tf_op jit(solution)/shard_map/pallas_call | solution.py:59
  33.1 0.2 collective-permute-start.9
  33.3 3.2 %collective-permute-done.9.refs_1_ = f32[64,256]{1,0:T(8,128)S(1)} collective-permute-done((f32[64,256]{1,0:T(8,128)S(1)}, f32[64,256]{1,0:T(8,128)S(1)}, u32[]{:S(2)}, u32[]{:S(2)}) %collective-permute-start.9) | collective-permute-done | bytes 65568 | tf_op jit(solution)/shard_map/ppermute | solution.py:603
  36.6 1.2 %collective-permute-done.7.refs_1_ = f32[2,512,128]{2,1,0:T(8,128)S(1)} collective-permute-done((f32[2,512,128]{2,1,0:T(8,128)S(1)}, f32[2,512,128]{2,1,0:T(8,128)S(1)}, u32[]{:S(2)}, u32[]{:S(2)}) %collective-permute-start.7) | collective-permute-done | bytes 524320 | tf_op jit(solution)/shard_map/ppermute | solution.py:639
  37.8 2.3 %shard_map.108.refs_6_ = f32[6,256,128]{2,1,0:T(8,128)S(1)} custom-call(s32[1]{0:T(128)} %bitcast.refs_0_, f32[2,512,128]{2,1,0:T(8,128)S(1)} %collective-permute-done.7.refs_1_, bf16[6,512,256]{2,1,0:T(8,128)(2,1)S(1)} %get-tuple-element.30.refs_2_, f32[6,512,128]{2,1,0:T(8,128)S(1)} %get-tuple-element.38.refs_2_.refs_3_, ...), custom_call_target="tpu_custom_call" | custom-call | flops 1 | bytes 1 | tf_op jit(solution)/shard_map/pallas_call | solution.py:59
  40.1 0.0 copy-start.5
  40.1 2.7 %collective-permute-start.10 = (f32[6,256,128]{2,1,0:T(8,128)S(1)}, f32[6,256,128]{2,1,0:T(8,128)S(1)}, u32[]{:S(2)}, u32[]{:S(2)}) collective-permute-start(f32[6,256,128]{2,1,0:T(8,128)S(1)} %shard_map.108.refs_6_), channel_id=1, source_target_pairs={{0,4},{4,0},{8,12},{12,8},{16,20},{20,16},{24,28},{28,24},{1,5},{5... | collective-permute-start | bytes 2359304 | tf_op jit(solution)/shard_map/ppermute | solution.py:581
  42.7 0.1 collective-permute-start.11
  42.8 1.3 %shard_map.109.refs_7_ = f32[3,256,128]{2,1,0:T(8,128)S(1)} custom-call(s32[1]{0:T(128)} %bitcast.refs_0_, f32[2,512,128]{2,1,0:T(8,128)S(1)} %collective-permute-done.7.refs_1_, bf16[6,512,256]{2,1,0:T(8,128)(2,1)S(1)} %get-tuple-element.30.refs_2_, f32[6,512,128]{2,1,0:T(8,128)S(1)} %get-tuple-element.38.refs_2_.refs_3_, ...), custom_call_target="tpu_custom_call" | custom-call | flops 1 | bytes 1 | tf_op jit(solution)/shard_map/pallas_call | solution.py:59
  44.1 4.9 %collective-permute-done.11.refs_9_ = f32[64,256]{1,0:T(8,128)S(1)} collective-permute-done((f32[64,256]{1,0:T(8,128)S(1)}, f32[64,256]{1,0:T(8,128)S(1)}, u32[]{:S(2)}, u32[]{:S(2)}) %collective-permute-start.11) | collective-permute-done | bytes 65568 | tf_op jit(solution)/shard_map/ppermute | solution.py:603
  49.0 0.0 collective-permute-done.10.refs_6_
  49.0 0.0 copy-done.5
  49.0 2.5 %shard_map.110 = (f32[256,1024]{1,0:T(8,128)}, f32[256,1536]{1,0:T(8,128)}) custom-call(s32[1]{0:T(128)} %bitcast.refs_0_, f32[2,512,128]{2,1,0:T(8,128)S(1)} %collective-permute-done.7.refs_1_, bf16[6,512,256]{2,1,0:T(8,128)(2,1)S(1)} %get-tuple-element.30.refs_2_, f32[6,512,128]{2,1,0:T(8,128)S(1)} %get-tuple-element.38.refs_2_.refs_3_, ...), custom_call_target="tpu_custom_call" | custom-call | flops 1 | bytes 1 | tf_op jit(solution)/shard_map/pallas_call | solution.py:59
  (9 shorter events, 0.2 us)
Async XLA Ops:
  0.6 2.1 %copy-start.2 = (f32[256,1024]{1,0:T(8,128)S(1)}, f32[256,1024]{1,0:T(8,128)}, u32[]{:S(2)}) copy-start(f32[256,1024]{1,0:T(8,128)} %refs_2_.3) | copy-start | bytes 3145732
  0.6 2.1 %copy-start.1 = (f32[256,1024]{1,0:T(8,128)S(1)}, f32[256,1024]{1,0:T(8,128)}, u32[]{:S(2)}) copy-start(f32[256,1024]{1,0:T(8,128)} %refs_1_.4) | copy-start | bytes 3145732
  0.7 2.1 %copy-start.4 = (f32[8,256]{1,0:T(8,128)S(1)}, f32[8,256]{1,0:T(8,128)}, u32[]{:S(2)}) copy-start(f32[8,256]{1,0:T(8,128)} %refs_0_.2) | copy-start | bytes 24580
  2.0 2.1 %copy-start = (f32[256,1536]{1,0:T(8,128)S(1)}, f32[256,1536]{1,0:T(8,128)}, u32[]{:S(2)}) copy-start(f32[256,1536]{1,0:T(8,128)} %refs_1_.5) | copy-start | bytes 4718596
  2.0 2.1 %collective-permute-start = (f32[2,256,128]{2,1,0:T(8,128)S(1)}, f32[2,256,128]{2,1,0:T(8,128)S(1)}, u32[]{:S(2)}, u32[]{:S(2)}) collective-permute-start(f32[2,256,128]{2,1,0:T(8,128)S(1)} %pad_maximum_fusion.1), channel_id=1, source_target_pairs={{0,4},{4,0},{8,12},{12,8},{16,20},{20,16},{24,28},{28,24},{1,5},{5... | collective-permute-start | bytes 786440 | tf_op jit(solution)/shard_map/ppermute | solution.py:581
  3.7 2.0 %collective-permute-start.1 = (f32[2,520,128]{2,1,0:T(8,128)S(1)}, f32[2,520,128]{2,1,0:T(8,128)S(1)}, u32[]{:S(2)}, u32[]{:S(2)}) collective-permute-start(f32[2,520,128]{2,1,0:T(8,128)S(1)} %get-tuple-element.24.refs_1_), channel_id=1, source_target_pairs={{0,4},{4,0},{8,12},{12,8},{16,20},{20,16},{24,28},{28,24},{1,5},{5... | collective-permute-start | bytes 1597448 | tf_op jit(solution)/shard_map/ppermute | solution.py:581
  4.2 4.1 %copy-start.3 = (f32[256,1024]{1,0:T(8,128)S(1)}, f32[256,1024]{1,0:T(8,128)}, u32[]{:S(2)}) copy-start(f32[256,1024]{1,0:T(8,128)} %refs_0_.3) | copy-start | bytes 3145732
  4.2 8.0 %collective-permute-start.5 = (f32[6,256,128]{2,1,0:T(8,128)S(1)}, f32[6,256,128]{2,1,0:T(8,128)S(1)}, u32[]{:S(2)}, u32[]{:S(2)}) collective-permute-start(f32[6,256,128]{2,1,0:T(8,128)S(1)} %get-tuple-element.25.refs_3_), channel_id=1, source_target_pairs={{0,4},{4,0},{8,12},{12,8},{16,20},{20,16},{24,28},{28,24},{1,5},{5... | collective-permute-start | bytes 2359304 | tf_op jit(solution)/shard_map/ppermute | solution.py:581
  5.7 9.5 %collective-permute-start.4 = (f32[520,128]{1,0:T(8,128)S(1)}, f32[520,128]{1,0:T(8,128)S(1)}, u32[]{:S(2)}, u32[]{:S(2)}) collective-permute-start(f32[520,128]{1,0:T(8,128)S(1)} %shard_map.97.refs_4_.refs_1_), channel_id=1, source_target_pairs={{8,0},{12,4},{0,8},{4,12},{24,16},{28,20},{16,24},{20,28},{9,1},{1... | collective-permute-start | bytes 798728 | tf_op jit(solution)/shard_map/ppermute | solution.py:590
  7.0 14.8 %collective-permute-start.3 = (f32[2,512,128]{2,1,0:T(8,128)S(1)}, f32[2,512,128]{2,1,0:T(8,128)S(1)}, u32[]{:S(2)}, u32[]{:S(2)}) collective-permute-start(f32[2,512,128]{2,1,0:T(8,128)S(1)} %get-tuple-element.23.refs_0_.refs_3_), channel_id=1, source_target_pairs={{0,16},{4,20},{8,24},{12,28},{1,17},{5,21},{9,25},{13,29},{2,18},{... | collective-permute-start | bytes 1572872 | tf_op jit(solution)/shard_map/ppermute | solution.py:590
  10.1 17.4 %collective-permute-start.2 = (f32[2,512,128]{2,1,0:T(8,128)S(1)}, f32[2,512,128]{2,1,0:T(8,128)S(1)}, u32[]{:S(2)}, u32[]{:S(2)}) collective-permute-start(f32[2,512,128]{2,1,0:T(8,128)S(1)} %shard_map.99), channel_id=1, source_target_pairs={{8,0},{0,8},{4,12},{16,24},{20,28},{9,1},{1,9},{5,13},{17,25},{21,... | collective-permute-start | bytes 1572872 | tf_op jit(solution)/shard_map/ppermute | solution.py:590
  15.2 12.2 %collective-permute-start.6 = (f32[520,128]{1,0:T(8,128)S(1)}, f32[520,128]{1,0:T(8,128)S(1)}, u32[]{:S(2)}, u32[]{:S(2)}) collective-permute-start(f32[520,128]{1,0:T(8,128)S(1)} %get-tuple-element.28.refs_1_), channel_id=1, source_target_pairs={{0,16},{4,20},{8,24},{12,28},{1,17},{5,21},{9,25},{13,29},{2,18},{... | collective-permute-start | bytes 798728 | tf_op jit(solution)/shard_map/ppermute | solution.py:590
  27.6 10.2 %collective-permute-start.7 = (f32[2,512,128]{2,1,0:T(8,128)S(1)}, f32[2,512,128]{2,1,0:T(8,128)S(1)}, u32[]{:S(2)}, u32[]{:S(2)}) collective-permute-start(f32[2,512,128]{2,1,0:T(8,128)S(1)} %shard_map.104.refs_7_), channel_id=1, source_target_pairs={{8,24},{0,16},{20,28},{28,20},{9,25},{1,17},{21,29},{29,21},{10,26... | collective-permute-start | bytes 1572872 | tf_op jit(solution)/shard_map/ppermute | solution.py:639
  29.9 2.1 %collective-permute-start.8 = (f32[520,128]{1,0:T(8,128)S(1)}, f32[520,128]{1,0:T(8,128)S(1)}, u32[]{:S(2)}, u32[]{:S(2)}) collective-permute-start(f32[520,128]{1,0:T(8,128)S(1)} %shard_map.103.refs_3_.refs_4_), channel_id=1, source_target_pairs={{0,4},{4,0},{8,12},{12,8},{16,20},{20,16},{24,28},{28,24},{1,5},{5... | collective-permute-start | bytes 798728 | tf_op jit(solution)/shard_map/ppermute | solution.py:581
  33.1 3.5 %collective-permute-start.9 = (f32[64,256]{1,0:T(8,128)S(1)}, f32[64,256]{1,0:T(8,128)S(1)}, u32[]{:S(2)}, u32[]{:S(2)}) collective-permute-start(f32[64,256]{1,0:T(8,128)S(1)} %get-tuple-element.37.refs_6_.refs_0_), channel_id=1, source_target_pairs={{0,1},{1,0},{2,3},{3,2},{4,5},{5,4},{6,7},{7,6},{8,9},{9,8},{10,11... | collective-permute-start | bytes 196616 | tf_op jit(solution)/shard_map/ppermute | solution.py:603
  40.1 9.0 %copy-start.5 = (f32[1024]{0:T(1024)S(1)}, f32[1024]{0:T(1024)}, u32[]{:S(2)}) copy-start(f32[1024]{0:T(1024)} %param.12) | copy-start | bytes 12292
  40.1 8.9 %collective-permute-start.10 = (f32[6,256,128]{2,1,0:T(8,128)S(1)}, f32[6,256,128]{2,1,0:T(8,128)S(1)}, u32[]{:S(2)}, u32[]{:S(2)}) collective-permute-start(f32[6,256,128]{2,1,0:T(8,128)S(1)} %shard_map.108.refs_6_), channel_id=1, source_target_pairs={{0,4},{4,0},{8,12},{12,8},{16,20},{20,16},{24,28},{28,24},{1,5},{5... | collective-permute-start | bytes 2359304 | tf_op jit(solution)/shard_map/ppermute | solution.py:581
  42.7 6.3 %collective-permute-start.11 = (f32[64,256]{1,0:T(8,128)S(1)}, f32[64,256]{1,0:T(8,128)S(1)}, u32[]{:S(2)}, u32[]{:S(2)}) collective-permute-start(f32[64,256]{1,0:T(8,128)S(1)} %shard_map.107.refs_6_.refs_8_), channel_id=1, source_target_pairs={{0,2},{1,3},{2,0},{3,1},{4,6},{5,7},{6,4},{7,5},{8,10},{9,11},{10,... | collective-permute-start | bytes 196616 | tf_op jit(solution)/shard_map/ppermute | solution.py:603

commit v6 on v5

--- a/solution.py
+++ b/solution.py
@@ -11,7 +11,7 @@
 HD = 128
 NEGATIVE = -1e30
 EPSILON = 1e-05
-ENERGY_ROWS = 64
+ENERGY_ROWS = 16
 F32 = jnp.float32
 BF16 = jnp.bfloat16
 NT = (((1,), (1,)), ((), ()))
@@ -549,24 +549,24 @@
     )
 
 
-def relay_kernel(me_ref, beside_ref, across_ref, out_ref):
+def relay_kernel(me_ref, own_ref, across_ref, out_ref):
     @pl.when((me_ref[0] & 1) == 0)
     def _():
-        out_ref[...] = beside_ref[...]
+        out_ref[...] = own_ref[...]
 
     @pl.when((me_ref[0] & 1) == 1)
     def _():
         out_ref[...] = across_ref[...]
 
 
-def relayed(me, beside, across, after):
+def relayed(me, own, across, after):
     return call(
         relay_kernel,
         [SMEM, VMEM, VMEM],
         VMEM,
-        jax.ShapeDtypeStruct(beside.shape, F32),
-        after=after,
-    )(me, beside, across)
+        jax.ShapeDtypeStruct(own.shape, F32),
+        after=after,
+    )(me, own, across)
 
 
 def body(q_lin, k_lin, v_lin, log_decay, lin_gain, q_soft, k_soft, v_soft):
@@ -603,11 +603,7 @@
         return lax.ppermute(array, "head", [(i, i ^ step) for i in range(heads)])
 
     def sent(distance, array):
-        return across(
-            array,
-            distance,
-            lambda c, e: c ^ distance < c or (square and distance == 1 and c == 0 and e == 0),
-        )
+        return across(array, distance, lambda c, e: c ^ distance < c)
 
     def stage(distance, carried, after, parts=2):
         return later_stage(
@@ -615,31 +611,30 @@
         )
 
     bits = chips.bit_length() - 1
-    arrived = {}
+    arrived, token = {}, inside
     if square:
         arrived[2] = sent(2, kv)
-        arrived[1] = sent(1, copied(kv, [inside]))
+        token = copied(kv, [inside])
+        arrived[1] = sent(1, token)
     else:
         for distance in range(1, chips):
             arrived[distance] = sent(distance, kv)
-    q_terms, *carried = own_stage(me_flag, q_soft, q_other, kv, [inside])
+    q_terms, *carried = own_stage(me_flag, q_soft, q_other, kv, [token])
     token = carried[0]
+    if square:
+        relay = relayed(me_flag, kv, arrived[2], [token])
+        arrived[3] = lax.ppermute(relay, "ctx", [(0, 6), (2, 4), (5, 7), (7, 5)])
     for bit in range(bits):
         last = bit == bits - 1
         theirs = across(total, 1 << bit, lambda c, e: not last or c ^ (1 << bit) < c)
         prefix, total = turn(me_flag, bit, total, theirs, prefix, last, [token])
         distance = 2 if square else bit + 1
         if not (square and last):
-            carried = stage(distance, carried, [prefix], 1)
+            carried = stage(distance, carried, [prefix, relay] if square else [prefix], 4)
             token = carried[0]
     prefix_other = swap(prefix)
-    token = prefix
-    if square:
-        relay = relayed(me_flag, arrived[1], arrived[2], [prefix])
-        arrived[3] = lax.ppermute(relay, "ctx", [(2, 6), (0, 4), (5, 7), (7, 5)])
-        token = relay
     linear, energy = linear_blocks(
-        me_flag, terms, inside, sums, prefix, prefix_other, others, [token]
+        me_flag, terms, inside, sums, prefix, prefix_other, others, []
     )
     energies, step = [], 1
     while step < heads:

time: 51.9 us -> 48.2 us (0.929)
  the two profiles are of different devices: /device:TPU:29 before, /device:TPU:6 now
where the time goes in v6:
time: 48.2 us; the launch traced here: 47.9 us
  Pallas kernels  21.9 us (45%)
  waiting for transfers between devices  12.4 us (26%)
  starting transfers between devices  10.9 us (23%)
  other arithmetic  1.31 us (3%)
  between operations  1.06 us (2%)
    pallas_call x16, Pallas kernels, call(): return lambda *operands: made(*operands, *after)  21.9 us
    ppermute x4, waiting for transfers between devices, across(): return lax.ppermute(array, 'ctx', pairs)  8.84 us
    ppermute x4, starting transfers between devices, across(): return lax.ppermute(array, 'ctx', pairs)  4.46 us
    ppermute x2, starting transfers between devices, exchanged(): return lax.ppermute(array, 'head', [(i, i ^ step) for i in range(heads)])  4.25 us
    ppermute x5, waiting for transfers between devices, swap(): return lax.ppermute(array, 'ctx', swap_pairs)  1.54 us
    ppermute x1, waiting for transfers between devices, body(): arrived[3] = lax.ppermute(relay, 'ctx', [(0, 6), (2, 4), (5, 7), (7, 5)])  1.3 us
    another operation x2, other arithmetic, halves(): jnp.stack([jnp.where(core == 0, b, a) for a, b in zip(early, late)])  1.3 us
    ppermute x1, starting transfers between devices, body(): arrived[3] = lax.ppermute(relay, 'ctx', [(0, 6), (2, 4), (5, 7), (7, 5)])  1.29 us
  transfers between devices with their start and end apart: 12, of which 6 were waited for; matrix products, arithmetic and copies ran while one was open for 0% of the time, Pallas kernels for 36%

profile of v6, /device:TPU:6, one launch (start us, length us, event | category | flops | bytes accessed | tf_op | source)
XLA Modules:
  0.0 47.9 jit_solution(12006128788195384327)
XLA Ops:
  0.6 0.0 copy-start.2
  0.6 0.0 copy-start.1
  0.7 0.0 copy-start.4
  0.7 1.3 %select_bitcast_fusion = (f32[1,256,128]{2,1,0:T(8,128)S(1)}, f32[1,256,128]{2,1,0:T(8,128)S(1)}, f32[1,256,128]{2,1,0:T(8,128)S(1)}, f32[1,256,128]{2,1,0:T(8,128)S(1)}) fusion(f32[256,256]{1,0:T(8,128)} %param.15, pred[]{:T(512)S(6)} %eq.2, f32[256,256]{1,0:T(8,128)} %param.14), kind=kLoop, calls=%fused_computation.2 | loop fusion | flops 131072 | bytes 1048577 | tf_op jit(solution)/shard_map/stack | solution.py:255
  2.0 0.0 copy-start
  2.0 0.1 collective-permute-start
  2.1 0.0 copy-done.2
  2.1 0.3 copy-done.1
  2.4 0.0 copy-done.4
  2.4 0.9 %shard_map.95 = (f32[2,520,128]{2,1,0:T(8,128)S(1)}, f32[8,256]{1,0:T(8,128)S(1)}) custom-call(f32[8,256]{1,0:T(8,128)S(1)} %copy-done.4, f32[256,1024]{1,0:T(8,128)S(1)} %copy-done.1, f32[256,1024]{1,0:T(8,128)S(1)} %copy-done.2, f32[2,256,128]{2,1,0:T(8,128)S(1)} %pad_maximum_fusion.refs_3_.refs_1_), custom_call_target="tpu_custom_call" | custom-call | flops 1 | bytes 1 | tf_op jit(solution)/shard_map/pallas_call | solution.py:59
  3.3 0.3 collective-permute-start.3
  3.6 0.0 collective-permute-done.refs_2_
  3.6 0.0 copy-done
  3.6 0.1 shard_map.96
  3.7 0.0 copy-start.3
  3.8 0.4 collective-permute-start.2
  4.1 1.3 %collective-permute-start.1 = (f32[2,512,128]{2,1,0:T(8,128)S(1)}, f32[2,512,128]{2,1,0:T(8,128)S(1)}, u32[]{:S(2)}, u32[]{:S(2)}) collective-permute-start(f32[2,512,128]{2,1,0:T(8,128)S(1)} %get-tuple-element.23.refs_0_.refs_3_.refs_1_), channel_id=1, source_target_pairs={{0,16},{4,20},{8,24},{12,28},{1,17},{5,21},{9,25},{13,29},{2,18},{... | collective-permute-start | bytes 1572872 | tf_op jit(solution)/shard_map/ppermute | solution.py:590
  5.4 0.0 collective-permute-done.3.refs_2_.refs_6_
  5.5 0.6 %collective-permute-start.6 = (f32[520,128]{1,0:T(8,128)S(1)}, f32[520,128]{1,0:T(8,128)S(1)}, u32[]{:S(2)}, u32[]{:S(2)}) collective-permute-start(f32[520,128]{1,0:T(8,128)S(1)} %shard_map.97.refs_4_.refs_1_), channel_id=1, source_target_pairs={{8,0},{12,4},{0,8},{4,12},{24,16},{28,20},{16,24},{20,28},{9,1},{1... | collective-permute-start | bytes 798728 | tf_op jit(solution)/shard_map/ppermute | solution.py:590
  6.1 0.0 copy-done.3
  6.1 1.7 %shard_map.98 = (f32[8,256,128]{2,1,0:T(8,128)S(1)}, bf16[8,256,256]{2,1,0:T(8,128)(2,1)S(1)}) custom-call(f32[256,1024]{1,0:T(8,128)S(1)} %copy-done.3, f32[256,1024]{1,0:T(8,128)S(1)} %copy-done.1, f32[256,1024]{1,0:T(8,128)S(1)} %copy-done.2, f32[8,256]{1,0:T(8,128)S(1)} %get-tuple-element.22.refs_4_.refs_3_, f32[520,128]{1,0:T(8,128)S(1)} %shard_map.97.refs_4_.refs_1_), custom_call_target="tpu_custom_call" | custom-call | flops 1 | bytes 1 | tf_op jit(solution)/shard_map/pallas_call | solution.py:59
  7.9 0.0 collective-permute-done.2.refs_2_
  7.9 2.9 %shard_map.100 = (bf16[6,512,256]{2,1,0:T(8,128)(2,1)S(1)}, f32[6,512,128]{2,1,0:T(8,128)S(1)}, f32[6,512,128]{2,1,0:T(8,128)S(1)}, f32[6,512,128]{2,1,0:T(8,128)S(1)}) custom-call(s32[1]{0:T(128)} %bitcast.refs_0_, f32[256,1536]{1,0:T(8,128)S(1)} %copy-done, f32[6,256,128]{2,1,0:T(8,128)S(1)} %collective-permute-done.2.refs_2_, ...), custom_call_target="tpu_custom_call" | custom-call | flops 1 | bytes 1 | tf_op jit(solution)/shard_map/pallas_call | solution.py:59
  10.8 3.4 %collective-permute-done.6.refs_2_ = f32[520,128]{1,0:T(8,128)S(1)} collective-permute-done((f32[520,128]{1,0:T(8,128)S(1)}, f32[520,128]{1,0:T(8,128)S(1)}, u32[]{:S(2)}, u32[]{:S(2)}) %collective-permute-start.6) | collective-permute-done | bytes 266272 | tf_op jit(solution)/shard_map/ppermute | solution.py:590
  14.2 0.1 shard_map.102
  14.2 1.3 %collective-permute-start.7 = (f32[520,128]{1,0:T(8,128)S(1)}, f32[520,128]{1,0:T(8,128)S(1)}, u32[]{:S(2)}, u32[]{:S(2)}) collective-permute-start(f32[520,128]{1,0:T(8,128)S(1)} %get-tuple-element.36.refs_1_), channel_id=1, source_target_pairs={{0,16},{4,20},{8,24},{12,28},{1,17},{5,21},{9,25},{13,29},{2,18},{... | collective-permute-start | bytes 798728 | tf_op jit(solution)/shard_map/ppermute | solution.py:590
  15.5 1.3 %collective-permute-start.5 = (f32[2,512,128]{2,1,0:T(8,128)S(1)}, f32[2,512,128]{2,1,0:T(8,128)S(1)}, u32[]{:S(2)}, u32[]{:S(2)}) collective-permute-start(f32[2,512,128]{2,1,0:T(8,128)S(1)} %shard_map.99.refs_4_), channel_id=1, source_target_pairs={{0,8},{4,12},{16,24},{20,28},{1,9},{5,13},{17,25},{21,29},{2,10},{... | collective-permute-start | bytes 1572872 | tf_op jit(solution)/shard_map/ppermute | solution.py:590
  16.8 3.9 %collective-permute-done.1.refs_2_.refs_1_ = f32[2,512,128]{2,1,0:T(8,128)S(1)} collective-permute-done((f32[2,512,128]{2,1,0:T(8,128)S(1)}, f32[2,512,128]{2,1,0:T(8,128)S(1)}, u32[]{:S(2)}, u32[]{:S(2)}) %collective-permute-start.1) | collective-permute-done | bytes 524320 | tf_op jit(solution)/shard_map/ppermute | solution.py:590
  20.8 1.3 %collective-permute-start.4 = (f32[2,512,128]{2,1,0:T(8,128)S(1)}, f32[2,512,128]{2,1,0:T(8,128)S(1)}, u32[]{:S(2)}, u32[]{:S(2)}) collective-permute-start(f32[2,512,128]{2,1,0:T(8,128)S(1)} %shard_map.101.refs_7_), channel_id=1, source_target_pairs={{0,24},{8,16},{20,28},{28,20},{1,25},{9,17},{21,29},{29,21},{2,26}... | collective-permute-start | bytes 1572872 | tf_op jit(solution)/shard_map/ppermute | solution.py:626
  22.1 4.4 %shard_map.103 = (f32[6,512,128]{2,1,0:T(8,128)S(1)}, f32[6,512,128]{2,1,0:T(8,128)S(1)}, f32[6,512,128]{2,1,0:T(8,128)S(1)}) custom-call(s32[1]{0:T(128)} %bitcast.refs_0_, f32[2,512,128]{2,1,0:T(8,128)S(1)} %collective-permute-done.1.refs_2_.refs_1_, ...), custom_call_target="tpu_custom_call", output_to_operand_aliasing={{0}: (3, {}), {1}: (4, {}), {2}: (5, {})} | custom-call | flops 1 | bytes 1 | tf_op jit(solution)/shard_map/pallas_call | solution.py:59
  26.5 0.0 collective-permute-done.7.refs_2_
  26.6 0.1 collective-permute-start.8
  26.7 1.5 %collective-permute-done.8.refs_5_ = f32[520,128]{1,0:T(8,128)S(1)} collective-permute-done((f32[520,128]{1,0:T(8,128)S(1)}, f32[520,128]{1,0:T(8,128)S(1)}, u32[]{:S(2)}, u32[]{:S(2)}) %collective-permute-start.8) | collective-permute-done | bytes 266272 | tf_op jit(solution)/shard_map/ppermute | solution.py:581
  28.2 1.0 %shard_map.105 = (f32[8,256,128]{2,1,0:T(8,128)S(1)}, f32[16,256]{1,0:T(8,128)S(1)}) custom-call(s32[1]{0:T(128)} %bitcast.refs_0_, bf16[8,256,256]{2,1,0:T(8,128)(2,1)S(1)} %get-tuple-element.35.refs_1_, f32[8,256,128]{2,1,0:T(8,128)S(1)} %get-tuple-element.26.refs_1_.refs_2_, f32[8,256]{1,0:T(8,128)S(1)} %get-tuple-element.22.refs_4_.refs_3_, ...), custom_call_target="tpu_custom_call" | custom-call | flops 1 | bytes 1 | tf_op jit(solution)/shard_map/pallas_call | solution.py:59
  29.2 1.6 %collective-permute-start.9 = (f32[16,256]{1,0:T(8,128)S(1)}, f32[16,256]{1,0:T(8,128)S(1)}, u32[]{:S(2)}, u32[]{:S(2)}) collective-permute-start(f32[16,256]{1,0:T(8,128)S(1)} %get-tuple-element.37.refs_6_.refs_0_), channel_id=1, source_target_pairs={{0,1},{1,0},{2,3},{3,2},{4,5},{5,4},{6,7},{7,6},{8,9},{9,8},{10,11... | collective-permute-start | bytes 49160 | tf_op jit(solution)/shard_map/ppermute | solution.py:603
  30.8 1.5 %collective-permute-done.5.refs_1_ = f32[2,512,128]{2,1,0:T(8,128)S(1)} collective-permute-done((f32[2,512,128]{2,1,0:T(8,128)S(1)}, f32[2,512,128]{2,1,0:T(8,128)S(1)}, u32[]{:S(2)}, u32[]{:S(2)}) %collective-permute-start.5) | collective-permute-done | bytes 524320 | tf_op jit(solution)/shard_map/ppermute | solution.py:590
  32.3 4.6 %shard_map.106 = (f32[6,512,128]{2,1,0:T(8,128)S(1)}, f32[6,512,128]{2,1,0:T(8,128)S(1)}, f32[6,512,128]{2,1,0:T(8,128)S(1)}) custom-call(s32[1]{0:T(128)} %bitcast.refs_0_, f32[2,512,128]{2,1,0:T(8,128)S(1)} %collective-permute-done.5.refs_1_, ...), custom_call_target="tpu_custom_call", output_to_operand_aliasing={{0}: (3, {}), {1}: (4, {}), {2}: (5, {})} | custom-call | flops 1 | bytes 1 | tf_op jit(solution)/shard_map/pallas_call | solution.py:59
  36.9 0.0 collective-permute-done.9.refs_1_
  36.9 1.3 %collective-permute-done.4.refs_1_ = f32[2,512,128]{2,1,0:T(8,128)S(1)} collective-permute-done((f32[2,512,128]{2,1,0:T(8,128)S(1)}, f32[2,512,128]{2,1,0:T(8,128)S(1)}, u32[]{:S(2)}, u32[]{:S(2)}) %collective-permute-start.4) | collective-permute-done | bytes 524320 | tf_op jit(solution)/shard_map/ppermute | solution.py:626
  38.2 2.3 %shard_map.108.refs_6_ = f32[6,256,128]{2,1,0:T(8,128)S(1)} custom-call(s32[1]{0:T(128)} %bitcast.refs_0_, f32[2,512,128]{2,1,0:T(8,128)S(1)} %collective-permute-done.4.refs_1_, bf16[6,512,256]{2,1,0:T(8,128)(2,1)S(1)} %get-tuple-element.28.refs_2_, f32[6,512,128]{2,1,0:T(8,128)S(1)} %get-tuple-element.38.refs_2_.refs_3_, ...), custom_call_target="tpu_custom_call" | custom-call | flops 1 | bytes 1 | tf_op jit(solution)/shard_map/pallas_call | solution.py:59
  40.5 0.0 copy-start.5
  40.5 0.1 collective-permute-start.10
  40.6 2.6 %collective-permute-start.11 = (f32[16,256]{1,0:T(8,128)S(1)}, f32[16,256]{1,0:T(8,128)S(1)}, u32[]{:S(2)}, u32[]{:S(2)}) collective-permute-start(f32[16,256]{1,0:T(8,128)S(1)} %shard_map.107.refs_6_.refs_8_), channel_id=1, source_target_pairs={{0,2},{1,3},{2,0},{3,1},{4,6},{5,7},{6,4},{7,5},{8,10},{9,11},{10,... | collective-permute-start | bytes 49160 | tf_op jit(solution)/shard_map/ppermute | solution.py:603
  43.2 1.3 %shard_map.109.refs_7_ = f32[3,256,128]{2,1,0:T(8,128)S(1)} custom-call(s32[1]{0:T(128)} %bitcast.refs_0_, f32[2,512,128]{2,1,0:T(8,128)S(1)} %collective-permute-done.4.refs_1_, bf16[6,512,256]{2,1,0:T(8,128)(2,1)S(1)} %get-tuple-element.28.refs_2_, f32[6,512,128]{2,1,0:T(8,128)S(1)} %get-tuple-element.38.refs_2_.refs_3_, ...), custom_call_target="tpu_custom_call" | custom-call | flops 1 | bytes 1 | tf_op jit(solution)/shard_map/pallas_call | solution.py:59
  44.5 0.8 %collective-permute-done.11.refs_9_ = f32[16,256]{1,0:T(8,128)S(1)} collective-permute-done((f32[16,256]{1,0:T(8,128)S(1)}, f32[16,256]{1,0:T(8,128)S(1)}, u32[]{:S(2)}, u32[]{:S(2)}) %collective-permute-start.11) | collective-permute-done | bytes 16416 | tf_op jit(solution)/shard_map/ppermute | solution.py:603
  45.3 0.0 collective-permute-done.10.refs_6_
  45.3 0.0 copy-done.5
  45.3 2.5 %shard_map.110 = (f32[256,1024]{1,0:T(8,128)}, f32[256,1536]{1,0:T(8,128)}) custom-call(s32[1]{0:T(128)} %bitcast.refs_0_, f32[2,512,128]{2,1,0:T(8,128)S(1)} %collective-permute-done.4.refs_1_, bf16[6,512,256]{2,1,0:T(8,128)(2,1)S(1)} %get-tuple-element.28.refs_2_, f32[6,512,128]{2,1,0:T(8,128)S(1)} %get-tuple-element.38.refs_2_.refs_3_, ...), custom_call_target="tpu_custom_call" | custom-call | flops 1 | bytes 1 | tf_op jit(solution)/shard_map/pallas_call | solution.py:59
  (7 shorter events, 0.2 us)
Async XLA Ops:
  0.6 1.5 %copy-start.2 = (f32[256,1024]{1,0:T(8,128)S(1)}, f32[256,1024]{1,0:T(8,128)}, u32[]{:S(2)}) copy-start(f32[256,1024]{1,0:T(8,128)} %refs_2_.3) | copy-start | bytes 3145732
  0.6 1.8 %copy-start.1 = (f32[256,1024]{1,0:T(8,128)S(1)}, f32[256,1024]{1,0:T(8,128)}, u32[]{:S(2)}) copy-start(f32[256,1024]{1,0:T(8,128)} %refs_1_.4) | copy-start | bytes 3145732
  0.7 1.8 %copy-start.4 = (f32[8,256]{1,0:T(8,128)S(1)}, f32[8,256]{1,0:T(8,128)}, u32[]{:S(2)}) copy-start(f32[8,256]{1,0:T(8,128)} %refs_0_.2) | copy-start | bytes 24580
  2.0 1.6 %copy-start = (f32[256,1536]{1,0:T(8,128)S(1)}, f32[256,1536]{1,0:T(8,128)}, u32[]{:S(2)}) copy-start(f32[256,1536]{1,0:T(8,128)} %refs_1_.5) | copy-start | bytes 4718596
  2.0 1.6 %collective-permute-start = (f32[2,256,128]{2,1,0:T(8,128)S(1)}, f32[2,256,128]{2,1,0:T(8,128)S(1)}, u32[]{:S(2)}, u32[]{:S(2)}) collective-permute-start(f32[2,256,128]{2,1,0:T(8,128)S(1)} %pad_maximum_fusion.1), channel_id=1, source_target_pairs={{0,4},{4,0},{8,12},{12,8},{16,20},{20,16},{24,28},{28,24},{1,5},{5... | collective-permute-start | bytes 786440 | tf_op jit(solution)/shard_map/ppermute | solution.py:581
  3.3 2.1 %collective-permute-start.3 = (f32[2,520,128]{2,1,0:T(8,128)S(1)}, f32[2,520,128]{2,1,0:T(8,128)S(1)}, u32[]{:S(2)}, u32[]{:S(2)}) collective-permute-start(f32[2,520,128]{2,1,0:T(8,128)S(1)} %get-tuple-element.25.refs_1_), channel_id=1, source_target_pairs={{0,4},{4,0},{8,12},{12,8},{16,20},{20,16},{24,28},{28,24},{1,5},{5... | collective-permute-start | bytes 1597448 | tf_op jit(solution)/shard_map/ppermute | solution.py:581
  3.7 2.4 %copy-start.3 = (f32[256,1024]{1,0:T(8,128)S(1)}, f32[256,1024]{1,0:T(8,128)}, u32[]{:S(2)}) copy-start(f32[256,1024]{1,0:T(8,128)} %refs_0_.3) | copy-start | bytes 3145732
  3.8 4.1 %collective-permute-start.2 = (f32[6,256,128]{2,1,0:T(8,128)S(1)}, f32[6,256,128]{2,1,0:T(8,128)S(1)}, u32[]{:S(2)}, u32[]{:S(2)}) collective-permute-start(f32[6,256,128]{2,1,0:T(8,128)S(1)} %get-tuple-element.24.refs_3_), channel_id=1, source_target_pairs={{0,4},{4,0},{8,12},{12,8},{16,20},{20,16},{24,28},{28,24},{1,5},{5... | collective-permute-start | bytes 2359304 | tf_op jit(solution)/shard_map/ppermute | solution.py:581
  4.1 16.6 %collective-permute-start.1 = (f32[2,512,128]{2,1,0:T(8,128)S(1)}, f32[2,512,128]{2,1,0:T(8,128)S(1)}, u32[]{:S(2)}, u32[]{:S(2)}) collective-permute-start(f32[2,512,128]{2,1,0:T(8,128)S(1)} %get-tuple-element.23.refs_0_.refs_3_.refs_1_), channel_id=1, source_target_pairs={{0,16},{4,20},{8,24},{12,28},{1,17},{5,21},{9,25},{13,29},{2,18},{... | collective-permute-start | bytes 1572872 | tf_op jit(solution)/shard_map/ppermute | solution.py:590
  5.5 8.7 %collective-permute-start.6 = (f32[520,128]{1,0:T(8,128)S(1)}, f32[520,128]{1,0:T(8,128)S(1)}, u32[]{:S(2)}, u32[]{:S(2)}) collective-permute-start(f32[520,128]{1,0:T(8,128)S(1)} %shard_map.97.refs_4_.refs_1_), channel_id=1, source_target_pairs={{8,0},{12,4},{0,8},{4,12},{24,16},{28,20},{16,24},{20,28},{9,1},{1... | collective-permute-start | bytes 798728 | tf_op jit(solution)/shard_map/ppermute | solution.py:590
  14.2 12.3 %collective-permute-start.7 = (f32[520,128]{1,0:T(8,128)S(1)}, f32[520,128]{1,0:T(8,128)S(1)}, u32[]{:S(2)}, u32[]{:S(2)}) collective-permute-start(f32[520,128]{1,0:T(8,128)S(1)} %get-tuple-element.36.refs_1_), channel_id=1, source_target_pairs={{0,16},{4,20},{8,24},{12,28},{1,17},{5,21},{9,25},{13,29},{2,18},{... | collective-permute-start | bytes 798728 | tf_op jit(solution)/shard_map/ppermute | solution.py:590
  15.5 16.7 %collective-permute-start.5 = (f32[2,512,128]{2,1,0:T(8,128)S(1)}, f32[2,512,128]{2,1,0:T(8,128)S(1)}, u32[]{:S(2)}, u32[]{:S(2)}) collective-permute-start(f32[2,512,128]{2,1,0:T(8,128)S(1)} %shard_map.99.refs_4_), channel_id=1, source_target_pairs={{0,8},{4,12},{16,24},{20,28},{1,9},{5,13},{17,25},{21,29},{2,10},{... | collective-permute-start | bytes 1572872 | tf_op jit(solution)/shard_map/ppermute | solution.py:590
  20.8 17.4 %collective-permute-start.4 = (f32[2,512,128]{2,1,0:T(8,128)S(1)}, f32[2,512,128]{2,1,0:T(8,128)S(1)}, u32[]{:S(2)}, u32[]{:S(2)}) collective-permute-start(f32[2,512,128]{2,1,0:T(8,128)S(1)} %shard_map.101.refs_7_), channel_id=1, source_target_pairs={{0,24},{8,16},{20,28},{28,20},{1,25},{9,17},{21,29},{29,21},{2,26}... | collective-permute-start | bytes 1572872 | tf_op jit(solution)/shard_map/ppermute | solution.py:626
  26.6 1.6 %collective-permute-start.8 = (f32[520,128]{1,0:T(8,128)S(1)}, f32[520,128]{1,0:T(8,128)S(1)}, u32[]{:S(2)}, u32[]{:S(2)}) collective-permute-start(f32[520,128]{1,0:T(8,128)S(1)} %shard_map.104.refs_4_), channel_id=1, source_target_pairs={{0,4},{4,0},{8,12},{12,8},{16,20},{20,16},{24,28},{28,24},{1,5},{5... | collective-permute-start | bytes 798728 | tf_op jit(solution)/shard_map/ppermute | solution.py:581
  29.2 7.7 %collective-permute-start.9 = (f32[16,256]{1,0:T(8,128)S(1)}, f32[16,256]{1,0:T(8,128)S(1)}, u32[]{:S(2)}, u32[]{:S(2)}) collective-permute-start(f32[16,256]{1,0:T(8,128)S(1)} %get-tuple-element.37.refs_6_.refs_0_), channel_id=1, source_target_pairs={{0,1},{1,0},{2,3},{3,2},{4,5},{5,4},{6,7},{7,6},{8,9},{9,8},{10,11... | collective-permute-start | bytes 49160 | tf_op jit(solution)/shard_map/ppermute | solution.py:603
  40.5 4.8 %copy-start.5 = (f32[1024]{0:T(1024)S(1)}, f32[1024]{0:T(1024)}, u32[]{:S(2)}) copy-start(f32[1024]{0:T(1024)} %param.12) | copy-start | bytes 12292
  40.5 4.8 %collective-permute-start.10 = (f32[6,256,128]{2,1,0:T(8,128)S(1)}, f32[6,256,128]{2,1,0:T(8,128)S(1)}, u32[]{:S(2)}, u32[]{:S(2)}) collective-permute-start(f32[6,256,128]{2,1,0:T(8,128)S(1)} %shard_map.108.refs_6_), channel_id=1, source_target_pairs={{0,4},{4,0},{8,12},{12,8},{16,20},{20,16},{24,28},{28,24},{1,5},{5... | collective-permute-start | bytes 2359304 | tf_op jit(solution)/shard_map/ppermute | solution.py:581
  40.6 4.7 %collective-permute-start.11 = (f32[16,256]{1,0:T(8,128)S(1)}, f32[16,256]{1,0:T(8,128)S(1)}, u32[]{:S(2)}, u32[]{:S(2)}) collective-permute-start(f32[16,256]{1,0:T(8,128)S(1)} %shard_map.107.refs_6_.refs_8_), channel_id=1, source_target_pairs={{0,2},{1,3},{2,0},{3,1},{4,6},{5,7},{6,4},{7,5},{8,10},{9,11},{10,... | collective-permute-start | bytes 49160 | tf_op jit(solution)/shard_map/ppermute | solution.py:603

commit v7 on v6

--- a/solution.py
+++ b/solution.py
@@ -627,29 +627,29 @@
     for bit in range(bits):
         last = bit == bits - 1
         theirs = across(total, 1 << bit, lambda c, e: not last or c ^ (1 << bit) < c)
-        prefix, total = turn(me_flag, bit, total, theirs, prefix, last, [token])
+        prefix, total = turn(me_flag, bit, total, theirs, prefix, last, [token] + ([arrived[1]] if square and last else []))
         distance = 2 if square else bit + 1
         if not (square and last):
             carried = stage(distance, carried, [prefix, relay] if square else [prefix], 4)
             token = carried[0]
     prefix_other = swap(prefix)
+    for distance in [1] if square else range(bits + 1, chips - 1):
+        carried = stage(distance, carried, [prefix], 4)
     linear, energy = linear_blocks(
-        me_flag, terms, inside, sums, prefix, prefix_other, others, []
+        me_flag, terms, inside, sums, prefix, prefix_other, others, [carried[0]]
     )
     energies, step = [], 1
     while step < heads:
         energies.append(step)
         step *= 2
     other = exchanged(energy, energies[0])
-    for distance in [1] if square else range(bits + 1, chips - 1):
-        carried = stage(distance, carried, [energy])
-    for step in energies[1:]:
-        energy = plus(energy, other, [carried[0]])
-        other = exchanged(energy, step)
-
     operands = [arrived[chips - 1], q_terms, *carried]
     group = q_terms.shape[0]
     theirs = last_stage(me_flag, chips - 1, "other", range(group), operands, [energy])
+    for step in energies[1:]:
+        energy = plus(energy, other, [theirs])
+        other = exchanged(energy, step)
+
     done = last_stage(me_flag, chips - 1, "own", range(group // 2), operands, [theirs])
     columns = q_lin.shape[1] * heads
     more = [swap(theirs), done, energy, other, lin_gain.reshape(1, -1), linear]

time: 48.2 us -> 46.6 us (0.967)
  waiting for transfers between devices: 12.4 us -> 10.8 us
    ppermute x2, waiting for transfers between devices: 0.75 us -> 2.9 us  [exchanged(): return lax.ppermute(array, 'head', [(i, i ^ step) for i in range(heads)])]
    ppermute x5, waiting for transfers between devices: 1.54 us -> 0.01 us  [swap(): return lax.ppermute(array, 'ctx', swap_pairs)]
    ppermute x4, waiting for transfers between devices: 8.84 us -> 7.37 us  [across(): return lax.ppermute(array, 'ctx', pairs)]
    ppermute x1, waiting for transfers between devices: 1.3 us -> 0.55 us  [body(): arrived[3] = lax.ppermute(relay, 'ctx', [(0, 6), (2, 4), (5, 7), (7, 5)])]
  transfers between devices with their start and end apart: 12 -> 12, of which waited for: 6 -> 5; matrix products, arithmetic and copies ran while one was open for 0% -> 0% of each run, Pallas kernels for 36% -> 37%
where the time goes in v7:
time: 46.6 us; the launch traced here: 46.3 us
  Pallas kernels  21.9 us (47%)
  starting transfers between devices  10.8 us (23%)
  waiting for transfers between devices  10.8 us (23%)
  other arithmetic  1.31 us (3%)
  between operations  1.05 us (2%)
    pallas_call x16, Pallas kernels, call(): return lambda *operands: made(*operands, *after)  21.9 us
    ppermute x4, waiting for transfers between devices, across(): return lax.ppermute(array, 'ctx', pairs)  7.37 us
    ppermute x4, starting transfers between devices, across(): return lax.ppermute(array, 'ctx', pairs)  4.46 us
    ppermute x2, starting transfers between devices, exchanged(): return lax.ppermute(array, 'head', [(i, i ^ step) for i in range(heads)])  4.24 us
    ppermute x2, waiting for transfers between devices, exchanged(): return lax.ppermute(array, 'head', [(i, i ^ step) for i in range(heads)])  2.9 us
    another operation x2, other arithmetic, halves(): jnp.stack([jnp.where(core == 0, b, a) for a, b in zip(early, late)])  1.3 us
    ppermute x1, starting transfers between devices, body(): arrived[3] = lax.ppermute(relay, 'ctx', [(0, 6), (2, 4), (5, 7), (7, 5)])  1.29 us
  transfers between devices with their start and end apart: 12, of which 5 were waited for; matrix products, arithmetic and copies ran while one was open for 0% of the time, Pallas kernels for 37%

profile of v7, /device:TPU:6, one launch (start us, length us, event | category | flops | bytes accessed | tf_op | source)
XLA Modules:
  0.0 46.3 jit_solution(13417249233446102891)
XLA Ops:
  0.6 0.0 copy-start.2
  0.6 0.0 copy-start.1
  0.7 0.0 copy-start.4
  0.7 1.3 %select_bitcast_fusion = (f32[1,256,128]{2,1,0:T(8,128)S(1)}, f32[1,256,128]{2,1,0:T(8,128)S(1)}, f32[1,256,128]{2,1,0:T(8,128)S(1)}, f32[1,256,128]{2,1,0:T(8,128)S(1)}) fusion(f32[256,256]{1,0:T(8,128)} %param.15, pred[]{:T(512)S(6)} %eq.2, f32[256,256]{1,0:T(8,128)} %param.14), kind=kLoop, calls=%fused_computation.2 | loop fusion | flops 131072 | bytes 1048577 | tf_op jit(solution)/shard_map/stack | solution.py:255
  2.0 0.0 copy-start
  2.0 0.1 collective-permute-start
  2.1 0.0 copy-done.2
  2.1 0.3 copy-done.1
  2.4 0.0 copy-done.4
  2.4 0.9 %shard_map.95 = (f32[2,520,128]{2,1,0:T(8,128)S(1)}, f32[8,256]{1,0:T(8,128)S(1)}) custom-call(f32[8,256]{1,0:T(8,128)S(1)} %copy-done.4, f32[256,1024]{1,0:T(8,128)S(1)} %copy-done.1, f32[256,1024]{1,0:T(8,128)S(1)} %copy-done.2, f32[2,256,128]{2,1,0:T(8,128)S(1)} %pad_maximum_fusion.refs_3_.refs_1_), custom_call_target="tpu_custom_call" | custom-call | flops 1 | bytes 1 | tf_op jit(solution)/shard_map/pallas_call | solution.py:59
  3.3 0.3 collective-permute-start.3
  3.6 0.0 collective-permute-done.refs_2_
  3.6 0.0 copy-done
  3.6 0.1 shard_map.96
  3.7 0.0 copy-start.3
  3.8 0.4 collective-permute-start.2
  4.1 1.3 %collective-permute-start.1 = (f32[2,512,128]{2,1,0:T(8,128)S(1)}, f32[2,512,128]{2,1,0:T(8,128)S(1)}, u32[]{:S(2)}, u32[]{:S(2)}) collective-permute-start(f32[2,512,128]{2,1,0:T(8,128)S(1)} %get-tuple-element.23.refs_0_.refs_3_.refs_1_), channel_id=1, source_target_pairs={{0,16},{4,20},{8,24},{12,28},{1,17},{5,21},{9,25},{13,29},{2,18},{... | collective-permute-start | bytes 1572872 | tf_op jit(solution)/shard_map/ppermute | solution.py:590
  5.4 0.0 collective-permute-done.3.refs_2_.refs_6_
  5.5 0.6 %collective-permute-start.6 = (f32[520,128]{1,0:T(8,128)S(1)}, f32[520,128]{1,0:T(8,128)S(1)}, u32[]{:S(2)}, u32[]{:S(2)}) collective-permute-start(f32[520,128]{1,0:T(8,128)S(1)} %shard_map.97.refs_4_.refs_1_), channel_id=1, source_target_pairs={{8,0},{12,4},{0,8},{4,12},{24,16},{28,20},{16,24},{20,28},{9,1},{1... | collective-permute-start | bytes 798728 | tf_op jit(solution)/shard_map/ppermute | solution.py:590
  6.1 0.0 copy-done.3
  6.1 1.7 %shard_map.98 = (f32[8,256,128]{2,1,0:T(8,128)S(1)}, bf16[8,256,256]{2,1,0:T(8,128)(2,1)S(1)}) custom-call(f32[256,1024]{1,0:T(8,128)S(1)} %copy-done.3, f32[256,1024]{1,0:T(8,128)S(1)} %copy-done.1, f32[256,1024]{1,0:T(8,128)S(1)} %copy-done.2, f32[8,256]{1,0:T(8,128)S(1)} %get-tuple-element.22.refs_4_.refs_3_, f32[520,128]{1,0:T(8,128)S(1)} %shard_map.97.refs_4_.refs_1_), custom_call_target="tpu_custom_call" | custom-call | flops 1 | bytes 1 | tf_op jit(solution)/shard_map/pallas_call | solution.py:59
  7.9 1.3 %collective-permute-start.5 = (f32[2,512,128]{2,1,0:T(8,128)S(1)}, f32[2,512,128]{2,1,0:T(8,128)S(1)}, u32[]{:S(2)}, u32[]{:S(2)}) collective-permute-start(f32[2,512,128]{2,1,0:T(8,128)S(1)} %shard_map.99.refs_4_), channel_id=1, source_target_pairs={{0,8},{4,12},{16,24},{20,28},{1,9},{5,13},{17,25},{21,29},{2,10},{... | collective-permute-start | bytes 1572872 | tf_op jit(solution)/shard_map/ppermute | solution.py:590
  9.2 0.0 collective-permute-done.2.refs_2_
  9.2 2.9 %shard_map.100 = (bf16[6,512,256]{2,1,0:T(8,128)(2,1)S(1)}, f32[6,512,128]{2,1,0:T(8,128)S(1)}, f32[6,512,128]{2,1,0:T(8,128)S(1)}, f32[6,512,128]{2,1,0:T(8,128)S(1)}) custom-call(s32[1]{0:T(128)} %bitcast.refs_0_, f32[256,1536]{1,0:T(8,128)S(1)} %copy-done, f32[6,256,128]{2,1,0:T(8,128)S(1)} %collective-permute-done.2.refs_2_, ...), custom_call_target="tpu_custom_call" | custom-call | flops 1 | bytes 1 | tf_op jit(solution)/shard_map/pallas_call | solution.py:59
  12.0 2.7 %collective-permute-done.6.refs_2_ = f32[520,128]{1,0:T(8,128)S(1)} collective-permute-done((f32[520,128]{1,0:T(8,128)S(1)}, f32[520,128]{1,0:T(8,128)S(1)}, u32[]{:S(2)}, u32[]{:S(2)}) %collective-permute-start.6) | collective-permute-done | bytes 266272 | tf_op jit(solution)/shard_map/ppermute | solution.py:590
  14.8 0.1 shard_map.102
  14.8 1.3 %collective-permute-start.7 = (f32[520,128]{1,0:T(8,128)S(1)}, f32[520,128]{1,0:T(8,128)S(1)}, u32[]{:S(2)}, u32[]{:S(2)}) collective-permute-start(f32[520,128]{1,0:T(8,128)S(1)} %get-tuple-element.35.refs_1_), channel_id=1, source_target_pairs={{0,16},{4,20},{8,24},{12,28},{1,17},{5,21},{9,25},{13,29},{2,18},{... | collective-permute-start | bytes 798728 | tf_op jit(solution)/shard_map/ppermute | solution.py:590
  16.1 4.6 %collective-permute-done.1.refs_2_.refs_1_ = f32[2,512,128]{2,1,0:T(8,128)S(1)} collective-permute-done((f32[2,512,128]{2,1,0:T(8,128)S(1)}, f32[2,512,128]{2,1,0:T(8,128)S(1)}, u32[]{:S(2)}, u32[]{:S(2)}) %collective-permute-start.1) | collective-permute-done | bytes 524320 | tf_op jit(solution)/shard_map/ppermute | solution.py:590
  20.8 1.3 %collective-permute-start.4 = (f32[2,512,128]{2,1,0:T(8,128)S(1)}, f32[2,512,128]{2,1,0:T(8,128)S(1)}, u32[]{:S(2)}, u32[]{:S(2)}) collective-permute-start(f32[2,512,128]{2,1,0:T(8,128)S(1)} %shard_map.101.refs_7_), channel_id=1, source_target_pairs={{0,24},{8,16},{20,28},{28,20},{1,25},{9,17},{21,29},{29,21},{2,26}... | collective-permute-start | bytes 1572872 | tf_op jit(solution)/shard_map/ppermute | solution.py:626
  22.1 4.4 %shard_map.103 = (f32[6,512,128]{2,1,0:T(8,128)S(1)}, f32[6,512,128]{2,1,0:T(8,128)S(1)}, f32[6,512,128]{2,1,0:T(8,128)S(1)}) custom-call(s32[1]{0:T(128)} %bitcast.refs_0_, f32[2,512,128]{2,1,0:T(8,128)S(1)} %collective-permute-done.1.refs_2_.refs_1_, ...), custom_call_target="tpu_custom_call", output_to_operand_aliasing={{0}: (3, {}), {1}: (4, {}), {2}: (5, {})} | custom-call | flops 1 | bytes 1 | tf_op jit(solution)/shard_map/pallas_call | solution.py:59
  26.5 0.0 collective-permute-done.5.refs_5_.refs_1_
  26.5 0.0 collective-permute-done.7.refs_2_
  26.6 0.1 collective-permute-start.8
  26.7 4.6 %shard_map.105 = (f32[6,512,128]{2,1,0:T(8,128)S(1)}, f32[6,512,128]{2,1,0:T(8,128)S(1)}, f32[6,512,128]{2,1,0:T(8,128)S(1)}) custom-call(s32[1]{0:T(128)} %bitcast.refs_0_, f32[2,512,128]{2,1,0:T(8,128)S(1)} %collective-permute-done.5.refs_5_.refs_1_, ...), custom_call_target="tpu_custom_call", output_to_operand_aliasing={{0}: (3, {}), {1}: (4, {}), {2}: (5, {})} | custom-call | flops 1 | bytes 1 | tf_op jit(solution)/shard_map/pallas_call | solution.py:59
  31.3 0.0 collective-permute-done.8.refs_5_
  31.3 1.0 %shard_map.106 = (f32[8,256,128]{2,1,0:T(8,128)S(1)}, f32[16,256]{1,0:T(8,128)S(1)}) custom-call(s32[1]{0:T(128)} %bitcast.refs_0_, bf16[8,256,256]{2,1,0:T(8,128)(2,1)S(1)} %get-tuple-element.39.refs_1_, f32[8,256,128]{2,1,0:T(8,128)S(1)} %get-tuple-element.26.refs_1_.refs_2_, f32[8,256]{1,0:T(8,128)S(1)} %get-tuple-element.22.refs_4_.refs_3_, ...), custom_call_target="tpu_custom_call" | custom-call | flops 1 | bytes 1 | tf_op jit(solution)/shard_map/pallas_call | solution.py:59
  32.3 0.6 %collective-permute-done.4.refs_1_ = f32[2,512,128]{2,1,0:T(8,128)S(1)} collective-permute-done((f32[2,512,128]{2,1,0:T(8,128)S(1)}, f32[2,512,128]{2,1,0:T(8,128)S(1)}, u32[]{:S(2)}, u32[]{:S(2)}) %collective-permute-start.4) | collective-permute-done | bytes 524320 | tf_op jit(solution)/shard_map/ppermute | solution.py:626
  32.9 2.3 %shard_map.107.refs_6_.refs_2_ = f32[6,256,128]{2,1,0:T(8,128)S(1)} custom-call(s32[1]{0:T(128)} %bitcast.refs_0_, f32[2,512,128]{2,1,0:T(8,128)S(1)} %collective-permute-done.4.refs_1_, bf16[6,512,256]{2,1,0:T(8,128)(2,1)S(1)} %get-tuple-element.28.refs_2_, f32[6,512,128]{2,1,0:T(8,128)S(1)} %get-tuple-element.36.refs_7_.refs_3_, ...), custom_call_target="tpu_custom_call" | custom-call | flops 1 | bytes 1 | tf_op jit(solution)/shard_map/pallas_call | solution.py:59
  35.1 0.1 collective-permute-start.9
  35.2 1.6 %collective-permute-start.10 = (f32[16,256]{1,0:T(8,128)S(1)}, f32[16,256]{1,0:T(8,128)S(1)}, u32[]{:S(2)}, u32[]{:S(2)}) collective-permute-start(f32[16,256]{1,0:T(8,128)S(1)} %get-tuple-element.40.refs_6_.refs_0_), channel_id=1, source_target_pairs={{0,1},{1,0},{2,3},{3,2},{4,5},{5,4},{6,7},{7,6},{8,9},{9,8},{10,11... | collective-permute-start | bytes 49160 | tf_op jit(solution)/shard_map/ppermute | solution.py:603
  36.9 2.2 %collective-permute-done.10.refs_1_ = f32[16,256]{1,0:T(8,128)S(1)} collective-permute-done((f32[16,256]{1,0:T(8,128)S(1)}, f32[16,256]{1,0:T(8,128)S(1)}, u32[]{:S(2)}, u32[]{:S(2)}) %collective-permute-start.10) | collective-permute-done | bytes 16416 | tf_op jit(solution)/shard_map/ppermute | solution.py:603
  39.0 0.0 copy-start.5
  39.0 2.6 %collective-permute-start.11 = (f32[16,256]{1,0:T(8,128)S(1)}, f32[16,256]{1,0:T(8,128)S(1)}, u32[]{:S(2)}, u32[]{:S(2)}) collective-permute-start(f32[16,256]{1,0:T(8,128)S(1)} %shard_map.109.refs_8_), channel_id=1, source_target_pairs={{0,2},{1,3},{2,0},{3,1},{4,6},{5,7},{6,4},{7,5},{8,10},{9,11},{10,... | collective-permute-start | bytes 49160 | tf_op jit(solution)/shard_map/ppermute | solution.py:603
  41.6 1.3 %shard_map.108.refs_7_ = f32[3,256,128]{2,1,0:T(8,128)S(1)} custom-call(s32[1]{0:T(128)} %bitcast.refs_0_, f32[2,512,128]{2,1,0:T(8,128)S(1)} %collective-permute-done.4.refs_1_, bf16[6,512,256]{2,1,0:T(8,128)(2,1)S(1)} %get-tuple-element.28.refs_2_, f32[6,512,128]{2,1,0:T(8,128)S(1)} %get-tuple-element.36.refs_7_.refs_3_, ...), custom_call_target="tpu_custom_call" | custom-call | flops 1 | bytes 1 | tf_op jit(solution)/shard_map/pallas_call | solution.py:59
  42.9 0.7 %collective-permute-done.11.refs_9_ = f32[16,256]{1,0:T(8,128)S(1)} collective-permute-done((f32[16,256]{1,0:T(8,128)S(1)}, f32[16,256]{1,0:T(8,128)S(1)}, u32[]{:S(2)}, u32[]{:S(2)}) %collective-permute-start.11) | collective-permute-done | bytes 16416 | tf_op jit(solution)/shard_map/ppermute | solution.py:603
  43.7 0.0 collective-permute-done.9.refs_6_
  43.7 0.0 copy-done.5
  43.7 2.5 %shard_map.110 = (f32[256,1024]{1,0:T(8,128)}, f32[256,1536]{1,0:T(8,128)}) custom-call(s32[1]{0:T(128)} %bitcast.refs_0_, f32[2,512,128]{2,1,0:T(8,128)S(1)} %collective-permute-done.4.refs_1_, bf16[6,512,256]{2,1,0:T(8,128)(2,1)S(1)} %get-tuple-element.28.refs_2_, f32[6,512,128]{2,1,0:T(8,128)S(1)} %get-tuple-element.36.refs_7_.refs_3_, ...), custom_call_target="tpu_custom_call" | custom-call | flops 1 | bytes 1 | tf_op jit(solution)/shard_map/pallas_call | solution.py:59
  (7 shorter events, 0.2 us)
Async XLA Ops:
  0.6 1.5 %copy-start.2 = (f32[256,1024]{1,0:T(8,128)S(1)}, f32[256,1024]{1,0:T(8,128)}, u32[]{:S(2)}) copy-start(f32[256,1024]{1,0:T(8,128)} %refs_2_.3) | copy-start | bytes 3145732
  0.6 1.8 %copy-start.1 = (f32[256,1024]{1,0:T(8,128)S(1)}, f32[256,1024]{1,0:T(8,128)}, u32[]{:S(2)}) copy-start(f32[256,1024]{1,0:T(8,128)} %refs_1_.4) | copy-start | bytes 3145732
  0.7 1.8 %copy-start.4 = (f32[8,256]{1,0:T(8,128)S(1)}, f32[8,256]{1,0:T(8,128)}, u32[]{:S(2)}) copy-start(f32[8,256]{1,0:T(8,128)} %refs_0_.2) | copy-start | bytes 24580
  2.0 1.6 %copy-start = (f32[256,1536]{1,0:T(8,128)S(1)}, f32[256,1536]{1,0:T(8,128)}, u32[]{:S(2)}) copy-start(f32[256,1536]{1,0:T(8,128)} %refs_1_.5) | copy-start | bytes 4718596
  2.0 1.6 %collective-permute-start = (f32[2,256,128]{2,1,0:T(8,128)S(1)}, f32[2,256,128]{2,1,0:T(8,128)S(1)}, u32[]{:S(2)}, u32[]{:S(2)}) collective-permute-start(f32[2,256,128]{2,1,0:T(8,128)S(1)} %pad_maximum_fusion.1), channel_id=1, source_target_pairs={{0,4},{4,0},{8,12},{12,8},{16,20},{20,16},{24,28},{28,24},{1,5},{5... | collective-permute-start | bytes 786440 | tf_op jit(solution)/shard_map/ppermute | solution.py:581
  3.3 2.1 %collective-permute-start.3 = (f32[2,520,128]{2,1,0:T(8,128)S(1)}, f32[2,520,128]{2,1,0:T(8,128)S(1)}, u32[]{:S(2)}, u32[]{:S(2)}) collective-permute-start(f32[2,520,128]{2,1,0:T(8,128)S(1)} %get-tuple-element.25.refs_1_), channel_id=1, source_target_pairs={{0,4},{4,0},{8,12},{12,8},{16,20},{20,16},{24,28},{28,24},{1,5},{5... | collective-permute-start | bytes 1597448 | tf_op jit(solution)/shard_map/ppermute | solution.py:581
  3.7 2.4 %copy-start.3 = (f32[256,1024]{1,0:T(8,128)S(1)}, f32[256,1024]{1,0:T(8,128)}, u32[]{:S(2)}) copy-start(f32[256,1024]{1,0:T(8,128)} %refs_0_.3) | copy-start | bytes 3145732
  3.8 5.4 %collective-permute-start.2 = (f32[6,256,128]{2,1,0:T(8,128)S(1)}, f32[6,256,128]{2,1,0:T(8,128)S(1)}, u32[]{:S(2)}, u32[]{:S(2)}) collective-permute-start(f32[6,256,128]{2,1,0:T(8,128)S(1)} %get-tuple-element.24.refs_3_), channel_id=1, source_target_pairs={{0,4},{4,0},{8,12},{12,8},{16,20},{20,16},{24,28},{28,24},{1,5},{5... | collective-permute-start | bytes 2359304 | tf_op jit(solution)/shard_map/ppermute | solution.py:581
  4.1 16.6 %collective-permute-start.1 = (f32[2,512,128]{2,1,0:T(8,128)S(1)}, f32[2,512,128]{2,1,0:T(8,128)S(1)}, u32[]{:S(2)}, u32[]{:S(2)}) collective-permute-start(f32[2,512,128]{2,1,0:T(8,128)S(1)} %get-tuple-element.23.refs_0_.refs_3_.refs_1_), channel_id=1, source_target_pairs={{0,16},{4,20},{8,24},{12,28},{1,17},{5,21},{9,25},{13,29},{2,18},{... | collective-permute-start | bytes 1572872 | tf_op jit(solution)/shard_map/ppermute | solution.py:590
  5.5 9.3 %collective-permute-start.6 = (f32[520,128]{1,0:T(8,128)S(1)}, f32[520,128]{1,0:T(8,128)S(1)}, u32[]{:S(2)}, u32[]{:S(2)}) collective-permute-start(f32[520,128]{1,0:T(8,128)S(1)} %shard_map.97.refs_4_.refs_1_), channel_id=1, source_target_pairs={{8,0},{12,4},{0,8},{4,12},{24,16},{28,20},{16,24},{20,28},{9,1},{1... | collective-permute-start | bytes 798728 | tf_op jit(solution)/shard_map/ppermute | solution.py:590
  7.9 18.7 %collective-permute-start.5 = (f32[2,512,128]{2,1,0:T(8,128)S(1)}, f32[2,512,128]{2,1,0:T(8,128)S(1)}, u32[]{:S(2)}, u32[]{:S(2)}) collective-permute-start(f32[2,512,128]{2,1,0:T(8,128)S(1)} %shard_map.99.refs_4_), channel_id=1, source_target_pairs={{0,8},{4,12},{16,24},{20,28},{1,9},{5,13},{17,25},{21,29},{2,10},{... | collective-permute-start | bytes 1572872 | tf_op jit(solution)/shard_map/ppermute | solution.py:590
  14.8 11.7 %collective-permute-start.7 = (f32[520,128]{1,0:T(8,128)S(1)}, f32[520,128]{1,0:T(8,128)S(1)}, u32[]{:S(2)}, u32[]{:S(2)}) collective-permute-start(f32[520,128]{1,0:T(8,128)S(1)} %get-tuple-element.35.refs_1_), channel_id=1, source_target_pairs={{0,16},{4,20},{8,24},{12,28},{1,17},{5,21},{9,25},{13,29},{2,18},{... | collective-permute-start | bytes 798728 | tf_op jit(solution)/shard_map/ppermute | solution.py:590
  20.8 12.0 %collective-permute-start.4 = (f32[2,512,128]{2,1,0:T(8,128)S(1)}, f32[2,512,128]{2,1,0:T(8,128)S(1)}, u32[]{:S(2)}, u32[]{:S(2)}) collective-permute-start(f32[2,512,128]{2,1,0:T(8,128)S(1)} %shard_map.101.refs_7_), channel_id=1, source_target_pairs={{0,24},{8,16},{20,28},{28,20},{1,25},{9,17},{21,29},{29,21},{2,26}... | collective-permute-start | bytes 1572872 | tf_op jit(solution)/shard_map/ppermute | solution.py:626
  26.6 4.7 %collective-permute-start.8 = (f32[520,128]{1,0:T(8,128)S(1)}, f32[520,128]{1,0:T(8,128)S(1)}, u32[]{:S(2)}, u32[]{:S(2)}) collective-permute-start(f32[520,128]{1,0:T(8,128)S(1)} %shard_map.104.refs_6_.refs_4_), channel_id=1, source_target_pairs={{0,4},{4,0},{8,12},{12,8},{16,20},{20,16},{24,28},{28,24},{1,5},{5... | collective-permute-start | bytes 798728 | tf_op jit(solution)/shard_map/ppermute | solution.py:581
  35.1 8.5 %collective-permute-start.9 = (f32[6,256,128]{2,1,0:T(8,128)S(1)}, f32[6,256,128]{2,1,0:T(8,128)S(1)}, u32[]{:S(2)}, u32[]{:S(2)}) collective-permute-start(f32[6,256,128]{2,1,0:T(8,128)S(1)} %shard_map.107.refs_6_.refs_2_), channel_id=1, source_target_pairs={{0,4},{4,0},{8,12},{12,8},{16,20},{20,16},{24,28},{28,24},{1,5},{5... | collective-permute-start | bytes 2359304 | tf_op jit(solution)/shard_map/ppermute | solution.py:581
  35.2 3.8 %collective-permute-start.10 = (f32[16,256]{1,0:T(8,128)S(1)}, f32[16,256]{1,0:T(8,128)S(1)}, u32[]{:S(2)}, u32[]{:S(2)}) collective-permute-start(f32[16,256]{1,0:T(8,128)S(1)} %get-tuple-element.40.refs_6_.refs_0_), channel_id=1, source_target_pairs={{0,1},{1,0},{2,3},{3,2},{4,5},{5,4},{6,7},{7,6},{8,9},{9,8},{10,11... | collective-permute-start | bytes 49160 | tf_op jit(solution)/shard_map/ppermute | solution.py:603
  39.0 4.6 %copy-start.5 = (f32[1024]{0:T(1024)S(1)}, f32[1024]{0:T(1024)}, u32[]{:S(2)}) copy-start(f32[1024]{0:T(1024)} %param.12) | copy-start | bytes 12292
  39.0 4.6 %collective-permute-start.11 = (f32[16,256]{1,0:T(8,128)S(1)}, f32[16,256]{1,0:T(8,128)S(1)}, u32[]{:S(2)}, u32[]{:S(2)}) collective-permute-start(f32[16,256]{1,0:T(8,128)S(1)} %shard_map.109.refs_8_), channel_id=1, source_target_pairs={{0,2},{1,3},{2,0},{3,1},{4,6},{5,7},{6,4},{7,5},{8,10},{9,11},{10,... | collective-permute-start | bytes 49160 | tf_op jit(solution)/shard_map/ppermute | solution.py:603

commit v8 on v7

--- a/solution.py
+++ b/solution.py
@@ -207,7 +207,7 @@
 
 
 def linear_kernel(me_ref, terms_ref, inside_ref, sums_ref, mine_ref, theirs_ref, other_ref, out_ref, energy_ref):
-    heads, tokens, _ = out_ref.shape
+    heads, tokens, _ = inside_ref.shape
     half = heads // 2
     core = me_ref[0] & 1
     leading = jnp.exp(sums_ref[...]).T
@@ -223,7 +223,7 @@
             wide = dot(terms_ref[h, :, :HD], jnp.concatenate([high, low], axis=1))
             carried = wide[:, :HD] + wide[:, HD:] + dot(terms_ref[h, :, HD:], high)
             linear = inside_ref[h] + leading[:, h : h + 1] * carried
-            out_ref[h] = linear
+            out_ref[:, h * HD : (h + 1) * HD] = linear
             squares = squares + linear * linear
     energy_ref[...] = lax.dot_general(
         jnp.ones((energy_ref.shape[0], HD), F32),
@@ -235,13 +235,13 @@
 
 
 def linear_blocks(me, terms, inside, sums, mine, theirs, other, after):
-    _, tokens, _ = inside.shape
+    heads, tokens, _ = inside.shape
     return call(
         linear_kernel,
         [SMEM] + [VMEM] * 6,
         [VMEM] * 2,
         [
-            jax.ShapeDtypeStruct(inside.shape, F32),
+            jax.ShapeDtypeStruct((tokens, heads * HD), F32),
             jax.ShapeDtypeStruct((ENERGY_ROWS, tokens), F32),
         ],
         after=after,
@@ -388,13 +388,12 @@
     )(me, q_soft, q_other, kv)
 
 
-def later_kernel(distance, parts, me_ref, kv_ref, q_ref, acc_ref, peak_ref, total_ref, acc_out, peak_out, total_out, keys_ref, values_ref):
-    group, rows, _ = q_ref.shape
-    size = rows // parts
+def later_kernel(distance, parts, heads, me_ref, kv_ref, q_ref, acc_ref, peak_ref, total_ref, acc_out, peak_out, total_out, keys_ref, values_ref):
+    size = q_ref.shape[1] // parts
     chip = me_ref[0] >> 1
 
     def where(i):
-        return i // parts, slice(i % parts * size, (i % parts + 1) * size)
+        return heads[i // parts], slice(i % parts * size, (i % parts + 1) * size)
 
     def score(i):
         return dot(score_terms(q_ref[where(i)]), keys_ref[...])
@@ -415,12 +414,12 @@
     @pl.when(lax.bitwise_xor(chip, distance) < chip)
     def _():
         fill_terms(kv_ref, keys_ref, values_ref)
-        run(parts * group, score, soften, gather)
-
-
-def later_stage(me, distance, kv, q_terms, acc, peak, total, after, parts):
-    return call(
-        functools.partial(later_kernel, distance, parts),
+        run(parts * len(heads), score, soften, gather)
+
+
+def later_stage(me, distance, heads, kv, q_terms, acc, peak, total, after, parts=4):
+    return call(
+        functools.partial(later_kernel, distance, parts, heads),
         [SMEM] + [VMEM] * 5,
         [VMEM] * 3,
         [jax.ShapeDtypeStruct(acc.shape, F32)] * 3,
@@ -443,29 +442,34 @@
     at = pl.ds(pl.multiple_of(side * tokens, tokens), tokens)
     copies = []
 
-    def copy_soft(source, whose, g):
-        to = pl.ds(pl.multiple_of((whose * group + g) * HD, HD), HD)
-        copies.append(pltpu.make_async_copy(source, soft_hbm.at[:, to], sems.at[len(copies)]))
+    def copy(source, target):
+        copies.append(pltpu.make_async_copy(source, target, sems.at[len(copies)]))
         return copies[-1]
 
+    def columns_of(whose, g, count):
+        return pl.ds(pl.multiple_of((whose * group + g) * HD, HD), count * HD)
+
     if columns is not None:
-        for g in range(group):
-            copy_soft(theirs_ref.at[g], 1 - core, g).start()
-        for g in range(done_ref.shape[0]):
-            copy_soft(done_ref.at[g], core, g).start()
+        blocks = [pl.ds(n * (tokens // 4), tokens // 4) for n in range(4)]
+        for block in blocks:
+            to = soft_hbm.at[block, columns_of(1 - core, 0, group)]
+            copy(theirs_ref.at[block], to).start()
         factor = lax.rsqrt((energy_ref[:8] + energy_other_ref[:8]) / columns + EPSILON)
         factor = factor.T[:, 0:1]
-        for h in range(linear_ref.shape[0]):
-            to = slice(h * HD, (h + 1) * HD)
-            lin_ref[h] = linear_ref[h] * factor * gain_ref[:, to]
-            copies.append(
-                pltpu.make_async_copy(lin_ref.at[h], lin_hbm.at[:, to], sems.at[len(copies)])
-            )
-            copies[-1].start()
-        own_copies = [copy_soft(out_ref.at[n], core, g) for n, g in enumerate(heads)]
+        for n, block in enumerate(blocks):
+            rows = slice(n * (tokens // 4), (n + 1) * (tokens // 4))
+            lin_ref[rows] = linear_ref[rows] * factor[rows] * gain_ref[...]
+            copy(lin_ref.at[block], lin_hbm.at[block]).start()
+        for block in blocks:
+            to = soft_hbm.at[block, columns_of(core, 0, group - len(heads))]
+            copy(done_ref.at[block], to).start()
+        own_copies = [
+            copy(out_ref.at[:, pl.ds(n * HD, HD)], soft_hbm.at[:, columns_of(core, g, 1)])
+            for n, g in enumerate(heads)
+        ]
 
     def finish(n, acc, total):
-        out_ref[n] = acc / jnp.sum(total, axis=1, keepdims=True)
+        out_ref[:, n * HD : (n + 1) * HD] = acc / jnp.sum(total, axis=1, keepdims=True)
         if columns is not None:
             own_copies[n].start()
 
@@ -495,29 +499,29 @@
         for n, g in enumerate(heads):
             finish(n, acc_ref[g, at], total_ref[g, at])
 
-    for copy in copies:
-        copy.wait()
+    for each in copies:
+        each.wait()
 
 
 def last_stage(me, distance, whose, heads, operands, after, extra=None):
     group, rows, _ = operands[1].shape
     tokens = rows // 2
-    part = jax.ShapeDtypeStruct((len(heads), tokens, HD), F32)
+    part = jax.ShapeDtypeStruct((tokens, len(heads) * HD), F32)
     scratch = term_scratch(operands[0].shape[1])
     out_shape, out_spec, columns = part, VMEM, None
     if extra is not None:
         columns, more = extra
         operands = [*operands, *more]
-        count = more[-1].shape[0]
+        linear = more[-1]
         out_shape = [
-            jax.ShapeDtypeStruct((tokens, count * HD), F32),
+            jax.ShapeDtypeStruct(linear.shape, F32),
             jax.ShapeDtypeStruct((tokens, 2 * group * HD), F32),
         ]
         out_spec = [HBM] * 2
         scratch = [
-            pltpu.VMEM((count, tokens, HD), F32),
+            pltpu.VMEM(linear.shape, F32),
             pltpu.VMEM(part.shape, F32),
-            pltpu.SemaphoreType.DMA((2 * group + count,)),
+            pltpu.SemaphoreType.DMA((12 + len(heads),)),
         ] + scratch
     return call(
         functools.partial(last_kernel, distance, whose, heads, columns),
@@ -605,9 +609,9 @@
     def sent(distance, array):
         return across(array, distance, lambda c, e: c ^ distance < c)
 
-    def stage(distance, carried, after, parts=2):
+    def stage(distance, heads, carried, after):
         return later_stage(
-            me_flag, distance, arrived[distance], q_terms, *carried, after, parts
+            me_flag, distance, heads, arrived[distance], q_terms, *carried, after
         )
 
     bits = chips.bit_length() - 1
@@ -620,6 +624,8 @@
         for distance in range(1, chips):
             arrived[distance] = sent(distance, kv)
     q_terms, *carried = own_stage(me_flag, q_soft, q_other, kv, [token])
+    group = q_terms.shape[0]
+    all_heads, front, back = range(group), range(group // 2), range(group // 2, group)
     token = carried[0]
     if square:
         relay = relayed(me_flag, kv, arrived[2], [token])
@@ -630,11 +636,13 @@
         prefix, total = turn(me_flag, bit, total, theirs, prefix, last, [token] + ([arrived[1]] if square and last else []))
         distance = 2 if square else bit + 1
         if not (square and last):
-            carried = stage(distance, carried, [prefix, relay] if square else [prefix], 4)
+            carried = stage(distance, all_heads, carried, [prefix, relay] if square else [prefix])
             token = carried[0]
     prefix_other = swap(prefix)
-    for distance in [1] if square else range(bits + 1, chips - 1):
-        carried = stage(distance, carried, [prefix], 4)
+    left = [1] if square else range(bits + 1, chips - 1)
+    for distance in left[:-1]:
+        carried = stage(distance, all_heads, carried, [prefix])
+    carried = stage(left[-1], front, carried, [prefix])
     linear, energy = linear_blocks(
         me_flag, terms, inside, sums, prefix, prefix_other, others, [carried[0]]
     )
@@ -643,20 +651,18 @@
         energies.append(step)
         step *= 2
     other = exchanged(energy, energies[0])
+    carried = stage(left[-1], back, carried, [energy])
     operands = [arrived[chips - 1], q_terms, *carried]
-    group = q_terms.shape[0]
-    theirs = last_stage(me_flag, chips - 1, "other", range(group), operands, [energy])
     for step in energies[1:]:
-        energy = plus(energy, other, [theirs])
+        energy = plus(energy, other, [carried[0]])
         other = exchanged(energy, step)
 
-    done = last_stage(me_flag, chips - 1, "own", range(group // 2), operands, [theirs])
+    theirs = last_stage(me_flag, chips - 1, "other", all_heads, operands, [energy])
+    done = last_stage(me_flag, chips - 1, "own", front, operands, [theirs])
     columns = q_lin.shape[1] * heads
     more = [swap(theirs), done, energy, other, lin_gain.reshape(1, -1), linear]
     return tuple(
-        last_stage(
-            me_flag, chips - 1, "own", range(group // 2, group), operands, [], (columns, more)
-        )
+        last_stage(me_flag, chips - 1, "own", back, operands, [], (columns, more))
     )
 
 

time: 46.6 us -> 44.3 us (0.951)
  waiting for transfers between devices: 10.8 us -> 8.13 us
    ppermute x2, waiting for transfers between devices: 2.9 us -> 0.75 us  [exchanged(): return lax.ppermute(array, 'head', [(i, i ^ step) for i in range(heads)])]
    ppermute x1, waiting for transfers between devices: 0.55 us -> 0.01 us  [body(): arrived[3] = lax.ppermute(relay, 'ctx', [(0, 6), (2, 4), (5, 7), (7, 5)])]
    pallas_call x16 -> x17, Pallas kernels: 21.9 us -> 22.3 us  [call(): return lambda *operands: made(*operands, *after)]
  transfers between devices with their start and end apart: 12 -> 12, of which waited for: 5 -> 3; matrix products, arithmetic and copies ran while one was open for 0% -> 0% of each run, Pallas kernels for 37% -> 40%
where the time goes in v8:
time: 44.3 us; the launch traced here: 44 us
  Pallas kernels  22.3 us (50%)
  starting transfers between devices  10.9 us (25%)
  waiting for transfers between devices  8.13 us (18%)
  other arithmetic  1.31 us (3%)
  between operations  1.08 us (2%)
    pallas_call x17, Pallas kernels, call(): return lambda *operands: made(*operands, *after)  22.3 us
    ppermute x4, waiting for transfers between devices, across(): return lax.ppermute(array, 'ctx', pairs)  7.36 us
    ppermute x4, starting transfers between devices, across(): return lax.ppermute(array, 'ctx', pairs)  4.46 us
    ppermute x2, starting transfers between devices, exchanged(): return lax.ppermute(array, 'head', [(i, i ^ step) for i in range(heads)])  4.24 us
    another operation x2, other arithmetic, halves(): jnp.stack([jnp.where(core == 0, b, a) for a, b in zip(early, late)])  1.3 us
    ppermute x1, starting transfers between devices, body(): arrived[3] = lax.ppermute(relay, 'ctx', [(0, 6), (2, 4), (5, 7), (7, 5)])  1.29 us
  transfers between devices with their start and end apart: 12, of which 3 were waited for; matrix products, arithmetic and copies ran while one was open for 0% of the time, Pallas kernels for 40%

profile of v8, /device:TPU:6, one launch (start us, length us, event | category | flops | bytes accessed | tf_op | source)
XLA Modules:
  0.0 44.0 jit_solution(1527235918644141113)
XLA Ops:
  0.6 0.0 copy-start.2
  0.6 0.0 copy-start.1
  0.7 0.0 copy-start.4
  0.7 1.3 %select_bitcast_fusion = (f32[1,256,128]{2,1,0:T(8,128)S(1)}, f32[1,256,128]{2,1,0:T(8,128)S(1)}, f32[1,256,128]{2,1,0:T(8,128)S(1)}, f32[1,256,128]{2,1,0:T(8,128)S(1)}) fusion(f32[256,256]{1,0:T(8,128)} %param.15, pred[]{:T(512)S(6)} %eq.2, f32[256,256]{1,0:T(8,128)} %param.14), kind=kLoop, calls=%fused_computation.2 | loop fusion | flops 131072 | bytes 1048577 | tf_op jit(solution)/shard_map/stack | solution.py:255
  2.0 0.0 copy-start
  2.0 0.1 collective-permute-start
  2.1 0.0 copy-done.2
  2.1 0.3 copy-done.1
  2.4 0.0 copy-done.4
  2.4 0.9 %shard_map.95 = (f32[2,520,128]{2,1,0:T(8,128)S(1)}, f32[8,256]{1,0:T(8,128)S(1)}) custom-call(f32[8,256]{1,0:T(8,128)S(1)} %copy-done.4, f32[256,1024]{1,0:T(8,128)S(1)} %copy-done.1, f32[256,1024]{1,0:T(8,128)S(1)} %copy-done.2, f32[2,256,128]{2,1,0:T(8,128)S(1)} %pad_maximum_fusion.refs_3_.refs_1_), custom_call_target="tpu_custom_call" | custom-call | flops 1 | bytes 1 | tf_op jit(solution)/shard_map/pallas_call | solution.py:59
  3.3 0.3 collective-permute-start.3
  3.6 0.0 collective-permute-done.refs_2_
  3.6 0.0 copy-done
  3.6 0.1 shard_map.96
  3.7 0.0 copy-start.3
  3.8 0.4 collective-permute-start.2
  4.1 1.3 %collective-permute-start.1 = (f32[2,512,128]{2,1,0:T(8,128)S(1)}, f32[2,512,128]{2,1,0:T(8,128)S(1)}, u32[]{:S(2)}, u32[]{:S(2)}) collective-permute-start(f32[2,512,128]{2,1,0:T(8,128)S(1)} %get-tuple-element.26.refs_0_.refs_3_.refs_1_), channel_id=1, source_target_pairs={{0,16},{4,20},{8,24},{12,28},{1,17},{5,21},{9,25},{13,29},{2,18},{... | collective-permute-start | bytes 1572872 | tf_op jit(solution)/shard_map/ppermute | solution.py:594
  5.4 0.0 collective-permute-done.3.refs_2_.refs_6_
  5.5 0.6 %collective-permute-start.6 = (f32[520,128]{1,0:T(8,128)S(1)}, f32[520,128]{1,0:T(8,128)S(1)}, u32[]{:S(2)}, u32[]{:S(2)}) collective-permute-start(f32[520,128]{1,0:T(8,128)S(1)} %shard_map.97.refs_4_.refs_1_), channel_id=1, source_target_pairs={{8,0},{12,4},{0,8},{4,12},{24,16},{28,20},{16,24},{20,28},{9,1},{1... | collective-permute-start | bytes 798728 | tf_op jit(solution)/shard_map/ppermute | solution.py:594
  6.1 0.0 copy-done.3
  6.1 1.7 %shard_map.98 = (f32[8,256,128]{2,1,0:T(8,128)S(1)}, bf16[8,256,256]{2,1,0:T(8,128)(2,1)S(1)}) custom-call(f32[256,1024]{1,0:T(8,128)S(1)} %copy-done.3, f32[256,1024]{1,0:T(8,128)S(1)} %copy-done.1, f32[256,1024]{1,0:T(8,128)S(1)} %copy-done.2, f32[8,256]{1,0:T(8,128)S(1)} %get-tuple-element.25.refs_4_.refs_3_, f32[520,128]{1,0:T(8,128)S(1)} %shard_map.97.refs_4_.refs_1_), custom_call_target="tpu_custom_call" | custom-call | flops 1 | bytes 1 | tf_op jit(solution)/shard_map/pallas_call | solution.py:59
  7.9 1.3 %collective-permute-start.5 = (f32[2,512,128]{2,1,0:T(8,128)S(1)}, f32[2,512,128]{2,1,0:T(8,128)S(1)}, u32[]{:S(2)}, u32[]{:S(2)}) collective-permute-start(f32[2,512,128]{2,1,0:T(8,128)S(1)} %shard_map.99.refs_4_), channel_id=1, source_target_pairs={{0,8},{4,12},{16,24},{20,28},{1,9},{5,13},{17,25},{21,29},{2,10},{... | collective-permute-start | bytes 1572872 | tf_op jit(solution)/shard_map/ppermute | solution.py:594
  9.2 0.0 collective-permute-done.2.refs_2_
  9.2 2.9 %shard_map.100 = (bf16[6,512,256]{2,1,0:T(8,128)(2,1)S(1)}, f32[6,512,128]{2,1,0:T(8,128)S(1)}, f32[6,512,128]{2,1,0:T(8,128)S(1)}, f32[6,512,128]{2,1,0:T(8,128)S(1)}) custom-call(s32[1]{0:T(128)} %bitcast.refs_0_, f32[256,1536]{1,0:T(8,128)S(1)} %copy-done, f32[6,256,128]{2,1,0:T(8,128)S(1)} %collective-permute-done.2.refs_2_, ...), custom_call_target="tpu_custom_call" | custom-call | flops 1 | bytes 1 | tf_op jit(solution)/shard_map/pallas_call | solution.py:59
  12.1 2.7 %collective-permute-done.6.refs_2_ = f32[520,128]{1,0:T(8,128)S(1)} collective-permute-done((f32[520,128]{1,0:T(8,128)S(1)}, f32[520,128]{1,0:T(8,128)S(1)}, u32[]{:S(2)}, u32[]{:S(2)}) %collective-permute-start.6) | collective-permute-done | bytes 266272 | tf_op jit(solution)/shard_map/ppermute | solution.py:594
  14.8 0.1 shard_map.102
  14.8 1.3 %collective-permute-start.7 = (f32[520,128]{1,0:T(8,128)S(1)}, f32[520,128]{1,0:T(8,128)S(1)}, u32[]{:S(2)}, u32[]{:S(2)}) collective-permute-start(f32[520,128]{1,0:T(8,128)S(1)} %get-tuple-element.38.refs_1_), channel_id=1, source_target_pairs={{0,16},{4,20},{8,24},{12,28},{1,17},{5,21},{9,25},{13,29},{2,18},{... | collective-permute-start | bytes 798728 | tf_op jit(solution)/shard_map/ppermute | solution.py:594
  16.1 4.6 %collective-permute-done.1.refs_2_.refs_1_ = f32[2,512,128]{2,1,0:T(8,128)S(1)} collective-permute-done((f32[2,512,128]{2,1,0:T(8,128)S(1)}, f32[2,512,128]{2,1,0:T(8,128)S(1)}, u32[]{:S(2)}, u32[]{:S(2)}) %collective-permute-start.1) | collective-permute-done | bytes 524320 | tf_op jit(solution)/shard_map/ppermute | solution.py:594
  20.8 1.3 %collective-permute-start.4 = (f32[2,512,128]{2,1,0:T(8,128)S(1)}, f32[2,512,128]{2,1,0:T(8,128)S(1)}, u32[]{:S(2)}, u32[]{:S(2)}) collective-permute-start(f32[2,512,128]{2,1,0:T(8,128)S(1)} %shard_map.101.refs_7_), channel_id=1, source_target_pairs={{0,24},{8,16},{20,28},{28,20},{1,25},{9,17},{21,29},{29,21},{2,26}... | collective-permute-start | bytes 1572872 | tf_op jit(solution)/shard_map/ppermute | solution.py:632
  22.1 4.4 %shard_map.103 = (f32[6,512,128]{2,1,0:T(8,128)S(1)}, f32[6,512,128]{2,1,0:T(8,128)S(1)}, f32[6,512,128]{2,1,0:T(8,128)S(1)}) custom-call(s32[1]{0:T(128)} %bitcast.refs_0_, f32[2,512,128]{2,1,0:T(8,128)S(1)} %collective-permute-done.1.refs_2_.refs_1_, ...), custom_call_target="tpu_custom_call", output_to_operand_aliasing={{0}: (3, {}), {1}: (4, {}), {2}: (5, {})} | custom-call | flops 1 | bytes 1 | tf_op jit(solution)/shard_map/pallas_call | solution.py:59
  26.5 0.0 collective-permute-done.5.refs_5_.refs_1_
  26.5 0.0 collective-permute-done.7.refs_2_
  26.6 0.1 collective-permute-start.8
  26.7 2.6 %shard_map.105 = (f32[6,512,128]{2,1,0:T(8,128)S(1)}, f32[6,512,128]{2,1,0:T(8,128)S(1)}, f32[6,512,128]{2,1,0:T(8,128)S(1)}) custom-call(s32[1]{0:T(128)} %bitcast.refs_0_, f32[2,512,128]{2,1,0:T(8,128)S(1)} %collective-permute-done.5.refs_5_.refs_1_, ...), custom_call_target="tpu_custom_call", output_to_operand_aliasing={{0}: (3, {}), {1}: (4, {}), {2}: (5, {})} | custom-call | flops 1 | bytes 1 | tf_op jit(solution)/shard_map/pallas_call | solution.py:59
  29.3 0.0 collective-permute-done.8.refs_5_
  29.3 1.0 %shard_map.106 = (f32[256,1024]{1,0:T(8,128)S(1)}, f32[16,256]{1,0:T(8,128)S(1)}) custom-call(s32[1]{0:T(128)} %bitcast.refs_0_, bf16[8,256,256]{2,1,0:T(8,128)(2,1)S(1)} %get-tuple-element.42.refs_1_, f32[8,256,128]{2,1,0:T(8,128)S(1)} %get-tuple-element.29.refs_1_.refs_2_, f32[8,256]{1,0:T(8,128)S(1)} %get-tuple-element.25.refs_4_.refs_3_, ...), custom_call_target="tpu_custom_call" | custom-call | flops 1 | bytes 1 | tf_op jit(solution)/shard_map/pallas_call | solution.py:59
  30.3 1.6 %collective-permute-start.9 = (f32[16,256]{1,0:T(8,128)S(1)}, f32[16,256]{1,0:T(8,128)S(1)}, u32[]{:S(2)}, u32[]{:S(2)}) collective-permute-start(f32[16,256]{1,0:T(8,128)S(1)} %get-tuple-element.43.refs_6_.refs_0_), channel_id=1, source_target_pairs={{0,1},{1,0},{2,3},{3,2},{4,5},{5,4},{6,7},{7,6},{8,9},{9,8},{10,11... | collective-permute-start | bytes 49160 | tf_op jit(solution)/shard_map/ppermute | solution.py:607
  31.9 2.4 %shard_map.107 = (f32[6,512,128]{2,1,0:T(8,128)S(1)}, f32[6,512,128]{2,1,0:T(8,128)S(1)}, f32[6,512,128]{2,1,0:T(8,128)S(1)}) custom-call(s32[1]{0:T(128)} %bitcast.refs_0_, f32[2,512,128]{2,1,0:T(8,128)S(1)} %collective-permute-done.5.refs_5_.refs_1_, ...), custom_call_target="tpu_custom_call", output_to_operand_aliasing={{0}: (3, {}), {1}: (4, {}), {2}: (5, {})} | custom-call | flops 1 | bytes 1 | tf_op jit(solution)/shard_map/pallas_call | solution.py:59
  34.3 0.0 collective-permute-done.9.refs_1_
  34.4 0.0 collective-permute-done.4.refs_1_
  34.4 2.3 %shard_map.109.refs_6_ = f32[256,768]{1,0:T(8,128)S(1)} custom-call(s32[1]{0:T(128)} %bitcast.refs_0_, f32[2,512,128]{2,1,0:T(8,128)S(1)} %collective-permute-done.4.refs_1_, bf16[6,512,256]{2,1,0:T(8,128)(2,1)S(1)} %get-tuple-element.31.refs_2_, f32[6,512,128]{2,1,0:T(8,128)S(1)} %get-tuple-element.44.refs_2_.refs_3_, ...), custom_call_target="tpu_custom_call" | custom-call | flops 1 | bytes 1 | tf_op jit(solution)/shard_map/pallas_call | solution.py:59
  36.7 0.0 copy-start.5
  36.7 0.1 collective-permute-start.10
  36.8 2.6 %collective-permute-start.11 = (f32[16,256]{1,0:T(8,128)S(1)}, f32[16,256]{1,0:T(8,128)S(1)}, u32[]{:S(2)}, u32[]{:S(2)}) collective-permute-start(f32[16,256]{1,0:T(8,128)S(1)} %shard_map.108.refs_6_.refs_8_), channel_id=1, source_target_pairs={{0,2},{1,3},{2,0},{3,1},{4,6},{5,7},{6,4},{7,5},{8,10},{9,11},{10,... | collective-permute-start | bytes 49160 | tf_op jit(solution)/shard_map/ppermute | solution.py:607
  39.4 1.3 %shard_map.110.refs_7_ = f32[256,384]{1,0:T(8,128)S(1)} custom-call(s32[1]{0:T(128)} %bitcast.refs_0_, f32[2,512,128]{2,1,0:T(8,128)S(1)} %collective-permute-done.4.refs_1_, bf16[6,512,256]{2,1,0:T(8,128)(2,1)S(1)} %get-tuple-element.31.refs_2_, f32[6,512,128]{2,1,0:T(8,128)S(1)} %get-tuple-element.44.refs_2_.refs_3_, ...), custom_call_target="tpu_custom_call" | custom-call | flops 1 | bytes 1 | tf_op jit(solution)/shard_map/pallas_call | solution.py:59
  40.7 0.7 %collective-permute-done.11.refs_9_ = f32[16,256]{1,0:T(8,128)S(1)} collective-permute-done((f32[16,256]{1,0:T(8,128)S(1)}, f32[16,256]{1,0:T(8,128)S(1)}, u32[]{:S(2)}, u32[]{:S(2)}) %collective-permute-start.11) | collective-permute-done | bytes 16416 | tf_op jit(solution)/shard_map/ppermute | solution.py:607
  41.5 0.0 collective-permute-done.10.refs_6_
  41.5 0.0 copy-done.5
  41.5 2.4 %shard_map.111 = (f32[256,1024]{1,0:T(8,128)}, f32[256,1536]{1,0:T(8,128)}) custom-call(s32[1]{0:T(128)} %bitcast.refs_0_, f32[2,512,128]{2,1,0:T(8,128)S(1)} %collective-permute-done.4.refs_1_, bf16[6,512,256]{2,1,0:T(8,128)(2,1)S(1)} %get-tuple-element.31.refs_2_, f32[6,512,128]{2,1,0:T(8,128)S(1)} %get-tuple-element.44.refs_2_.refs_3_, ...), custom_call_target="tpu_custom_call" | custom-call | flops 1 | bytes 1 | tf_op jit(solution)/shard_map/pallas_call | solution.py:59
  (7 shorter events, 0.2 us)
Async XLA Ops:
  0.6 1.5 %copy-start.2 = (f32[256,1024]{1,0:T(8,128)S(1)}, f32[256,1024]{1,0:T(8,128)}, u32[]{:S(2)}) copy-start(f32[256,1024]{1,0:T(8,128)} %refs_2_.3) | copy-start | bytes 3145732
  0.6 1.8 %copy-start.1 = (f32[256,1024]{1,0:T(8,128)S(1)}, f32[256,1024]{1,0:T(8,128)}, u32[]{:S(2)}) copy-start(f32[256,1024]{1,0:T(8,128)} %refs_1_.4) | copy-start | bytes 3145732
  0.7 1.8 %copy-start.4 = (f32[8,256]{1,0:T(8,128)S(1)}, f32[8,256]{1,0:T(8,128)}, u32[]{:S(2)}) copy-start(f32[8,256]{1,0:T(8,128)} %refs_0_.2) | copy-start | bytes 24580
  2.0 1.6 %copy-start = (f32[256,1536]{1,0:T(8,128)S(1)}, f32[256,1536]{1,0:T(8,128)}, u32[]{:S(2)}) copy-start(f32[256,1536]{1,0:T(8,128)} %refs_1_.5) | copy-start | bytes 4718596
  2.0 1.6 %collective-permute-start = (f32[2,256,128]{2,1,0:T(8,128)S(1)}, f32[2,256,128]{2,1,0:T(8,128)S(1)}, u32[]{:S(2)}, u32[]{:S(2)}) collective-permute-start(f32[2,256,128]{2,1,0:T(8,128)S(1)} %pad_maximum_fusion.1), channel_id=1, source_target_pairs={{0,4},{4,0},{8,12},{12,8},{16,20},{20,16},{24,28},{28,24},{1,5},{5... | collective-permute-start | bytes 786440 | tf_op jit(solution)/shard_map/ppermute | solution.py:585
  3.3 2.1 %collective-permute-start.3 = (f32[2,520,128]{2,1,0:T(8,128)S(1)}, f32[2,520,128]{2,1,0:T(8,128)S(1)}, u32[]{:S(2)}, u32[]{:S(2)}) collective-permute-start(f32[2,520,128]{2,1,0:T(8,128)S(1)} %get-tuple-element.28.refs_1_), channel_id=1, source_target_pairs={{0,4},{4,0},{8,12},{12,8},{16,20},{20,16},{24,28},{28,24},{1,5},{5... | collective-permute-start | bytes 1597448 | tf_op jit(solution)/shard_map/ppermute | solution.py:585
  3.7 2.4 %copy-start.3 = (f32[256,1024]{1,0:T(8,128)S(1)}, f32[256,1024]{1,0:T(8,128)}, u32[]{:S(2)}) copy-start(f32[256,1024]{1,0:T(8,128)} %refs_0_.3) | copy-start | bytes 3145732
  3.8 5.4 %collective-permute-start.2 = (f32[6,256,128]{2,1,0:T(8,128)S(1)}, f32[6,256,128]{2,1,0:T(8,128)S(1)}, u32[]{:S(2)}, u32[]{:S(2)}) collective-permute-start(f32[6,256,128]{2,1,0:T(8,128)S(1)} %get-tuple-element.27.refs_3_), channel_id=1, source_target_pairs={{0,4},{4,0},{8,12},{12,8},{16,20},{20,16},{24,28},{28,24},{1,5},{5... | collective-permute-start | bytes 2359304 | tf_op jit(solution)/shard_map/ppermute | solution.py:585
  4.1 16.6 %collective-permute-start.1 = (f32[2,512,128]{2,1,0:T(8,128)S(1)}, f32[2,512,128]{2,1,0:T(8,128)S(1)}, u32[]{:S(2)}, u32[]{:S(2)}) collective-permute-start(f32[2,512,128]{2,1,0:T(8,128)S(1)} %get-tuple-element.26.refs_0_.refs_3_.refs_1_), channel_id=1, source_target_pairs={{0,16},{4,20},{8,24},{12,28},{1,17},{5,21},{9,25},{13,29},{2,18},{... | collective-permute-start | bytes 1572872 | tf_op jit(solution)/shard_map/ppermute | solution.py:594
  5.5 9.3 %collective-permute-start.6 = (f32[520,128]{1,0:T(8,128)S(1)}, f32[520,128]{1,0:T(8,128)S(1)}, u32[]{:S(2)}, u32[]{:S(2)}) collective-permute-start(f32[520,128]{1,0:T(8,128)S(1)} %shard_map.97.refs_4_.refs_1_), channel_id=1, source_target_pairs={{8,0},{12,4},{0,8},{4,12},{24,16},{28,20},{16,24},{20,28},{9,1},{1... | collective-permute-start | bytes 798728 | tf_op jit(solution)/shard_map/ppermute | solution.py:594
  7.9 18.7 %collective-permute-start.5 = (f32[2,512,128]{2,1,0:T(8,128)S(1)}, f32[2,512,128]{2,1,0:T(8,128)S(1)}, u32[]{:S(2)}, u32[]{:S(2)}) collective-permute-start(f32[2,512,128]{2,1,0:T(8,128)S(1)} %shard_map.99.refs_4_), channel_id=1, source_target_pairs={{0,8},{4,12},{16,24},{20,28},{1,9},{5,13},{17,25},{21,29},{2,10},{... | collective-permute-start | bytes 1572872 | tf_op jit(solution)/shard_map/ppermute | solution.py:594
  14.8 11.7 %collective-permute-start.7 = (f32[520,128]{1,0:T(8,128)S(1)}, f32[520,128]{1,0:T(8,128)S(1)}, u32[]{:S(2)}, u32[]{:S(2)}) collective-permute-start(f32[520,128]{1,0:T(8,128)S(1)} %get-tuple-element.38.refs_1_), channel_id=1, source_target_pairs={{0,16},{4,20},{8,24},{12,28},{1,17},{5,21},{9,25},{13,29},{2,18},{... | collective-permute-start | bytes 798728 | tf_op jit(solution)/shard_map/ppermute | solution.py:594
  20.8 13.6 %collective-permute-start.4 = (f32[2,512,128]{2,1,0:T(8,128)S(1)}, f32[2,512,128]{2,1,0:T(8,128)S(1)}, u32[]{:S(2)}, u32[]{:S(2)}) collective-permute-start(f32[2,512,128]{2,1,0:T(8,128)S(1)} %shard_map.101.refs_7_), channel_id=1, source_target_pairs={{0,24},{8,16},{20,28},{28,20},{1,25},{9,17},{21,29},{29,21},{2,26}... | collective-permute-start | bytes 1572872 | tf_op jit(solution)/shard_map/ppermute | solution.py:632
  26.6 2.7 %collective-permute-start.8 = (f32[520,128]{1,0:T(8,128)S(1)}, f32[520,128]{1,0:T(8,128)S(1)}, u32[]{:S(2)}, u32[]{:S(2)}) collective-permute-start(f32[520,128]{1,0:T(8,128)S(1)} %shard_map.104.refs_6_.refs_4_), channel_id=1, source_target_pairs={{0,4},{4,0},{8,12},{12,8},{16,20},{20,16},{24,28},{28,24},{1,5},{5... | collective-permute-start | bytes 798728 | tf_op jit(solution)/shard_map/ppermute | solution.py:585
  30.3 4.0 %collective-permute-start.9 = (f32[16,256]{1,0:T(8,128)S(1)}, f32[16,256]{1,0:T(8,128)S(1)}, u32[]{:S(2)}, u32[]{:S(2)}) collective-permute-start(f32[16,256]{1,0:T(8,128)S(1)} %get-tuple-element.43.refs_6_.refs_0_), channel_id=1, source_target_pairs={{0,1},{1,0},{2,3},{3,2},{4,5},{5,4},{6,7},{7,6},{8,9},{9,8},{10,11... | collective-permute-start | bytes 49160 | tf_op jit(solution)/shard_map/ppermute | solution.py:607
  36.7 4.8 %copy-start.5 = (f32[1024]{0:T(1024)S(1)}, f32[1024]{0:T(1024)}, u32[]{:S(2)}) copy-start(f32[1024]{0:T(1024)} %param.12) | copy-start | bytes 12292
  36.7 4.8 %collective-permute-start.10 = (f32[256,768]{1,0:T(8,128)S(1)}, f32[256,768]{1,0:T(8,128)S(1)}, u32[]{:S(2)}, u32[]{:S(2)}) collective-permute-start(f32[256,768]{1,0:T(8,128)S(1)} %shard_map.109.refs_6_), channel_id=1, source_target_pairs={{0,4},{4,0},{8,12},{12,8},{16,20},{20,16},{24,28},{28,24},{1,5},{5... | collective-permute-start | bytes 2359304 | tf_op jit(solution)/shard_map/ppermute | solution.py:585
  36.8 4.7 %collective-permute-start.11 = (f32[16,256]{1,0:T(8,128)S(1)}, f32[16,256]{1,0:T(8,128)S(1)}, u32[]{:S(2)}, u32[]{:S(2)}) collective-permute-start(f32[16,256]{1,0:T(8,128)S(1)} %shard_map.108.refs_6_.refs_8_), channel_id=1, source_target_pairs={{0,2},{1,3},{2,0},{3,1},{4,6},{5,7},{6,4},{7,5},{8,10},{9,11},{10,... | collective-permute-start | bytes 49160 | tf_op jit(solution)/shard_map/ppermute | solution.py:607

commit v9 on v8

--- a/solution.py
+++ b/solution.py
@@ -12,6 +12,7 @@
 NEGATIVE = -1e30
 EPSILON = 1e-05
 ENERGY_ROWS = 16
+HEADROOM = 60.0
 F32 = jnp.float32
 BF16 = jnp.bfloat16
 NT = (((1,), (1,)), ((), ()))
@@ -297,13 +298,21 @@
 
 
 def fill_terms(kv_ref, keys_ref, values_ref):
-    k_high, k_low = split(kv_ref[0].T)
+    keys = kv_ref[0].T
+    k_high, k_low = split(keys)
     keys_ref[:HD] = k_high
     keys_ref[HD : 2 * HD] = k_high
     keys_ref[2 * HD :] = k_low
     v_high, v_low = split(kv_ref[1])
     values_ref[:, :HD] = v_high
     values_ref[:, HD:] = v_low
+    return keys
+
+
+def bounded(keys, limit_ref):
+    longest = jnp.max(jnp.sum(keys * keys, axis=0, keepdims=True)) * jnp.max(limit_ref[0:1])
+    room = jnp.max(limit_ref[1:2])
+    return jnp.logical_and(room > 0.0, longest <= room * room)
 
 
 def lane_max(array):
@@ -333,7 +342,7 @@
     return wide[:, :HD] + wide[:, HD:] + dot(low, values[:, :HD])
 
 
-def own_kernel(factor, me_ref, q_ref, q_other_ref, kv_ref, q_out, acc_out, peak_out, total_out, keys_ref, values_ref):
+def own_kernel(factor, me_ref, q_ref, q_other_ref, kv_ref, q_out, acc_out, peak_out, total_out, limit_ref, keys_ref, values_ref):
     group, tokens = q_out.shape[0], q_ref.shape[0]
     core = me_ref[0] & 1
     first = core == 0
@@ -350,7 +359,9 @@
         at = pl.ds(pl.multiple_of((core * group + g) * HD, HD), HD)
         mine, other = q_ref[:, at], q_other_ref[g]
         queries = jnp.where(first, mine, other) if i % 2 == 0 else jnp.where(first, other, mine)
-        pair = jnp.concatenate(split(queries * factor), axis=1)
+        queries = queries * factor
+        lengths.append(jnp.sum(queries * queries, axis=1, keepdims=True))
+        pair = jnp.concatenate(split(queries), axis=1)
         q_out[g, rows] = pair
         s = dot(score_terms(pair), keys_ref[:, keys])
         edge = jnp.where(seen, s[:, rows], NEGATIVE)
@@ -359,6 +370,7 @@
     def soften(i, s):
         g, rows, _ = where(i)
         peak = jnp.max(lane_max(s), axis=1, keepdims=True)
+        lowest.append(peak)
         peak_out[g, rows] = jnp.broadcast_to(peak, (tokens, HD))
         high, low, total_out[g, rows] = weigh(s, peak, jnp.zeros((tokens, HD), F32))
         return high, low
@@ -367,7 +379,12 @@
         g, rows, keys = where(i)
         acc_out[g, rows] = summed(*terms, values_ref[keys])
 
+    lengths, lowest = [], []
     run(2 * group, score, soften, gather)
+    longest = jnp.max(functools.reduce(jnp.maximum, lengths))
+    room = HEADROOM + jnp.min(functools.reduce(jnp.minimum, lowest))
+    row = lax.broadcasted_iota(jnp.int32, limit_ref.shape, 0)
+    limit_ref[...] = jnp.where(row == 0, longest, room)
 
 
 def term_scratch(keys):
@@ -381,14 +398,20 @@
     return call(
         functools.partial(own_kernel, math.log2(math.e) / math.sqrt(HD)),
         [SMEM] + [VMEM] * 3,
-        [VMEM] * 4,
-        [jax.ShapeDtypeStruct((group, 2 * tokens, 2 * HD), BF16), stat, stat, stat],
+        [VMEM] * 5,
+        [
+            jax.ShapeDtypeStruct((group, 2 * tokens, 2 * HD), BF16),
+            stat,
+            stat,
+            stat,
+            jax.ShapeDtypeStruct((8, HD), F32),
+        ],
         term_scratch(2 * tokens),
         after=after,
     )(me, q_soft, q_other, kv)
 
 
-def later_kernel(distance, parts, heads, me_ref, kv_ref, q_ref, acc_ref, peak_ref, total_ref, acc_out, peak_out, total_out, keys_ref, values_ref):
+def later_kernel(distance, parts, heads, me_ref, kv_ref, q_ref, acc_ref, peak_ref, total_ref, limit_ref, acc_out, peak_out, total_out, keys_ref, values_ref):
     size = q_ref.shape[1] // parts
     chip = me_ref[0] >> 1
 
@@ -411,25 +434,41 @@
         at = where(i)
         acc_out[at] = acc_ref[at] * terms[2] + summed(*terms[:2], values_ref[...])
 
+    def soften_same(i, s):
+        at = where(i)
+        high, low, total_out[at] = weigh(s, peak_ref[at], total_ref[at])
+        return high, low
+
+    def gather_same(i, terms):
+        at = where(i)
+        acc_out[at] = acc_ref[at] + summed(*terms, values_ref[...])
+
     @pl.when(lax.bitwise_xor(chip, distance) < chip)
     def _():
-        fill_terms(kv_ref, keys_ref, values_ref)
-        run(parts * len(heads), score, soften, gather)
-
-
-def later_stage(me, distance, heads, kv, q_terms, acc, peak, total, after, parts=4):
+        same = bounded(fill_terms(kv_ref, keys_ref, values_ref), limit_ref)
+
+        @pl.when(same)
+        def _():
+            run(parts * len(heads), score, soften_same, gather_same)
+
+        @pl.when(jnp.logical_not(same))
+        def _():
+            run(parts * len(heads), score, soften, gather)
+
+
+def later_stage(me, distance, heads, kv, q_terms, acc, peak, total, limit, after, parts=4):
     return call(
         functools.partial(later_kernel, distance, parts, heads),
-        [SMEM] + [VMEM] * 5,
+        [SMEM] + [VMEM] * 6,
         [VMEM] * 3,
         [jax.ShapeDtypeStruct(acc.shape, F32)] * 3,
         term_scratch(kv.shape[1]),
         alias={3: 0, 4: 1, 5: 2},
         after=after,
-    )(me, kv, q_terms, acc, peak, total)
-
-
-def last_kernel(distance, whose, heads, columns, me_ref, kv_ref, q_ref, acc_ref, peak_ref, total_ref, *refs):
+    )(me, kv, q_terms, acc, peak, total, limit)
+
+
+def last_kernel(distance, whose, heads, columns, me_ref, kv_ref, q_ref, acc_ref, peak_ref, total_ref, limit_ref, *refs):
     if columns is None:
         out_ref, keys_ref, values_ref = refs
     else:
@@ -487,12 +526,26 @@
         new = summed(high, low, values_ref[...])
         finish(n, acc_ref[heads[n], at] * shrink + new, total)
 
+    def soften_same(n, s):
+        return weigh(s, peak_ref[heads[n], at], total_ref[heads[n], at])
+
+    def gather_same(n, terms):
+        high, low, total = terms
+        finish(n, acc_ref[heads[n], at] + summed(high, low, values_ref[...]), total)
+
     visible = lax.bitwise_xor(chip, distance) < chip
 
     @pl.when(visible)
     def _():
-        fill_terms(kv_ref, keys_ref, values_ref)
-        run(len(heads), score, soften, gather)
+        same = bounded(fill_terms(kv_ref, keys_ref, values_ref), limit_ref)
+
+        @pl.when(same)
+        def _():
+            run(len(heads), score, soften_same, gather_same)
+
+        @pl.when(jnp.logical_not(same))
+        def _():
+            run(len(heads), score, soften, gather)
 
     @pl.when(jnp.logical_not(visible))
     def _():
@@ -611,7 +664,7 @@
 
     def stage(distance, heads, carried, after):
         return later_stage(
-            me_flag, distance, heads, arrived[distance], q_terms, *carried, after
+            me_flag, distance, heads, arrived[distance], q_terms, *carried, limit, after
         )
 
     bits = chips.bit_length() - 1
@@ -623,7 +676,7 @@
     else:
         for distance in range(1, chips):
             arrived[distance] = sent(distance, kv)
-    q_terms, *carried = own_stage(me_flag, q_soft, q_other, kv, [token])
+    q_terms, *carried, limit = own_stage(me_flag, q_soft, q_other, kv, [token])
     group = q_terms.shape[0]
     all_heads, front, back = range(group), range(group // 2), range(group // 2, group)
     token = carried[0]
@@ -652,7 +705,7 @@
         step *= 2
     other = exchanged(energy, energies[0])
     carried = stage(left[-1], back, carried, [energy])
-    operands = [arrived[chips - 1], q_terms, *carried]
+    operands = [arrived[chips - 1], q_terms, *carried, limit]
     for step in energies[1:]:
         energy = plus(energy, other, [carried[0]])
         other = exchanged(energy, step)

time: 44.3 us -> 45.6 us (1.029)
  Pallas kernels: 22.3 us -> 23.5 us
    pallas_call x17, Pallas kernels: 22.3 us -> 23.5 us  [call(): return lambda *operands: made(*operands, *after)]
  transfers between devices with their start and end apart: 12 -> 12, of which waited for: 3 -> 3; matrix products, arithmetic and copies ran while one was open for 0% -> 0% of each run, Pallas kernels for 40% -> 41%
where the time goes in v9:
time: 45.6 us; the launch traced here: 45.3 us
  Pallas kernels  23.5 us (52%)
  starting transfers between devices  11 us (24%)
  waiting for transfers between devices  8 us (18%)
  other arithmetic  1.31 us (3%)
  between operations  1.12 us (2%)
    pallas_call x17, Pallas kernels, call(): return lambda *operands: made(*operands, *after)  23.5 us
    ppermute x4, waiting for transfers between devices, across(): return lax.ppermute(array, 'ctx', pairs)  7.2 us
    ppermute x4, starting transfers between devices, across(): return lax.ppermute(array, 'ctx', pairs)  4.46 us
    ppermute x2, starting transfers between devices, exchanged(): return lax.ppermute(array, 'head', [(i, i ^ step) for i in range(heads)])  4.18 us
    another operation x2, other arithmetic, halves(): jnp.stack([jnp.where(core == 0, b, a) for a, b in zip(early, late)])  1.3 us
    ppermute x1, starting transfers between devices, body(): arrived[3] = lax.ppermute(relay, 'ctx', [(0, 6), (2, 4), (5, 7), (7, 5)])  1.29 us
    ppermute x5, starting transfers between devices, swap(): return lax.ppermute(array, 'ctx', swap_pairs)  1.07 us
  transfers between devices with their start and end apart: 12, of which 3 were waited for; matrix products, arithmetic and copies ran while one was open for 0% of the time, Pallas kernels for 41%

profile of v9, /device:TPU:6, one launch (start us, length us, event | category | flops | bytes accessed | tf_op | source)
XLA Modules:
  0.0 45.3 jit_solution(10011714251350176893)
XLA Ops:
  0.6 0.0 copy-start.2
  0.6 0.0 copy-start.1
  0.7 0.0 copy-start.4
  0.7 1.3 %select_bitcast_fusion = (f32[1,256,128]{2,1,0:T(8,128)S(1)}, f32[1,256,128]{2,1,0:T(8,128)S(1)}, f32[1,256,128]{2,1,0:T(8,128)S(1)}, f32[1,256,128]{2,1,0:T(8,128)S(1)}) fusion(f32[256,256]{1,0:T(8,128)} %param.15, pred[]{:T(512)S(6)} %eq.2, f32[256,256]{1,0:T(8,128)} %param.14), kind=kLoop, calls=%fused_computation.2 | loop fusion | flops 131072 | bytes 1048577 | tf_op jit(solution)/shard_map/stack | solution.py:256
  2.0 0.0 copy-start
  2.0 0.1 collective-permute-start
  2.1 0.0 copy-done.2
  2.1 0.3 copy-done.1
  2.4 0.0 copy-done.4
  2.4 0.9 %shard_map.95 = (f32[2,520,128]{2,1,0:T(8,128)S(1)}, f32[8,256]{1,0:T(8,128)S(1)}) custom-call(f32[8,256]{1,0:T(8,128)S(1)} %copy-done.4, f32[256,1024]{1,0:T(8,128)S(1)} %copy-done.1, f32[256,1024]{1,0:T(8,128)S(1)} %copy-done.2, f32[2,256,128]{2,1,0:T(8,128)S(1)} %pad_maximum_fusion.refs_3_.refs_1_), custom_call_target="tpu_custom_call" | custom-call | flops 1 | bytes 1 | tf_op jit(solution)/shard_map/pallas_call | solution.py:60
  3.3 0.3 collective-permute-start.3
  3.6 0.0 collective-permute-done.refs_2_
  3.6 0.0 copy-done
  3.6 0.1 shard_map.96
  3.7 0.0 copy-start.3
  3.8 0.4 collective-permute-start.2
  4.1 1.3 %collective-permute-start.1 = (f32[2,512,128]{2,1,0:T(8,128)S(1)}, f32[2,512,128]{2,1,0:T(8,128)S(1)}, u32[]{:S(2)}, u32[]{:S(2)}) collective-permute-start(f32[2,512,128]{2,1,0:T(8,128)S(1)} %get-tuple-element.27.refs_0_.refs_3_.refs_1_), channel_id=1, source_target_pairs={{0,16},{4,20},{8,24},{12,28},{1,17},{5,21},{9,25},{13,29},{2,18},{... | collective-permute-start | bytes 1572872 | tf_op jit(solution)/shard_map/ppermute | solution.py:647
  5.4 0.0 collective-permute-done.3.refs_2_.refs_6_
  5.5 0.6 %collective-permute-start.6 = (f32[520,128]{1,0:T(8,128)S(1)}, f32[520,128]{1,0:T(8,128)S(1)}, u32[]{:S(2)}, u32[]{:S(2)}) collective-permute-start(f32[520,128]{1,0:T(8,128)S(1)} %shard_map.97.refs_4_.refs_1_), channel_id=1, source_target_pairs={{8,0},{12,4},{0,8},{4,12},{24,16},{28,20},{16,24},{20,28},{9,1},{1... | collective-permute-start | bytes 798728 | tf_op jit(solution)/shard_map/ppermute | solution.py:647
  6.1 0.0 copy-done.3
  6.1 1.7 %shard_map.98 = (f32[8,256,128]{2,1,0:T(8,128)S(1)}, bf16[8,256,256]{2,1,0:T(8,128)(2,1)S(1)}) custom-call(f32[256,1024]{1,0:T(8,128)S(1)} %copy-done.3, f32[256,1024]{1,0:T(8,128)S(1)} %copy-done.1, f32[256,1024]{1,0:T(8,128)S(1)} %copy-done.2, f32[8,256]{1,0:T(8,128)S(1)} %get-tuple-element.26.refs_4_.refs_3_, f32[520,128]{1,0:T(8,128)S(1)} %shard_map.97.refs_4_.refs_1_), custom_call_target="tpu_custom_call" | custom-call | flops 1 | bytes 1 | tf_op jit(solution)/shard_map/pallas_call | solution.py:60
  7.9 1.3 %collective-permute-start.5 = (f32[2,512,128]{2,1,0:T(8,128)S(1)}, f32[2,512,128]{2,1,0:T(8,128)S(1)}, u32[]{:S(2)}, u32[]{:S(2)}) collective-permute-start(f32[2,512,128]{2,1,0:T(8,128)S(1)} %shard_map.99.refs_4_), channel_id=1, source_target_pairs={{0,8},{4,12},{16,24},{20,28},{1,9},{5,13},{17,25},{21,29},{2,10},{... | collective-permute-start | bytes 1572872 | tf_op jit(solution)/shard_map/ppermute | solution.py:647
  9.2 0.0 collective-permute-done.2.refs_2_
  9.2 3.0 %shard_map.100 = (bf16[6,512,256]{2,1,0:T(8,128)(2,1)S(1)}, f32[6,512,128]{2,1,0:T(8,128)S(1)}, f32[6,512,128]{2,1,0:T(8,128)S(1)}, f32[6,512,128]{2,1,0:T(8,128)S(1)}, f32[8,128]{1,0:T(8,128)S(1)}) custom-call(s32[1]{0:T(128)} %bitcast.refs_0_, f32[256,1536]{1,0:T(8,128)S(1)} %copy-done, f32[6,256,128]{2,1,0:T(8,128)S(1)} %collective-permute-done.2.refs_2_, ...), custom_call_target="tpu_custom_call" | custom-call | flops 1 | bytes 1 | tf_op jit(solution)/shard_map/pallas_call | solution.py:60
  12.2 2.6 %collective-permute-done.6.refs_2_ = f32[520,128]{1,0:T(8,128)S(1)} collective-permute-done((f32[520,128]{1,0:T(8,128)S(1)}, f32[520,128]{1,0:T(8,128)S(1)}, u32[]{:S(2)}, u32[]{:S(2)}) %collective-permute-start.6) | collective-permute-done | bytes 266272 | tf_op jit(solution)/shard_map/ppermute | solution.py:647
  14.8 0.1 shard_map.102
  14.8 1.3 %collective-permute-start.7 = (f32[520,128]{1,0:T(8,128)S(1)}, f32[520,128]{1,0:T(8,128)S(1)}, u32[]{:S(2)}, u32[]{:S(2)}) collective-permute-start(f32[520,128]{1,0:T(8,128)S(1)} %get-tuple-element.40.refs_1_), channel_id=1, source_target_pairs={{0,16},{4,20},{8,24},{12,28},{1,17},{5,21},{9,25},{13,29},{2,18},{... | collective-permute-start | bytes 798728 | tf_op jit(solution)/shard_map/ppermute | solution.py:647
  16.1 4.6 %collective-permute-done.1.refs_2_.refs_1_ = f32[2,512,128]{2,1,0:T(8,128)S(1)} collective-permute-done((f32[2,512,128]{2,1,0:T(8,128)S(1)}, f32[2,512,128]{2,1,0:T(8,128)S(1)}, u32[]{:S(2)}, u32[]{:S(2)}) %collective-permute-start.1) | collective-permute-done | bytes 524320 | tf_op jit(solution)/shard_map/ppermute | solution.py:647
  20.8 1.3 %collective-permute-start.4 = (f32[2,512,128]{2,1,0:T(8,128)S(1)}, f32[2,512,128]{2,1,0:T(8,128)S(1)}, u32[]{:S(2)}, u32[]{:S(2)}) collective-permute-start(f32[2,512,128]{2,1,0:T(8,128)S(1)} %shard_map.101.refs_8_), channel_id=1, source_target_pairs={{0,24},{8,16},{20,28},{28,20},{1,25},{9,17},{21,29},{29,21},{2,26}... | collective-permute-start | bytes 1572872 | tf_op jit(solution)/shard_map/ppermute | solution.py:685
  22.1 4.9 %shard_map.103 = (f32[6,512,128]{2,1,0:T(8,128)S(1)}, f32[6,512,128]{2,1,0:T(8,128)S(1)}, f32[6,512,128]{2,1,0:T(8,128)S(1)}) custom-call(s32[1]{0:T(128)} %bitcast.refs_0_, f32[2,512,128]{2,1,0:T(8,128)S(1)} %collective-permute-done.1.refs_2_.refs_1_, ...), custom_call_target="tpu_custom_call", output_to_operand_aliasing={{0}: (3, {}), {1}: (4, {}), {2}: (5, {})} | custom-call | flops 1 | bytes 1 | tf_op jit(solution)/shard_map/pallas_call | solution.py:60
  27.1 0.0 collective-permute-done.5.refs_5_.refs_1_
  27.1 0.0 collective-permute-done.7.refs_2_
  27.1 0.1 shard_map.104.refs_7_.refs_4_
  27.1 0.1 collective-permute-start.8
  27.2 2.6 %shard_map.105 = (f32[6,512,128]{2,1,0:T(8,128)S(1)}, f32[6,512,128]{2,1,0:T(8,128)S(1)}, f32[6,512,128]{2,1,0:T(8,128)S(1)}) custom-call(s32[1]{0:T(128)} %bitcast.refs_0_, f32[2,512,128]{2,1,0:T(8,128)S(1)} %collective-permute-done.5.refs_5_.refs_1_, ...), custom_call_target="tpu_custom_call", output_to_operand_aliasing={{0}: (3, {}), {1}: (4, {}), {2}: (5, {})} | custom-call | flops 1 | bytes 1 | tf_op jit(solution)/shard_map/pallas_call | solution.py:60
  29.8 0.0 collective-permute-done.8.refs_5_
  29.8 1.0 %shard_map.106 = (f32[256,1024]{1,0:T(8,128)S(1)}, f32[16,256]{1,0:T(8,128)S(1)}) custom-call(s32[1]{0:T(128)} %bitcast.refs_0_, bf16[8,256,256]{2,1,0:T(8,128)(2,1)S(1)} %get-tuple-element.44.refs_1_, f32[8,256,128]{2,1,0:T(8,128)S(1)} %get-tuple-element.30.refs_1_.refs_2_, f32[8,256]{1,0:T(8,128)S(1)} %get-tuple-element.26.refs_4_.refs_3_, ...), custom_call_target="tpu_custom_call" | custom-call | flops 1 | bytes 1 | tf_op jit(solution)/shard_map/pallas_call | solution.py:60
  30.8 1.6 %collective-permute-start.9 = (f32[16,256]{1,0:T(8,128)S(1)}, f32[16,256]{1,0:T(8,128)S(1)}, u32[]{:S(2)}, u32[]{:S(2)}) collective-permute-start(f32[16,256]{1,0:T(8,128)S(1)} %get-tuple-element.45.refs_7_.refs_0_), channel_id=1, source_target_pairs={{0,1},{1,0},{2,3},{3,2},{4,5},{5,4},{6,7},{7,6},{8,9},{9,8},{10,11... | collective-permute-start | bytes 49160 | tf_op jit(solution)/shard_map/ppermute | solution.py:660
  32.4 2.5 %shard_map.107 = (f32[6,512,128]{2,1,0:T(8,128)S(1)}, f32[6,512,128]{2,1,0:T(8,128)S(1)}, f32[6,512,128]{2,1,0:T(8,128)S(1)}) custom-call(s32[1]{0:T(128)} %bitcast.refs_0_, f32[2,512,128]{2,1,0:T(8,128)S(1)} %collective-permute-done.5.refs_5_.refs_1_, ...), custom_call_target="tpu_custom_call", output_to_operand_aliasing={{0}: (3, {}), {1}: (4, {}), {2}: (5, {})} | custom-call | flops 1 | bytes 1 | tf_op jit(solution)/shard_map/pallas_call | solution.py:60
  34.9 0.0 collective-permute-done.9.refs_1_
  34.9 0.0 collective-permute-done.4.refs_1_
  35.0 2.6 %shard_map.109.refs_7_ = f32[256,768]{1,0:T(8,128)S(1)} custom-call(s32[1]{0:T(128)} %bitcast.refs_0_, f32[2,512,128]{2,1,0:T(8,128)S(1)} %collective-permute-done.4.refs_1_, bf16[6,512,256]{2,1,0:T(8,128)(2,1)S(1)} %get-tuple-element.32.refs_2_, f32[6,512,128]{2,1,0:T(8,128)S(1)} %get-tuple-element.46.refs_2_.refs_3_, ...), custom_call_target="tpu_custom_call" | custom-call | flops 1 | bytes 1 | tf_op jit(solution)/shard_map/pallas_call | solution.py:60
  37.6 0.0 copy-start.5
  37.6 0.3 collective-permute-start.10
  37.9 2.6 %collective-permute-start.11 = (f32[16,256]{1,0:T(8,128)S(1)}, f32[16,256]{1,0:T(8,128)S(1)}, u32[]{:S(2)}, u32[]{:S(2)}) collective-permute-start(f32[16,256]{1,0:T(8,128)S(1)} %shard_map.108.refs_7_.refs_9_), channel_id=1, source_target_pairs={{0,2},{1,3},{2,0},{3,1},{4,6},{5,7},{6,4},{7,5},{8,10},{9,11},{10,... | collective-permute-start | bytes 49160 | tf_op jit(solution)/shard_map/ppermute | solution.py:660
  40.5 1.4 %shard_map.110.refs_8_ = f32[256,384]{1,0:T(8,128)S(1)} custom-call(s32[1]{0:T(128)} %bitcast.refs_0_, f32[2,512,128]{2,1,0:T(8,128)S(1)} %collective-permute-done.4.refs_1_, bf16[6,512,256]{2,1,0:T(8,128)(2,1)S(1)} %get-tuple-element.32.refs_2_, f32[6,512,128]{2,1,0:T(8,128)S(1)} %get-tuple-element.46.refs_2_.refs_3_, ...), custom_call_target="tpu_custom_call" | custom-call | flops 1 | bytes 1 | tf_op jit(solution)/shard_map/pallas_call | solution.py:60
  41.9 0.8 %collective-permute-done.11.refs_10_ = f32[16,256]{1,0:T(8,128)S(1)} collective-permute-done((f32[16,256]{1,0:T(8,128)S(1)}, f32[16,256]{1,0:T(8,128)S(1)}, u32[]{:S(2)}, u32[]{:S(2)}) %collective-permute-start.11) | collective-permute-done | bytes 16416 | tf_op jit(solution)/shard_map/ppermute | solution.py:660
  42.6 0.0 collective-permute-done.10.refs_7_
  42.6 0.0 copy-done.5
  42.6 2.5 %shard_map.111 = (f32[256,1024]{1,0:T(8,128)}, f32[256,1536]{1,0:T(8,128)}) custom-call(s32[1]{0:T(128)} %bitcast.refs_0_, f32[2,512,128]{2,1,0:T(8,128)S(1)} %collective-permute-done.4.refs_1_, bf16[6,512,256]{2,1,0:T(8,128)(2,1)S(1)} %get-tuple-element.32.refs_2_, f32[6,512,128]{2,1,0:T(8,128)S(1)} %get-tuple-element.46.refs_2_.refs_3_, ...), custom_call_target="tpu_custom_call" | custom-call | flops 1 | bytes 1 | tf_op jit(solution)/shard_map/pallas_call | solution.py:60
  (6 shorter events, 0.2 us)
Async XLA Ops:
  0.6 1.5 %copy-start.2 = (f32[256,1024]{1,0:T(8,128)S(1)}, f32[256,1024]{1,0:T(8,128)}, u32[]{:S(2)}) copy-start(f32[256,1024]{1,0:T(8,128)} %refs_2_.3) | copy-start | bytes 3145732
  0.6 1.8 %copy-start.1 = (f32[256,1024]{1,0:T(8,128)S(1)}, f32[256,1024]{1,0:T(8,128)}, u32[]{:S(2)}) copy-start(f32[256,1024]{1,0:T(8,128)} %refs_1_.4) | copy-start | bytes 3145732
  0.7 1.8 %copy-start.4 = (f32[8,256]{1,0:T(8,128)S(1)}, f32[8,256]{1,0:T(8,128)}, u32[]{:S(2)}) copy-start(f32[8,256]{1,0:T(8,128)} %refs_0_.2) | copy-start | bytes 24580
  2.0 1.6 %copy-start = (f32[256,1536]{1,0:T(8,128)S(1)}, f32[256,1536]{1,0:T(8,128)}, u32[]{:S(2)}) copy-start(f32[256,1536]{1,0:T(8,128)} %refs_1_.5) | copy-start | bytes 4718596
  2.0 1.6 %collective-permute-start = (f32[2,256,128]{2,1,0:T(8,128)S(1)}, f32[2,256,128]{2,1,0:T(8,128)S(1)}, u32[]{:S(2)}, u32[]{:S(2)}) collective-permute-start(f32[2,256,128]{2,1,0:T(8,128)S(1)} %pad_maximum_fusion.1), channel_id=1, source_target_pairs={{0,4},{4,0},{8,12},{12,8},{16,20},{20,16},{24,28},{28,24},{1,5},{5... | collective-permute-start | bytes 786440 | tf_op jit(solution)/shard_map/ppermute | solution.py:638
  3.3 2.1 %collective-permute-start.3 = (f32[2,520,128]{2,1,0:T(8,128)S(1)}, f32[2,520,128]{2,1,0:T(8,128)S(1)}, u32[]{:S(2)}, u32[]{:S(2)}) collective-permute-start(f32[2,520,128]{2,1,0:T(8,128)S(1)} %get-tuple-element.29.refs_1_), channel_id=1, source_target_pairs={{0,4},{4,0},{8,12},{12,8},{16,20},{20,16},{24,28},{28,24},{1,5},{5... | collective-permute-start | bytes 1597448 | tf_op jit(solution)/shard_map/ppermute | solution.py:638
  3.7 2.4 %copy-start.3 = (f32[256,1024]{1,0:T(8,128)S(1)}, f32[256,1024]{1,0:T(8,128)}, u32[]{:S(2)}) copy-start(f32[256,1024]{1,0:T(8,128)} %refs_0_.3) | copy-start | bytes 3145732
  3.8 5.4 %collective-permute-start.2 = (f32[6,256,128]{2,1,0:T(8,128)S(1)}, f32[6,256,128]{2,1,0:T(8,128)S(1)}, u32[]{:S(2)}, u32[]{:S(2)}) collective-permute-start(f32[6,256,128]{2,1,0:T(8,128)S(1)} %get-tuple-element.28.refs_3_), channel_id=1, source_target_pairs={{0,4},{4,0},{8,12},{12,8},{16,20},{20,16},{24,28},{28,24},{1,5},{5... | collective-permute-start | bytes 2359304 | tf_op jit(solution)/shard_map/ppermute | solution.py:638
  4.1 16.6 %collective-permute-start.1 = (f32[2,512,128]{2,1,0:T(8,128)S(1)}, f32[2,512,128]{2,1,0:T(8,128)S(1)}, u32[]{:S(2)}, u32[]{:S(2)}) collective-permute-start(f32[2,512,128]{2,1,0:T(8,128)S(1)} %get-tuple-element.27.refs_0_.refs_3_.refs_1_), channel_id=1, source_target_pairs={{0,16},{4,20},{8,24},{12,28},{1,17},{5,21},{9,25},{13,29},{2,18},{... | collective-permute-start | bytes 1572872 | tf_op jit(solution)/shard_map/ppermute | solution.py:647
  5.5 9.3 %collective-permute-start.6 = (f32[520,128]{1,0:T(8,128)S(1)}, f32[520,128]{1,0:T(8,128)S(1)}, u32[]{:S(2)}, u32[]{:S(2)}) collective-permute-start(f32[520,128]{1,0:T(8,128)S(1)} %shard_map.97.refs_4_.refs_1_), channel_id=1, source_target_pairs={{8,0},{12,4},{0,8},{4,12},{24,16},{28,20},{16,24},{20,28},{9,1},{1... | collective-permute-start | bytes 798728 | tf_op jit(solution)/shard_map/ppermute | solution.py:647
  7.9 19.2 %collective-permute-start.5 = (f32[2,512,128]{2,1,0:T(8,128)S(1)}, f32[2,512,128]{2,1,0:T(8,128)S(1)}, u32[]{:S(2)}, u32[]{:S(2)}) collective-permute-start(f32[2,512,128]{2,1,0:T(8,128)S(1)} %shard_map.99.refs_4_), channel_id=1, source_target_pairs={{0,8},{4,12},{16,24},{20,28},{1,9},{5,13},{17,25},{21,29},{2,10},{... | collective-permute-start | bytes 1572872 | tf_op jit(solution)/shard_map/ppermute | solution.py:647
  14.8 12.2 %collective-permute-start.7 = (f32[520,128]{1,0:T(8,128)S(1)}, f32[520,128]{1,0:T(8,128)S(1)}, u32[]{:S(2)}, u32[]{:S(2)}) collective-permute-start(f32[520,128]{1,0:T(8,128)S(1)} %get-tuple-element.40.refs_1_), channel_id=1, source_target_pairs={{0,16},{4,20},{8,24},{12,28},{1,17},{5,21},{9,25},{13,29},{2,18},{... | collective-permute-start | bytes 798728 | tf_op jit(solution)/shard_map/ppermute | solution.py:647
  20.8 14.1 %collective-permute-start.4 = (f32[2,512,128]{2,1,0:T(8,128)S(1)}, f32[2,512,128]{2,1,0:T(8,128)S(1)}, u32[]{:S(2)}, u32[]{:S(2)}) collective-permute-start(f32[2,512,128]{2,1,0:T(8,128)S(1)} %shard_map.101.refs_8_), channel_id=1, source_target_pairs={{0,24},{8,16},{20,28},{28,20},{1,25},{9,17},{21,29},{29,21},{2,26}... | collective-permute-start | bytes 1572872 | tf_op jit(solution)/shard_map/ppermute | solution.py:685
  27.1 2.6 %collective-permute-start.8 = (f32[520,128]{1,0:T(8,128)S(1)}, f32[520,128]{1,0:T(8,128)S(1)}, u32[]{:S(2)}, u32[]{:S(2)}) collective-permute-start(f32[520,128]{1,0:T(8,128)S(1)} %shard_map.104.refs_7_.refs_4_), channel_id=1, source_target_pairs={{0,4},{4,0},{8,12},{12,8},{16,20},{20,16},{24,28},{28,24},{1,5},{5... | collective-permute-start | bytes 798728 | tf_op jit(solution)/shard_map/ppermute | solution.py:638
  30.8 4.2 %collective-permute-start.9 = (f32[16,256]{1,0:T(8,128)S(1)}, f32[16,256]{1,0:T(8,128)S(1)}, u32[]{:S(2)}, u32[]{:S(2)}) collective-permute-start(f32[16,256]{1,0:T(8,128)S(1)} %get-tuple-element.45.refs_7_.refs_0_), channel_id=1, source_target_pairs={{0,1},{1,0},{2,3},{3,2},{4,5},{5,4},{6,7},{7,6},{8,9},{9,8},{10,11... | collective-permute-start | bytes 49160 | tf_op jit(solution)/shard_map/ppermute | solution.py:660
  37.6 5.1 %copy-start.5 = (f32[1024]{0:T(1024)S(1)}, f32[1024]{0:T(1024)}, u32[]{:S(2)}) copy-start(f32[1024]{0:T(1024)} %param.12) | copy-start | bytes 12292
  37.6 5.0 %collective-permute-start.10 = (f32[256,768]{1,0:T(8,128)S(1)}, f32[256,768]{1,0:T(8,128)S(1)}, u32[]{:S(2)}, u32[]{:S(2)}) collective-permute-start(f32[256,768]{1,0:T(8,128)S(1)} %shard_map.109.refs_7_), channel_id=1, source_target_pairs={{0,4},{4,0},{8,12},{12,8},{16,20},{20,16},{24,28},{28,24},{1,5},{5... | collective-permute-start | bytes 2359304 | tf_op jit(solution)/shard_map/ppermute | solution.py:638
  37.9 4.7 %collective-permute-start.11 = (f32[16,256]{1,0:T(8,128)S(1)}, f32[16,256]{1,0:T(8,128)S(1)}, u32[]{:S(2)}, u32[]{:S(2)}) collective-permute-start(f32[16,256]{1,0:T(8,128)S(1)} %shard_map.108.refs_7_.refs_9_), channel_id=1, source_target_pairs={{0,2},{1,3},{2,0},{3,1},{4,6},{5,7},{6,4},{7,5},{8,10},{9,11},{10,... | collective-permute-start | bytes 49160 | tf_op jit(solution)/shard_map/ppermute | solution.py:660

commit v10 on v8

--- a/solution.py
+++ b/solution.py
@@ -256,30 +256,28 @@
     return mine, theirs
 
 
-def pair_kernel(me_ref, mine_ref, other_ref, q_ref, out_ref, send_ref):
-    tokens = mine_ref.shape[1]
+def pair_kernel(me_ref, mine_ref, other_ref, q_ref, early_ref, late_ref, send_ref):
     group = send_ref.shape[0]
     core = me_ref[0] & 1
     first = core == 0
-    for side in range(2):
-        mine, other = mine_ref[side], other_ref[side]
-        out_ref[side, :tokens] = jnp.where(first, mine, other)
-        out_ref[side, tokens:] = jnp.where(first, other, mine)
+    mine, other = mine_ref[...], other_ref[...]
+    early_ref[...] = jnp.where(first, mine, other)
+    late_ref[...] = jnp.where(first, other, mine)
     for g in range(group):
         at = pl.ds(pl.multiple_of(((1 - core) * group + g) * HD, HD), HD)
         send_ref[g] = q_ref[:, at]
 
 
 def pair_block(me, mine, other, q_soft, after):
-    _, tokens, _ = mine.shape
-    group = q_soft.shape[1] // (2 * HD)
+    tokens, width = q_soft.shape
     return call(
         pair_kernel,
         [SMEM] + [VMEM] * 3,
-        [VMEM] * 2,
+        [VMEM] * 3,
         [
-            jax.ShapeDtypeStruct((2, 2 * tokens, HD), F32),
-            jax.ShapeDtypeStruct((group, tokens, HD), F32),
+            jax.ShapeDtypeStruct(mine.shape, F32),
+            jax.ShapeDtypeStruct(mine.shape, F32),
+            jax.ShapeDtypeStruct((width // (2 * HD), tokens, HD), F32),
         ],
         after=after,
     )(me, mine, other, q_soft)
@@ -296,14 +294,18 @@
     gather(count - 1, before)
 
 
-def fill_terms(kv_ref, keys_ref, values_ref):
-    k_high, k_low = split(kv_ref[0].T)
-    keys_ref[:HD] = k_high
-    keys_ref[HD : 2 * HD] = k_high
-    keys_ref[2 * HD :] = k_low
-    v_high, v_low = split(kv_ref[1])
-    values_ref[:, :HD] = v_high
-    values_ref[:, HD:] = v_low
+def fill_terms(kv_refs, keys_ref, values_ref):
+    start = 0
+    for kv_ref in kv_refs:
+        at = slice(start, start + kv_ref.shape[1])
+        start = at.stop
+        k_high, k_low = split(kv_ref[0].T)
+        keys_ref[:HD, at] = k_high
+        keys_ref[HD : 2 * HD, at] = k_high
+        keys_ref[2 * HD :, at] = k_low
+        v_high, v_low = split(kv_ref[1])
+        values_ref[at, :HD] = v_high
+        values_ref[at, HD:] = v_low
 
 
 def lane_max(array):
@@ -333,11 +335,11 @@
     return wide[:, :HD] + wide[:, HD:] + dot(low, values[:, :HD])
 
 
-def own_kernel(factor, me_ref, q_ref, q_other_ref, kv_ref, q_out, acc_out, peak_out, total_out, keys_ref, values_ref):
+def own_kernel(factor, me_ref, q_ref, q_other_ref, early_ref, late_ref, q_out, acc_out, peak_out, total_out, keys_ref, values_ref):
     group, tokens = q_out.shape[0], q_ref.shape[0]
     core = me_ref[0] & 1
     first = core == 0
-    fill_terms(kv_ref, keys_ref, values_ref)
+    fill_terms([early_ref, late_ref], keys_ref, values_ref)
     seen = lax.broadcasted_iota(jnp.int32, (tokens, tokens), 1)
     seen = seen <= lax.broadcasted_iota(jnp.int32, (tokens, tokens), 0)
 
@@ -374,18 +376,18 @@
     return [pltpu.VMEM((3 * HD, keys), BF16), pltpu.VMEM((keys, 2 * HD), BF16)]
 
 
-def own_stage(me, q_soft, q_other, kv, after):
+def own_stage(me, q_soft, q_other, early, late, after):
     tokens, width = q_soft.shape
     group = width // (2 * HD)
     stat = jax.ShapeDtypeStruct((group, 2 * tokens, HD), F32)
     return call(
         functools.partial(own_kernel, math.log2(math.e) / math.sqrt(HD)),
-        [SMEM] + [VMEM] * 3,
+        [SMEM] + [VMEM] * 4,
         [VMEM] * 4,
         [jax.ShapeDtypeStruct((group, 2 * tokens, 2 * HD), BF16), stat, stat, stat],
         term_scratch(2 * tokens),
         after=after,
-    )(me, q_soft, q_other, kv)
+    )(me, q_soft, q_other, early, late)
 
 
 def later_kernel(distance, parts, heads, me_ref, kv_ref, q_ref, acc_ref, peak_ref, total_ref, acc_out, peak_out, total_out, keys_ref, values_ref):
@@ -413,7 +415,7 @@
 
     @pl.when(lax.bitwise_xor(chip, distance) < chip)
     def _():
-        fill_terms(kv_ref, keys_ref, values_ref)
+        fill_terms([kv_ref], keys_ref, values_ref)
         run(parts * len(heads), score, soften, gather)
 
 
@@ -491,7 +493,7 @@
 
     @pl.when(visible)
     def _():
-        fill_terms(kv_ref, keys_ref, values_ref)
+        fill_terms([kv_ref], keys_ref, values_ref)
         run(len(heads), score, soften, gather)
 
     @pl.when(jnp.logical_not(visible))
@@ -553,24 +555,29 @@
     )
 
 
-def relay_kernel(me_ref, own_ref, across_ref, out_ref):
+def relay_kernel(me_ref, early_ref, late_ref, across_early_ref, across_late_ref, out_ref):
+    tokens = early_ref.shape[1]
+
     @pl.when((me_ref[0] & 1) == 0)
     def _():
-        out_ref[...] = own_ref[...]
+        out_ref[:, :tokens] = early_ref[...]
+        out_ref[:, tokens:] = late_ref[...]
 
     @pl.when((me_ref[0] & 1) == 1)
     def _():
-        out_ref[...] = across_ref[...]
+        out_ref[:, :tokens] = across_early_ref[...]
+        out_ref[:, tokens:] = across_late_ref[...]
 
 
 def relayed(me, own, across, after):
+    sides, tokens, _ = own[0].shape
     return call(
         relay_kernel,
-        [SMEM, VMEM, VMEM],
+        [SMEM] + [VMEM] * 4,
         VMEM,
-        jax.ShapeDtypeStruct(own.shape, F32),
-        after=after,
-    )(me, own, across)
+        jax.ShapeDtypeStruct((sides, 2 * tokens, HD), F32),
+        after=after,
+    )(me, *own, *across)
 
 
 def body(q_lin, k_lin, v_lin, log_decay, lin_gain, q_soft, k_soft, v_soft):
@@ -598,7 +605,8 @@
     kv_other = swap(kv_send)
     states, sums = local_states(log_decay, k_lin, v_lin, [kv_mine])
     others = swap(states)
-    kv, q_send = pair_block(me_flag, kv_mine, kv_other, q_soft, [sums])
+    early, late, q_send = pair_block(me_flag, kv_mine, kv_other, q_soft, [sums])
+    kv = (early, late)
     q_other = swap(q_send)
     total, prefix = chip_total(me_flag, states, others, [q_send]), None
     inside, terms = inside_blocks(q_lin, k_lin, v_lin, sums, [total])
@@ -609,40 +617,50 @@
     def sent(distance, array):
         return across(array, distance, lambda c, e: c ^ distance < c)
 
-    def stage(distance, heads, carried, after):
+    def stage(distance, half, heads, carried, after):
         return later_stage(
-            me_flag, distance, heads, arrived[distance], q_terms, *carried, after
+            me_flag, distance, heads, arrived[distance][half], q_terms, *carried, after
         )
 
     bits = chips.bit_length() - 1
     arrived, token = {}, inside
     if square:
-        arrived[2] = sent(2, kv)
-        token = copied(kv, [inside])
-        arrived[1] = sent(1, token)
+        first = sent(2, early)
+        token = copied(late, [inside])
+        arrived[2] = (first, sent(2, token))
+        token = copied(early, [token])
+        arrived[1] = (sent(1, token),)
     else:
         for distance in range(1, chips):
-            arrived[distance] = sent(distance, kv)
-    q_terms, *carried = own_stage(me_flag, q_soft, q_other, kv, [token])
+            arrived[distance] = tuple(sent(distance, array) for array in kv)
+    q_terms, *carried = own_stage(me_flag, q_soft, q_other, *kv, [token])
     group = q_terms.shape[0]
     all_heads, front, back = range(group), range(group // 2), range(group // 2, group)
+
     token = carried[0]
-    if square:
-        relay = relayed(me_flag, kv, arrived[2], [token])
-        arrived[3] = lax.ppermute(relay, "ctx", [(0, 6), (2, 4), (5, 7), (7, 5)])
     for bit in range(bits):
         last = bit == bits - 1
         theirs = across(total, 1 << bit, lambda c, e: not last or c ^ (1 << bit) < c)
-        prefix, total = turn(me_flag, bit, total, theirs, prefix, last, [token] + ([arrived[1]] if square and last else []))
-        distance = 2 if square else bit + 1
-        if not (square and last):
-            carried = stage(distance, all_heads, carried, [prefix, relay] if square else [prefix])
+        waits = [token] + ([arrived[1][1] if last else arrived[2][0]] if square else [])
+        prefix, total = turn(me_flag, bit, total, theirs, prefix, last, waits)
+        if square and bit == 0:
+            carried = stage(2, 0, all_heads, carried, [prefix])
+            token = copied(late, [carried[0]])
+            arrived[1] += (sent(1, token),)
+            relay = relayed(me_flag, kv, arrived[2], [token, arrived[1][0]])
+            arrived[3] = lax.ppermute(relay, "ctx", [(0, 6), (2, 4), (5, 7), (7, 5)])
+            carried = stage(2, 1, all_heads, carried, [relay, arrived[1][0]])
+            carried = stage(1, 0, all_heads, carried, [])
+            token = carried[0]
+        elif not square:
+            for half in range(2):
+                carried = stage(bit + 1, half, all_heads, carried, [prefix])
             token = carried[0]
     prefix_other = swap(prefix)
-    left = [1] if square else range(bits + 1, chips - 1)
-    for distance in left[:-1]:
-        carried = stage(distance, all_heads, carried, [prefix])
-    carried = stage(left[-1], front, carried, [prefix])
+    left = [(1, 1)] if square else [(d, h) for d in range(bits + 1, chips - 1) for h in range(2)]
+    for distance, half in left[:-1]:
+        carried = stage(distance, half, all_heads, carried, [prefix])
+    carried = stage(*left[-1], front, carried, [prefix])
     linear, energy = linear_blocks(
         me_flag, terms, inside, sums, prefix, prefix_other, others, [carried[0]]
     )
@@ -651,12 +669,15 @@
         energies.append(step)
         step *= 2
     other = exchanged(energy, energies[0])
-    carried = stage(left[-1], back, carried, [energy])
-    operands = [arrived[chips - 1], q_terms, *carried]
+    carried = stage(*left[-1], back, carried, [energy])
     for step in energies[1:]:
         energy = plus(energy, other, [carried[0]])
         other = exchanged(energy, step)
 
+    if not square:
+        relay = arrived[chips - 1]
+        arrived[3] = relayed(me_flag, relay, relay, [])
+    operands = [arrived[3], q_terms, *carried]
     theirs = last_stage(me_flag, chips - 1, "other", all_heads, operands, [energy])
     done = last_stage(me_flag, chips - 1, "own", front, operands, [theirs])
     columns = q_lin.shape[1] * heads

time: 44.3 us -> 49.6 us (1.12)
  Pallas kernels: 22.3 us -> 26.2 us
  starting transfers between devices: 10.9 us -> 13.4 us
  waiting for transfers between devices: 8.13 us -> 6.88 us
    pallas_call x17 -> x21, Pallas kernels: 22.3 us -> 26.2 us  [call(): return lambda *operands: made(*operands, *after)]
    ppermute x4 -> x6, waiting for transfers between devices: 7.36 us -> 4.51 us  [across(): return lax.ppermute(array, 'ctx', pairs)]
    ppermute x4 -> x6, starting transfers between devices: 4.46 us -> 7.05 us  [across(): return lax.ppermute(array, 'ctx', pairs)]
    ppermute x5, waiting for transfers between devices: 0.01 us -> 1.2 us  [swap(): return lax.ppermute(array, 'ctx', swap_pairs)]
  transfers between devices with their start and end apart: 12 -> 14, of which waited for: 3 -> 5; matrix products, arithmetic and copies ran while one was open for 0% -> 0% of each run, Pallas kernels for 40% -> 43%
where the time goes in v10:
time: 49.6 us; the launch traced here: 49.3 us
  Pallas kernels  26.2 us (53%)
  starting transfers between devices  13.4 us (27%)
  waiting for transfers between devices  6.88 us (14%)
  other arithmetic  1.31 us (3%)
  between operations  1.13 us (2%)
    pallas_call x21, Pallas kernels, call(): return lambda *operands: made(*operands, *after)  26.2 us
    ppermute x6, starting transfers between devices, across(): return lax.ppermute(array, 'ctx', pairs)  7.05 us
    ppermute x6, waiting for transfers between devices, across(): return lax.ppermute(array, 'ctx', pairs)  4.51 us
    ppermute x2, starting transfers between devices, exchanged(): return lax.ppermute(array, 'head', [(i, i ^ step) for i in range(heads)])  4.24 us
    another operation x2, other arithmetic, halves(): jnp.stack([jnp.where(core == 0, b, a) for a, b in zip(early, late)])  1.3 us
    ppermute x1, starting transfers between devices, body(): arrived[3] = lax.ppermute(relay, 'ctx', [(0, 6), (2, 4), (5, 7), (7, 5)])  1.29 us
    ppermute x5, waiting for transfers between devices, swap(): return lax.ppermute(array, 'ctx', swap_pairs)  1.2 us
    ppermute x2, waiting for transfers between devices, exchanged(): return lax.ppermute(array, 'head', [(i, i ^ step) for i in range(heads)])  1.16 us
  transfers between devices with their start and end apart: 14, of which 5 were waited for; matrix products, arithmetic and copies ran while one was open for 0% of the time, Pallas kernels for 43%

profile of v10, /device:TPU:6, one launch (start us, length us, event | category | flops | bytes accessed | tf_op | source)
XLA Modules:
  0.0 49.3 jit_solution(1264391746499761470)
XLA Ops:
  0.6 0.0 copy-start.2
  0.6 0.0 copy-start.1
  0.7 0.0 copy-start.4
  0.7 1.3 %select_bitcast_fusion = (f32[1,256,128]{2,1,0:T(8,128)S(1)}, f32[1,256,128]{2,1,0:T(8,128)S(1)}, f32[1,256,128]{2,1,0:T(8,128)S(1)}, f32[1,256,128]{2,1,0:T(8,128)S(1)}) fusion(f32[256,256]{1,0:T(8,128)} %param.15, pred[]{:T(512)S(6)} %eq.2, f32[256,256]{1,0:T(8,128)} %param.14), kind=kLoop, calls=%fused_computation.2 | loop fusion | flops 131072 | bytes 1048577 | tf_op jit(solution)/shard_map/stack | solution.py:255
  2.0 0.0 copy-start
  2.0 0.1 collective-permute-start
  2.1 0.0 copy-done.2
  2.1 0.3 copy-done.1
  2.4 0.0 copy-done.4
  2.4 0.9 %shard_map.95 = (f32[2,520,128]{2,1,0:T(8,128)S(1)}, f32[8,256]{1,0:T(8,128)S(1)}) custom-call(f32[8,256]{1,0:T(8,128)S(1)} %copy-done.4, f32[256,1024]{1,0:T(8,128)S(1)} %copy-done.1, f32[256,1024]{1,0:T(8,128)S(1)} %copy-done.2, f32[2,256,128]{2,1,0:T(8,128)S(1)} %pad_maximum_fusion.refs_3_.refs_1_), custom_call_target="tpu_custom_call" | custom-call | flops 1 | bytes 1 | tf_op jit(solution)/shard_map/pallas_call | solution.py:59
  3.3 0.3 collective-permute-start.2
  3.6 0.0 collective-permute-done.refs_2_
  3.6 0.0 copy-done
  3.6 0.1 shard_map.96
  3.7 0.0 copy-start.3
  3.8 0.4 collective-permute-start.4
  4.1 1.2 %collective-permute-done.2.refs_2_.refs_6_ = f32[2,520,128]{2,1,0:T(8,128)S(1)} collective-permute-done((f32[2,520,128]{2,1,0:T(8,128)S(1)}, f32[2,520,128]{2,1,0:T(8,128)S(1)}, u32[]{:S(2)}, u32[]{:S(2)}) %collective-permute-start.2) | collective-permute-done | bytes 532512 | tf_op jit(solution)/shard_map/ppermute | solution.py:592
  5.4 0.6 %collective-permute-start.5 = (f32[520,128]{1,0:T(8,128)S(1)}, f32[520,128]{1,0:T(8,128)S(1)}, u32[]{:S(2)}, u32[]{:S(2)}) collective-permute-start(f32[520,128]{1,0:T(8,128)S(1)} %shard_map.97.refs_4_.refs_1_), channel_id=1, source_target_pairs={{8,0},{12,4},{0,8},{4,12},{24,16},{28,20},{16,24},{20,28},{9,1},{1... | collective-permute-start | bytes 798728 | tf_op jit(solution)/shard_map/ppermute | solution.py:601
  6.0 1.3 %collective-permute-start.1 = (f32[2,256,128]{2,1,0:T(8,128)S(1)}, f32[2,256,128]{2,1,0:T(8,128)S(1)}, u32[]{:S(2)}, u32[]{:S(2)}) collective-permute-start(f32[2,256,128]{2,1,0:T(8,128)S(1)} %get-tuple-element.33.refs_0_.refs_3_.refs_1_), channel_id=1, source_target_pairs={{0,16},{4,20},{8,24},{12,28},{1,17},{5,21},{9,25},{13,29},{2,18},{... | collective-permute-start | bytes 786440 | tf_op jit(solution)/shard_map/ppermute | solution.py:601
  7.3 0.0 copy-done.3
  7.3 1.7 %shard_map.98 = (f32[8,256,128]{2,1,0:T(8,128)S(1)}, bf16[8,256,256]{2,1,0:T(8,128)(2,1)S(1)}) custom-call(f32[256,1024]{1,0:T(8,128)S(1)} %copy-done.3, f32[256,1024]{1,0:T(8,128)S(1)} %copy-done.1, f32[256,1024]{1,0:T(8,128)S(1)} %copy-done.2, f32[8,256]{1,0:T(8,128)S(1)} %get-tuple-element.32.refs_4_.refs_3_, f32[520,128]{1,0:T(8,128)S(1)} %shard_map.97.refs_4_.refs_1_), custom_call_target="tpu_custom_call" | custom-call | flops 1 | bytes 1 | tf_op jit(solution)/shard_map/pallas_call | solution.py:59
  9.0 1.3 %collective-permute-start.6 = (f32[2,256,128]{2,1,0:T(8,128)S(1)}, f32[2,256,128]{2,1,0:T(8,128)S(1)}, u32[]{:S(2)}, u32[]{:S(2)}) collective-permute-start(f32[2,256,128]{2,1,0:T(8,128)S(1)} %shard_map.100.refs_5_), channel_id=1, source_target_pairs={{0,8},{4,12},{16,24},{20,28},{1,9},{5,13},{17,25},{21,29},{2,10},{... | collective-permute-start | bytes 786440 | tf_op jit(solution)/shard_map/ppermute | solution.py:601
  10.3 1.3 %collective-permute-start.3 = (f32[2,256,128]{2,1,0:T(8,128)S(1)}, f32[2,256,128]{2,1,0:T(8,128)S(1)}, u32[]{:S(2)}, u32[]{:S(2)}) collective-permute-start(f32[2,256,128]{2,1,0:T(8,128)S(1)} %shard_map.99.refs_1_), channel_id=1, source_target_pairs={{0,16},{4,20},{8,24},{12,28},{1,17},{5,21},{9,25},{13,29},{2,18},{... | collective-permute-start | bytes 786440 | tf_op jit(solution)/shard_map/ppermute | solution.py:601
  11.6 0.0 collective-permute-done.4.refs_2_
  11.7 2.9 %shard_map.101 = (bf16[6,512,256]{2,1,0:T(8,128)(2,1)S(1)}, f32[6,512,128]{2,1,0:T(8,128)S(1)}, f32[6,512,128]{2,1,0:T(8,128)S(1)}, f32[6,512,128]{2,1,0:T(8,128)S(1)}) custom-call(s32[1]{0:T(128)} %bitcast.refs_0_, f32[256,1536]{1,0:T(8,128)S(1)} %copy-done, f32[6,256,128]{2,1,0:T(8,128)S(1)} %collective-permute-done.4.refs_2_, ...), custom_call_target="tpu_custom_call" | custom-call | flops 1 | bytes 1 | tf_op jit(solution)/shard_map/pallas_call | solution.py:59
  14.5 2.5 %collective-permute-done.1.refs_4_.refs_1_.refs_3_ = f32[2,256,128]{2,1,0:T(8,128)S(1)} collective-permute-done((f32[2,256,128]{2,1,0:T(8,128)S(1)}, f32[2,256,128]{2,1,0:T(8,128)S(1)}, u32[]{:S(2)}, u32[]{:S(2)}) %collective-permute-start.1) | collective-permute-done | bytes 262176 | tf_op jit(solution)/shard_map/ppermute | solution.py:601
  17.0 0.0 collective-permute-done.5.refs_2_
  17.0 0.1 shard_map.102
  17.1 1.3 %collective-permute-start.9 = (f32[520,128]{1,0:T(8,128)S(1)}, f32[520,128]{1,0:T(8,128)S(1)}, u32[]{:S(2)}, u32[]{:S(2)}) collective-permute-start(f32[520,128]{1,0:T(8,128)S(1)} %get-tuple-element.52.refs_1_), channel_id=1, source_target_pairs={{0,16},{4,20},{8,24},{12,28},{1,17},{5,21},{9,25},{13,29},{2,18},{... | collective-permute-start | bytes 798728 | tf_op jit(solution)/shard_map/ppermute | solution.py:601
  18.4 3.1 %shard_map.103 = (f32[6,512,128]{2,1,0:T(8,128)S(1)}, f32[6,512,128]{2,1,0:T(8,128)S(1)}, f32[6,512,128]{2,1,0:T(8,128)S(1)}) custom-call(s32[1]{0:T(128)} %bitcast.refs_0_, f32[2,256,128]{2,1,0:T(8,128)S(1)} %collective-permute-done.1.refs_4_.refs_1_.refs_3_, ...), custom_call_target="tpu_custom_call", output_to_operand_aliasing={{0}: (3, {}), {1}: (4, {}), {2}: (5, {})} | custom-call | flops 1 | bytes 1 | tf_op jit(solution)/shard_map/pallas_call | solution.py:59
  21.6 1.3 %collective-permute-start.8 = (f32[2,256,128]{2,1,0:T(8,128)S(1)}, f32[2,256,128]{2,1,0:T(8,128)S(1)}, u32[]{:S(2)}, u32[]{:S(2)}) collective-permute-start(f32[2,256,128]{2,1,0:T(8,128)S(1)} %shard_map.104.refs_5_), channel_id=1, source_target_pairs={{0,8},{4,12},{16,24},{20,28},{1,9},{5,13},{17,25},{21,29},{2,10},{... | collective-permute-start | bytes 786440 | tf_op jit(solution)/shard_map/ppermute | solution.py:601
  22.9 0.0 collective-permute-done.6.refs_6_.refs_7_.refs_1_
  22.9 0.0 collective-permute-done.3.refs_4_.refs_1_
  23.0 1.3 %collective-permute-start.7 = (f32[2,512,128]{2,1,0:T(8,128)S(1)}, f32[2,512,128]{2,1,0:T(8,128)S(1)}, u32[]{:S(2)}, u32[]{:S(2)}) collective-permute-start(f32[2,512,128]{2,1,0:T(8,128)S(1)} %shard_map.105.refs_6_), channel_id=1, source_target_pairs={{0,24},{8,16},{20,28},{28,20},{1,25},{9,17},{21,29},{29,21},{2,26}... | collective-permute-start | bytes 1572872 | tf_op jit(solution)/shard_map/ppermute | solution.py:651
  24.3 3.3 %shard_map.106 = (f32[6,512,128]{2,1,0:T(8,128)S(1)}, f32[6,512,128]{2,1,0:T(8,128)S(1)}, f32[6,512,128]{2,1,0:T(8,128)S(1)}) custom-call(s32[1]{0:T(128)} %bitcast.refs_0_, f32[2,256,128]{2,1,0:T(8,128)S(1)} %collective-permute-done.3.refs_4_.refs_1_, ...), custom_call_target="tpu_custom_call", output_to_operand_aliasing={{0}: (3, {}), {1}: (4, {}), {2}: (5, {})} | custom-call | flops 1 | bytes 1 | tf_op jit(solution)/shard_map/pallas_call | solution.py:59
  27.6 3.1 %shard_map.107 = (f32[6,512,128]{2,1,0:T(8,128)S(1)}, f32[6,512,128]{2,1,0:T(8,128)S(1)}, f32[6,512,128]{2,1,0:T(8,128)S(1)}) custom-call(s32[1]{0:T(128)} %bitcast.refs_0_, f32[2,256,128]{2,1,0:T(8,128)S(1)} %collective-permute-done.6.refs_6_.refs_7_.refs_1_, ...), custom_call_target="tpu_custom_call", output_to_operand_aliasing={{0}: (3, {}), {1}: (4, {}), {2}: (5, {})} | custom-call | flops 1 | bytes 1 | tf_op jit(solution)/shard_map/pallas_call | solution.py:59
  30.7 2.0 %collective-permute-done.8.refs_5_.refs_1_ = f32[2,256,128]{2,1,0:T(8,128)S(1)} collective-permute-done((f32[2,256,128]{2,1,0:T(8,128)S(1)}, f32[2,256,128]{2,1,0:T(8,128)S(1)}, u32[]{:S(2)}, u32[]{:S(2)}) %collective-permute-start.8) | collective-permute-done | bytes 262176 | tf_op jit(solution)/shard_map/ppermute | solution.py:601
  32.7 0.0 collective-permute-done.9.refs_2_
  32.8 0.1 collective-permute-start.10
  32.9 1.8 %shard_map.109 = (f32[6,512,128]{2,1,0:T(8,128)S(1)}, f32[6,512,128]{2,1,0:T(8,128)S(1)}, f32[6,512,128]{2,1,0:T(8,128)S(1)}) custom-call(s32[1]{0:T(128)} %bitcast.refs_0_, f32[2,256,128]{2,1,0:T(8,128)S(1)} %collective-permute-done.8.refs_5_.refs_1_, ...), custom_call_target="tpu_custom_call", output_to_operand_aliasing={{0}: (3, {}), {1}: (4, {}), {2}: (5, {})} | custom-call | flops 1 | bytes 1 | tf_op jit(solution)/shard_map/pallas_call | solution.py:59
  34.6 0.0 collective-permute-done.10.refs_5_
  34.6 1.0 %shard_map.110 = (f32[256,1024]{1,0:T(8,128)S(1)}, f32[16,256]{1,0:T(8,128)S(1)}) custom-call(s32[1]{0:T(128)} %bitcast.refs_0_, bf16[8,256,256]{2,1,0:T(8,128)(2,1)S(1)} %get-tuple-element.56.refs_1_, f32[8,256,128]{2,1,0:T(8,128)S(1)} %get-tuple-element.37.refs_1_.refs_2_, f32[8,256]{1,0:T(8,128)S(1)} %get-tuple-element.32.refs_4_.refs_3_, ...), custom_call_target="tpu_custom_call" | custom-call | flops 1 | bytes 1 | tf_op jit(solution)/shard_map/pallas_call | solution.py:59
  35.6 1.6 %collective-permute-start.11 = (f32[16,256]{1,0:T(8,128)S(1)}, f32[16,256]{1,0:T(8,128)S(1)}, u32[]{:S(2)}, u32[]{:S(2)}) collective-permute-start(f32[16,256]{1,0:T(8,128)S(1)} %get-tuple-element.57.refs_6_.refs_0_), channel_id=1, source_target_pairs={{0,1},{1,0},{2,3},{3,2},{4,5},{5,4},{6,7},{7,6},{8,9},{9,8},{10,11... | collective-permute-start | bytes 49160 | tf_op jit(solution)/shard_map/ppermute | solution.py:615
  37.2 1.8 %shard_map.111 = (f32[6,512,128]{2,1,0:T(8,128)S(1)}, f32[6,512,128]{2,1,0:T(8,128)S(1)}, f32[6,512,128]{2,1,0:T(8,128)S(1)}) custom-call(s32[1]{0:T(128)} %bitcast.refs_0_, f32[2,256,128]{2,1,0:T(8,128)S(1)} %collective-permute-done.8.refs_5_.refs_1_, ...), custom_call_target="tpu_custom_call", output_to_operand_aliasing={{0}: (3, {}), {1}: (4, {}), {2}: (5, {})} | custom-call | flops 1 | bytes 1 | tf_op jit(solution)/shard_map/pallas_call | solution.py:59
  39.0 0.4 collective-permute-done.11.refs_1_
  39.4 0.0 collective-permute-done.7.refs_1_
  39.4 2.5 %shard_map.113.refs_6_ = f32[256,768]{1,0:T(8,128)S(1)} custom-call(s32[1]{0:T(128)} %bitcast.refs_0_, f32[2,512,128]{2,1,0:T(8,128)S(1)} %collective-permute-done.7.refs_1_, bf16[6,512,256]{2,1,0:T(8,128)(2,1)S(1)} %get-tuple-element.38.refs_2_, f32[6,512,128]{2,1,0:T(8,128)S(1)} %get-tuple-element.58.refs_2_.refs_3_, ...), custom_call_target="tpu_custom_call" | custom-call | flops 1 | bytes 1 | tf_op jit(solution)/shard_map/pallas_call | solution.py:59
  41.9 0.0 copy-start.5
  41.9 0.1 collective-permute-start.12
  42.0 2.6 %collective-permute-start.13 = (f32[16,256]{1,0:T(8,128)S(1)}, f32[16,256]{1,0:T(8,128)S(1)}, u32[]{:S(2)}, u32[]{:S(2)}) collective-permute-start(f32[16,256]{1,0:T(8,128)S(1)} %shard_map.112.refs_6_.refs_8_), channel_id=1, source_target_pairs={{0,2},{1,3},{2,0},{3,1},{4,6},{5,7},{6,4},{7,5},{8,10},{9,11},{10,... | collective-permute-start | bytes 49160 | tf_op jit(solution)/shard_map/ppermute | solution.py:615
  44.7 1.3 %shard_map.114.refs_7_ = f32[256,384]{1,0:T(8,128)S(1)} custom-call(s32[1]{0:T(128)} %bitcast.refs_0_, f32[2,512,128]{2,1,0:T(8,128)S(1)} %collective-permute-done.7.refs_1_, bf16[6,512,256]{2,1,0:T(8,128)(2,1)S(1)} %get-tuple-element.38.refs_2_, f32[6,512,128]{2,1,0:T(8,128)S(1)} %get-tuple-element.58.refs_2_.refs_3_, ...), custom_call_target="tpu_custom_call" | custom-call | flops 1 | bytes 1 | tf_op jit(solution)/shard_map/pallas_call | solution.py:59
  46.0 0.8 %collective-permute-done.13.refs_9_ = f32[16,256]{1,0:T(8,128)S(1)} collective-permute-done((f32[16,256]{1,0:T(8,128)S(1)}, f32[16,256]{1,0:T(8,128)S(1)}, u32[]{:S(2)}, u32[]{:S(2)}) %collective-permute-start.13) | collective-permute-done | bytes 16416 | tf_op jit(solution)/shard_map/ppermute | solution.py:615
  46.7 0.0 collective-permute-done.12.refs_6_
  46.7 0.0 copy-done.5
  46.7 2.4 %shard_map.115 = (f32[256,1024]{1,0:T(8,128)}, f32[256,1536]{1,0:T(8,128)}) custom-call(s32[1]{0:T(128)} %bitcast.refs_0_, f32[2,512,128]{2,1,0:T(8,128)S(1)} %collective-permute-done.7.refs_1_, bf16[6,512,256]{2,1,0:T(8,128)(2,1)S(1)} %get-tuple-element.38.refs_2_, f32[6,512,128]{2,1,0:T(8,128)S(1)} %get-tuple-element.58.refs_2_.refs_3_, ...), custom_call_target="tpu_custom_call" | custom-call | flops 1 | bytes 1 | tf_op jit(solution)/shard_map/pallas_call | solution.py:59
  (9 shorter events, 0.2 us)
Async XLA Ops:
  0.6 1.5 %copy-start.2 = (f32[256,1024]{1,0:T(8,128)S(1)}, f32[256,1024]{1,0:T(8,128)}, u32[]{:S(2)}) copy-start(f32[256,1024]{1,0:T(8,128)} %refs_2_.3) | copy-start | bytes 3145732
  0.6 1.8 %copy-start.1 = (f32[256,1024]{1,0:T(8,128)S(1)}, f32[256,1024]{1,0:T(8,128)}, u32[]{:S(2)}) copy-start(f32[256,1024]{1,0:T(8,128)} %refs_1_.4) | copy-start | bytes 3145732
  0.7 1.8 %copy-start.4 = (f32[8,256]{1,0:T(8,128)S(1)}, f32[8,256]{1,0:T(8,128)}, u32[]{:S(2)}) copy-start(f32[8,256]{1,0:T(8,128)} %refs_0_.2) | copy-start | bytes 24580
  2.0 1.6 %copy-start = (f32[256,1536]{1,0:T(8,128)S(1)}, f32[256,1536]{1,0:T(8,128)}, u32[]{:S(2)}) copy-start(f32[256,1536]{1,0:T(8,128)} %refs_1_.5) | copy-start | bytes 4718596
  2.0 1.6 %collective-permute-start = (f32[2,256,128]{2,1,0:T(8,128)S(1)}, f32[2,256,128]{2,1,0:T(8,128)S(1)}, u32[]{:S(2)}, u32[]{:S(2)}) collective-permute-start(f32[2,256,128]{2,1,0:T(8,128)S(1)} %pad_maximum_fusion.1), channel_id=1, source_target_pairs={{0,4},{4,0},{8,12},{12,8},{16,20},{20,16},{24,28},{28,24},{1,5},{5... | collective-permute-start | bytes 786440 | tf_op jit(solution)/shard_map/ppermute | solution.py:592
  3.3 2.0 %collective-permute-start.2 = (f32[2,520,128]{2,1,0:T(8,128)S(1)}, f32[2,520,128]{2,1,0:T(8,128)S(1)}, u32[]{:S(2)}, u32[]{:S(2)}) collective-permute-start(f32[2,520,128]{2,1,0:T(8,128)S(1)} %get-tuple-element.35.refs_1_), channel_id=1, source_target_pairs={{0,4},{4,0},{8,12},{12,8},{16,20},{20,16},{24,28},{28,24},{1,5},{5... | collective-permute-start | bytes 1597448 | tf_op jit(solution)/shard_map/ppermute | solution.py:592
  3.7 3.5 %copy-start.3 = (f32[256,1024]{1,0:T(8,128)S(1)}, f32[256,1024]{1,0:T(8,128)}, u32[]{:S(2)}) copy-start(f32[256,1024]{1,0:T(8,128)} %refs_0_.3) | copy-start | bytes 3145732
  3.8 7.9 %collective-permute-start.4 = (f32[6,256,128]{2,1,0:T(8,128)S(1)}, f32[6,256,128]{2,1,0:T(8,128)S(1)}, u32[]{:S(2)}, u32[]{:S(2)}) collective-permute-start(f32[6,256,128]{2,1,0:T(8,128)S(1)} %get-tuple-element.36.refs_3_), channel_id=1, source_target_pairs={{0,4},{4,0},{8,12},{12,8},{16,20},{20,16},{24,28},{28,24},{1,5},{5... | collective-permute-start | bytes 2359304 | tf_op jit(solution)/shard_map/ppermute | solution.py:592
  5.4 11.7 %collective-permute-start.5 = (f32[520,128]{1,0:T(8,128)S(1)}, f32[520,128]{1,0:T(8,128)S(1)}, u32[]{:S(2)}, u32[]{:S(2)}) collective-permute-start(f32[520,128]{1,0:T(8,128)S(1)} %shard_map.97.refs_4_.refs_1_), channel_id=1, source_target_pairs={{8,0},{12,4},{0,8},{4,12},{24,16},{28,20},{16,24},{20,28},{9,1},{1... | collective-permute-start | bytes 798728 | tf_op jit(solution)/shard_map/ppermute | solution.py:601
  6.0 11.1 %collective-permute-start.1 = (f32[2,256,128]{2,1,0:T(8,128)S(1)}, f32[2,256,128]{2,1,0:T(8,128)S(1)}, u32[]{:S(2)}, u32[]{:S(2)}) collective-permute-start(f32[2,256,128]{2,1,0:T(8,128)S(1)} %get-tuple-element.33.refs_0_.refs_3_.refs_1_), channel_id=1, source_target_pairs={{0,16},{4,20},{8,24},{12,28},{1,17},{5,21},{9,25},{13,29},{2,18},{... | collective-permute-start | bytes 786440 | tf_op jit(solution)/shard_map/ppermute | solution.py:601
  9.0 13.9 %collective-permute-start.6 = (f32[2,256,128]{2,1,0:T(8,128)S(1)}, f32[2,256,128]{2,1,0:T(8,128)S(1)}, u32[]{:S(2)}, u32[]{:S(2)}) collective-permute-start(f32[2,256,128]{2,1,0:T(8,128)S(1)} %shard_map.100.refs_5_), channel_id=1, source_target_pairs={{0,8},{4,12},{16,24},{20,28},{1,9},{5,13},{17,25},{21,29},{2,10},{... | collective-permute-start | bytes 786440 | tf_op jit(solution)/shard_map/ppermute | solution.py:601
  10.3 12.6 %collective-permute-start.3 = (f32[2,256,128]{2,1,0:T(8,128)S(1)}, f32[2,256,128]{2,1,0:T(8,128)S(1)}, u32[]{:S(2)}, u32[]{:S(2)}) collective-permute-start(f32[2,256,128]{2,1,0:T(8,128)S(1)} %shard_map.99.refs_1_), channel_id=1, source_target_pairs={{0,16},{4,20},{8,24},{12,28},{1,17},{5,21},{9,25},{13,29},{2,18},{... | collective-permute-start | bytes 786440 | tf_op jit(solution)/shard_map/ppermute | solution.py:601
  17.1 15.6 %collective-permute-start.9 = (f32[520,128]{1,0:T(8,128)S(1)}, f32[520,128]{1,0:T(8,128)S(1)}, u32[]{:S(2)}, u32[]{:S(2)}) collective-permute-start(f32[520,128]{1,0:T(8,128)S(1)} %get-tuple-element.52.refs_1_), channel_id=1, source_target_pairs={{0,16},{4,20},{8,24},{12,28},{1,17},{5,21},{9,25},{13,29},{2,18},{... | collective-permute-start | bytes 798728 | tf_op jit(solution)/shard_map/ppermute | solution.py:601
  21.6 11.1 %collective-permute-start.8 = (f32[2,256,128]{2,1,0:T(8,128)S(1)}, f32[2,256,128]{2,1,0:T(8,128)S(1)}, u32[]{:S(2)}, u32[]{:S(2)}) collective-permute-start(f32[2,256,128]{2,1,0:T(8,128)S(1)} %shard_map.104.refs_5_), channel_id=1, source_target_pairs={{0,8},{4,12},{16,24},{20,28},{1,9},{5,13},{17,25},{21,29},{2,10},{... | collective-permute-start | bytes 786440 | tf_op jit(solution)/shard_map/ppermute | solution.py:601
  23.0 16.4 %collective-permute-start.7 = (f32[2,512,128]{2,1,0:T(8,128)S(1)}, f32[2,512,128]{2,1,0:T(8,128)S(1)}, u32[]{:S(2)}, u32[]{:S(2)}) collective-permute-start(f32[2,512,128]{2,1,0:T(8,128)S(1)} %shard_map.105.refs_6_), channel_id=1, source_target_pairs={{0,24},{8,16},{20,28},{28,20},{1,25},{9,17},{21,29},{29,21},{2,26}... | collective-permute-start | bytes 1572872 | tf_op jit(solution)/shard_map/ppermute | solution.py:651
  32.8 1.9 %collective-permute-start.10 = (f32[520,128]{1,0:T(8,128)S(1)}, f32[520,128]{1,0:T(8,128)S(1)}, u32[]{:S(2)}, u32[]{:S(2)}) collective-permute-start(f32[520,128]{1,0:T(8,128)S(1)} %shard_map.108.refs_6_.refs_4_), channel_id=1, source_target_pairs={{0,4},{4,0},{8,12},{12,8},{16,20},{20,16},{24,28},{28,24},{1,5},{5... | collective-permute-start | bytes 798728 | tf_op jit(solution)/shard_map/ppermute | solution.py:592
  35.6 3.8 %collective-permute-start.11 = (f32[16,256]{1,0:T(8,128)S(1)}, f32[16,256]{1,0:T(8,128)S(1)}, u32[]{:S(2)}, u32[]{:S(2)}) collective-permute-start(f32[16,256]{1,0:T(8,128)S(1)} %get-tuple-element.57.refs_6_.refs_0_), channel_id=1, source_target_pairs={{0,1},{1,0},{2,3},{3,2},{4,5},{5,4},{6,7},{7,6},{8,9},{9,8},{10,11... | collective-permute-start | bytes 49160 | tf_op jit(solution)/shard_map/ppermute | solution.py:615
  41.9 4.8 %copy-start.5 = (f32[1024]{0:T(1024)S(1)}, f32[1024]{0:T(1024)}, u32[]{:S(2)}) copy-start(f32[1024]{0:T(1024)} %param.12) | copy-start | bytes 12292
  41.9 4.8 %collective-permute-start.12 = (f32[256,768]{1,0:T(8,128)S(1)}, f32[256,768]{1,0:T(8,128)S(1)}, u32[]{:S(2)}, u32[]{:S(2)}) collective-permute-start(f32[256,768]{1,0:T(8,128)S(1)} %shard_map.113.refs_6_), channel_id=1, source_target_pairs={{0,4},{4,0},{8,12},{12,8},{16,20},{20,16},{24,28},{28,24},{1,5},{5... | collective-permute-start | bytes 2359304 | tf_op jit(solution)/shard_map/ppermute | solution.py:592
  42.0 4.7 %collective-permute-start.13 = (f32[16,256]{1,0:T(8,128)S(1)}, f32[16,256]{1,0:T(8,128)S(1)}, u32[]{:S(2)}, u32[]{:S(2)}) collective-permute-start(f32[16,256]{1,0:T(8,128)S(1)} %shard_map.112.refs_6_.refs_8_), channel_id=1, source_target_pairs={{0,2},{1,3},{2,0},{3,1},{4,6},{5,7},{6,4},{7,5},{8,10},{9,11},{10,... | collective-permute-start | bytes 49160 | tf_op jit(solution)/shard_map/ppermute | solution.py:615

commit v11 on v8

--- a/solution.py
+++ b/solution.py
@@ -296,6 +296,19 @@
     gather(count - 1, before)
 
 
+def run_loop(trips, count, score, soften, gather):
+    def trip(j, carry):
+        run(
+            count,
+            lambda i: score((j, i)),
+            lambda i, scores: soften((j, i), scores),
+            lambda i, terms: gather((j, i), terms),
+        )
+        return carry
+
+    lax.fori_loop(0, trips, trip, 0)
+
+
 def fill_terms(kv_ref, keys_ref, values_ref):
     k_high, k_low = split(kv_ref[0].T)
     keys_ref[:HD] = k_high
@@ -341,20 +354,22 @@
     seen = lax.broadcasted_iota(jnp.int32, (tokens, tokens), 1)
     seen = seen <= lax.broadcasted_iota(jnp.int32, (tokens, tokens), 0)
 
-    def where(i):
+    def where(step):
+        j, i = step
         t = i % 2
-        return i // 2, slice(t * tokens, (t + 1) * tokens), slice(0, (t + 1) * tokens)
+        return 2 * j + i // 2, slice(t * tokens, (t + 1) * tokens), slice(0, (t + 1) * tokens)
 
     def score(i):
         g, rows, keys = where(i)
         at = pl.ds(pl.multiple_of((core * group + g) * HD, HD), HD)
         mine, other = q_ref[:, at], q_other_ref[g]
-        queries = jnp.where(first, mine, other) if i % 2 == 0 else jnp.where(first, other, mine)
+        early = i[1] % 2 == 0
+        queries = jnp.where(first, mine, other) if early else jnp.where(first, other, mine)
         pair = jnp.concatenate(split(queries * factor), axis=1)
         q_out[g, rows] = pair
         s = dot(score_terms(pair), keys_ref[:, keys])
         edge = jnp.where(seen, s[:, rows], NEGATIVE)
-        return edge if i % 2 == 0 else jnp.concatenate([s[:, :tokens], edge], axis=1)
+        return edge if early else jnp.concatenate([s[:, :tokens], edge], axis=1)
 
     def soften(i, s):
         g, rows, _ = where(i)
@@ -367,7 +382,7 @@
         g, rows, keys = where(i)
         acc_out[g, rows] = summed(*terms, values_ref[keys])
 
-    run(2 * group, score, soften, gather)
+    run_loop(group // 2, 4, score, soften, gather)
 
 
 def term_scratch(keys):
@@ -390,10 +405,13 @@
 
 def later_kernel(distance, parts, heads, me_ref, kv_ref, q_ref, acc_ref, peak_ref, total_ref, acc_out, peak_out, total_out, keys_ref, values_ref):
     size = q_ref.shape[1] // parts
+    per = 2 if len(heads) % 2 == 0 else 1
     chip = me_ref[0] >> 1
 
     def where(i):
-        return heads[i // parts], slice(i % parts * size, (i % parts + 1) * size)
+        j, n = i
+        head = heads[0] + j * per + n // parts
+        return head, slice(n % parts * size, (n % parts + 1) * size)
 
     def score(i):
         return dot(score_terms(q_ref[where(i)]), keys_ref[...])
@@ -414,7 +432,7 @@
     @pl.when(lax.bitwise_xor(chip, distance) < chip)
     def _():
         fill_terms(kv_ref, keys_ref, values_ref)
-        run(parts * len(heads), score, soften, gather)
+        run_loop(len(heads) // per, parts * per, score, soften, gather)
 
 
 def later_stage(me, distance, heads, kv, q_terms, acc, peak, total, after, parts=4):
@@ -469,30 +487,40 @@
         ]
 
     def finish(n, acc, total):
-        out_ref[:, n * HD : (n + 1) * HD] = acc / jnp.sum(total, axis=1, keepdims=True)
+        to = pl.ds(pl.multiple_of(n * HD, HD), HD)
+        out_ref[:, to] = acc / jnp.sum(total, axis=1, keepdims=True)
         if columns is not None:
             own_copies[n].start()
 
     def score(n):
-        return dot(score_terms(q_ref[heads[n], at]), keys_ref[...])
+        return dot(score_terms(q_ref[heads[0] + n, at]), keys_ref[...])
 
     def soften(n, s):
-        old = peak_ref[heads[n], at]
+        old = peak_ref[heads[0] + n, at]
         peak = jnp.maximum(jnp.max(lane_max(s), axis=1, keepdims=True), old)
         shrink = jnp.exp2(old - peak)
-        return *weigh(s, peak, total_ref[heads[n], at] * shrink), shrink
+        return *weigh(s, peak, total_ref[heads[0] + n, at] * shrink), shrink
 
     def gather(n, terms):
         high, low, total, shrink = terms
         new = summed(high, low, values_ref[...])
-        finish(n, acc_ref[heads[n], at] * shrink + new, total)
+        finish(n, acc_ref[heads[0] + n, at] * shrink + new, total)
 
     visible = lax.bitwise_xor(chip, distance) < chip
 
     @pl.when(visible)
     def _():
         fill_terms(kv_ref, keys_ref, values_ref)
-        run(len(heads), score, soften, gather)
+        if columns is None and len(heads) % 2 == 0:
+            run_loop(
+                len(heads) // 2,
+                2,
+                lambda i: score(2 * i[0] + i[1]),
+                lambda i, scores: soften(2 * i[0] + i[1], scores),
+                lambda i, terms: gather(2 * i[0] + i[1], terms),
+            )
+        else:
+            run(len(heads), score, soften, gather)
 
     @pl.when(jnp.logical_not(visible))
     def _():

time: 44.3 us -> 45.2 us (1.020)
  Pallas kernels: 22.3 us -> 23.6 us
    pallas_call x17, Pallas kernels: 22.3 us -> 23.6 us  [call(): return lambda *operands: made(*operands, *after)]
  transfers between devices with their start and end apart: 12 -> 12, of which waited for: 3 -> 3; matrix products, arithmetic and copies ran while one was open for 0% -> 0% of each run, Pallas kernels for 40% -> 41%
where the time goes in v11:
time: 45.2 us; the launch traced here: 44.9 us
  Pallas kernels  23.6 us (52%)
  starting transfers between devices  11 us (24%)
  waiting for transfers between devices  7.73 us (17%)
  other arithmetic  1.31 us (3%)
  between operations  0.93 us (2%)
    pallas_call x17, Pallas kernels, call(): return lambda *operands: made(*operands, *after)  23.6 us
    ppermute x4, waiting for transfers between devices, across(): return lax.ppermute(array, 'ctx', pairs)  6.99 us
    ppermute x4, starting transfers between devices, across(): return lax.ppermute(array, 'ctx', pairs)  4.46 us
    ppermute x2, starting transfers between devices, exchanged(): return lax.ppermute(array, 'head', [(i, i ^ step) for i in range(heads)])  4.2 us
    another operation x2, other arithmetic, halves(): jnp.stack([jnp.where(core == 0, b, a) for a, b in zip(early, late)])  1.3 us
    ppermute x1, starting transfers between devices, body(): arrived[3] = lax.ppermute(relay, 'ctx', [(0, 6), (2, 4), (5, 7), (7, 5)])  1.29 us
    ppermute x5, starting transfers between devices, swap(): return lax.ppermute(array, 'ctx', swap_pairs)  1.05 us
  transfers between devices with their start and end apart: 12, of which 3 were waited for; matrix products, arithmetic and copies ran while one was open for 0% of the time, Pallas kernels for 41%

profile of v11, /device:TPU:6, one launch (start us, length us, event | category | flops | bytes accessed | tf_op | source)
XLA Modules:
  0.0 44.9 jit_solution(13560371793791748472)
XLA Ops:
  0.6 0.0 copy-start.2
  0.6 0.0 copy-start.1
  0.7 0.0 copy-start.4
  0.7 1.3 %select_bitcast_fusion = (f32[1,256,128]{2,1,0:T(8,128)S(1)}, f32[1,256,128]{2,1,0:T(8,128)S(1)}, f32[1,256,128]{2,1,0:T(8,128)S(1)}, f32[1,256,128]{2,1,0:T(8,128)S(1)}) fusion(f32[256,256]{1,0:T(8,128)} %param.15, pred[]{:T(512)S(6)} %eq.2, f32[256,256]{1,0:T(8,128)} %param.14), kind=kLoop, calls=%fused_computation.2 | loop fusion | flops 131072 | bytes 1048577 | tf_op jit(solution)/shard_map/stack | solution.py:255
  2.0 0.0 copy-start
  2.0 0.1 collective-permute-start
  2.1 0.0 copy-done.2
  2.1 0.3 copy-done.1
  2.4 0.0 copy-done.4
  2.4 0.9 %shard_map.95 = (f32[2,520,128]{2,1,0:T(8,128)S(1)}, f32[8,256]{1,0:T(8,128)S(1)}) custom-call(f32[8,256]{1,0:T(8,128)S(1)} %copy-done.4, f32[256,1024]{1,0:T(8,128)S(1)} %copy-done.1, f32[256,1024]{1,0:T(8,128)S(1)} %copy-done.2, f32[2,256,128]{2,1,0:T(8,128)S(1)} %pad_maximum_fusion.refs_3_.refs_1_), custom_call_target="tpu_custom_call" | custom-call | flops 1 | bytes 1 | tf_op jit(solution)/shard_map/pallas_call | solution.py:59
  3.3 0.3 collective-permute-start.3
  3.6 0.0 collective-permute-done.refs_2_
  3.6 0.0 copy-done
  3.6 0.1 shard_map.96
  3.7 0.0 copy-start.3
  3.8 0.4 collective-permute-start.2
  4.1 1.3 %collective-permute-start.1 = (f32[2,512,128]{2,1,0:T(8,128)S(1)}, f32[2,512,128]{2,1,0:T(8,128)S(1)}, u32[]{:S(2)}, u32[]{:S(2)}) collective-permute-start(f32[2,512,128]{2,1,0:T(8,128)S(1)} %get-tuple-element.26.refs_0_.refs_3_.refs_1_), channel_id=1, source_target_pairs={{0,16},{4,20},{8,24},{12,28},{1,17},{5,21},{9,25},{13,29},{2,18},{... | collective-permute-start | bytes 1572872 | tf_op jit(solution)/shard_map/ppermute | solution.py:622
  5.4 0.0 collective-permute-done.3.refs_2_.refs_6_
  5.5 0.6 %collective-permute-start.6 = (f32[520,128]{1,0:T(8,128)S(1)}, f32[520,128]{1,0:T(8,128)S(1)}, u32[]{:S(2)}, u32[]{:S(2)}) collective-permute-start(f32[520,128]{1,0:T(8,128)S(1)} %shard_map.97.refs_4_.refs_1_), channel_id=1, source_target_pairs={{8,0},{12,4},{0,8},{4,12},{24,16},{28,20},{16,24},{20,28},{9,1},{1... | collective-permute-start | bytes 798728 | tf_op jit(solution)/shard_map/ppermute | solution.py:622
  6.1 0.0 copy-done.3
  6.1 1.7 %shard_map.98 = (f32[8,256,128]{2,1,0:T(8,128)S(1)}, bf16[8,256,256]{2,1,0:T(8,128)(2,1)S(1)}) custom-call(f32[256,1024]{1,0:T(8,128)S(1)} %copy-done.3, f32[256,1024]{1,0:T(8,128)S(1)} %copy-done.1, f32[256,1024]{1,0:T(8,128)S(1)} %copy-done.2, f32[8,256]{1,0:T(8,128)S(1)} %get-tuple-element.25.refs_4_.refs_3_, f32[520,128]{1,0:T(8,128)S(1)} %shard_map.97.refs_4_.refs_1_), custom_call_target="tpu_custom_call" | custom-call | flops 1 | bytes 1 | tf_op jit(solution)/shard_map/pallas_call | solution.py:59
  7.9 1.3 %collective-permute-start.5 = (f32[2,512,128]{2,1,0:T(8,128)S(1)}, f32[2,512,128]{2,1,0:T(8,128)S(1)}, u32[]{:S(2)}, u32[]{:S(2)}) collective-permute-start(f32[2,512,128]{2,1,0:T(8,128)S(1)} %shard_map.99.refs_4_), channel_id=1, source_target_pairs={{0,8},{4,12},{16,24},{20,28},{1,9},{5,13},{17,25},{21,29},{2,10},{... | collective-permute-start | bytes 1572872 | tf_op jit(solution)/shard_map/ppermute | solution.py:622
  9.2 0.0 collective-permute-done.2.refs_2_
  9.2 3.2 %shard_map.100 = (bf16[6,512,256]{2,1,0:T(8,128)(2,1)S(1)}, f32[6,512,128]{2,1,0:T(8,128)S(1)}, f32[6,512,128]{2,1,0:T(8,128)S(1)}, f32[6,512,128]{2,1,0:T(8,128)S(1)}) custom-call(s32[1]{0:T(128)} %bitcast.refs_0_, f32[256,1536]{1,0:T(8,128)S(1)} %copy-done, f32[6,256,128]{2,1,0:T(8,128)S(1)} %collective-permute-done.2.refs_2_, ...), custom_call_target="tpu_custom_call" | custom-call | flops 1 | bytes 1 | tf_op jit(solution)/shard_map/pallas_call | solution.py:59
  12.4 2.4 %collective-permute-done.6.refs_2_ = f32[520,128]{1,0:T(8,128)S(1)} collective-permute-done((f32[520,128]{1,0:T(8,128)S(1)}, f32[520,128]{1,0:T(8,128)S(1)}, u32[]{:S(2)}, u32[]{:S(2)}) %collective-permute-start.6) | collective-permute-done | bytes 266272 | tf_op jit(solution)/shard_map/ppermute | solution.py:622
  14.8 0.1 shard_map.102
  14.8 1.3 %collective-permute-start.7 = (f32[520,128]{1,0:T(8,128)S(1)}, f32[520,128]{1,0:T(8,128)S(1)}, u32[]{:S(2)}, u32[]{:S(2)}) collective-permute-start(f32[520,128]{1,0:T(8,128)S(1)} %get-tuple-element.38.refs_1_), channel_id=1, source_target_pairs={{0,16},{4,20},{8,24},{12,28},{1,17},{5,21},{9,25},{13,29},{2,18},{... | collective-permute-start | bytes 798728 | tf_op jit(solution)/shard_map/ppermute | solution.py:622
  16.1 4.6 %collective-permute-done.1.refs_2_.refs_1_ = f32[2,512,128]{2,1,0:T(8,128)S(1)} collective-permute-done((f32[2,512,128]{2,1,0:T(8,128)S(1)}, f32[2,512,128]{2,1,0:T(8,128)S(1)}, u32[]{:S(2)}, u32[]{:S(2)}) %collective-permute-start.1) | collective-permute-done | bytes 524320 | tf_op jit(solution)/shard_map/ppermute | solution.py:622
  20.8 1.3 %collective-permute-start.4 = (f32[2,512,128]{2,1,0:T(8,128)S(1)}, f32[2,512,128]{2,1,0:T(8,128)S(1)}, u32[]{:S(2)}, u32[]{:S(2)}) collective-permute-start(f32[2,512,128]{2,1,0:T(8,128)S(1)} %shard_map.101.refs_7_), channel_id=1, source_target_pairs={{0,24},{8,16},{20,28},{28,20},{1,25},{9,17},{21,29},{29,21},{2,26}... | collective-permute-start | bytes 1572872 | tf_op jit(solution)/shard_map/ppermute | solution.py:660
  22.1 4.6 %shard_map.103 = (f32[6,512,128]{2,1,0:T(8,128)S(1)}, f32[6,512,128]{2,1,0:T(8,128)S(1)}, f32[6,512,128]{2,1,0:T(8,128)S(1)}) custom-call(s32[1]{0:T(128)} %bitcast.refs_0_, f32[2,512,128]{2,1,0:T(8,128)S(1)} %collective-permute-done.1.refs_2_.refs_1_, ...), custom_call_target="tpu_custom_call", output_to_operand_aliasing={{0}: (3, {}), {1}: (4, {}), {2}: (5, {})} | custom-call | flops 1 | bytes 1 | tf_op jit(solution)/shard_map/pallas_call | solution.py:59
  26.7 0.0 collective-permute-done.5.refs_5_.refs_1_
  26.7 0.0 collective-permute-done.7.refs_2_
  26.8 0.1 collective-permute-start.8
  26.8 2.7 %shard_map.105 = (f32[6,512,128]{2,1,0:T(8,128)S(1)}, f32[6,512,128]{2,1,0:T(8,128)S(1)}, f32[6,512,128]{2,1,0:T(8,128)S(1)}) custom-call(s32[1]{0:T(128)} %bitcast.refs_0_, f32[2,512,128]{2,1,0:T(8,128)S(1)} %collective-permute-done.5.refs_5_.refs_1_, ...), custom_call_target="tpu_custom_call", output_to_operand_aliasing={{0}: (3, {}), {1}: (4, {}), {2}: (5, {})} | custom-call | flops 1 | bytes 1 | tf_op jit(solution)/shard_map/pallas_call | solution.py:59
  29.6 0.0 collective-permute-done.8.refs_5_
  29.6 1.0 %shard_map.106 = (f32[256,1024]{1,0:T(8,128)S(1)}, f32[16,256]{1,0:T(8,128)S(1)}) custom-call(s32[1]{0:T(128)} %bitcast.refs_0_, bf16[8,256,256]{2,1,0:T(8,128)(2,1)S(1)} %get-tuple-element.42.refs_1_, f32[8,256,128]{2,1,0:T(8,128)S(1)} %get-tuple-element.29.refs_1_.refs_2_, f32[8,256]{1,0:T(8,128)S(1)} %get-tuple-element.25.refs_4_.refs_3_, ...), custom_call_target="tpu_custom_call" | custom-call | flops 1 | bytes 1 | tf_op jit(solution)/shard_map/pallas_call | solution.py:59
  30.6 1.6 %collective-permute-start.9 = (f32[16,256]{1,0:T(8,128)S(1)}, f32[16,256]{1,0:T(8,128)S(1)}, u32[]{:S(2)}, u32[]{:S(2)}) collective-permute-start(f32[16,256]{1,0:T(8,128)S(1)} %get-tuple-element.43.refs_6_.refs_0_), channel_id=1, source_target_pairs={{0,1},{1,0},{2,3},{3,2},{4,5},{5,4},{6,7},{7,6},{8,9},{9,8},{10,11... | collective-permute-start | bytes 49160 | tf_op jit(solution)/shard_map/ppermute | solution.py:635
  32.2 2.7 %shard_map.107 = (f32[6,512,128]{2,1,0:T(8,128)S(1)}, f32[6,512,128]{2,1,0:T(8,128)S(1)}, f32[6,512,128]{2,1,0:T(8,128)S(1)}) custom-call(s32[1]{0:T(128)} %bitcast.refs_0_, f32[2,512,128]{2,1,0:T(8,128)S(1)} %collective-permute-done.5.refs_5_.refs_1_, ...), custom_call_target="tpu_custom_call", output_to_operand_aliasing={{0}: (3, {}), {1}: (4, {}), {2}: (5, {})} | custom-call | flops 1 | bytes 1 | tf_op jit(solution)/shard_map/pallas_call | solution.py:59
  34.9 0.0 collective-permute-done.9.refs_1_
  35.0 0.0 collective-permute-done.4.refs_1_
  35.0 2.6 %shard_map.109.refs_6_ = f32[256,768]{1,0:T(8,128)S(1)} custom-call(s32[1]{0:T(128)} %bitcast.refs_0_, f32[2,512,128]{2,1,0:T(8,128)S(1)} %collective-permute-done.4.refs_1_, bf16[6,512,256]{2,1,0:T(8,128)(2,1)S(1)} %get-tuple-element.31.refs_2_, f32[6,512,128]{2,1,0:T(8,128)S(1)} %get-tuple-element.44.refs_2_.refs_3_, ...), custom_call_target="tpu_custom_call" | custom-call | flops 1 | bytes 1 | tf_op jit(solution)/shard_map/pallas_call | solution.py:59
  37.6 0.0 copy-start.5
  37.6 0.3 collective-permute-start.10
  37.9 2.6 %collective-permute-start.11 = (f32[16,256]{1,0:T(8,128)S(1)}, f32[16,256]{1,0:T(8,128)S(1)}, u32[]{:S(2)}, u32[]{:S(2)}) collective-permute-start(f32[16,256]{1,0:T(8,128)S(1)} %shard_map.108.refs_6_.refs_8_), channel_id=1, source_target_pairs={{0,2},{1,3},{2,0},{3,1},{4,6},{5,7},{6,4},{7,5},{8,10},{9,11},{10,... | collective-permute-start | bytes 49160 | tf_op jit(solution)/shard_map/ppermute | solution.py:635
  40.5 1.3 %shard_map.110.refs_7_ = f32[256,384]{1,0:T(8,128)S(1)} custom-call(s32[1]{0:T(128)} %bitcast.refs_0_, f32[2,512,128]{2,1,0:T(8,128)S(1)} %collective-permute-done.4.refs_1_, bf16[6,512,256]{2,1,0:T(8,128)(2,1)S(1)} %get-tuple-element.31.refs_2_, f32[6,512,128]{2,1,0:T(8,128)S(1)} %get-tuple-element.44.refs_2_.refs_3_, ...), custom_call_target="tpu_custom_call" | custom-call | flops 1 | bytes 1 | tf_op jit(solution)/shard_map/pallas_call | solution.py:59
  41.8 0.7 %collective-permute-done.11.refs_9_ = f32[16,256]{1,0:T(8,128)S(1)} collective-permute-done((f32[16,256]{1,0:T(8,128)S(1)}, f32[16,256]{1,0:T(8,128)S(1)}, u32[]{:S(2)}, u32[]{:S(2)}) %collective-permute-start.11) | collective-permute-done | bytes 16416 | tf_op jit(solution)/shard_map/ppermute | solution.py:635
  42.5 0.0 collective-permute-done.10.refs_6_
  42.5 0.0 copy-done.5
  42.5 2.4 %shard_map.111 = (f32[256,1024]{1,0:T(8,128)}, f32[256,1536]{1,0:T(8,128)}) custom-call(s32[1]{0:T(128)} %bitcast.refs_0_, f32[2,512,128]{2,1,0:T(8,128)S(1)} %collective-permute-done.4.refs_1_, bf16[6,512,256]{2,1,0:T(8,128)(2,1)S(1)} %get-tuple-element.31.refs_2_, f32[6,512,128]{2,1,0:T(8,128)S(1)} %get-tuple-element.44.refs_2_.refs_3_, ...), custom_call_target="tpu_custom_call" | custom-call | flops 1 | bytes 1 | tf_op jit(solution)/shard_map/pallas_call | solution.py:59
  (7 shorter events, 0.2 us)
Async XLA Ops:
  0.6 1.5 %copy-start.2 = (f32[256,1024]{1,0:T(8,128)S(1)}, f32[256,1024]{1,0:T(8,128)}, u32[]{:S(2)}) copy-start(f32[256,1024]{1,0:T(8,128)} %refs_2_.3) | copy-start | bytes 3145732
  0.6 1.8 %copy-start.1 = (f32[256,1024]{1,0:T(8,128)S(1)}, f32[256,1024]{1,0:T(8,128)}, u32[]{:S(2)}) copy-start(f32[256,1024]{1,0:T(8,128)} %refs_1_.4) | copy-start | bytes 3145732
  0.7 1.8 %copy-start.4 = (f32[8,256]{1,0:T(8,128)S(1)}, f32[8,256]{1,0:T(8,128)}, u32[]{:S(2)}) copy-start(f32[8,256]{1,0:T(8,128)} %refs_0_.2) | copy-start | bytes 24580
  2.0 1.6 %copy-start = (f32[256,1536]{1,0:T(8,128)S(1)}, f32[256,1536]{1,0:T(8,128)}, u32[]{:S(2)}) copy-start(f32[256,1536]{1,0:T(8,128)} %refs_1_.5) | copy-start | bytes 4718596
  2.0 1.6 %collective-permute-start = (f32[2,256,128]{2,1,0:T(8,128)S(1)}, f32[2,256,128]{2,1,0:T(8,128)S(1)}, u32[]{:S(2)}, u32[]{:S(2)}) collective-permute-start(f32[2,256,128]{2,1,0:T(8,128)S(1)} %pad_maximum_fusion.1), channel_id=1, source_target_pairs={{0,4},{4,0},{8,12},{12,8},{16,20},{20,16},{24,28},{28,24},{1,5},{5... | collective-permute-start | bytes 786440 | tf_op jit(solution)/shard_map/ppermute | solution.py:613
  3.3 2.1 %collective-permute-start.3 = (f32[2,520,128]{2,1,0:T(8,128)S(1)}, f32[2,520,128]{2,1,0:T(8,128)S(1)}, u32[]{:S(2)}, u32[]{:S(2)}) collective-permute-start(f32[2,520,128]{2,1,0:T(8,128)S(1)} %get-tuple-element.28.refs_1_), channel_id=1, source_target_pairs={{0,4},{4,0},{8,12},{12,8},{16,20},{20,16},{24,28},{28,24},{1,5},{5... | collective-permute-start | bytes 1597448 | tf_op jit(solution)/shard_map/ppermute | solution.py:613
  3.7 2.4 %copy-start.3 = (f32[256,1024]{1,0:T(8,128)S(1)}, f32[256,1024]{1,0:T(8,128)}, u32[]{:S(2)}) copy-start(f32[256,1024]{1,0:T(8,128)} %refs_0_.3) | copy-start | bytes 3145732
  3.8 5.4 %collective-permute-start.2 = (f32[6,256,128]{2,1,0:T(8,128)S(1)}, f32[6,256,128]{2,1,0:T(8,128)S(1)}, u32[]{:S(2)}, u32[]{:S(2)}) collective-permute-start(f32[6,256,128]{2,1,0:T(8,128)S(1)} %get-tuple-element.27.refs_3_), channel_id=1, source_target_pairs={{0,4},{4,0},{8,12},{12,8},{16,20},{20,16},{24,28},{28,24},{1,5},{5... | collective-permute-start | bytes 2359304 | tf_op jit(solution)/shard_map/ppermute | solution.py:613
  4.1 16.6 %collective-permute-start.1 = (f32[2,512,128]{2,1,0:T(8,128)S(1)}, f32[2,512,128]{2,1,0:T(8,128)S(1)}, u32[]{:S(2)}, u32[]{:S(2)}) collective-permute-start(f32[2,512,128]{2,1,0:T(8,128)S(1)} %get-tuple-element.26.refs_0_.refs_3_.refs_1_), channel_id=1, source_target_pairs={{0,16},{4,20},{8,24},{12,28},{1,17},{5,21},{9,25},{13,29},{2,18},{... | collective-permute-start | bytes 1572872 | tf_op jit(solution)/shard_map/ppermute | solution.py:622
  5.5 9.3 %collective-permute-start.6 = (f32[520,128]{1,0:T(8,128)S(1)}, f32[520,128]{1,0:T(8,128)S(1)}, u32[]{:S(2)}, u32[]{:S(2)}) collective-permute-start(f32[520,128]{1,0:T(8,128)S(1)} %shard_map.97.refs_4_.refs_1_), channel_id=1, source_target_pairs={{8,0},{12,4},{0,8},{4,12},{24,16},{28,20},{16,24},{20,28},{9,1},{1... | collective-permute-start | bytes 798728 | tf_op jit(solution)/shard_map/ppermute | solution.py:622
  7.9 18.8 %collective-permute-start.5 = (f32[2,512,128]{2,1,0:T(8,128)S(1)}, f32[2,512,128]{2,1,0:T(8,128)S(1)}, u32[]{:S(2)}, u32[]{:S(2)}) collective-permute-start(f32[2,512,128]{2,1,0:T(8,128)S(1)} %shard_map.99.refs_4_), channel_id=1, source_target_pairs={{0,8},{4,12},{16,24},{20,28},{1,9},{5,13},{17,25},{21,29},{2,10},{... | collective-permute-start | bytes 1572872 | tf_op jit(solution)/shard_map/ppermute | solution.py:622
  14.8 11.9 %collective-permute-start.7 = (f32[520,128]{1,0:T(8,128)S(1)}, f32[520,128]{1,0:T(8,128)S(1)}, u32[]{:S(2)}, u32[]{:S(2)}) collective-permute-start(f32[520,128]{1,0:T(8,128)S(1)} %get-tuple-element.38.refs_1_), channel_id=1, source_target_pairs={{0,16},{4,20},{8,24},{12,28},{1,17},{5,21},{9,25},{13,29},{2,18},{... | collective-permute-start | bytes 798728 | tf_op jit(solution)/shard_map/ppermute | solution.py:622
  20.8 14.2 %collective-permute-start.4 = (f32[2,512,128]{2,1,0:T(8,128)S(1)}, f32[2,512,128]{2,1,0:T(8,128)S(1)}, u32[]{:S(2)}, u32[]{:S(2)}) collective-permute-start(f32[2,512,128]{2,1,0:T(8,128)S(1)} %shard_map.101.refs_7_), channel_id=1, source_target_pairs={{0,24},{8,16},{20,28},{28,20},{1,25},{9,17},{21,29},{29,21},{2,26}... | collective-permute-start | bytes 1572872 | tf_op jit(solution)/shard_map/ppermute | solution.py:660
  26.8 2.8 %collective-permute-start.8 = (f32[520,128]{1,0:T(8,128)S(1)}, f32[520,128]{1,0:T(8,128)S(1)}, u32[]{:S(2)}, u32[]{:S(2)}) collective-permute-start(f32[520,128]{1,0:T(8,128)S(1)} %shard_map.104.refs_6_.refs_4_), channel_id=1, source_target_pairs={{0,4},{4,0},{8,12},{12,8},{16,20},{20,16},{24,28},{28,24},{1,5},{5... | collective-permute-start | bytes 798728 | tf_op jit(solution)/shard_map/ppermute | solution.py:613
  30.6 4.3 %collective-permute-start.9 = (f32[16,256]{1,0:T(8,128)S(1)}, f32[16,256]{1,0:T(8,128)S(1)}, u32[]{:S(2)}, u32[]{:S(2)}) collective-permute-start(f32[16,256]{1,0:T(8,128)S(1)} %get-tuple-element.43.refs_6_.refs_0_), channel_id=1, source_target_pairs={{0,1},{1,0},{2,3},{3,2},{4,5},{5,4},{6,7},{7,6},{8,9},{9,8},{10,11... | collective-permute-start | bytes 49160 | tf_op jit(solution)/shard_map/ppermute | solution.py:635
  37.6 4.9 %copy-start.5 = (f32[1024]{0:T(1024)S(1)}, f32[1024]{0:T(1024)}, u32[]{:S(2)}) copy-start(f32[1024]{0:T(1024)} %param.12) | copy-start | bytes 12292
  37.6 4.9 %collective-permute-start.10 = (f32[256,768]{1,0:T(8,128)S(1)}, f32[256,768]{1,0:T(8,128)S(1)}, u32[]{:S(2)}, u32[]{:S(2)}) collective-permute-start(f32[256,768]{1,0:T(8,128)S(1)} %shard_map.109.refs_6_), channel_id=1, source_target_pairs={{0,4},{4,0},{8,12},{12,8},{16,20},{20,16},{24,28},{28,24},{1,5},{5... | collective-permute-start | bytes 2359304 | tf_op jit(solution)/shard_map/ppermute | solution.py:613
  37.9 4.6 %collective-permute-start.11 = (f32[16,256]{1,0:T(8,128)S(1)}, f32[16,256]{1,0:T(8,128)S(1)}, u32[]{:S(2)}, u32[]{:S(2)}) collective-permute-start(f32[16,256]{1,0:T(8,128)S(1)} %shard_map.108.refs_6_.refs_8_), channel_id=1, source_target_pairs={{0,2},{1,3},{2,0},{3,1},{4,6},{5,7},{6,4},{7,5},{8,10},{9,11},{10,... | collective-permute-start | bytes 49160 | tf_op jit(solution)/shard_map/ppermute | solution.py:635

commit v12 on v8

--- a/solution.py
+++ b/solution.py
@@ -300,7 +300,8 @@
     k_high, k_low = split(kv_ref[0].T)
     keys_ref[:HD] = k_high
     keys_ref[HD : 2 * HD] = k_high
-    keys_ref[2 * HD :] = k_low
+    keys_ref[2 * HD : 3 * HD] = k_low
+    keys_ref[3 * HD :] = k_low
     v_high, v_low = split(kv_ref[1])
     values_ref[:, :HD] = v_high
     values_ref[:, HD:] = v_low
@@ -311,6 +312,10 @@
     for c in range(1, array.shape[1] // HD):
         peak = jnp.maximum(peak, array[:, c * HD : (c + 1) * HD])
     return peak
+
+
+def deep_terms(pair):
+    return jnp.concatenate([pair, pair], axis=1)
 
 
 def score_terms(pair):
@@ -328,6 +333,12 @@
     return jnp.concatenate(high, axis=1), jnp.concatenate(low, axis=1), total
 
 
+def summed_stacked(high, low, values):
+    rows = high.shape[0]
+    wide = dot(jnp.concatenate([high, low], axis=0), values)
+    return wide[:rows, :HD] + wide[:rows, HD:] + (wide[rows:, :HD] + wide[rows:, HD:])
+
+
 def summed(high, low, values):
     wide = dot(high, values)
     return wide[:, :HD] + wide[:, HD:] + dot(low, values[:, :HD])
@@ -352,7 +363,7 @@
         queries = jnp.where(first, mine, other) if i % 2 == 0 else jnp.where(first, other, mine)
         pair = jnp.concatenate(split(queries * factor), axis=1)
         q_out[g, rows] = pair
-        s = dot(score_terms(pair), keys_ref[:, keys])
+        s = dot(score_terms(pair), keys_ref[: 3 * HD, keys])
         edge = jnp.where(seen, s[:, rows], NEGATIVE)
         return edge if i % 2 == 0 else jnp.concatenate([s[:, :tokens], edge], axis=1)
 
@@ -371,7 +382,7 @@
 
 
 def term_scratch(keys):
-    return [pltpu.VMEM((3 * HD, keys), BF16), pltpu.VMEM((keys, 2 * HD), BF16)]
+    return [pltpu.VMEM((4 * HD, keys), BF16), pltpu.VMEM((keys, 2 * HD), BF16)]
 
 
 def own_stage(me, q_soft, q_other, kv, after):
@@ -388,7 +399,7 @@
     )(me, q_soft, q_other, kv)
 
 
-def later_kernel(distance, parts, heads, me_ref, kv_ref, q_ref, acc_ref, peak_ref, total_ref, acc_out, peak_out, total_out, keys_ref, values_ref):
+def later_kernel(distance, parts, heads, deep, stacked, me_ref, kv_ref, q_ref, acc_ref, peak_ref, total_ref, acc_out, peak_out, total_out, keys_ref, values_ref):
     size = q_ref.shape[1] // parts
     chip = me_ref[0] >> 1
 
@@ -396,7 +407,9 @@
         return heads[i // parts], slice(i % parts * size, (i % parts + 1) * size)
 
     def score(i):
-        return dot(score_terms(q_ref[where(i)]), keys_ref[...])
+        if deep:
+            return dot(deep_terms(q_ref[where(i)]), keys_ref[...])
+        return dot(score_terms(q_ref[where(i)]), keys_ref[: 3 * HD])
 
     def soften(i, s):
         at = where(i)
@@ -409,7 +422,8 @@
 
     def gather(i, terms):
         at = where(i)
-        acc_out[at] = acc_ref[at] * terms[2] + summed(*terms[:2], values_ref[...])
+        product = summed_stacked if stacked else summed
+        acc_out[at] = acc_ref[at] * terms[2] + product(*terms[:2], values_ref[...])
 
     @pl.when(lax.bitwise_xor(chip, distance) < chip)
     def _():
@@ -417,9 +431,9 @@
         run(parts * len(heads), score, soften, gather)
 
 
-def later_stage(me, distance, heads, kv, q_terms, acc, peak, total, after, parts=4):
-    return call(
-        functools.partial(later_kernel, distance, parts, heads),
+def later_stage(me, distance, heads, kv, q_terms, acc, peak, total, after, deep=False, stacked=False, parts=4):
+    return call(
+        functools.partial(later_kernel, distance, parts, heads, deep, stacked),
         [SMEM] + [VMEM] * 5,
         [VMEM] * 3,
         [jax.ShapeDtypeStruct(acc.shape, F32)] * 3,
@@ -429,7 +443,7 @@
     )(me, kv, q_terms, acc, peak, total)
 
 
-def last_kernel(distance, whose, heads, columns, me_ref, kv_ref, q_ref, acc_ref, peak_ref, total_ref, *refs):
+def last_kernel(distance, whose, heads, columns, deep, stacked, me_ref, kv_ref, q_ref, acc_ref, peak_ref, total_ref, *refs):
     if columns is None:
         out_ref, keys_ref, values_ref = refs
     else:
@@ -474,7 +488,9 @@
             own_copies[n].start()
 
     def score(n):
-        return dot(score_terms(q_ref[heads[n], at]), keys_ref[...])
+        if deep:
+            return dot(deep_terms(q_ref[heads[n], at]), keys_ref[...])
+        return dot(score_terms(q_ref[heads[n], at]), keys_ref[: 3 * HD])
 
     def soften(n, s):
         old = peak_ref[heads[n], at]
@@ -484,7 +500,7 @@
 
     def gather(n, terms):
         high, low, total, shrink = terms
-        new = summed(high, low, values_ref[...])
+        new = (summed_stacked if stacked else summed)(high, low, values_ref[...])
         finish(n, acc_ref[heads[n], at] * shrink + new, total)
 
     visible = lax.bitwise_xor(chip, distance) < chip
@@ -503,7 +519,7 @@
         each.wait()
 
 
-def last_stage(me, distance, whose, heads, operands, after, extra=None):
+def last_stage(me, distance, whose, heads, operands, after, extra=None, deep=False, stacked=False):
     group, rows, _ = operands[1].shape
     tokens = rows // 2
     part = jax.ShapeDtypeStruct((tokens, len(heads) * HD), F32)
@@ -524,7 +540,7 @@
             pltpu.SemaphoreType.DMA((12 + len(heads),)),
         ] + scratch
     return call(
-        functools.partial(last_kernel, distance, whose, heads, columns),
+        functools.partial(last_kernel, distance, whose, heads, columns, deep, stacked),
         [SMEM] + [VMEM] * len(operands),
         out_spec,
         out_shape,
@@ -609,9 +625,9 @@
     def sent(distance, array):
         return across(array, distance, lambda c, e: c ^ distance < c)
 
-    def stage(distance, heads, carried, after):
+    def stage(distance, heads, carried, after, deep=False, stacked=False):
         return later_stage(
-            me_flag, distance, heads, arrived[distance], q_terms, *carried, after
+            me_flag, distance, heads, arrived[distance], q_terms, *carried, after, deep, stacked
         )
 
     bits = chips.bit_length() - 1
@@ -636,13 +652,14 @@
         prefix, total = turn(me_flag, bit, total, theirs, prefix, last, [token] + ([arrived[1]] if square and last else []))
         distance = 2 if square else bit + 1
         if not (square and last):
-            carried = stage(distance, all_heads, carried, [prefix, relay] if square else [prefix])
+            waits = [prefix, relay] if square else [prefix]
+            carried = stage(distance, all_heads, carried, waits, stacked=True)
             token = carried[0]
     prefix_other = swap(prefix)
     left = [1] if square else range(bits + 1, chips - 1)
     for distance in left[:-1]:
         carried = stage(distance, all_heads, carried, [prefix])
-    carried = stage(left[-1], front, carried, [prefix])
+    carried = stage(left[-1], front, carried, [prefix], deep=True)
     linear, energy = linear_blocks(
         me_flag, terms, inside, sums, prefix, prefix_other, others, [carried[0]]
     )
@@ -657,7 +674,9 @@
         energy = plus(energy, other, [carried[0]])
         other = exchanged(energy, step)
 
-    theirs = last_stage(me_flag, chips - 1, "other", all_heads, operands, [energy])
+    theirs = last_stage(
+        me_flag, chips - 1, "other", all_heads, operands, [energy], deep=True, stacked=True
+    )
     done = last_stage(me_flag, chips - 1, "own", front, operands, [theirs])
     columns = q_lin.shape[1] * heads
     more = [swap(theirs), done, energy, other, lin_gain.reshape(1, -1), linear]

time: 44.3 us -> 44.9 us (1.014)
  Pallas kernels: 22.3 us -> 22.9 us
    pallas_call x17, Pallas kernels: 22.3 us -> 22.9 us  [call(): return lambda *operands: made(*operands, *after)]
where the time goes in v12:
time: 44.9 us; the launch traced here: 44.7 us
  Pallas kernels  22.9 us (51%)
  starting transfers between devices  10.9 us (24%)
  waiting for transfers between devices  8.12 us (18%)
  other arithmetic  1.31 us (3%)
  between operations  1.08 us (2%)
    pallas_call x17, Pallas kernels, call(): return lambda *operands: made(*operands, *after)  22.9 us
    ppermute x4, waiting for transfers between devices, across(): return lax.ppermute(array, 'ctx', pairs)  7.36 us
    ppermute x4, starting transfers between devices, across(): return lax.ppermute(array, 'ctx', pairs)  4.46 us
    ppermute x2, starting transfers between devices, exchanged(): return lax.ppermute(array, 'head', [(i, i ^ step) for i in range(heads)])  4.25 us
    another operation x2, other arithmetic, halves(): jnp.stack([jnp.where(core == 0, b, a) for a, b in zip(early, late)])  1.3 us
    ppermute x1, starting transfers between devices, body(): arrived[3] = lax.ppermute(relay, 'ctx', [(0, 6), (2, 4), (5, 7), (7, 5)])  1.29 us
  transfers between devices with their start and end apart: 12, of which 3 were waited for; matrix products, arithmetic and copies ran while one was open for 0% of the time, Pallas kernels for 40%

profile of v12, /device:TPU:6, one launch (start us, length us, event | category | flops | bytes accessed | tf_op | source)
XLA Modules:
  0.0 44.7 jit_solution(1493919563678988769)
XLA Ops:
  0.6 0.0 copy-start.2
  0.6 0.0 copy-start.1
  0.7 0.0 copy-start.4
  0.7 1.3 %select_bitcast_fusion = (f32[1,256,128]{2,1,0:T(8,128)S(1)}, f32[1,256,128]{2,1,0:T(8,128)S(1)}, f32[1,256,128]{2,1,0:T(8,128)S(1)}, f32[1,256,128]{2,1,0:T(8,128)S(1)}) fusion(f32[256,256]{1,0:T(8,128)} %param.15, pred[]{:T(512)S(6)} %eq.2, f32[256,256]{1,0:T(8,128)} %param.14), kind=kLoop, calls=%fused_computation.2 | loop fusion | flops 131072 | bytes 1048577 | tf_op jit(solution)/shard_map/stack | solution.py:255
  2.0 0.0 copy-start
  2.0 0.1 collective-permute-start
  2.1 0.0 copy-done.2
  2.1 0.3 copy-done.1
  2.4 0.0 copy-done.4
  2.4 0.9 %shard_map.95 = (f32[2,520,128]{2,1,0:T(8,128)S(1)}, f32[8,256]{1,0:T(8,128)S(1)}) custom-call(f32[8,256]{1,0:T(8,128)S(1)} %copy-done.4, f32[256,1024]{1,0:T(8,128)S(1)} %copy-done.1, f32[256,1024]{1,0:T(8,128)S(1)} %copy-done.2, f32[2,256,128]{2,1,0:T(8,128)S(1)} %pad_maximum_fusion.refs_3_.refs_1_), custom_call_target="tpu_custom_call" | custom-call | flops 1 | bytes 1 | tf_op jit(solution)/shard_map/pallas_call | solution.py:59
  3.3 0.3 collective-permute-start.3
  3.6 0.0 collective-permute-done.refs_2_
  3.6 0.0 copy-done
  3.6 0.1 shard_map.96
  3.7 0.0 copy-start.3
  3.8 0.4 collective-permute-start.2
  4.1 1.3 %collective-permute-start.1 = (f32[2,512,128]{2,1,0:T(8,128)S(1)}, f32[2,512,128]{2,1,0:T(8,128)S(1)}, u32[]{:S(2)}, u32[]{:S(2)}) collective-permute-start(f32[2,512,128]{2,1,0:T(8,128)S(1)} %get-tuple-element.26.refs_0_.refs_3_.refs_1_), channel_id=1, source_target_pairs={{0,16},{4,20},{8,24},{12,28},{1,17},{5,21},{9,25},{13,29},{2,18},{... | collective-permute-start | bytes 1572872 | tf_op jit(solution)/shard_map/ppermute | solution.py:610
  5.4 0.0 collective-permute-done.3.refs_2_.refs_6_
  5.5 0.6 %collective-permute-start.6 = (f32[520,128]{1,0:T(8,128)S(1)}, f32[520,128]{1,0:T(8,128)S(1)}, u32[]{:S(2)}, u32[]{:S(2)}) collective-permute-start(f32[520,128]{1,0:T(8,128)S(1)} %shard_map.97.refs_4_.refs_1_), channel_id=1, source_target_pairs={{8,0},{12,4},{0,8},{4,12},{24,16},{28,20},{16,24},{20,28},{9,1},{1... | collective-permute-start | bytes 798728 | tf_op jit(solution)/shard_map/ppermute | solution.py:610
  6.1 0.0 copy-done.3
  6.1 1.7 %shard_map.98 = (f32[8,256,128]{2,1,0:T(8,128)S(1)}, bf16[8,256,256]{2,1,0:T(8,128)(2,1)S(1)}) custom-call(f32[256,1024]{1,0:T(8,128)S(1)} %copy-done.3, f32[256,1024]{1,0:T(8,128)S(1)} %copy-done.1, f32[256,1024]{1,0:T(8,128)S(1)} %copy-done.2, f32[8,256]{1,0:T(8,128)S(1)} %get-tuple-element.25.refs_4_.refs_3_, f32[520,128]{1,0:T(8,128)S(1)} %shard_map.97.refs_4_.refs_1_), custom_call_target="tpu_custom_call" | custom-call | flops 1 | bytes 1 | tf_op jit(solution)/shard_map/pallas_call | solution.py:59
  7.9 1.3 %collective-permute-start.5 = (f32[2,512,128]{2,1,0:T(8,128)S(1)}, f32[2,512,128]{2,1,0:T(8,128)S(1)}, u32[]{:S(2)}, u32[]{:S(2)}) collective-permute-start(f32[2,512,128]{2,1,0:T(8,128)S(1)} %shard_map.99.refs_4_), channel_id=1, source_target_pairs={{0,8},{4,12},{16,24},{20,28},{1,9},{5,13},{17,25},{21,29},{2,10},{... | collective-permute-start | bytes 1572872 | tf_op jit(solution)/shard_map/ppermute | solution.py:610
  9.2 0.0 collective-permute-done.2.refs_2_
  9.2 2.9 %shard_map.100 = (bf16[6,512,256]{2,1,0:T(8,128)(2,1)S(1)}, f32[6,512,128]{2,1,0:T(8,128)S(1)}, f32[6,512,128]{2,1,0:T(8,128)S(1)}, f32[6,512,128]{2,1,0:T(8,128)S(1)}) custom-call(s32[1]{0:T(128)} %bitcast.refs_0_, f32[256,1536]{1,0:T(8,128)S(1)} %copy-done, f32[6,256,128]{2,1,0:T(8,128)S(1)} %collective-permute-done.2.refs_2_, ...), custom_call_target="tpu_custom_call" | custom-call | flops 1 | bytes 1 | tf_op jit(solution)/shard_map/pallas_call | solution.py:59
  12.1 2.7 %collective-permute-done.6.refs_2_ = f32[520,128]{1,0:T(8,128)S(1)} collective-permute-done((f32[520,128]{1,0:T(8,128)S(1)}, f32[520,128]{1,0:T(8,128)S(1)}, u32[]{:S(2)}, u32[]{:S(2)}) %collective-permute-start.6) | collective-permute-done | bytes 266272 | tf_op jit(solution)/shard_map/ppermute | solution.py:610
  14.8 0.1 shard_map.102
  14.8 1.3 %collective-permute-start.7 = (f32[520,128]{1,0:T(8,128)S(1)}, f32[520,128]{1,0:T(8,128)S(1)}, u32[]{:S(2)}, u32[]{:S(2)}) collective-permute-start(f32[520,128]{1,0:T(8,128)S(1)} %get-tuple-element.38.refs_1_), channel_id=1, source_target_pairs={{0,16},{4,20},{8,24},{12,28},{1,17},{5,21},{9,25},{13,29},{2,18},{... | collective-permute-start | bytes 798728 | tf_op jit(solution)/shard_map/ppermute | solution.py:610
  16.1 4.6 %collective-permute-done.1.refs_2_.refs_1_ = f32[2,512,128]{2,1,0:T(8,128)S(1)} collective-permute-done((f32[2,512,128]{2,1,0:T(8,128)S(1)}, f32[2,512,128]{2,1,0:T(8,128)S(1)}, u32[]{:S(2)}, u32[]{:S(2)}) %collective-permute-start.1) | collective-permute-done | bytes 524320 | tf_op jit(solution)/shard_map/ppermute | solution.py:610
  20.8 1.3 %collective-permute-start.4 = (f32[2,512,128]{2,1,0:T(8,128)S(1)}, f32[2,512,128]{2,1,0:T(8,128)S(1)}, u32[]{:S(2)}, u32[]{:S(2)}) collective-permute-start(f32[2,512,128]{2,1,0:T(8,128)S(1)} %shard_map.101.refs_7_), channel_id=1, source_target_pairs={{0,24},{8,16},{20,28},{28,20},{1,25},{9,17},{21,29},{29,21},{2,26}... | collective-permute-start | bytes 1572872 | tf_op jit(solution)/shard_map/ppermute | solution.py:648
  22.1 4.9 %shard_map.103 = (f32[6,512,128]{2,1,0:T(8,128)S(1)}, f32[6,512,128]{2,1,0:T(8,128)S(1)}, f32[6,512,128]{2,1,0:T(8,128)S(1)}) custom-call(s32[1]{0:T(128)} %bitcast.refs_0_, f32[2,512,128]{2,1,0:T(8,128)S(1)} %collective-permute-done.1.refs_2_.refs_1_, ...), custom_call_target="tpu_custom_call", output_to_operand_aliasing={{0}: (3, {}), {1}: (4, {}), {2}: (5, {})} | custom-call | flops 1 | bytes 1 | tf_op jit(solution)/shard_map/pallas_call | solution.py:59
  27.0 0.0 collective-permute-done.5.refs_5_.refs_1_
  27.0 0.0 collective-permute-done.7.refs_2_
  27.1 0.1 collective-permute-start.8
  27.2 2.6 %shard_map.105 = (f32[6,512,128]{2,1,0:T(8,128)S(1)}, f32[6,512,128]{2,1,0:T(8,128)S(1)}, f32[6,512,128]{2,1,0:T(8,128)S(1)}) custom-call(s32[1]{0:T(128)} %bitcast.refs_0_, f32[2,512,128]{2,1,0:T(8,128)S(1)} %collective-permute-done.5.refs_5_.refs_1_, ...), custom_call_target="tpu_custom_call", output_to_operand_aliasing={{0}: (3, {}), {1}: (4, {}), {2}: (5, {})} | custom-call | flops 1 | bytes 1 | tf_op jit(solution)/shard_map/pallas_call | solution.py:59
  29.8 0.0 collective-permute-done.8.refs_5_
  29.8 1.0 %shard_map.106 = (f32[256,1024]{1,0:T(8,128)S(1)}, f32[16,256]{1,0:T(8,128)S(1)}) custom-call(s32[1]{0:T(128)} %bitcast.refs_0_, bf16[8,256,256]{2,1,0:T(8,128)(2,1)S(1)} %get-tuple-element.42.refs_1_, f32[8,256,128]{2,1,0:T(8,128)S(1)} %get-tuple-element.29.refs_1_.refs_2_, f32[8,256]{1,0:T(8,128)S(1)} %get-tuple-element.25.refs_4_.refs_3_, ...), custom_call_target="tpu_custom_call" | custom-call | flops 1 | bytes 1 | tf_op jit(solution)/shard_map/pallas_call | solution.py:59
  30.8 1.6 %collective-permute-start.9 = (f32[16,256]{1,0:T(8,128)S(1)}, f32[16,256]{1,0:T(8,128)S(1)}, u32[]{:S(2)}, u32[]{:S(2)}) collective-permute-start(f32[16,256]{1,0:T(8,128)S(1)} %get-tuple-element.43.refs_6_.refs_0_), channel_id=1, source_target_pairs={{0,1},{1,0},{2,3},{3,2},{4,5},{5,4},{6,7},{7,6},{8,9},{9,8},{10,11... | collective-permute-start | bytes 49160 | tf_op jit(solution)/shard_map/ppermute | solution.py:623
  32.4 2.4 %shard_map.107 = (f32[6,512,128]{2,1,0:T(8,128)S(1)}, f32[6,512,128]{2,1,0:T(8,128)S(1)}, f32[6,512,128]{2,1,0:T(8,128)S(1)}) custom-call(s32[1]{0:T(128)} %bitcast.refs_0_, f32[2,512,128]{2,1,0:T(8,128)S(1)} %collective-permute-done.5.refs_5_.refs_1_, ...), custom_call_target="tpu_custom_call", output_to_operand_aliasing={{0}: (3, {}), {1}: (4, {}), {2}: (5, {})} | custom-call | flops 1 | bytes 1 | tf_op jit(solution)/shard_map/pallas_call | solution.py:59
  34.8 0.0 collective-permute-done.9.refs_1_
  34.8 0.0 collective-permute-done.4.refs_1_
  34.9 2.5 %shard_map.109.refs_6_ = f32[256,768]{1,0:T(8,128)S(1)} custom-call(s32[1]{0:T(128)} %bitcast.refs_0_, f32[2,512,128]{2,1,0:T(8,128)S(1)} %collective-permute-done.4.refs_1_, bf16[6,512,256]{2,1,0:T(8,128)(2,1)S(1)} %get-tuple-element.31.refs_2_, f32[6,512,128]{2,1,0:T(8,128)S(1)} %get-tuple-element.44.refs_2_.refs_3_, ...), custom_call_target="tpu_custom_call" | custom-call | flops 1 | bytes 1 | tf_op jit(solution)/shard_map/pallas_call | solution.py:59
  37.3 0.0 copy-start.5
  37.3 0.1 collective-permute-start.10
  37.4 2.6 %collective-permute-start.11 = (f32[16,256]{1,0:T(8,128)S(1)}, f32[16,256]{1,0:T(8,128)S(1)}, u32[]{:S(2)}, u32[]{:S(2)}) collective-permute-start(f32[16,256]{1,0:T(8,128)S(1)} %shard_map.108.refs_6_.refs_8_), channel_id=1, source_target_pairs={{0,2},{1,3},{2,0},{3,1},{4,6},{5,7},{6,4},{7,5},{8,10},{9,11},{10,... | collective-permute-start | bytes 49160 | tf_op jit(solution)/shard_map/ppermute | solution.py:623
  40.1 1.3 %shard_map.110.refs_7_ = f32[256,384]{1,0:T(8,128)S(1)} custom-call(s32[1]{0:T(128)} %bitcast.refs_0_, f32[2,512,128]{2,1,0:T(8,128)S(1)} %collective-permute-done.4.refs_1_, bf16[6,512,256]{2,1,0:T(8,128)(2,1)S(1)} %get-tuple-element.31.refs_2_, f32[6,512,128]{2,1,0:T(8,128)S(1)} %get-tuple-element.44.refs_2_.refs_3_, ...), custom_call_target="tpu_custom_call" | custom-call | flops 1 | bytes 1 | tf_op jit(solution)/shard_map/pallas_call | solution.py:59
  41.4 0.7 %collective-permute-done.11.refs_9_ = f32[16,256]{1,0:T(8,128)S(1)} collective-permute-done((f32[16,256]{1,0:T(8,128)S(1)}, f32[16,256]{1,0:T(8,128)S(1)}, u32[]{:S(2)}, u32[]{:S(2)}) %collective-permute-start.11) | collective-permute-done | bytes 16416 | tf_op jit(solution)/shard_map/ppermute | solution.py:623
  42.1 0.0 collective-permute-done.10.refs_6_
  42.1 0.0 copy-done.5
  42.1 2.4 %shard_map.111 = (f32[256,1024]{1,0:T(8,128)}, f32[256,1536]{1,0:T(8,128)}) custom-call(s32[1]{0:T(128)} %bitcast.refs_0_, f32[2,512,128]{2,1,0:T(8,128)S(1)} %collective-permute-done.4.refs_1_, bf16[6,512,256]{2,1,0:T(8,128)(2,1)S(1)} %get-tuple-element.31.refs_2_, f32[6,512,128]{2,1,0:T(8,128)S(1)} %get-tuple-element.44.refs_2_.refs_3_, ...), custom_call_target="tpu_custom_call" | custom-call | flops 1 | bytes 1 | tf_op jit(solution)/shard_map/pallas_call | solution.py:59
  (7 shorter events, 0.2 us)
Async XLA Ops:
  0.6 1.5 %copy-start.2 = (f32[256,1024]{1,0:T(8,128)S(1)}, f32[256,1024]{1,0:T(8,128)}, u32[]{:S(2)}) copy-start(f32[256,1024]{1,0:T(8,128)} %refs_2_.3) | copy-start | bytes 3145732
  0.6 1.8 %copy-start.1 = (f32[256,1024]{1,0:T(8,128)S(1)}, f32[256,1024]{1,0:T(8,128)}, u32[]{:S(2)}) copy-start(f32[256,1024]{1,0:T(8,128)} %refs_1_.4) | copy-start | bytes 3145732
  0.7 1.8 %copy-start.4 = (f32[8,256]{1,0:T(8,128)S(1)}, f32[8,256]{1,0:T(8,128)}, u32[]{:S(2)}) copy-start(f32[8,256]{1,0:T(8,128)} %refs_0_.2) | copy-start | bytes 24580
  2.0 1.6 %copy-start = (f32[256,1536]{1,0:T(8,128)S(1)}, f32[256,1536]{1,0:T(8,128)}, u32[]{:S(2)}) copy-start(f32[256,1536]{1,0:T(8,128)} %refs_1_.5) | copy-start | bytes 4718596
  2.0 1.6 %collective-permute-start = (f32[2,256,128]{2,1,0:T(8,128)S(1)}, f32[2,256,128]{2,1,0:T(8,128)S(1)}, u32[]{:S(2)}, u32[]{:S(2)}) collective-permute-start(f32[2,256,128]{2,1,0:T(8,128)S(1)} %pad_maximum_fusion.1), channel_id=1, source_target_pairs={{0,4},{4,0},{8,12},{12,8},{16,20},{20,16},{24,28},{28,24},{1,5},{5... | collective-permute-start | bytes 786440 | tf_op jit(solution)/shard_map/ppermute | solution.py:601
  3.3 2.1 %collective-permute-start.3 = (f32[2,520,128]{2,1,0:T(8,128)S(1)}, f32[2,520,128]{2,1,0:T(8,128)S(1)}, u32[]{:S(2)}, u32[]{:S(2)}) collective-permute-start(f32[2,520,128]{2,1,0:T(8,128)S(1)} %get-tuple-element.28.refs_1_), channel_id=1, source_target_pairs={{0,4},{4,0},{8,12},{12,8},{16,20},{20,16},{24,28},{28,24},{1,5},{5... | collective-permute-start | bytes 1597448 | tf_op jit(solution)/shard_map/ppermute | solution.py:601
  3.7 2.4 %copy-start.3 = (f32[256,1024]{1,0:T(8,128)S(1)}, f32[256,1024]{1,0:T(8,128)}, u32[]{:S(2)}) copy-start(f32[256,1024]{1,0:T(8,128)} %refs_0_.3) | copy-start | bytes 3145732
  3.8 5.4 %collective-permute-start.2 = (f32[6,256,128]{2,1,0:T(8,128)S(1)}, f32[6,256,128]{2,1,0:T(8,128)S(1)}, u32[]{:S(2)}, u32[]{:S(2)}) collective-permute-start(f32[6,256,128]{2,1,0:T(8,128)S(1)} %get-tuple-element.27.refs_3_), channel_id=1, source_target_pairs={{0,4},{4,0},{8,12},{12,8},{16,20},{20,16},{24,28},{28,24},{1,5},{5... | collective-permute-start | bytes 2359304 | tf_op jit(solution)/shard_map/ppermute | solution.py:601
  4.1 16.6 %collective-permute-start.1 = (f32[2,512,128]{2,1,0:T(8,128)S(1)}, f32[2,512,128]{2,1,0:T(8,128)S(1)}, u32[]{:S(2)}, u32[]{:S(2)}) collective-permute-start(f32[2,512,128]{2,1,0:T(8,128)S(1)} %get-tuple-element.26.refs_0_.refs_3_.refs_1_), channel_id=1, source_target_pairs={{0,16},{4,20},{8,24},{12,28},{1,17},{5,21},{9,25},{13,29},{2,18},{... | collective-permute-start | bytes 1572872 | tf_op jit(solution)/shard_map/ppermute | solution.py:610
  5.5 9.3 %collective-permute-start.6 = (f32[520,128]{1,0:T(8,128)S(1)}, f32[520,128]{1,0:T(8,128)S(1)}, u32[]{:S(2)}, u32[]{:S(2)}) collective-permute-start(f32[520,128]{1,0:T(8,128)S(1)} %shard_map.97.refs_4_.refs_1_), channel_id=1, source_target_pairs={{8,0},{12,4},{0,8},{4,12},{24,16},{28,20},{16,24},{20,28},{9,1},{1... | collective-permute-start | bytes 798728 | tf_op jit(solution)/shard_map/ppermute | solution.py:610
  7.9 19.2 %collective-permute-start.5 = (f32[2,512,128]{2,1,0:T(8,128)S(1)}, f32[2,512,128]{2,1,0:T(8,128)S(1)}, u32[]{:S(2)}, u32[]{:S(2)}) collective-permute-start(f32[2,512,128]{2,1,0:T(8,128)S(1)} %shard_map.99.refs_4_), channel_id=1, source_target_pairs={{0,8},{4,12},{16,24},{20,28},{1,9},{5,13},{17,25},{21,29},{2,10},{... | collective-permute-start | bytes 1572872 | tf_op jit(solution)/shard_map/ppermute | solution.py:610
  14.8 12.2 %collective-permute-start.7 = (f32[520,128]{1,0:T(8,128)S(1)}, f32[520,128]{1,0:T(8,128)S(1)}, u32[]{:S(2)}, u32[]{:S(2)}) collective-permute-start(f32[520,128]{1,0:T(8,128)S(1)} %get-tuple-element.38.refs_1_), channel_id=1, source_target_pairs={{0,16},{4,20},{8,24},{12,28},{1,17},{5,21},{9,25},{13,29},{2,18},{... | collective-permute-start | bytes 798728 | tf_op jit(solution)/shard_map/ppermute | solution.py:610
  20.8 14.0 %collective-permute-start.4 = (f32[2,512,128]{2,1,0:T(8,128)S(1)}, f32[2,512,128]{2,1,0:T(8,128)S(1)}, u32[]{:S(2)}, u32[]{:S(2)}) collective-permute-start(f32[2,512,128]{2,1,0:T(8,128)S(1)} %shard_map.101.refs_7_), channel_id=1, source_target_pairs={{0,24},{8,16},{20,28},{28,20},{1,25},{9,17},{21,29},{29,21},{2,26}... | collective-permute-start | bytes 1572872 | tf_op jit(solution)/shard_map/ppermute | solution.py:648
  27.1 2.7 %collective-permute-start.8 = (f32[520,128]{1,0:T(8,128)S(1)}, f32[520,128]{1,0:T(8,128)S(1)}, u32[]{:S(2)}, u32[]{:S(2)}) collective-permute-start(f32[520,128]{1,0:T(8,128)S(1)} %shard_map.104.refs_6_.refs_4_), channel_id=1, source_target_pairs={{0,4},{4,0},{8,12},{12,8},{16,20},{20,16},{24,28},{28,24},{1,5},{5... | collective-permute-start | bytes 798728 | tf_op jit(solution)/shard_map/ppermute | solution.py:601
  30.8 4.0 %collective-permute-start.9 = (f32[16,256]{1,0:T(8,128)S(1)}, f32[16,256]{1,0:T(8,128)S(1)}, u32[]{:S(2)}, u32[]{:S(2)}) collective-permute-start(f32[16,256]{1,0:T(8,128)S(1)} %get-tuple-element.43.refs_6_.refs_0_), channel_id=1, source_target_pairs={{0,1},{1,0},{2,3},{3,2},{4,5},{5,4},{6,7},{7,6},{8,9},{9,8},{10,11... | collective-permute-start | bytes 49160 | tf_op jit(solution)/shard_map/ppermute | solution.py:623
  37.3 4.8 %copy-start.5 = (f32[1024]{0:T(1024)S(1)}, f32[1024]{0:T(1024)}, u32[]{:S(2)}) copy-start(f32[1024]{0:T(1024)} %param.12) | copy-start | bytes 12292
  37.3 4.8 %collective-permute-start.10 = (f32[256,768]{1,0:T(8,128)S(1)}, f32[256,768]{1,0:T(8,128)S(1)}, u32[]{:S(2)}, u32[]{:S(2)}) collective-permute-start(f32[256,768]{1,0:T(8,128)S(1)} %shard_map.109.refs_6_), channel_id=1, source_target_pairs={{0,4},{4,0},{8,12},{12,8},{16,20},{20,16},{24,28},{28,24},{1,5},{5... | collective-permute-start | bytes 2359304 | tf_op jit(solution)/shard_map/ppermute | solution.py:601
  37.4 4.7 %collective-permute-start.11 = (f32[16,256]{1,0:T(8,128)S(1)}, f32[16,256]{1,0:T(8,128)S(1)}, u32[]{:S(2)}, u32[]{:S(2)}) collective-permute-start(f32[16,256]{1,0:T(8,128)S(1)} %shard_map.108.refs_6_.refs_8_), channel_id=1, source_target_pairs={{0,2},{1,3},{2,0},{3,1},{4,6},{5,7},{6,4},{7,5},{8,10},{9,11},{10,... | collective-permute-start | bytes 49160 | tf_op jit(solution)/shard_map/ppermute | solution.py:623

commit v13 on v8

--- a/solution.py
+++ b/solution.py
@@ -220,8 +220,9 @@
             prior = jnp.where(core == side, mine_ref[at], theirs_ref[at])
             prior = jnp.where(core == 1, prior * decay[i : i + 1] + other_ref[side, at], prior)
             high, low = split(prior)
-            wide = dot(terms_ref[h, :, :HD], jnp.concatenate([high, low], axis=1))
-            carried = wide[:, :HD] + wide[:, HD:] + dot(terms_ref[h, :, HD:], high)
+            carried = dot(
+                score_terms(terms_ref[h]), jnp.concatenate([high, high, low], axis=0)
+            )
             linear = inside_ref[h] + leading[:, h : h + 1] * carried
             out_ref[:, h * HD : (h + 1) * HD] = linear
             squares = squares + linear * linear
@@ -388,7 +389,13 @@
     )(me, q_soft, q_other, kv)
 
 
-def later_kernel(distance, parts, heads, me_ref, kv_ref, q_ref, acc_ref, peak_ref, total_ref, acc_out, peak_out, total_out, keys_ref, values_ref):
+def later_kernel(distance, parts, heads, fresh, me_ref, *refs):
+    if fresh:
+        kv_ref, q_ref, acc_ref, peak_ref, total_ref = refs[:5]
+        acc_out, peak_out, total_out, keys_ref, values_ref = refs[5:]
+    else:
+        keys_ref, values_ref, q_ref, acc_ref, peak_ref, total_ref = refs[:6]
+        acc_out, peak_out, total_out = refs[6:]
     size = q_ref.shape[1] // parts
     chip = me_ref[0] >> 1
 
@@ -413,28 +420,47 @@
 
     @pl.when(lax.bitwise_xor(chip, distance) < chip)
     def _():
-        fill_terms(kv_ref, keys_ref, values_ref)
+        if fresh:
+            fill_terms(kv_ref, keys_ref, values_ref)
         run(parts * len(heads), score, soften, gather)
 
 
+def term_shapes(keys):
+    return [
+        jax.ShapeDtypeStruct((3 * HD, keys), BF16),
+        jax.ShapeDtypeStruct((keys, 2 * HD), BF16),
+    ]
+
+
 def later_stage(me, distance, heads, kv, q_terms, acc, peak, total, after, parts=4):
-    return call(
-        functools.partial(later_kernel, distance, parts, heads),
-        [SMEM] + [VMEM] * 5,
-        [VMEM] * 3,
-        [jax.ShapeDtypeStruct(acc.shape, F32)] * 3,
-        term_scratch(kv.shape[1]),
-        alias={3: 0, 4: 1, 5: 2},
-        after=after,
-    )(me, kv, q_terms, acc, peak, total)
-
-
-def last_kernel(distance, whose, heads, columns, me_ref, kv_ref, q_ref, acc_ref, peak_ref, total_ref, *refs):
-    if columns is None:
-        out_ref, keys_ref, values_ref = refs
+    fresh = not isinstance(kv, tuple)
+    operands = [kv] if fresh else list(kv)
+    shift = 1 + len(operands)
+    out_shape = [jax.ShapeDtypeStruct(acc.shape, F32)] * 3
+    if fresh:
+        out_shape += term_shapes(kv.shape[1])
+    out = call(
+        functools.partial(later_kernel, distance, parts, heads, fresh),
+        [SMEM] + [VMEM] * (len(operands) + 4),
+        [VMEM] * len(out_shape),
+        out_shape,
+        alias={shift + 1: 0, shift + 2: 1, shift + 3: 2},
+        after=after,
+    )(me, *operands, q_terms, acc, peak, total)
+    return out[:3], tuple(out[3:]) if fresh else kv
+
+
+def last_kernel(distance, whose, heads, columns, me_ref, *refs):
+    fresh = whose == "other"
+    if fresh:
+        kv_ref, q_ref, acc_ref, peak_ref, total_ref, out_ref, keys_ref, values_ref = refs
     else:
+        keys_ref, values_ref, q_ref, acc_ref, peak_ref, total_ref, *refs = refs
+    if columns is not None:
         theirs_ref, done_ref, energy_ref, energy_other_ref, gain_ref, linear_ref = refs[:6]
-        lin_hbm, soft_hbm, lin_ref, out_ref, sems, keys_ref, values_ref = refs[6:]
+        lin_hbm, soft_hbm, lin_ref, out_ref, sems = refs[6:]
+    elif not fresh:
+        (out_ref,) = refs
     group, rows, _ = q_ref.shape
     tokens = rows // 2
     core, chip = me_ref[0] & 1, me_ref[0] >> 1
@@ -456,17 +482,19 @@
             copy(theirs_ref.at[block], to).start()
         factor = lax.rsqrt((energy_ref[:8] + energy_other_ref[:8]) / columns + EPSILON)
         factor = factor.T[:, 0:1]
-        for n, block in enumerate(blocks):
-            rows = slice(n * (tokens // 4), (n + 1) * (tokens // 4))
-            lin_ref[rows] = linear_ref[rows] * factor[rows] * gain_ref[...]
-            copy(lin_ref.at[block], lin_hbm.at[block]).start()
         for block in blocks:
             to = soft_hbm.at[block, columns_of(core, 0, group - len(heads))]
             copy(done_ref.at[block], to).start()
+        lin_copies = [copy(lin_ref.at[block], lin_hbm.at[block]) for block in blocks]
         own_copies = [
             copy(out_ref.at[:, pl.ds(n * HD, HD)], soft_hbm.at[:, columns_of(core, g, 1)])
             for n, g in enumerate(heads)
         ]
+
+    def scale_rows(n):
+        rows = slice(n * (tokens // 4), (n + 1) * (tokens // 4))
+        lin_ref[rows] = linear_ref[rows] * factor[rows] * gain_ref[...]
+        lin_copies[n].start()
 
     def finish(n, acc, total):
         out_ref[:, n * HD : (n + 1) * HD] = acc / jnp.sum(total, axis=1, keepdims=True)
@@ -487,28 +515,41 @@
         new = summed(high, low, values_ref[...])
         finish(n, acc_ref[heads[n], at] * shrink + new, total)
 
+    def gather_and_scale(n, terms):
+        gather(n, terms)
+        if n == 0:
+            for block in range(2, 4):
+                scale_rows(block)
+
+    if columns is not None:
+        for block in range(2):
+            scale_rows(block)
     visible = lax.bitwise_xor(chip, distance) < chip
 
     @pl.when(visible)
     def _():
-        fill_terms(kv_ref, keys_ref, values_ref)
-        run(len(heads), score, soften, gather)
+        if fresh:
+            fill_terms(kv_ref, keys_ref, values_ref)
+        run(len(heads), score, soften, gather if columns is None else gather_and_scale)
 
     @pl.when(jnp.logical_not(visible))
     def _():
         for n, g in enumerate(heads):
             finish(n, acc_ref[g, at], total_ref[g, at])
+        if columns is not None:
+            for block in range(2, 4):
+                scale_rows(block)
 
     for each in copies:
         each.wait()
 
 
-def last_stage(me, distance, whose, heads, operands, after, extra=None):
-    group, rows, _ = operands[1].shape
+def last_stage(me, distance, whose, heads, kv, operands, after, extra=None):
+    group, rows, _ = operands[0].shape
     tokens = rows // 2
     part = jax.ShapeDtypeStruct((tokens, len(heads) * HD), F32)
-    scratch = term_scratch(operands[0].shape[1])
-    out_shape, out_spec, columns = part, VMEM, None
+    fresh, columns, scratch = whose == "other", None, []
+    operands = [kv, *operands] if fresh else [*kv, *operands]
     if extra is not None:
         columns, more = extra
         operands = [*operands, *more]
@@ -522,7 +563,10 @@
             pltpu.VMEM(linear.shape, F32),
             pltpu.VMEM(part.shape, F32),
             pltpu.SemaphoreType.DMA((12 + len(heads),)),
-        ] + scratch
+        ]
+    else:
+        out_shape = [part] + (term_shapes(kv.shape[1]) if fresh else [])
+        out_spec = [VMEM] * len(out_shape)
     return call(
         functools.partial(last_kernel, distance, whose, heads, columns),
         [SMEM] + [VMEM] * len(operands),
@@ -609,10 +653,8 @@
     def sent(distance, array):
         return across(array, distance, lambda c, e: c ^ distance < c)
 
-    def stage(distance, heads, carried, after):
-        return later_stage(
-            me_flag, distance, heads, arrived[distance], q_terms, *carried, after
-        )
+    def stage(kv, distance, heads, carried, after):
+        return later_stage(me_flag, distance, heads, kv, q_terms, *carried, after)
 
     bits = chips.bit_length() - 1
     arrived, token = {}, inside
@@ -636,13 +678,14 @@
         prefix, total = turn(me_flag, bit, total, theirs, prefix, last, [token] + ([arrived[1]] if square and last else []))
         distance = 2 if square else bit + 1
         if not (square and last):
-            carried = stage(distance, all_heads, carried, [prefix, relay] if square else [prefix])
+            waits = [prefix, relay] if square else [prefix]
+            carried, _ = stage(arrived[distance], distance, all_heads, carried, waits)
             token = carried[0]
     prefix_other = swap(prefix)
     left = [1] if square else range(bits + 1, chips - 1)
     for distance in left[:-1]:
-        carried = stage(distance, all_heads, carried, [prefix])
-    carried = stage(left[-1], front, carried, [prefix])
+        carried, _ = stage(arrived[distance], distance, all_heads, carried, [prefix])
+    carried, kept = stage(arrived[left[-1]], left[-1], front, carried, [prefix])
     linear, energy = linear_blocks(
         me_flag, terms, inside, sums, prefix, prefix_other, others, [carried[0]]
     )
@@ -651,18 +694,20 @@
         energies.append(step)
         step *= 2
     other = exchanged(energy, energies[0])
-    carried = stage(left[-1], back, carried, [energy])
-    operands = [arrived[chips - 1], q_terms, *carried]
+    carried, _ = stage(kept, left[-1], back, carried, [energy])
+    operands = [q_terms, *carried]
     for step in energies[1:]:
         energy = plus(energy, other, [carried[0]])
         other = exchanged(energy, step)
 
-    theirs = last_stage(me_flag, chips - 1, "other", all_heads, operands, [energy])
-    done = last_stage(me_flag, chips - 1, "own", front, operands, [theirs])
+    theirs, *kept = last_stage(
+        me_flag, chips - 1, "other", all_heads, arrived[chips - 1], operands, [energy]
+    )
+    (done,) = last_stage(me_flag, chips - 1, "own", front, kept, operands, [])
     columns = q_lin.shape[1] * heads
     more = [swap(theirs), done, energy, other, lin_gain.reshape(1, -1), linear]
     return tuple(
-        last_stage(me_flag, chips - 1, "own", back, operands, [], (columns, more))
+        last_stage(me_flag, chips - 1, "own", back, kept, operands, [], (columns, more))
     )
 
 

time: 44.3 us -> 45 us (1.016)
  Pallas kernels: 22.3 us -> 22.9 us
    pallas_call x17, Pallas kernels: 22.3 us -> 22.9 us  [call(): return lambda *operands: made(*operands, *after)]
  transfers between devices with their start and end apart: 12 -> 12, of which waited for: 3 -> 3; matrix products, arithmetic and copies ran while one was open for 0% -> 0% of each run, Pallas kernels for 40% -> 41%
where the time goes in v13:
time: 45 us; the launch traced here: 44.8 us
  Pallas kernels  22.9 us (51%)
  starting transfers between devices  10.9 us (24%)
  waiting for transfers between devices  8.29 us (18%)
  other arithmetic  1.31 us (3%)
  between operations  1.05 us (2%)
    pallas_call x17, Pallas kernels, call(): return lambda *operands: made(*operands, *after)  22.9 us
    ppermute x4, waiting for transfers between devices, across(): return lax.ppermute(array, 'ctx', pairs)  7.37 us
    ppermute x4, starting transfers between devices, across(): return lax.ppermute(array, 'ctx', pairs)  4.46 us
    ppermute x2, starting transfers between devices, exchanged(): return lax.ppermute(array, 'head', [(i, i ^ step) for i in range(heads)])  4.23 us
    another operation x2, other arithmetic, halves(): jnp.stack([jnp.where(core == 0, b, a) for a, b in zip(early, late)])  1.3 us
    ppermute x1, starting transfers between devices, body(): arrived[3] = lax.ppermute(relay, 'ctx', [(0, 6), (2, 4), (5, 7), (7, 5)])  1.29 us
    ppermute x2, waiting for transfers between devices, exchanged(): return lax.ppermute(array, 'head', [(i, i ^ step) for i in range(heads)])  0.9 us
  transfers between devices with their start and end apart: 12, of which 3 were waited for; matrix products, arithmetic and copies ran while one was open for 0% of the time, Pallas kernels for 41%

profile of v13, /device:TPU:6, one launch (start us, length us, event | category | flops | bytes accessed | tf_op | source)
XLA Modules:
  0.0 44.8 jit_solution(15442746457017188683)
XLA Ops:
  0.6 0.0 copy-start.2
  0.6 0.0 copy-start.1
  0.7 0.0 copy-start.4
  0.7 1.3 %select_bitcast_fusion = (f32[1,256,128]{2,1,0:T(8,128)S(1)}, f32[1,256,128]{2,1,0:T(8,128)S(1)}, f32[1,256,128]{2,1,0:T(8,128)S(1)}, f32[1,256,128]{2,1,0:T(8,128)S(1)}) fusion(f32[256,256]{1,0:T(8,128)} %param.15, pred[]{:T(512)S(6)} %eq.2, f32[256,256]{1,0:T(8,128)} %param.14), kind=kLoop, calls=%fused_computation.2 | loop fusion | flops 131072 | bytes 1048577 | tf_op jit(solution)/shard_map/stack | solution.py:256
  2.0 0.0 copy-start
  2.0 0.1 collective-permute-start
  2.1 0.0 copy-done.2
  2.1 0.3 copy-done.1
  2.4 0.0 copy-done.4
  2.4 0.9 %shard_map.95 = (f32[2,520,128]{2,1,0:T(8,128)S(1)}, f32[8,256]{1,0:T(8,128)S(1)}) custom-call(f32[8,256]{1,0:T(8,128)S(1)} %copy-done.4, f32[256,1024]{1,0:T(8,128)S(1)} %copy-done.1, f32[256,1024]{1,0:T(8,128)S(1)} %copy-done.2, f32[2,256,128]{2,1,0:T(8,128)S(1)} %pad_maximum_fusion.refs_3_.refs_1_), custom_call_target="tpu_custom_call" | custom-call | flops 1 | bytes 1 | tf_op jit(solution)/shard_map/pallas_call | solution.py:59
  3.3 0.3 collective-permute-start.3
  3.6 0.0 collective-permute-done.refs_2_
  3.6 0.0 copy-done
  3.6 0.1 shard_map.96
  3.7 0.0 copy-start.3
  3.8 0.4 collective-permute-start.2
  4.1 1.3 %collective-permute-start.1 = (f32[2,512,128]{2,1,0:T(8,128)S(1)}, f32[2,512,128]{2,1,0:T(8,128)S(1)}, u32[]{:S(2)}, u32[]{:S(2)}) collective-permute-start(f32[2,512,128]{2,1,0:T(8,128)S(1)} %get-tuple-element.31.refs_0_.refs_3_.refs_1_), channel_id=1, source_target_pairs={{0,16},{4,20},{8,24},{12,28},{1,17},{5,21},{9,25},{13,29},{2,18},{... | collective-permute-start | bytes 1572872 | tf_op jit(solution)/shard_map/ppermute | solution.py:638
  5.4 0.0 collective-permute-done.3.refs_2_.refs_6_
  5.5 0.6 %collective-permute-start.6 = (f32[520,128]{1,0:T(8,128)S(1)}, f32[520,128]{1,0:T(8,128)S(1)}, u32[]{:S(2)}, u32[]{:S(2)}) collective-permute-start(f32[520,128]{1,0:T(8,128)S(1)} %shard_map.97.refs_4_.refs_1_), channel_id=1, source_target_pairs={{8,0},{12,4},{0,8},{4,12},{24,16},{28,20},{16,24},{20,28},{9,1},{1... | collective-permute-start | bytes 798728 | tf_op jit(solution)/shard_map/ppermute | solution.py:638
  6.1 0.0 copy-done.3
  6.1 1.7 %shard_map.98 = (f32[8,256,128]{2,1,0:T(8,128)S(1)}, bf16[8,256,256]{2,1,0:T(8,128)(2,1)S(1)}) custom-call(f32[256,1024]{1,0:T(8,128)S(1)} %copy-done.3, f32[256,1024]{1,0:T(8,128)S(1)} %copy-done.1, f32[256,1024]{1,0:T(8,128)S(1)} %copy-done.2, f32[8,256]{1,0:T(8,128)S(1)} %get-tuple-element.30.refs_4_.refs_3_, f32[520,128]{1,0:T(8,128)S(1)} %shard_map.97.refs_4_.refs_1_), custom_call_target="tpu_custom_call" | custom-call | flops 1 | bytes 1 | tf_op jit(solution)/shard_map/pallas_call | solution.py:59
  7.9 1.3 %collective-permute-start.5 = (f32[2,512,128]{2,1,0:T(8,128)S(1)}, f32[2,512,128]{2,1,0:T(8,128)S(1)}, u32[]{:S(2)}, u32[]{:S(2)}) collective-permute-start(f32[2,512,128]{2,1,0:T(8,128)S(1)} %shard_map.99.refs_4_), channel_id=1, source_target_pairs={{0,8},{4,12},{16,24},{20,28},{1,9},{5,13},{17,25},{21,29},{2,10},{... | collective-permute-start | bytes 1572872 | tf_op jit(solution)/shard_map/ppermute | solution.py:638
  9.2 0.0 collective-permute-done.2.refs_2_
  9.2 2.9 %shard_map.100 = (bf16[6,512,256]{2,1,0:T(8,128)(2,1)S(1)}, f32[6,512,128]{2,1,0:T(8,128)S(1)}, f32[6,512,128]{2,1,0:T(8,128)S(1)}, f32[6,512,128]{2,1,0:T(8,128)S(1)}) custom-call(s32[1]{0:T(128)} %bitcast.refs_0_, f32[256,1536]{1,0:T(8,128)S(1)} %copy-done, f32[6,256,128]{2,1,0:T(8,128)S(1)} %collective-permute-done.2.refs_2_, ...), custom_call_target="tpu_custom_call" | custom-call | flops 1 | bytes 1 | tf_op jit(solution)/shard_map/pallas_call | solution.py:59
  12.0 2.7 %collective-permute-done.6.refs_2_ = f32[520,128]{1,0:T(8,128)S(1)} collective-permute-done((f32[520,128]{1,0:T(8,128)S(1)}, f32[520,128]{1,0:T(8,128)S(1)}, u32[]{:S(2)}, u32[]{:S(2)}) %collective-permute-start.6) | collective-permute-done | bytes 266272 | tf_op jit(solution)/shard_map/ppermute | solution.py:638
  14.8 0.1 shard_map.102
  14.8 1.3 %collective-permute-start.7 = (f32[520,128]{1,0:T(8,128)S(1)}, f32[520,128]{1,0:T(8,128)S(1)}, u32[]{:S(2)}, u32[]{:S(2)}) collective-permute-start(f32[520,128]{1,0:T(8,128)S(1)} %get-tuple-element.43.refs_1_), channel_id=1, source_target_pairs={{0,16},{4,20},{8,24},{12,28},{1,17},{5,21},{9,25},{13,29},{2,18},{... | collective-permute-start | bytes 798728 | tf_op jit(solution)/shard_map/ppermute | solution.py:638
  16.1 4.6 %collective-permute-done.1.refs_2_.refs_1_ = f32[2,512,128]{2,1,0:T(8,128)S(1)} collective-permute-done((f32[2,512,128]{2,1,0:T(8,128)S(1)}, f32[2,512,128]{2,1,0:T(8,128)S(1)}, u32[]{:S(2)}, u32[]{:S(2)}) %collective-permute-start.1) | collective-permute-done | bytes 524320 | tf_op jit(solution)/shard_map/ppermute | solution.py:638
  20.8 1.3 %collective-permute-start.4 = (f32[2,512,128]{2,1,0:T(8,128)S(1)}, f32[2,512,128]{2,1,0:T(8,128)S(1)}, u32[]{:S(2)}, u32[]{:S(2)}) collective-permute-start(f32[2,512,128]{2,1,0:T(8,128)S(1)} %shard_map.101.refs_7_), channel_id=1, source_target_pairs={{0,24},{8,16},{20,28},{28,20},{1,25},{9,17},{21,29},{29,21},{2,26}... | collective-permute-start | bytes 1572872 | tf_op jit(solution)/shard_map/ppermute | solution.py:674
  22.1 5.2 %shard_map.103 = (f32[6,512,128]{2,1,0:T(8,128)S(1)}, f32[6,512,128]{2,1,0:T(8,128)S(1)}, f32[6,512,128]{2,1,0:T(8,128)S(1)}, bf16[384,512]{1,0:T(8,128)(2,1)}, bf16[512,256]{1,0:T(8,128)(2,1)}) custom-call(s32[1]{0:T(128)} %bitcast.refs_0_, ...), custom_call_target="tpu_custom_call", output_to_operand_aliasing={{0}: (3, {}), {1}: (4, {}), {2}: (5, {})} | custom-call | flops 1 | bytes 1 | tf_op jit(solution)/shard_map/pallas_call | solution.py:59
  27.4 0.0 collective-permute-done.5.refs_5_.refs_1_
  27.4 0.0 collective-permute-done.7.refs_2_
  27.4 0.1 collective-permute-start.8
  27.5 2.7 %shard_map.105 = (f32[6,512,128]{2,1,0:T(8,128)S(1)}, f32[6,512,128]{2,1,0:T(8,128)S(1)}, f32[6,512,128]{2,1,0:T(8,128)S(1)}, bf16[384,512]{1,0:T(8,128)(2,1)S(1)}, bf16[512,256]{1,0:T(8,128)(2,1)S(1)}) custom-call(s32[1]{0:T(128)} %bitcast.refs_0_, ...), custom_call_target="tpu_custom_call", output_to_operand_aliasing={{0}: (3, {}), {1}: (4, {}), {2}: (5, {})} | custom-call | flops 1 | bytes 1 | tf_op jit(solution)/shard_map/pallas_call | solution.py:59
  30.2 0.0 collective-permute-done.8.refs_5_
  30.2 1.0 %shard_map.106 = (f32[256,1024]{1,0:T(8,128)S(1)}, f32[16,256]{1,0:T(8,128)S(1)}) custom-call(s32[1]{0:T(128)} %bitcast.refs_0_, bf16[8,256,256]{2,1,0:T(8,128)(2,1)S(1)} %get-tuple-element.49.refs_1_, f32[8,256,128]{2,1,0:T(8,128)S(1)} %get-tuple-element.34.refs_1_.refs_2_, f32[8,256]{1,0:T(8,128)S(1)} %get-tuple-element.30.refs_4_.refs_3_, ...), custom_call_target="tpu_custom_call" | custom-call | flops 1 | bytes 1 | tf_op jit(solution)/shard_map/pallas_call | solution.py:59
  31.2 1.6 %collective-permute-start.9 = (f32[16,256]{1,0:T(8,128)S(1)}, f32[16,256]{1,0:T(8,128)S(1)}, u32[]{:S(2)}, u32[]{:S(2)}) collective-permute-start(f32[16,256]{1,0:T(8,128)S(1)} %get-tuple-element.50.refs_7_.refs_0_), channel_id=1, source_target_pairs={{0,1},{1,0},{2,3},{3,2},{4,5},{5,4},{6,7},{7,6},{8,9},{9,8},{10,11... | collective-permute-start | bytes 49160 | tf_op jit(solution)/shard_map/ppermute | solution.py:651
  32.8 2.4 %shard_map.107 = (f32[6,512,128]{2,1,0:T(8,128)S(1)}, f32[6,512,128]{2,1,0:T(8,128)S(1)}, f32[6,512,128]{2,1,0:T(8,128)S(1)}) custom-call(s32[1]{0:T(128)} %bitcast.refs_0_, bf16[384,512]{1,0:T(8,128)(2,1)S(1)} %get-tuple-element.44.refs_1_, ...), custom_call_target="tpu_custom_call", output_to_operand_aliasing={{0}: (4, {}), {1}: (5, {}), {2}: (6, {})} | custom-call | flops 1 | bytes 1 | tf_op jit(solution)/shard_map/pallas_call | solution.py:59
  35.2 0.0 collective-permute-done.9.refs_1_
  35.3 0.0 collective-permute-done.4.refs_1_
  35.3 2.3 %shard_map.109 = (f32[256,768]{1,0:T(8,128)S(1)}, bf16[384,512]{1,0:T(8,128)(2,1)S(1)}, bf16[512,256]{1,0:T(8,128)(2,1)S(1)}) custom-call(s32[1]{0:T(128)} %bitcast.refs_0_, f32[2,512,128]{2,1,0:T(8,128)S(1)} %collective-permute-done.4.refs_1_, bf16[6,512,256]{2,1,0:T(8,128)(2,1)S(1)} %get-tuple-element.36.refs_2_.refs_3_, ...), custom_call_target="tpu_custom_call" | custom-call | flops 1 | bytes 1 | tf_op jit(solution)/shard_map/pallas_call | solution.py:59
  37.6 0.1 collective-permute-start.10
  37.7 2.6 %collective-permute-start.11 = (f32[16,256]{1,0:T(8,128)S(1)}, f32[16,256]{1,0:T(8,128)S(1)}, u32[]{:S(2)}, u32[]{:S(2)}) collective-permute-start(f32[16,256]{1,0:T(8,128)S(1)} %shard_map.108.refs_6_.refs_9_), channel_id=1, source_target_pairs={{0,2},{1,3},{2,0},{3,1},{4,6},{5,7},{6,4},{7,5},{8,10},{9,11},{10,... | collective-permute-start | bytes 49160 | tf_op jit(solution)/shard_map/ppermute | solution.py:651
  40.4 0.0 copy-start.5
  40.4 1.2 %shard_map.110.refs_8_ = f32[256,384]{1,0:T(8,128)S(1)} custom-call(s32[1]{0:T(128)} %bitcast.refs_0_, bf16[384,512]{1,0:T(8,128)(2,1)S(1)} %get-tuple-element.54.refs_1_, bf16[512,256]{1,0:T(8,128)(2,1)S(1)} %get-tuple-element.55.refs_2_, bf16[6,512,256]{2,1,0:T(8,128)(2,1)S(1)} %get-tuple-element.36.refs_2_.refs_3_, ...), custom_call_target="tpu_custom_call" | custom-call | flops 1 | bytes 1 | tf_op jit(solution)/shard_map/pallas_call | solution.py:59
  41.5 0.9 %collective-permute-done.11.refs_10_ = f32[16,256]{1,0:T(8,128)S(1)} collective-permute-done((f32[16,256]{1,0:T(8,128)S(1)}, f32[16,256]{1,0:T(8,128)S(1)}, u32[]{:S(2)}, u32[]{:S(2)}) %collective-permute-start.11) | collective-permute-done | bytes 16416 | tf_op jit(solution)/shard_map/ppermute | solution.py:651
  42.4 0.0 collective-permute-done.10.refs_7_
  42.4 0.0 copy-done.5
  42.4 2.2 %shard_map.111 = (f32[256,1024]{1,0:T(8,128)}, f32[256,1536]{1,0:T(8,128)}) custom-call(s32[1]{0:T(128)} %bitcast.refs_0_, bf16[384,512]{1,0:T(8,128)(2,1)S(1)} %get-tuple-element.54.refs_1_, bf16[512,256]{1,0:T(8,128)(2,1)S(1)} %get-tuple-element.55.refs_2_, bf16[6,512,256]{2,1,0:T(8,128)(2,1)S(1)} %get-tuple-element.36.refs_2_.refs_3_, ...), custom_call_target="tpu_custom_call" | custom-call | flops 1 | bytes 1 | tf_op jit(solution)/shard_map/pallas_call | solution.py:59
  (7 shorter events, 0.2 us)
Async XLA Ops:
  0.6 1.5 %copy-start.2 = (f32[256,1024]{1,0:T(8,128)S(1)}, f32[256,1024]{1,0:T(8,128)}, u32[]{:S(2)}) copy-start(f32[256,1024]{1,0:T(8,128)} %refs_2_.3) | copy-start | bytes 3145732
  0.6 1.8 %copy-start.1 = (f32[256,1024]{1,0:T(8,128)S(1)}, f32[256,1024]{1,0:T(8,128)}, u32[]{:S(2)}) copy-start(f32[256,1024]{1,0:T(8,128)} %refs_1_.4) | copy-start | bytes 3145732
  0.7 1.8 %copy-start.4 = (f32[8,256]{1,0:T(8,128)S(1)}, f32[8,256]{1,0:T(8,128)}, u32[]{:S(2)}) copy-start(f32[8,256]{1,0:T(8,128)} %refs_0_.2) | copy-start | bytes 24580
  2.0 1.6 %copy-start = (f32[256,1536]{1,0:T(8,128)S(1)}, f32[256,1536]{1,0:T(8,128)}, u32[]{:S(2)}) copy-start(f32[256,1536]{1,0:T(8,128)} %refs_1_.5) | copy-start | bytes 4718596
  2.0 1.6 %collective-permute-start = (f32[2,256,128]{2,1,0:T(8,128)S(1)}, f32[2,256,128]{2,1,0:T(8,128)S(1)}, u32[]{:S(2)}, u32[]{:S(2)}) collective-permute-start(f32[2,256,128]{2,1,0:T(8,128)S(1)} %pad_maximum_fusion.1), channel_id=1, source_target_pairs={{0,4},{4,0},{8,12},{12,8},{16,20},{20,16},{24,28},{28,24},{1,5},{5... | collective-permute-start | bytes 786440 | tf_op jit(solution)/shard_map/ppermute | solution.py:629
  3.3 2.1 %collective-permute-start.3 = (f32[2,520,128]{2,1,0:T(8,128)S(1)}, f32[2,520,128]{2,1,0:T(8,128)S(1)}, u32[]{:S(2)}, u32[]{:S(2)}) collective-permute-start(f32[2,520,128]{2,1,0:T(8,128)S(1)} %get-tuple-element.33.refs_1_), channel_id=1, source_target_pairs={{0,4},{4,0},{8,12},{12,8},{16,20},{20,16},{24,28},{28,24},{1,5},{5... | collective-permute-start | bytes 1597448 | tf_op jit(solution)/shard_map/ppermute | solution.py:629
  3.7 2.4 %copy-start.3 = (f32[256,1024]{1,0:T(8,128)S(1)}, f32[256,1024]{1,0:T(8,128)}, u32[]{:S(2)}) copy-start(f32[256,1024]{1,0:T(8,128)} %refs_0_.3) | copy-start | bytes 3145732
  3.8 5.4 %collective-permute-start.2 = (f32[6,256,128]{2,1,0:T(8,128)S(1)}, f32[6,256,128]{2,1,0:T(8,128)S(1)}, u32[]{:S(2)}, u32[]{:S(2)}) collective-permute-start(f32[6,256,128]{2,1,0:T(8,128)S(1)} %get-tuple-element.32.refs_3_), channel_id=1, source_target_pairs={{0,4},{4,0},{8,12},{12,8},{16,20},{20,16},{24,28},{28,24},{1,5},{5... | collective-permute-start | bytes 2359304 | tf_op jit(solution)/shard_map/ppermute | solution.py:629
  4.1 16.6 %collective-permute-start.1 = (f32[2,512,128]{2,1,0:T(8,128)S(1)}, f32[2,512,128]{2,1,0:T(8,128)S(1)}, u32[]{:S(2)}, u32[]{:S(2)}) collective-permute-start(f32[2,512,128]{2,1,0:T(8,128)S(1)} %get-tuple-element.31.refs_0_.refs_3_.refs_1_), channel_id=1, source_target_pairs={{0,16},{4,20},{8,24},{12,28},{1,17},{5,21},{9,25},{13,29},{2,18},{... | collective-permute-start | bytes 1572872 | tf_op jit(solution)/shard_map/ppermute | solution.py:638
  5.5 9.3 %collective-permute-start.6 = (f32[520,128]{1,0:T(8,128)S(1)}, f32[520,128]{1,0:T(8,128)S(1)}, u32[]{:S(2)}, u32[]{:S(2)}) collective-permute-start(f32[520,128]{1,0:T(8,128)S(1)} %shard_map.97.refs_4_.refs_1_), channel_id=1, source_target_pairs={{8,0},{12,4},{0,8},{4,12},{24,16},{28,20},{16,24},{20,28},{9,1},{1... | collective-permute-start | bytes 798728 | tf_op jit(solution)/shard_map/ppermute | solution.py:638
  7.9 19.5 %collective-permute-start.5 = (f32[2,512,128]{2,1,0:T(8,128)S(1)}, f32[2,512,128]{2,1,0:T(8,128)S(1)}, u32[]{:S(2)}, u32[]{:S(2)}) collective-permute-start(f32[2,512,128]{2,1,0:T(8,128)S(1)} %shard_map.99.refs_4_), channel_id=1, source_target_pairs={{0,8},{4,12},{16,24},{20,28},{1,9},{5,13},{17,25},{21,29},{2,10},{... | collective-permute-start | bytes 1572872 | tf_op jit(solution)/shard_map/ppermute | solution.py:638
  14.8 12.5 %collective-permute-start.7 = (f32[520,128]{1,0:T(8,128)S(1)}, f32[520,128]{1,0:T(8,128)S(1)}, u32[]{:S(2)}, u32[]{:S(2)}) collective-permute-start(f32[520,128]{1,0:T(8,128)S(1)} %get-tuple-element.43.refs_1_), channel_id=1, source_target_pairs={{0,16},{4,20},{8,24},{12,28},{1,17},{5,21},{9,25},{13,29},{2,18},{... | collective-permute-start | bytes 798728 | tf_op jit(solution)/shard_map/ppermute | solution.py:638
  20.8 14.5 %collective-permute-start.4 = (f32[2,512,128]{2,1,0:T(8,128)S(1)}, f32[2,512,128]{2,1,0:T(8,128)S(1)}, u32[]{:S(2)}, u32[]{:S(2)}) collective-permute-start(f32[2,512,128]{2,1,0:T(8,128)S(1)} %shard_map.101.refs_7_), channel_id=1, source_target_pairs={{0,24},{8,16},{20,28},{28,20},{1,25},{9,17},{21,29},{29,21},{2,26}... | collective-permute-start | bytes 1572872 | tf_op jit(solution)/shard_map/ppermute | solution.py:674
  27.4 2.8 %collective-permute-start.8 = (f32[520,128]{1,0:T(8,128)S(1)}, f32[520,128]{1,0:T(8,128)S(1)}, u32[]{:S(2)}, u32[]{:S(2)}) collective-permute-start(f32[520,128]{1,0:T(8,128)S(1)} %shard_map.104.refs_6_.refs_4_), channel_id=1, source_target_pairs={{0,4},{4,0},{8,12},{12,8},{16,20},{20,16},{24,28},{28,24},{1,5},{5... | collective-permute-start | bytes 798728 | tf_op jit(solution)/shard_map/ppermute | solution.py:629
  31.2 4.0 %collective-permute-start.9 = (f32[16,256]{1,0:T(8,128)S(1)}, f32[16,256]{1,0:T(8,128)S(1)}, u32[]{:S(2)}, u32[]{:S(2)}) collective-permute-start(f32[16,256]{1,0:T(8,128)S(1)} %get-tuple-element.50.refs_7_.refs_0_), channel_id=1, source_target_pairs={{0,1},{1,0},{2,3},{3,2},{4,5},{5,4},{6,7},{7,6},{8,9},{9,8},{10,11... | collective-permute-start | bytes 49160 | tf_op jit(solution)/shard_map/ppermute | solution.py:651
  37.6 4.8 %collective-permute-start.10 = (f32[256,768]{1,0:T(8,128)S(1)}, f32[256,768]{1,0:T(8,128)S(1)}, u32[]{:S(2)}, u32[]{:S(2)}) collective-permute-start(f32[256,768]{1,0:T(8,128)S(1)} %get-tuple-element.56), channel_id=1, source_target_pairs={{0,4},{4,0},{8,12},{12,8},{16,20},{20,16},{24,28},{28,24},{1,5},{5... | collective-permute-start | bytes 2359304 | tf_op jit(solution)/shard_map/ppermute | solution.py:629
  37.7 4.7 %collective-permute-start.11 = (f32[16,256]{1,0:T(8,128)S(1)}, f32[16,256]{1,0:T(8,128)S(1)}, u32[]{:S(2)}, u32[]{:S(2)}) collective-permute-start(f32[16,256]{1,0:T(8,128)S(1)} %shard_map.108.refs_6_.refs_9_), channel_id=1, source_target_pairs={{0,2},{1,3},{2,0},{3,1},{4,6},{5,7},{6,4},{7,5},{8,10},{9,11},{10,... | collective-permute-start | bytes 49160 | tf_op jit(solution)/shard_map/ppermute | solution.py:651
  40.4 2.1 %copy-start.5 = (f32[1024]{0:T(1024)S(1)}, f32[1024]{0:T(1024)}, u32[]{:S(2)}) copy-start(f32[1024]{0:T(1024)} %param.12) | copy-start | bytes 12292

commit v14 on v13

--- a/solution.py
+++ b/solution.py
@@ -432,22 +432,26 @@
     ]
 
 
-def later_stage(me, distance, heads, kv, q_terms, acc, peak, total, after, parts=4):
+def later_stage(me, distance, heads, kv, q_terms, acc, peak, total, after, keep, parts=4):
     fresh = not isinstance(kv, tuple)
     operands = [kv] if fresh else list(kv)
     shift = 1 + len(operands)
     out_shape = [jax.ShapeDtypeStruct(acc.shape, F32)] * 3
-    if fresh:
+    scratch = []
+    if fresh and keep:
         out_shape += term_shapes(kv.shape[1])
+    elif fresh:
+        scratch = [pltpu.VMEM(each.shape, each.dtype) for each in term_shapes(kv.shape[1])]
     out = call(
         functools.partial(later_kernel, distance, parts, heads, fresh),
         [SMEM] + [VMEM] * (len(operands) + 4),
         [VMEM] * len(out_shape),
         out_shape,
+        scratch,
         alias={shift + 1: 0, shift + 2: 1, shift + 3: 2},
         after=after,
     )(me, *operands, q_terms, acc, peak, total)
-    return out[:3], tuple(out[3:]) if fresh else kv
+    return out[:3], tuple(out[3:])
 
 
 def last_kernel(distance, whose, heads, columns, me_ref, *refs):
@@ -653,8 +657,8 @@
     def sent(distance, array):
         return across(array, distance, lambda c, e: c ^ distance < c)
 
-    def stage(kv, distance, heads, carried, after):
-        return later_stage(me_flag, distance, heads, kv, q_terms, *carried, after)
+    def stage(kv, distance, heads, carried, after, keep=False):
+        return later_stage(me_flag, distance, heads, kv, q_terms, *carried, after, keep)
 
     bits = chips.bit_length() - 1
     arrived, token = {}, inside
@@ -685,7 +689,7 @@
     left = [1] if square else range(bits + 1, chips - 1)
     for distance in left[:-1]:
         carried, _ = stage(arrived[distance], distance, all_heads, carried, [prefix])
-    carried, kept = stage(arrived[left[-1]], left[-1], front, carried, [prefix])
+    carried, kept = stage(arrived[left[-1]], left[-1], front, carried, [prefix], True)
     linear, energy = linear_blocks(
         me_flag, terms, inside, sums, prefix, prefix_other, others, [carried[0]]
     )
@@ -696,6 +700,7 @@
     other = exchanged(energy, energies[0])
     carried, _ = stage(kept, left[-1], back, carried, [energy])
     operands = [q_terms, *carried]
+    split_at = 2 * group // 3
     for step in energies[1:]:
         energy = plus(energy, other, [carried[0]])
         other = exchanged(energy, step)
@@ -703,11 +708,11 @@
     theirs, *kept = last_stage(
         me_flag, chips - 1, "other", all_heads, arrived[chips - 1], operands, [energy]
     )
-    (done,) = last_stage(me_flag, chips - 1, "own", front, kept, operands, [])
+    (done,) = last_stage(me_flag, chips - 1, "own", all_heads[:split_at], kept, operands, [])
     columns = q_lin.shape[1] * heads
     more = [swap(theirs), done, energy, other, lin_gain.reshape(1, -1), linear]
     return tuple(
-        last_stage(me_flag, chips - 1, "own", back, kept, operands, [], (columns, more))
+        last_stage(me_flag, chips - 1, "own", all_heads[split_at:], kept, operands, [], (columns, more))
     )
 
 

time: 45 us -> 44 us (0.978)
  Pallas kernels: 22.9 us -> 22.3 us
    pallas_call x17, Pallas kernels: 22.9 us -> 22.3 us  [call(): return lambda *operands: made(*operands, *after)]
where the time goes in v14:
time: 44 us; the launch traced here: 43.8 us
  Pallas kernels  22.3 us (51%)
  starting transfers between devices  10.9 us (25%)
  waiting for transfers between devices  7.9 us (18%)
  other arithmetic  1.31 us (3%)
  between operations  1.07 us (2%)
    pallas_call x17, Pallas kernels, call(): return lambda *operands: made(*operands, *after)  22.3 us
    ppermute x4, waiting for transfers between devices, across(): return lax.ppermute(array, 'ctx', pairs)  7.36 us
    ppermute x4, starting transfers between devices, across(): return lax.ppermute(array, 'ctx', pairs)  4.46 us
    ppermute x2, starting transfers between devices, exchanged(): return lax.ppermute(array, 'head', [(i, i ^ step) for i in range(heads)])  4.24 us
    another operation x2, other arithmetic, halves(): jnp.stack([jnp.where(core == 0, b, a) for a, b in zip(early, late)])  1.3 us
    ppermute x1, starting transfers between devices, body(): arrived[3] = lax.ppermute(relay, 'ctx', [(0, 6), (2, 4), (5, 7), (7, 5)])  1.29 us
  transfers between devices with their start and end apart: 12, of which 3 were waited for; matrix products, arithmetic and copies ran while one was open for 0% of the time, Pallas kernels for 41%

profile of v14, /device:TPU:6, one launch (start us, length us, event | category | flops | bytes accessed | tf_op | source)
XLA Modules:
  0.0 43.8 jit_solution(17978137434271401558)
XLA Ops:
  0.6 0.0 copy-start.2
  0.6 0.0 copy-start.1
  0.7 0.0 copy-start.4
  0.7 1.3 %select_bitcast_fusion = (f32[1,256,128]{2,1,0:T(8,128)S(1)}, f32[1,256,128]{2,1,0:T(8,128)S(1)}, f32[1,256,128]{2,1,0:T(8,128)S(1)}, f32[1,256,128]{2,1,0:T(8,128)S(1)}) fusion(f32[256,256]{1,0:T(8,128)} %param.15, pred[]{:T(512)S(6)} %eq.2, f32[256,256]{1,0:T(8,128)} %param.14), kind=kLoop, calls=%fused_computation.2 | loop fusion | flops 131072 | bytes 1048577 | tf_op jit(solution)/shard_map/stack | solution.py:256
  2.0 0.0 copy-start
  2.0 0.1 collective-permute-start
  2.1 0.0 copy-done.2
  2.1 0.3 copy-done.1
  2.4 0.0 copy-done.4
  2.4 0.9 %shard_map.95 = (f32[2,520,128]{2,1,0:T(8,128)S(1)}, f32[8,256]{1,0:T(8,128)S(1)}) custom-call(f32[8,256]{1,0:T(8,128)S(1)} %copy-done.4, f32[256,1024]{1,0:T(8,128)S(1)} %copy-done.1, f32[256,1024]{1,0:T(8,128)S(1)} %copy-done.2, f32[2,256,128]{2,1,0:T(8,128)S(1)} %pad_maximum_fusion.refs_3_.refs_1_), custom_call_target="tpu_custom_call" | custom-call | flops 1 | bytes 1 | tf_op jit(solution)/shard_map/pallas_call | solution.py:59
  3.3 0.3 collective-permute-start.3
  3.6 0.0 collective-permute-done.refs_2_
  3.6 0.0 copy-done
  3.6 0.1 shard_map.96
  3.7 0.0 copy-start.3
  3.8 0.4 collective-permute-start.2
  4.1 1.3 %collective-permute-start.1 = (f32[2,512,128]{2,1,0:T(8,128)S(1)}, f32[2,512,128]{2,1,0:T(8,128)S(1)}, u32[]{:S(2)}, u32[]{:S(2)}) collective-permute-start(f32[2,512,128]{2,1,0:T(8,128)S(1)} %get-tuple-element.31.refs_0_.refs_3_.refs_1_), channel_id=1, source_target_pairs={{0,16},{4,20},{8,24},{12,28},{1,17},{5,21},{9,25},{13,29},{2,18},{... | collective-permute-start | bytes 1572872 | tf_op jit(solution)/shard_map/ppermute | solution.py:642
  5.4 0.0 collective-permute-done.3.refs_2_.refs_6_
  5.5 0.6 %collective-permute-start.6 = (f32[520,128]{1,0:T(8,128)S(1)}, f32[520,128]{1,0:T(8,128)S(1)}, u32[]{:S(2)}, u32[]{:S(2)}) collective-permute-start(f32[520,128]{1,0:T(8,128)S(1)} %shard_map.97.refs_4_.refs_1_), channel_id=1, source_target_pairs={{8,0},{12,4},{0,8},{4,12},{24,16},{28,20},{16,24},{20,28},{9,1},{1... | collective-permute-start | bytes 798728 | tf_op jit(solution)/shard_map/ppermute | solution.py:642
  6.1 0.0 copy-done.3
  6.1 1.7 %shard_map.98 = (f32[8,256,128]{2,1,0:T(8,128)S(1)}, bf16[8,256,256]{2,1,0:T(8,128)(2,1)S(1)}) custom-call(f32[256,1024]{1,0:T(8,128)S(1)} %copy-done.3, f32[256,1024]{1,0:T(8,128)S(1)} %copy-done.1, f32[256,1024]{1,0:T(8,128)S(1)} %copy-done.2, f32[8,256]{1,0:T(8,128)S(1)} %get-tuple-element.30.refs_4_.refs_3_, f32[520,128]{1,0:T(8,128)S(1)} %shard_map.97.refs_4_.refs_1_), custom_call_target="tpu_custom_call" | custom-call | flops 1 | bytes 1 | tf_op jit(solution)/shard_map/pallas_call | solution.py:59
  7.9 1.3 %collective-permute-start.5 = (f32[2,512,128]{2,1,0:T(8,128)S(1)}, f32[2,512,128]{2,1,0:T(8,128)S(1)}, u32[]{:S(2)}, u32[]{:S(2)}) collective-permute-start(f32[2,512,128]{2,1,0:T(8,128)S(1)} %shard_map.99.refs_4_), channel_id=1, source_target_pairs={{0,8},{4,12},{16,24},{20,28},{1,9},{5,13},{17,25},{21,29},{2,10},{... | collective-permute-start | bytes 1572872 | tf_op jit(solution)/shard_map/ppermute | solution.py:642
  9.2 0.0 collective-permute-done.2.refs_2_
  9.2 2.9 %shard_map.100 = (bf16[6,512,256]{2,1,0:T(8,128)(2,1)S(1)}, f32[6,512,128]{2,1,0:T(8,128)S(1)}, f32[6,512,128]{2,1,0:T(8,128)S(1)}, f32[6,512,128]{2,1,0:T(8,128)S(1)}) custom-call(s32[1]{0:T(128)} %bitcast.refs_0_, f32[256,1536]{1,0:T(8,128)S(1)} %copy-done, f32[6,256,128]{2,1,0:T(8,128)S(1)} %collective-permute-done.2.refs_2_, ...), custom_call_target="tpu_custom_call" | custom-call | flops 1 | bytes 1 | tf_op jit(solution)/shard_map/pallas_call | solution.py:59
  12.1 2.7 %collective-permute-done.6.refs_2_ = f32[520,128]{1,0:T(8,128)S(1)} collective-permute-done((f32[520,128]{1,0:T(8,128)S(1)}, f32[520,128]{1,0:T(8,128)S(1)}, u32[]{:S(2)}, u32[]{:S(2)}) %collective-permute-start.6) | collective-permute-done | bytes 266272 | tf_op jit(solution)/shard_map/ppermute | solution.py:642
  14.8 0.1 shard_map.102
  14.8 1.3 %collective-permute-start.7 = (f32[520,128]{1,0:T(8,128)S(1)}, f32[520,128]{1,0:T(8,128)S(1)}, u32[]{:S(2)}, u32[]{:S(2)}) collective-permute-start(f32[520,128]{1,0:T(8,128)S(1)} %get-tuple-element.43.refs_1_), channel_id=1, source_target_pairs={{0,16},{4,20},{8,24},{12,28},{1,17},{5,21},{9,25},{13,29},{2,18},{... | collective-permute-start | bytes 798728 | tf_op jit(solution)/shard_map/ppermute | solution.py:642
  16.1 4.6 %collective-permute-done.1.refs_2_.refs_1_ = f32[2,512,128]{2,1,0:T(8,128)S(1)} collective-permute-done((f32[2,512,128]{2,1,0:T(8,128)S(1)}, f32[2,512,128]{2,1,0:T(8,128)S(1)}, u32[]{:S(2)}, u32[]{:S(2)}) %collective-permute-start.1) | collective-permute-done | bytes 524320 | tf_op jit(solution)/shard_map/ppermute | solution.py:642
  20.8 1.3 %collective-permute-start.4 = (f32[2,512,128]{2,1,0:T(8,128)S(1)}, f32[2,512,128]{2,1,0:T(8,128)S(1)}, u32[]{:S(2)}, u32[]{:S(2)}) collective-permute-start(f32[2,512,128]{2,1,0:T(8,128)S(1)} %shard_map.101.refs_7_), channel_id=1, source_target_pairs={{0,24},{8,16},{20,28},{28,20},{1,25},{9,17},{21,29},{29,21},{2,26}... | collective-permute-start | bytes 1572872 | tf_op jit(solution)/shard_map/ppermute | solution.py:678
  22.1 4.4 %shard_map.103 = (f32[6,512,128]{2,1,0:T(8,128)S(1)}, f32[6,512,128]{2,1,0:T(8,128)S(1)}, f32[6,512,128]{2,1,0:T(8,128)S(1)}) custom-call(s32[1]{0:T(128)} %bitcast.refs_0_, f32[2,512,128]{2,1,0:T(8,128)S(1)} %collective-permute-done.1.refs_2_.refs_1_, ...), custom_call_target="tpu_custom_call", output_to_operand_aliasing={{0}: (3, {}), {1}: (4, {}), {2}: (5, {})} | custom-call | flops 1 | bytes 1 | tf_op jit(solution)/shard_map/pallas_call | solution.py:59
  26.5 0.0 collective-permute-done.5.refs_5_.refs_1_
  26.5 0.0 collective-permute-done.7.refs_2_
  26.6 0.1 collective-permute-start.8
  26.7 2.7 %shard_map.105 = (f32[6,512,128]{2,1,0:T(8,128)S(1)}, f32[6,512,128]{2,1,0:T(8,128)S(1)}, f32[6,512,128]{2,1,0:T(8,128)S(1)}, bf16[384,512]{1,0:T(8,128)(2,1)S(1)}, bf16[512,256]{1,0:T(8,128)(2,1)S(1)}) custom-call(s32[1]{0:T(128)} %bitcast.refs_0_, ...), custom_call_target="tpu_custom_call", output_to_operand_aliasing={{0}: (3, {}), {1}: (4, {}), {2}: (5, {})} | custom-call | flops 1 | bytes 1 | tf_op jit(solution)/shard_map/pallas_call | solution.py:59
  29.4 0.0 collective-permute-done.8.refs_5_
  29.4 1.0 %shard_map.106 = (f32[256,1024]{1,0:T(8,128)S(1)}, f32[16,256]{1,0:T(8,128)S(1)}) custom-call(s32[1]{0:T(128)} %bitcast.refs_0_, bf16[8,256,256]{2,1,0:T(8,128)(2,1)S(1)} %get-tuple-element.49.refs_1_, f32[8,256,128]{2,1,0:T(8,128)S(1)} %get-tuple-element.34.refs_1_.refs_2_, f32[8,256]{1,0:T(8,128)S(1)} %get-tuple-element.30.refs_4_.refs_3_, ...), custom_call_target="tpu_custom_call" | custom-call | flops 1 | bytes 1 | tf_op jit(solution)/shard_map/pallas_call | solution.py:59
  30.4 1.6 %collective-permute-start.9 = (f32[16,256]{1,0:T(8,128)S(1)}, f32[16,256]{1,0:T(8,128)S(1)}, u32[]{:S(2)}, u32[]{:S(2)}) collective-permute-start(f32[16,256]{1,0:T(8,128)S(1)} %get-tuple-element.50.refs_7_.refs_0_), channel_id=1, source_target_pairs={{0,1},{1,0},{2,3},{3,2},{4,5},{5,4},{6,7},{7,6},{8,9},{9,8},{10,11... | collective-permute-start | bytes 49160 | tf_op jit(solution)/shard_map/ppermute | solution.py:655
  32.1 2.4 %shard_map.107 = (f32[6,512,128]{2,1,0:T(8,128)S(1)}, f32[6,512,128]{2,1,0:T(8,128)S(1)}, f32[6,512,128]{2,1,0:T(8,128)S(1)}) custom-call(s32[1]{0:T(128)} %bitcast.refs_0_, bf16[384,512]{1,0:T(8,128)(2,1)S(1)} %get-tuple-element.44.refs_1_, ...), custom_call_target="tpu_custom_call", output_to_operand_aliasing={{0}: (4, {}), {1}: (5, {}), {2}: (6, {})} | custom-call | flops 1 | bytes 1 | tf_op jit(solution)/shard_map/pallas_call | solution.py:59
  34.5 0.0 collective-permute-done.9.refs_1_
  34.5 0.0 collective-permute-done.4.refs_1_
  34.5 2.4 %shard_map.109 = (f32[256,768]{1,0:T(8,128)S(1)}, bf16[384,512]{1,0:T(8,128)(2,1)S(1)}, bf16[512,256]{1,0:T(8,128)(2,1)S(1)}) custom-call(s32[1]{0:T(128)} %bitcast.refs_0_, f32[2,512,128]{2,1,0:T(8,128)S(1)} %collective-permute-done.4.refs_1_, bf16[6,512,256]{2,1,0:T(8,128)(2,1)S(1)} %get-tuple-element.36.refs_2_.refs_3_, ...), custom_call_target="tpu_custom_call" | custom-call | flops 1 | bytes 1 | tf_op jit(solution)/shard_map/pallas_call | solution.py:59
  36.9 0.1 collective-permute-start.10
  37.0 2.6 %collective-permute-start.11 = (f32[16,256]{1,0:T(8,128)S(1)}, f32[16,256]{1,0:T(8,128)S(1)}, u32[]{:S(2)}, u32[]{:S(2)}) collective-permute-start(f32[16,256]{1,0:T(8,128)S(1)} %shard_map.108.refs_6_.refs_9_), channel_id=1, source_target_pairs={{0,2},{1,3},{2,0},{3,1},{4,6},{5,7},{6,4},{7,5},{8,10},{9,11},{10,... | collective-permute-start | bytes 49160 | tf_op jit(solution)/shard_map/ppermute | solution.py:655
  39.7 0.0 copy-start.5
  39.7 1.5 %shard_map.110.refs_8_ = f32[256,512]{1,0:T(8,128)S(1)} custom-call(s32[1]{0:T(128)} %bitcast.refs_0_, bf16[384,512]{1,0:T(8,128)(2,1)S(1)} %get-tuple-element.54.refs_1_, bf16[512,256]{1,0:T(8,128)(2,1)S(1)} %get-tuple-element.55.refs_2_, bf16[6,512,256]{2,1,0:T(8,128)(2,1)S(1)} %get-tuple-element.36.refs_2_.refs_3_, ...), custom_call_target="tpu_custom_call" | custom-call | flops 1 | bytes 1 | tf_op jit(solution)/shard_map/pallas_call | solution.py:59
  41.2 0.5 %collective-permute-done.11.refs_10_ = f32[16,256]{1,0:T(8,128)S(1)} collective-permute-done((f32[16,256]{1,0:T(8,128)S(1)}, f32[16,256]{1,0:T(8,128)S(1)}, u32[]{:S(2)}, u32[]{:S(2)}) %collective-permute-start.11) | collective-permute-done | bytes 16416 | tf_op jit(solution)/shard_map/ppermute | solution.py:655
  41.7 0.0 collective-permute-done.10.refs_7_
  41.7 0.0 copy-done.5
  41.7 1.9 %shard_map.111 = (f32[256,1024]{1,0:T(8,128)}, f32[256,1536]{1,0:T(8,128)}) custom-call(s32[1]{0:T(128)} %bitcast.refs_0_, bf16[384,512]{1,0:T(8,128)(2,1)S(1)} %get-tuple-element.54.refs_1_, bf16[512,256]{1,0:T(8,128)(2,1)S(1)} %get-tuple-element.55.refs_2_, bf16[6,512,256]{2,1,0:T(8,128)(2,1)S(1)} %get-tuple-element.36.refs_2_.refs_3_, ...), custom_call_target="tpu_custom_call" | custom-call | flops 1 | bytes 1 | tf_op jit(solution)/shard_map/pallas_call | solution.py:59
  (7 shorter events, 0.2 us)
Async XLA Ops:
  0.6 1.5 %copy-start.2 = (f32[256,1024]{1,0:T(8,128)S(1)}, f32[256,1024]{1,0:T(8,128)}, u32[]{:S(2)}) copy-start(f32[256,1024]{1,0:T(8,128)} %refs_2_.3) | copy-start | bytes 3145732
  0.6 1.8 %copy-start.1 = (f32[256,1024]{1,0:T(8,128)S(1)}, f32[256,1024]{1,0:T(8,128)}, u32[]{:S(2)}) copy-start(f32[256,1024]{1,0:T(8,128)} %refs_1_.4) | copy-start | bytes 3145732
  0.7 1.8 %copy-start.4 = (f32[8,256]{1,0:T(8,128)S(1)}, f32[8,256]{1,0:T(8,128)}, u32[]{:S(2)}) copy-start(f32[8,256]{1,0:T(8,128)} %refs_0_.2) | copy-start | bytes 24580
  2.0 1.6 %copy-start = (f32[256,1536]{1,0:T(8,128)S(1)}, f32[256,1536]{1,0:T(8,128)}, u32[]{:S(2)}) copy-start(f32[256,1536]{1,0:T(8,128)} %refs_1_.5) | copy-start | bytes 4718596
  2.0 1.6 %collective-permute-start = (f32[2,256,128]{2,1,0:T(8,128)S(1)}, f32[2,256,128]{2,1,0:T(8,128)S(1)}, u32[]{:S(2)}, u32[]{:S(2)}) collective-permute-start(f32[2,256,128]{2,1,0:T(8,128)S(1)} %pad_maximum_fusion.1), channel_id=1, source_target_pairs={{0,4},{4,0},{8,12},{12,8},{16,20},{20,16},{24,28},{28,24},{1,5},{5... | collective-permute-start | bytes 786440 | tf_op jit(solution)/shard_map/ppermute | solution.py:633
  3.3 2.1 %collective-permute-start.3 = (f32[2,520,128]{2,1,0:T(8,128)S(1)}, f32[2,520,128]{2,1,0:T(8,128)S(1)}, u32[]{:S(2)}, u32[]{:S(2)}) collective-permute-start(f32[2,520,128]{2,1,0:T(8,128)S(1)} %get-tuple-element.33.refs_1_), channel_id=1, source_target_pairs={{0,4},{4,0},{8,12},{12,8},{16,20},{20,16},{24,28},{28,24},{1,5},{5... | collective-permute-start | bytes 1597448 | tf_op jit(solution)/shard_map/ppermute | solution.py:633
  3.7 2.4 %copy-start.3 = (f32[256,1024]{1,0:T(8,128)S(1)}, f32[256,1024]{1,0:T(8,128)}, u32[]{:S(2)}) copy-start(f32[256,1024]{1,0:T(8,128)} %refs_0_.3) | copy-start | bytes 3145732
  3.8 5.4 %collective-permute-start.2 = (f32[6,256,128]{2,1,0:T(8,128)S(1)}, f32[6,256,128]{2,1,0:T(8,128)S(1)}, u32[]{:S(2)}, u32[]{:S(2)}) collective-permute-start(f32[6,256,128]{2,1,0:T(8,128)S(1)} %get-tuple-element.32.refs_3_), channel_id=1, source_target_pairs={{0,4},{4,0},{8,12},{12,8},{16,20},{20,16},{24,28},{28,24},{1,5},{5... | collective-permute-start | bytes 2359304 | tf_op jit(solution)/shard_map/ppermute | solution.py:633
  4.1 16.6 %collective-permute-start.1 = (f32[2,512,128]{2,1,0:T(8,128)S(1)}, f32[2,512,128]{2,1,0:T(8,128)S(1)}, u32[]{:S(2)}, u32[]{:S(2)}) collective-permute-start(f32[2,512,128]{2,1,0:T(8,128)S(1)} %get-tuple-element.31.refs_0_.refs_3_.refs_1_), channel_id=1, source_target_pairs={{0,16},{4,20},{8,24},{12,28},{1,17},{5,21},{9,25},{13,29},{2,18},{... | collective-permute-start | bytes 1572872 | tf_op jit(solution)/shard_map/ppermute | solution.py:642
  5.5 9.3 %collective-permute-start.6 = (f32[520,128]{1,0:T(8,128)S(1)}, f32[520,128]{1,0:T(8,128)S(1)}, u32[]{:S(2)}, u32[]{:S(2)}) collective-permute-start(f32[520,128]{1,0:T(8,128)S(1)} %shard_map.97.refs_4_.refs_1_), channel_id=1, source_target_pairs={{8,0},{12,4},{0,8},{4,12},{24,16},{28,20},{16,24},{20,28},{9,1},{1... | collective-permute-start | bytes 798728 | tf_op jit(solution)/shard_map/ppermute | solution.py:642
  7.9 18.7 %collective-permute-start.5 = (f32[2,512,128]{2,1,0:T(8,128)S(1)}, f32[2,512,128]{2,1,0:T(8,128)S(1)}, u32[]{:S(2)}, u32[]{:S(2)}) collective-permute-start(f32[2,512,128]{2,1,0:T(8,128)S(1)} %shard_map.99.refs_4_), channel_id=1, source_target_pairs={{0,8},{4,12},{16,24},{20,28},{1,9},{5,13},{17,25},{21,29},{2,10},{... | collective-permute-start | bytes 1572872 | tf_op jit(solution)/shard_map/ppermute | solution.py:642
  14.8 11.7 %collective-permute-start.7 = (f32[520,128]{1,0:T(8,128)S(1)}, f32[520,128]{1,0:T(8,128)S(1)}, u32[]{:S(2)}, u32[]{:S(2)}) collective-permute-start(f32[520,128]{1,0:T(8,128)S(1)} %get-tuple-element.43.refs_1_), channel_id=1, source_target_pairs={{0,16},{4,20},{8,24},{12,28},{1,17},{5,21},{9,25},{13,29},{2,18},{... | collective-permute-start | bytes 798728 | tf_op jit(solution)/shard_map/ppermute | solution.py:642
  20.8 13.7 %collective-permute-start.4 = (f32[2,512,128]{2,1,0:T(8,128)S(1)}, f32[2,512,128]{2,1,0:T(8,128)S(1)}, u32[]{:S(2)}, u32[]{:S(2)}) collective-permute-start(f32[2,512,128]{2,1,0:T(8,128)S(1)} %shard_map.101.refs_7_), channel_id=1, source_target_pairs={{0,24},{8,16},{20,28},{28,20},{1,25},{9,17},{21,29},{29,21},{2,26}... | collective-permute-start | bytes 1572872 | tf_op jit(solution)/shard_map/ppermute | solution.py:678
  26.6 2.8 %collective-permute-start.8 = (f32[520,128]{1,0:T(8,128)S(1)}, f32[520,128]{1,0:T(8,128)S(1)}, u32[]{:S(2)}, u32[]{:S(2)}) collective-permute-start(f32[520,128]{1,0:T(8,128)S(1)} %shard_map.104.refs_6_.refs_4_), channel_id=1, source_target_pairs={{0,4},{4,0},{8,12},{12,8},{16,20},{20,16},{24,28},{28,24},{1,5},{5... | collective-permute-start | bytes 798728 | tf_op jit(solution)/shard_map/ppermute | solution.py:633
  30.4 4.0 %collective-permute-start.9 = (f32[16,256]{1,0:T(8,128)S(1)}, f32[16,256]{1,0:T(8,128)S(1)}, u32[]{:S(2)}, u32[]{:S(2)}) collective-permute-start(f32[16,256]{1,0:T(8,128)S(1)} %get-tuple-element.50.refs_7_.refs_0_), channel_id=1, source_target_pairs={{0,1},{1,0},{2,3},{3,2},{4,5},{5,4},{6,7},{7,6},{8,9},{9,8},{10,11... | collective-permute-start | bytes 49160 | tf_op jit(solution)/shard_map/ppermute | solution.py:655
  36.9 4.8 %collective-permute-start.10 = (f32[256,768]{1,0:T(8,128)S(1)}, f32[256,768]{1,0:T(8,128)S(1)}, u32[]{:S(2)}, u32[]{:S(2)}) collective-permute-start(f32[256,768]{1,0:T(8,128)S(1)} %get-tuple-element.56), channel_id=1, source_target_pairs={{0,4},{4,0},{8,12},{12,8},{16,20},{20,16},{24,28},{28,24},{1,5},{5... | collective-permute-start | bytes 2359304 | tf_op jit(solution)/shard_map/ppermute | solution.py:633
  37.0 4.7 %collective-permute-start.11 = (f32[16,256]{1,0:T(8,128)S(1)}, f32[16,256]{1,0:T(8,128)S(1)}, u32[]{:S(2)}, u32[]{:S(2)}) collective-permute-start(f32[16,256]{1,0:T(8,128)S(1)} %shard_map.108.refs_6_.refs_9_), channel_id=1, source_target_pairs={{0,2},{1,3},{2,0},{3,1},{4,6},{5,7},{6,4},{7,5},{8,10},{9,11},{10,... | collective-permute-start | bytes 49160 | tf_op jit(solution)/shard_map/ppermute | solution.py:655
  39.7 2.1 %copy-start.5 = (f32[1024]{0:T(1024)S(1)}, f32[1024]{0:T(1024)}, u32[]{:S(2)}) copy-start(f32[1024]{0:T(1024)} %param.12) | copy-start | bytes 12292

commit v15 on v14

--- a/solution.py
+++ b/solution.py
@@ -11,7 +11,7 @@
 HD = 128
 NEGATIVE = -1e30
 EPSILON = 1e-05
-ENERGY_ROWS = 16
+ENERGY_ROWS = 8
 F32 = jnp.float32
 BF16 = jnp.bfloat16
 NT = (((1,), (1,)), ((), ()))
@@ -700,7 +700,7 @@
     other = exchanged(energy, energies[0])
     carried, _ = stage(kept, left[-1], back, carried, [energy])
     operands = [q_terms, *carried]
-    split_at = 2 * group // 3
+    split_at = max(1, group - 1)
     for step in energies[1:]:
         energy = plus(energy, other, [carried[0]])
         other = exchanged(energy, step)

time: 44 us -> 44 us (level)
  transfers between devices with their start and end apart: 12 -> 12, of which waited for: 3 -> 3; matrix products, arithmetic and copies ran while one was open for 0% -> 0% of each run, Pallas kernels for 41% -> 42%
where the time goes in v15:
time: 44 us; the launch traced here: 43.6 us
  Pallas kernels  22.5 us (51%)
  starting transfers between devices  10.9 us (25%)
  waiting for transfers between devices  7.49 us (17%)
  other arithmetic  1.31 us (3%)
  between operations  1.07 us (2%)
    pallas_call x17, Pallas kernels, call(): return lambda *operands: made(*operands, *after)  22.5 us
    ppermute x4, waiting for transfers between devices, across(): return lax.ppermute(array, 'ctx', pairs)  7.36 us
    ppermute x4, starting transfers between devices, across(): return lax.ppermute(array, 'ctx', pairs)  4.46 us
    ppermute x2, starting transfers between devices, exchanged(): return lax.ppermute(array, 'head', [(i, i ^ step) for i in range(heads)])  4.25 us
    another operation x2, other arithmetic, halves(): jnp.stack([jnp.where(core == 0, b, a) for a, b in zip(early, late)])  1.3 us
    ppermute x1, starting transfers between devices, body(): arrived[3] = lax.ppermute(relay, 'ctx', [(0, 6), (2, 4), (5, 7), (7, 5)])  1.29 us
  transfers between devices with their start and end apart: 12, of which 3 were waited for; matrix products, arithmetic and copies ran while one was open for 0% of the time, Pallas kernels for 42%

profile of v15, /device:TPU:6, one launch (start us, length us, event | category | flops | bytes accessed | tf_op | source)
XLA Modules:
  0.0 43.6 jit_solution(11842575773039306129)
XLA Ops:
  0.6 0.0 copy-start.2
  0.6 0.0 copy-start.1
  0.7 0.0 copy-start.4
  0.7 1.3 %select_bitcast_fusion = (f32[1,256,128]{2,1,0:T(8,128)S(1)}, f32[1,256,128]{2,1,0:T(8,128)S(1)}, f32[1,256,128]{2,1,0:T(8,128)S(1)}, f32[1,256,128]{2,1,0:T(8,128)S(1)}) fusion(f32[256,256]{1,0:T(8,128)} %param.15, pred[]{:T(512)S(6)} %eq.2, f32[256,256]{1,0:T(8,128)} %param.14), kind=kLoop, calls=%fused_computation.2 | loop fusion | flops 131072 | bytes 1048577 | tf_op jit(solution)/shard_map/stack | solution.py:256
  2.0 0.0 copy-start
  2.0 0.1 collective-permute-start
  2.1 0.0 copy-done.2
  2.1 0.3 copy-done.1
  2.4 0.0 copy-done.4
  2.4 0.9 %shard_map.95 = (f32[2,520,128]{2,1,0:T(8,128)S(1)}, f32[8,256]{1,0:T(8,128)S(1)}) custom-call(f32[8,256]{1,0:T(8,128)S(1)} %copy-done.4, f32[256,1024]{1,0:T(8,128)S(1)} %copy-done.1, f32[256,1024]{1,0:T(8,128)S(1)} %copy-done.2, f32[2,256,128]{2,1,0:T(8,128)S(1)} %pad_maximum_fusion.refs_3_.refs_1_), custom_call_target="tpu_custom_call" | custom-call | flops 1 | bytes 1 | tf_op jit(solution)/shard_map/pallas_call | solution.py:59
  3.3 0.3 collective-permute-start.3
  3.6 0.0 collective-permute-done.refs_2_
  3.6 0.0 copy-done
  3.6 0.1 shard_map.96
  3.7 0.0 copy-start.3
  3.8 0.4 collective-permute-start.2
  4.1 1.3 %collective-permute-start.1 = (f32[2,512,128]{2,1,0:T(8,128)S(1)}, f32[2,512,128]{2,1,0:T(8,128)S(1)}, u32[]{:S(2)}, u32[]{:S(2)}) collective-permute-start(f32[2,512,128]{2,1,0:T(8,128)S(1)} %get-tuple-element.31.refs_0_.refs_3_.refs_1_), channel_id=1, source_target_pairs={{0,16},{4,20},{8,24},{12,28},{1,17},{5,21},{9,25},{13,29},{2,18},{... | collective-permute-start | bytes 1572872 | tf_op jit(solution)/shard_map/ppermute | solution.py:642
  5.4 0.0 collective-permute-done.3.refs_2_.refs_6_
  5.5 0.6 %collective-permute-start.6 = (f32[520,128]{1,0:T(8,128)S(1)}, f32[520,128]{1,0:T(8,128)S(1)}, u32[]{:S(2)}, u32[]{:S(2)}) collective-permute-start(f32[520,128]{1,0:T(8,128)S(1)} %shard_map.97.refs_4_.refs_1_), channel_id=1, source_target_pairs={{8,0},{12,4},{0,8},{4,12},{24,16},{28,20},{16,24},{20,28},{9,1},{1... | collective-permute-start | bytes 798728 | tf_op jit(solution)/shard_map/ppermute | solution.py:642
  6.1 0.0 copy-done.3
  6.1 1.7 %shard_map.98 = (f32[8,256,128]{2,1,0:T(8,128)S(1)}, bf16[8,256,256]{2,1,0:T(8,128)(2,1)S(1)}) custom-call(f32[256,1024]{1,0:T(8,128)S(1)} %copy-done.3, f32[256,1024]{1,0:T(8,128)S(1)} %copy-done.1, f32[256,1024]{1,0:T(8,128)S(1)} %copy-done.2, f32[8,256]{1,0:T(8,128)S(1)} %get-tuple-element.30.refs_4_.refs_3_, f32[520,128]{1,0:T(8,128)S(1)} %shard_map.97.refs_4_.refs_1_), custom_call_target="tpu_custom_call" | custom-call | flops 1 | bytes 1 | tf_op jit(solution)/shard_map/pallas_call | solution.py:59
  7.9 1.3 %collective-permute-start.5 = (f32[2,512,128]{2,1,0:T(8,128)S(1)}, f32[2,512,128]{2,1,0:T(8,128)S(1)}, u32[]{:S(2)}, u32[]{:S(2)}) collective-permute-start(f32[2,512,128]{2,1,0:T(8,128)S(1)} %shard_map.99.refs_4_), channel_id=1, source_target_pairs={{0,8},{4,12},{16,24},{20,28},{1,9},{5,13},{17,25},{21,29},{2,10},{... | collective-permute-start | bytes 1572872 | tf_op jit(solution)/shard_map/ppermute | solution.py:642
  9.2 0.0 collective-permute-done.2.refs_2_
  9.2 2.9 %shard_map.100 = (bf16[6,512,256]{2,1,0:T(8,128)(2,1)S(1)}, f32[6,512,128]{2,1,0:T(8,128)S(1)}, f32[6,512,128]{2,1,0:T(8,128)S(1)}, f32[6,512,128]{2,1,0:T(8,128)S(1)}) custom-call(s32[1]{0:T(128)} %bitcast.refs_0_, f32[256,1536]{1,0:T(8,128)S(1)} %copy-done, f32[6,256,128]{2,1,0:T(8,128)S(1)} %collective-permute-done.2.refs_2_, ...), custom_call_target="tpu_custom_call" | custom-call | flops 1 | bytes 1 | tf_op jit(solution)/shard_map/pallas_call | solution.py:59
  12.1 2.7 %collective-permute-done.6.refs_2_ = f32[520,128]{1,0:T(8,128)S(1)} collective-permute-done((f32[520,128]{1,0:T(8,128)S(1)}, f32[520,128]{1,0:T(8,128)S(1)}, u32[]{:S(2)}, u32[]{:S(2)}) %collective-permute-start.6) | collective-permute-done | bytes 266272 | tf_op jit(solution)/shard_map/ppermute | solution.py:642
  14.8 0.1 shard_map.102
  14.8 1.3 %collective-permute-start.7 = (f32[520,128]{1,0:T(8,128)S(1)}, f32[520,128]{1,0:T(8,128)S(1)}, u32[]{:S(2)}, u32[]{:S(2)}) collective-permute-start(f32[520,128]{1,0:T(8,128)S(1)} %get-tuple-element.43.refs_1_), channel_id=1, source_target_pairs={{0,16},{4,20},{8,24},{12,28},{1,17},{5,21},{9,25},{13,29},{2,18},{... | collective-permute-start | bytes 798728 | tf_op jit(solution)/shard_map/ppermute | solution.py:642
  16.1 4.6 %collective-permute-done.1.refs_2_.refs_1_ = f32[2,512,128]{2,1,0:T(8,128)S(1)} collective-permute-done((f32[2,512,128]{2,1,0:T(8,128)S(1)}, f32[2,512,128]{2,1,0:T(8,128)S(1)}, u32[]{:S(2)}, u32[]{:S(2)}) %collective-permute-start.1) | collective-permute-done | bytes 524320 | tf_op jit(solution)/shard_map/ppermute | solution.py:642
  20.8 1.3 %collective-permute-start.4 = (f32[2,512,128]{2,1,0:T(8,128)S(1)}, f32[2,512,128]{2,1,0:T(8,128)S(1)}, u32[]{:S(2)}, u32[]{:S(2)}) collective-permute-start(f32[2,512,128]{2,1,0:T(8,128)S(1)} %shard_map.101.refs_7_), channel_id=1, source_target_pairs={{0,24},{8,16},{20,28},{28,20},{1,25},{9,17},{21,29},{29,21},{2,26}... | collective-permute-start | bytes 1572872 | tf_op jit(solution)/shard_map/ppermute | solution.py:678
  22.1 4.4 %shard_map.103 = (f32[6,512,128]{2,1,0:T(8,128)S(1)}, f32[6,512,128]{2,1,0:T(8,128)S(1)}, f32[6,512,128]{2,1,0:T(8,128)S(1)}) custom-call(s32[1]{0:T(128)} %bitcast.refs_0_, f32[2,512,128]{2,1,0:T(8,128)S(1)} %collective-permute-done.1.refs_2_.refs_1_, ...), custom_call_target="tpu_custom_call", output_to_operand_aliasing={{0}: (3, {}), {1}: (4, {}), {2}: (5, {})} | custom-call | flops 1 | bytes 1 | tf_op jit(solution)/shard_map/pallas_call | solution.py:59
  26.5 0.0 collective-permute-done.5.refs_5_.refs_1_
  26.5 0.0 collective-permute-done.7.refs_2_
  26.6 0.1 collective-permute-start.8
  26.7 2.7 %shard_map.105 = (f32[6,512,128]{2,1,0:T(8,128)S(1)}, f32[6,512,128]{2,1,0:T(8,128)S(1)}, f32[6,512,128]{2,1,0:T(8,128)S(1)}, bf16[384,512]{1,0:T(8,128)(2,1)S(1)}, bf16[512,256]{1,0:T(8,128)(2,1)S(1)}) custom-call(s32[1]{0:T(128)} %bitcast.refs_0_, ...), custom_call_target="tpu_custom_call", output_to_operand_aliasing={{0}: (3, {}), {1}: (4, {}), {2}: (5, {})} | custom-call | flops 1 | bytes 1 | tf_op jit(solution)/shard_map/pallas_call | solution.py:59
  29.4 0.0 collective-permute-done.8.refs_5_
  29.4 1.0 %shard_map.106 = (f32[256,1024]{1,0:T(8,128)S(1)}, f32[8,256]{1,0:T(8,128)S(1)}) custom-call(s32[1]{0:T(128)} %bitcast.refs_0_, bf16[8,256,256]{2,1,0:T(8,128)(2,1)S(1)} %get-tuple-element.49.refs_1_, f32[8,256,128]{2,1,0:T(8,128)S(1)} %get-tuple-element.34.refs_1_.refs_2_, f32[8,256]{1,0:T(8,128)S(1)} %get-tuple-element.30.refs_4_.refs_3_, ...), custom_call_target="tpu_custom_call" | custom-call | flops 1 | bytes 1 | tf_op jit(solution)/shard_map/pallas_call | solution.py:59
  30.4 1.6 %collective-permute-start.9 = (f32[8,256]{1,0:T(8,128)S(1)}, f32[8,256]{1,0:T(8,128)S(1)}, u32[]{:S(2)}, u32[]{:S(2)}) collective-permute-start(f32[8,256]{1,0:T(8,128)S(1)} %get-tuple-element.50.refs_7_.refs_0_), channel_id=1, source_target_pairs={{0,1},{1,0},{2,3},{3,2},{4,5},{5,4},{6,7},{7,6},{8,9},{9,8},{10,11... | collective-permute-start | bytes 24584 | tf_op jit(solution)/shard_map/ppermute | solution.py:655
  32.0 2.4 %shard_map.107 = (f32[6,512,128]{2,1,0:T(8,128)S(1)}, f32[6,512,128]{2,1,0:T(8,128)S(1)}, f32[6,512,128]{2,1,0:T(8,128)S(1)}) custom-call(s32[1]{0:T(128)} %bitcast.refs_0_, bf16[384,512]{1,0:T(8,128)(2,1)S(1)} %get-tuple-element.44.refs_1_, ...), custom_call_target="tpu_custom_call", output_to_operand_aliasing={{0}: (4, {}), {1}: (5, {}), {2}: (6, {})} | custom-call | flops 1 | bytes 1 | tf_op jit(solution)/shard_map/pallas_call | solution.py:59
  34.4 0.0 collective-permute-done.9.refs_1_
  34.5 0.0 collective-permute-done.4.refs_1_
  34.5 2.4 %shard_map.109 = (f32[256,768]{1,0:T(8,128)S(1)}, bf16[384,512]{1,0:T(8,128)(2,1)S(1)}, bf16[512,256]{1,0:T(8,128)(2,1)S(1)}) custom-call(s32[1]{0:T(128)} %bitcast.refs_0_, f32[2,512,128]{2,1,0:T(8,128)S(1)} %collective-permute-done.4.refs_1_, bf16[6,512,256]{2,1,0:T(8,128)(2,1)S(1)} %get-tuple-element.36.refs_2_.refs_3_, ...), custom_call_target="tpu_custom_call" | custom-call | flops 1 | bytes 1 | tf_op jit(solution)/shard_map/pallas_call | solution.py:59
  36.9 0.1 collective-permute-start.10
  37.0 2.6 %collective-permute-start.11 = (f32[8,256]{1,0:T(8,128)S(1)}, f32[8,256]{1,0:T(8,128)S(1)}, u32[]{:S(2)}, u32[]{:S(2)}) collective-permute-start(f32[8,256]{1,0:T(8,128)S(1)} %shard_map.108.refs_6_.refs_9_), channel_id=1, source_target_pairs={{0,2},{1,3},{2,0},{3,1},{4,6},{5,7},{6,4},{7,5},{8,10},{9,11},{10,... | collective-permute-start | bytes 24584 | tf_op jit(solution)/shard_map/ppermute | solution.py:655
  39.6 0.0 copy-start.5
  39.6 1.8 %shard_map.110.refs_8_ = f32[256,640]{1,0:T(8,128)S(1)} custom-call(s32[1]{0:T(128)} %bitcast.refs_0_, bf16[384,512]{1,0:T(8,128)(2,1)S(1)} %get-tuple-element.54.refs_1_, bf16[512,256]{1,0:T(8,128)(2,1)S(1)} %get-tuple-element.55.refs_2_, bf16[6,512,256]{2,1,0:T(8,128)(2,1)S(1)} %get-tuple-element.36.refs_2_.refs_3_, ...), custom_call_target="tpu_custom_call" | custom-call | flops 1 | bytes 1 | tf_op jit(solution)/shard_map/pallas_call | solution.py:59
  41.5 0.1 collective-permute-done.11.refs_10_
  41.6 0.0 collective-permute-done.10.refs_7_
  41.6 0.0 copy-done.5
  41.6 1.8 %shard_map.111 = (f32[256,1024]{1,0:T(8,128)}, f32[256,1536]{1,0:T(8,128)}) custom-call(s32[1]{0:T(128)} %bitcast.refs_0_, bf16[384,512]{1,0:T(8,128)(2,1)S(1)} %get-tuple-element.54.refs_1_, bf16[512,256]{1,0:T(8,128)(2,1)S(1)} %get-tuple-element.55.refs_2_, bf16[6,512,256]{2,1,0:T(8,128)(2,1)S(1)} %get-tuple-element.36.refs_2_.refs_3_, ...), custom_call_target="tpu_custom_call" | custom-call | flops 1 | bytes 1 | tf_op jit(solution)/shard_map/pallas_call | solution.py:59
  (7 shorter events, 0.2 us)
Async XLA Ops:
  0.6 1.5 %copy-start.2 = (f32[256,1024]{1,0:T(8,128)S(1)}, f32[256,1024]{1,0:T(8,128)}, u32[]{:S(2)}) copy-start(f32[256,1024]{1,0:T(8,128)} %refs_2_.3) | copy-start | bytes 3145732
  0.6 1.8 %copy-start.1 = (f32[256,1024]{1,0:T(8,128)S(1)}, f32[256,1024]{1,0:T(8,128)}, u32[]{:S(2)}) copy-start(f32[256,1024]{1,0:T(8,128)} %refs_1_.4) | copy-start | bytes 3145732
  0.7 1.8 %copy-start.4 = (f32[8,256]{1,0:T(8,128)S(1)}, f32[8,256]{1,0:T(8,128)}, u32[]{:S(2)}) copy-start(f32[8,256]{1,0:T(8,128)} %refs_0_.2) | copy-start | bytes 24580
  2.0 1.6 %copy-start = (f32[256,1536]{1,0:T(8,128)S(1)}, f32[256,1536]{1,0:T(8,128)}, u32[]{:S(2)}) copy-start(f32[256,1536]{1,0:T(8,128)} %refs_1_.5) | copy-start | bytes 4718596
  2.0 1.6 %collective-permute-start = (f32[2,256,128]{2,1,0:T(8,128)S(1)}, f32[2,256,128]{2,1,0:T(8,128)S(1)}, u32[]{:S(2)}, u32[]{:S(2)}) collective-permute-start(f32[2,256,128]{2,1,0:T(8,128)S(1)} %pad_maximum_fusion.1), channel_id=1, source_target_pairs={{0,4},{4,0},{8,12},{12,8},{16,20},{20,16},{24,28},{28,24},{1,5},{5... | collective-permute-start | bytes 786440 | tf_op jit(solution)/shard_map/ppermute | solution.py:633
  3.3 2.1 %collective-permute-start.3 = (f32[2,520,128]{2,1,0:T(8,128)S(1)}, f32[2,520,128]{2,1,0:T(8,128)S(1)}, u32[]{:S(2)}, u32[]{:S(2)}) collective-permute-start(f32[2,520,128]{2,1,0:T(8,128)S(1)} %get-tuple-element.33.refs_1_), channel_id=1, source_target_pairs={{0,4},{4,0},{8,12},{12,8},{16,20},{20,16},{24,28},{28,24},{1,5},{5... | collective-permute-start | bytes 1597448 | tf_op jit(solution)/shard_map/ppermute | solution.py:633
  3.7 2.4 %copy-start.3 = (f32[256,1024]{1,0:T(8,128)S(1)}, f32[256,1024]{1,0:T(8,128)}, u32[]{:S(2)}) copy-start(f32[256,1024]{1,0:T(8,128)} %refs_0_.3) | copy-start | bytes 3145732
  3.8 5.4 %collective-permute-start.2 = (f32[6,256,128]{2,1,0:T(8,128)S(1)}, f32[6,256,128]{2,1,0:T(8,128)S(1)}, u32[]{:S(2)}, u32[]{:S(2)}) collective-permute-start(f32[6,256,128]{2,1,0:T(8,128)S(1)} %get-tuple-element.32.refs_3_), channel_id=1, source_target_pairs={{0,4},{4,0},{8,12},{12,8},{16,20},{20,16},{24,28},{28,24},{1,5},{5... | collective-permute-start | bytes 2359304 | tf_op jit(solution)/shard_map/ppermute | solution.py:633
  4.1 16.6 %collective-permute-start.1 = (f32[2,512,128]{2,1,0:T(8,128)S(1)}, f32[2,512,128]{2,1,0:T(8,128)S(1)}, u32[]{:S(2)}, u32[]{:S(2)}) collective-permute-start(f32[2,512,128]{2,1,0:T(8,128)S(1)} %get-tuple-element.31.refs_0_.refs_3_.refs_1_), channel_id=1, source_target_pairs={{0,16},{4,20},{8,24},{12,28},{1,17},{5,21},{9,25},{13,29},{2,18},{... | collective-permute-start | bytes 1572872 | tf_op jit(solution)/shard_map/ppermute | solution.py:642
  5.5 9.3 %collective-permute-start.6 = (f32[520,128]{1,0:T(8,128)S(1)}, f32[520,128]{1,0:T(8,128)S(1)}, u32[]{:S(2)}, u32[]{:S(2)}) collective-permute-start(f32[520,128]{1,0:T(8,128)S(1)} %shard_map.97.refs_4_.refs_1_), channel_id=1, source_target_pairs={{8,0},{12,4},{0,8},{4,12},{24,16},{28,20},{16,24},{20,28},{9,1},{1... | collective-permute-start | bytes 798728 | tf_op jit(solution)/shard_map/ppermute | solution.py:642
  7.9 18.7 %collective-permute-start.5 = (f32[2,512,128]{2,1,0:T(8,128)S(1)}, f32[2,512,128]{2,1,0:T(8,128)S(1)}, u32[]{:S(2)}, u32[]{:S(2)}) collective-permute-start(f32[2,512,128]{2,1,0:T(8,128)S(1)} %shard_map.99.refs_4_), channel_id=1, source_target_pairs={{0,8},{4,12},{16,24},{20,28},{1,9},{5,13},{17,25},{21,29},{2,10},{... | collective-permute-start | bytes 1572872 | tf_op jit(solution)/shard_map/ppermute | solution.py:642
  14.8 11.7 %collective-permute-start.7 = (f32[520,128]{1,0:T(8,128)S(1)}, f32[520,128]{1,0:T(8,128)S(1)}, u32[]{:S(2)}, u32[]{:S(2)}) collective-permute-start(f32[520,128]{1,0:T(8,128)S(1)} %get-tuple-element.43.refs_1_), channel_id=1, source_target_pairs={{0,16},{4,20},{8,24},{12,28},{1,17},{5,21},{9,25},{13,29},{2,18},{... | collective-permute-start | bytes 798728 | tf_op jit(solution)/shard_map/ppermute | solution.py:642
  20.8 13.7 %collective-permute-start.4 = (f32[2,512,128]{2,1,0:T(8,128)S(1)}, f32[2,512,128]{2,1,0:T(8,128)S(1)}, u32[]{:S(2)}, u32[]{:S(2)}) collective-permute-start(f32[2,512,128]{2,1,0:T(8,128)S(1)} %shard_map.101.refs_7_), channel_id=1, source_target_pairs={{0,24},{8,16},{20,28},{28,20},{1,25},{9,17},{21,29},{29,21},{2,26}... | collective-permute-start | bytes 1572872 | tf_op jit(solution)/shard_map/ppermute | solution.py:678
  26.6 2.8 %collective-permute-start.8 = (f32[520,128]{1,0:T(8,128)S(1)}, f32[520,128]{1,0:T(8,128)S(1)}, u32[]{:S(2)}, u32[]{:S(2)}) collective-permute-start(f32[520,128]{1,0:T(8,128)S(1)} %shard_map.104.refs_6_.refs_4_), channel_id=1, source_target_pairs={{0,4},{4,0},{8,12},{12,8},{16,20},{20,16},{24,28},{28,24},{1,5},{5... | collective-permute-start | bytes 798728 | tf_op jit(solution)/shard_map/ppermute | solution.py:633
  30.4 4.0 %collective-permute-start.9 = (f32[8,256]{1,0:T(8,128)S(1)}, f32[8,256]{1,0:T(8,128)S(1)}, u32[]{:S(2)}, u32[]{:S(2)}) collective-permute-start(f32[8,256]{1,0:T(8,128)S(1)} %get-tuple-element.50.refs_7_.refs_0_), channel_id=1, source_target_pairs={{0,1},{1,0},{2,3},{3,2},{4,5},{5,4},{6,7},{7,6},{8,9},{9,8},{10,11... | collective-permute-start | bytes 24584 | tf_op jit(solution)/shard_map/ppermute | solution.py:655
  36.9 4.7 %collective-permute-start.10 = (f32[256,768]{1,0:T(8,128)S(1)}, f32[256,768]{1,0:T(8,128)S(1)}, u32[]{:S(2)}, u32[]{:S(2)}) collective-permute-start(f32[256,768]{1,0:T(8,128)S(1)} %get-tuple-element.56), channel_id=1, source_target_pairs={{0,4},{4,0},{8,12},{12,8},{16,20},{20,16},{24,28},{28,24},{1,5},{5... | collective-permute-start | bytes 2359304 | tf_op jit(solution)/shard_map/ppermute | solution.py:633
  37.0 4.6 %collective-permute-start.11 = (f32[8,256]{1,0:T(8,128)S(1)}, f32[8,256]{1,0:T(8,128)S(1)}, u32[]{:S(2)}, u32[]{:S(2)}) collective-permute-start(f32[8,256]{1,0:T(8,128)S(1)} %shard_map.108.refs_6_.refs_9_), channel_id=1, source_target_pairs={{0,2},{1,3},{2,0},{3,1},{4,6},{5,7},{6,4},{7,5},{8,10},{9,11},{10,... | collective-permute-start | bytes 24584 | tf_op jit(solution)/shard_map/ppermute | solution.py:655
  39.6 2.0 %copy-start.5 = (f32[1024]{0:T(1024)S(1)}, f32[1024]{0:T(1024)}, u32[]{:S(2)}) copy-start(f32[1024]{0:T(1024)} %param.12) | copy-start | bytes 12292
